TPU v7x, 32 devices: a whole 2x2x4 slice. The times are simulated.
32 devices in a mesh: dp: 16 (over z, y, x), mp: 2 (over core).
Axes of the slice: x: 2, y: 2, z: 4, core: 2. Of those that a mesh axis runs over, the one named last changes fastest.
Arguments:
- pixels: bfloat16 [32768, 768], P('dp'), may hold values from -6 to 6
- target: bfloat16 [32768, 768], P('dp'), may hold values from -6 to 6
- band_ids: int32 [32768, 768], P('dp'), may hold values from 0 to 2, as said below
- kept_index: int32 [128, 64], P('dp'), may hold values from 0 to 255, as said below
- intersection: int32 [128, 256], P('dp'), may hold values 0 or 1
- gsd_scale: int32 [128], P('dp'), may hold values from 1 to 8
- enc_attn: float32 [4, 1024, 1024], P(None, 'dp', 'mp')
- enc_mlp: float32 [2, 1024, 4096], P(None, 'dp', 'mp'), may hold values from -0.1875 to 0.1875
- dec_attn: float32 [4, 512, 512], P(None, 'dp', 'mp')
- dec_mlp: float32 [2, 512, 2048], P(None, 'dp', 'mp'), may hold values from -0.25 to 0.25
- patch_embed: float32 [768, 1024], P(None, 'dp'), may hold values from -0.21875 to 0.21875
- bridge: float32 [1024, 512], P('dp'), may hold values from -0.1875 to 0.1875
- predict: float32 [512, 768], P('dp'), may hold values from -0.25 to 0.25
- vectors: float32 [11520], P('dp')
- first_enc_attn: float32 [4, 1024, 1024], P(None, 'dp', 'mp'), may hold values from -7.4505806e-08 to 7.4505806e-08
- first_enc_mlp: float32 [2, 1024, 4096], P(None, 'dp', 'mp'), may hold values from -7.4505806e-08 to 7.4505806e-08
- first_dec_attn: float32 [4, 512, 512], P(None, 'dp', 'mp'), may hold values from -7.4505806e-08 to 7.4505806e-08
- first_dec_mlp: float32 [2, 512, 2048], P(None, 'dp', 'mp'), may hold values from -7.4505806e-08 to 7.4505806e-08
- first_patch_embed: float32 [768, 1024], P(None, 'dp'), may hold values from -7.4505806e-08 to 7.4505806e-08
- first_bridge: float32 [1024, 512], P('dp'), may hold values from -7.4505806e-08 to 7.4505806e-08
- first_predict: float32 [512, 768], P('dp'), may hold values from -7.4505806e-08 to 7.4505806e-08
- first_vectors: float32 [11520], P('dp'), may hold values from -2.3841858e-07 to 2.3841858e-07
- second_enc_attn: float32 [4, 1024, 1024], P(None, 'dp', 'mp'), may hold values from 2.2930394e-18 to 9.1721575e-18
- second_enc_mlp: float32 [2, 1024, 4096], P(None, 'dp', 'mp'), may hold values from 2.2930394e-18 to 9.1721575e-18
- second_dec_attn: float32 [4, 512, 512], P(None, 'dp', 'mp'), may hold values from 2.2930394e-18 to 9.1721575e-18
- second_dec_mlp: float32 [2, 512, 2048], P(None, 'dp', 'mp'), may hold values from 2.2930394e-18 to 9.1721575e-18
- second_patch_embed: float32 [768, 1024], P(None, 'dp'), may hold values from 2.2930394e-18 to 9.1721575e-18
- second_bridge: float32 [1024, 512], P('dp'), may hold values from 2.2930394e-18 to 9.1721575e-18
- second_predict: float32 [512, 768], P('dp'), may hold values from 2.2930394e-18 to 9.1721575e-18
- second_vectors: float32 [11520], P('dp'), may hold values from 2.2930395e-17 to 9.172158e-17
- ema_enc_attn: float32 [4, 1024, 1024], P(None, 'dp', 'mp'), may hold values from -0.1875 to 0.1875
- ema_enc_mlp: float32 [2, 1024, 4096], P(None, 'dp', 'mp'), may hold values from -0.1875 to 0.1875
- ema_patch_embed: float32 [768, 1024], P(None, 'dp'), may hold values from -0.21875 to 0.21875
Outputs:
- loss: float32 [], replicated
- band_weight: float32 [3], replicated
- grad_norm: float32 [], replicated
- next_enc_attn: float32 [4, 1024, 1024], P(None, 'dp', 'mp')
- next_enc_mlp: float32 [2, 1024, 4096], P(None, 'dp', 'mp')
- next_dec_attn: float32 [4, 512, 512], P(None, 'dp', 'mp')
- next_dec_mlp: float32 [2, 512, 2048], P(None, 'dp', 'mp')
- next_patch_embed: float32 [768, 1024], P(None, 'dp')
- next_bridge: float32 [1024, 512], P('dp')
- next_predict: float32 [512, 768], P('dp')
- next_vectors: float32 [11520], P('dp')
- next_first_enc_attn: float32 [4, 1024, 1024], P(None, 'dp', 'mp')
- next_first_enc_mlp: float32 [2, 1024, 4096], P(None, 'dp', 'mp')
- next_first_dec_attn: float32 [4, 512, 512], P(None, 'dp', 'mp')
- next_first_dec_mlp: float32 [2, 512, 2048], P(None, 'dp', 'mp')
- next_first_patch_embed: float32 [768, 1024], P(None, 'dp')
- next_first_bridge: float32 [1024, 512], P('dp')
- next_first_predict: float32 [512, 768], P('dp')
- next_first_vectors: float32 [11520], P('dp')
- next_second_enc_attn: float32 [4, 1024, 1024], P(None, 'dp', 'mp')
- next_second_enc_mlp: float32 [2, 1024, 4096], P(None, 'dp', 'mp')
- next_second_dec_attn: float32 [4, 512, 512], P(None, 'dp', 'mp')
- next_second_dec_mlp: float32 [2, 512, 2048], P(None, 'dp', 'mp')
- next_second_patch_embed: float32 [768, 1024], P(None, 'dp')
- next_second_bridge: float32 [1024, 512], P('dp')
- next_second_predict: float32 [512, 768], P('dp')
- next_second_vectors: float32 [11520], P('dp')
- next_ema_enc_attn: float32 [4, 1024, 1024], P(None, 'dp', 'mp')
- next_ema_enc_mlp: float32 [2, 1024, 4096], P(None, 'dp', 'mp')
- next_ema_patch_embed: float32 [768, 1024], P(None, 'dp')
Inputs may be any that keep to these rules, and one draw needn't show every extreme that they name: `kept_index`: each row names 64 different patches of its image. `band_ids`: the first 3 pixels of every patch are of bands 0, 1, 2 in that order.
All inputs are finite; a program needn't handle non-finite values. No bound on the sum of `intersection` on one device may be relied on, other than what follows from the above.
Results may differ from a plain program's by a relative error of at most 0.0082.
Values may be sent and summed in bfloat16 or wider, within the bound.
A program may use at most 256 MiB of HBM per device.

v0:
```python
import jax
import jax.numpy as jnp
from jax import lax
from jax.sharding import PartitionSpec as P

D = 1024
DH = 64
E = 512
DDH = 32
GRID = 16
NB = 3
STEP = 10


EPS_LN = 1e-06
EPS_C = 0.01
CLIP = 0.0002
BETA_ONE = 0.9
BETA_TWO = 0.999
ADAM_EPS = 1e-12
RATE_MAT = 0.06
RATE_VEC = 0.5
DECAY_MAT = 0.05
EMA_KEEP = 0.9
REF_GSD = 4.0


def layer_norm(token_rows, gain_vec, bias_vec):
    centred = token_rows - jnp.mean(token_rows, axis=-1, keepdims=True)
    spread = jnp.mean(centred * centred, axis=-1, keepdims=True)
    return centred * lax.rsqrt(spread + EPS_LN) * gain_vec + bias_vec


def position_table(gsd_values, feature_width, grid_side):
    positions = jnp.arange(grid_side * grid_side, dtype=jnp.int32)
    row_pos = (positions // grid_side).astype(jnp.float32)
    col_pos = (positions % grid_side).astype(jnp.float32)
    quarter = feature_width // 4
    frequency = jnp.exp(-jnp.log(10000.0) * jnp.arange(quarter).astype(jnp.float32) / quarter)
    gsd_ratio = gsd_values.astype(jnp.float32)[:, None, None] / REF_GSD
    row_arg = row_pos[None, :, None] * gsd_ratio * frequency
    col_arg = col_pos[None, :, None] * gsd_ratio * frequency
    return jnp.concatenate(
        [jnp.sin(row_arg), jnp.cos(row_arg), jnp.sin(col_arg), jnp.cos(col_arg)], axis=-1
    )


def split_vectors(flat_vec, enc_width, dec_width):
    lengths = [enc_width] * 7 + [dec_width] * 7
    pieces = []
    offset = 0
    for length in lengths:
        pieces.append(flat_vec[offset : offset + length])
        offset = offset + length
    pieces.append(flat_vec[offset:])
    return pieces


def plain_dot(left, right):
    return jnp.dot(left, right, preferred_element_type=jnp.float32)


def contract_rows(left, right):
    return lax.dot_general(
        left, right, (((0,), (0,)), ((), ())), preferred_element_type=jnp.float32
    )


def contract_cols(left, right):
    return lax.dot_general(
        left, right, (((1,), (1,)), ((), ())), preferred_element_type=jnp.float32
    )


def mp_total(partial_rows):
    return lax.psum(partial_rows.astype(jnp.bfloat16), "mp").astype(jnp.float32)


def mp_back(partial_rows):
    return lax.psum(partial_rows.astype(jnp.bfloat16), "mp").astype(jnp.float32)


def block_forward(token_rows, attn_stack, mlp_stack, norms, sequences, head_dim):
    gain_a, bias_a, gain_b, bias_b = norms
    row_count = token_rows.shape[0]
    local_width = attn_stack.shape[2]
    heads_here = local_width // head_dim
    normed_a = layer_norm(token_rows, gain_a, bias_a).astype(jnp.bfloat16)
    queries = (
        plain_dot(normed_a, attn_stack[0])
        .astype(jnp.bfloat16)
        .reshape(sequences, -1, heads_here, head_dim)
    )
    key_rows = (
        plain_dot(normed_a, attn_stack[1])
        .astype(jnp.bfloat16)
        .reshape(sequences, -1, heads_here, head_dim)
    )
    values = (
        plain_dot(normed_a, attn_stack[2])
        .astype(jnp.bfloat16)
        .reshape(sequences, -1, heads_here, head_dim)
    )
    scores = jnp.einsum(
        "bqhd,bkhd->bhqk", queries, key_rows, preferred_element_type=jnp.float32
    ) * head_dim ** (-0.5)
    row_top = jnp.max(scores, axis=-1, keepdims=True)
    log_total = row_top + jnp.log(jnp.sum(jnp.exp(scores - row_top), axis=-1, keepdims=True))
    weights_soft = jnp.exp(scores - log_total).astype(jnp.bfloat16)
    mixed = jnp.einsum("bhqk,bkhd->bqhd", weights_soft, values, preferred_element_type=jnp.float32)
    mixed = mixed.astype(jnp.bfloat16).reshape(row_count, local_width)
    after_attn = token_rows + mp_total(contract_cols(mixed, attn_stack[3]))
    normed_b = layer_norm(after_attn, gain_b, bias_b).astype(jnp.bfloat16)
    upward = plain_dot(normed_b, mlp_stack[0])
    hidden = jax.nn.gelu(upward).astype(jnp.bfloat16)
    result = after_attn + mp_total(contract_cols(hidden, mlp_stack[1]))
    saved = (
        token_rows,
        normed_a,
        queries,
        key_rows,
        values,
        log_total,
        mixed,
        after_attn,
        normed_b,
        upward,
        hidden,
    )
    return (result, saved)


def block_backward(grad_out, saved, attn_stack, mlp_stack, norms, sequences, head_dim):
    (
        token_rows,
        normed_a,
        queries,
        key_rows,
        values,
        log_total,
        mixed,
        after_attn,
        normed_b,
        upward,
        hidden,
    ) = saved
    gain_a, bias_a, gain_b, bias_b = norms
    row_count, local_width = mixed.shape
    heads_here = local_width // head_dim
    score_scale = head_dim ** (-0.5)
    grad_low = grad_out.astype(jnp.bfloat16)
    grad_down = contract_rows(grad_low, hidden)
    grad_hidden = plain_dot(grad_low, mlp_stack[1])
    _, gelu_back = jax.vjp(jax.nn.gelu, upward)
    grad_upward = gelu_back(grad_hidden)[0].astype(jnp.bfloat16)
    grad_up = contract_rows(normed_b, grad_upward)
    grad_normed_b = mp_back(contract_cols(grad_upward, mlp_stack[0]))
    _, norm_back_b = jax.vjp(layer_norm, after_attn, gain_b, bias_b)
    grad_after, grad_gain_b, grad_bias_b = norm_back_b(grad_normed_b)
    grad_after = grad_after + grad_out
    grad_attn_low = grad_after.astype(jnp.bfloat16)
    grad_out_proj = contract_rows(grad_attn_low, mixed)
    grad_mixed = plain_dot(grad_attn_low, attn_stack[3]).astype(jnp.bfloat16)
    grad_mixed = grad_mixed.reshape(sequences, -1, heads_here, head_dim)
    scores = (
        jnp.einsum("bqhd,bkhd->bhqk", queries, key_rows, preferred_element_type=jnp.float32)
        * score_scale
    )
    weights_soft = jnp.exp(scores - log_total)
    grad_values = (
        jnp.einsum(
            "bhqk,bqhd->bkhd",
            weights_soft.astype(jnp.bfloat16),
            grad_mixed,
            preferred_element_type=jnp.float32,
        )
        .astype(jnp.bfloat16)
        .reshape(row_count, local_width)
    )
    grad_soft = jnp.einsum(
        "bqhd,bkhd->bhqk", grad_mixed, values, preferred_element_type=jnp.float32
    )
    grad_scores = weights_soft * (
        grad_soft - jnp.sum(weights_soft * grad_soft, axis=-1, keepdims=True)
    )
    grad_scores = grad_scores.astype(jnp.bfloat16)
    grad_queries = (
        (
            jnp.einsum("bhqk,bkhd->bqhd", grad_scores, key_rows, preferred_element_type=jnp.float32)
            * score_scale
        )
        .astype(jnp.bfloat16)
        .reshape(row_count, local_width)
    )
    grad_keys = (
        (
            jnp.einsum("bhqk,bqhd->bkhd", grad_scores, queries, preferred_element_type=jnp.float32)
            * score_scale
        )
        .astype(jnp.bfloat16)
        .reshape(row_count, local_width)
    )
    grad_attn = jnp.stack(
        [
            contract_rows(normed_a, grad_queries),
            contract_rows(normed_a, grad_keys),
            contract_rows(normed_a, grad_values),
            grad_out_proj,
        ]
    )
    grad_normed_a = mp_back(
        contract_cols(grad_queries, attn_stack[0])
        + contract_cols(grad_keys, attn_stack[1])
        + contract_cols(grad_values, attn_stack[2])
    )
    _, norm_back_a = jax.vjp(layer_norm, token_rows, gain_a, bias_a)
    grad_rows, grad_gain_a, grad_bias_a = norm_back_a(grad_normed_a)
    return (
        grad_rows + grad_after,
        grad_attn,
        jnp.stack([grad_up, grad_down]),
        [grad_gain_a, grad_bias_a, grad_gain_b, grad_bias_b],
    )


def adam_update(master, gradient, first_old, second_old, step_rate, decay_rate):
    first_new = BETA_ONE * first_old + (1.0 - BETA_ONE) * gradient
    second_new = BETA_TWO * second_old + (1.0 - BETA_TWO) * gradient * gradient
    first_hat = first_new / (1.0 - BETA_ONE**STEP)
    second_hat = second_new / (1.0 - BETA_TWO**STEP)
    updated = master - step_rate * (
        first_hat / (jnp.sqrt(second_hat) + ADAM_EPS) + decay_rate * master
    )
    return (updated, first_new, second_new)


def per_device(
    pixels,
    target,
    band_ids,
    kept_index,
    intersection,
    gsd_scale,
    enc_attn,
    enc_mlp,
    dec_attn,
    dec_mlp,
    patch_embed,
    bridge,
    predict,
    vectors,
    first_enc_attn,
    first_enc_mlp,
    first_dec_attn,
    first_dec_mlp,
    first_patch_embed,
    first_bridge,
    first_predict,
    first_vectors,
    second_enc_attn,
    second_enc_mlp,
    second_dec_attn,
    second_dec_mlp,
    second_patch_embed,
    second_bridge,
    second_predict,
    second_vectors,
    ema_enc_attn,
    ema_enc_mlp,
    ema_patch_embed,
):
    masters = (enc_attn, enc_mlp, dec_attn, dec_mlp, patch_embed, bridge, predict, vectors)
    firsts = (
        first_enc_attn,
        first_enc_mlp,
        first_dec_attn,
        first_dec_mlp,
        first_patch_embed,
        first_bridge,
        first_predict,
        first_vectors,
    )
    seconds = (
        second_enc_attn,
        second_enc_mlp,
        second_dec_attn,
        second_dec_mlp,
        second_patch_embed,
        second_bridge,
        second_predict,
        second_vectors,
    )
    gathered = (
        lax.all_gather(enc_attn.astype(jnp.bfloat16), "dp", axis=1, tiled=True),
        lax.all_gather(enc_mlp.astype(jnp.bfloat16), "dp", axis=1, tiled=True),
        lax.all_gather(dec_attn.astype(jnp.bfloat16), "dp", axis=1, tiled=True),
        lax.all_gather(dec_mlp.astype(jnp.bfloat16), "dp", axis=1, tiled=True),
        lax.all_gather(patch_embed.astype(jnp.bfloat16), "dp", axis=1, tiled=True),
        lax.all_gather(bridge.astype(jnp.bfloat16), "dp", axis=0, tiled=True),
        lax.all_gather(predict.astype(jnp.bfloat16), "dp", axis=0, tiled=True),
        lax.all_gather(vectors.astype(jnp.bfloat16), "dp", axis=0, tiled=True),
    )
    enc_attn_w, enc_mlp_w, dec_attn_w, dec_mlp_w, embed_w, bridge_w, predict_w, vector_low = (
        gathered
    )
    pieces = split_vectors(vector_low.astype(jnp.float32), D, E)
    images, keep_count = kept_index.shape
    patch_count = intersection.shape[1]
    patch_index = jnp.arange(patch_count, dtype=jnp.int32)
    kept_flags = jnp.any(kept_index[:, :, None] == patch_index[None, None, :], axis=1).astype(
        jnp.float32
    )
    patch_weight = ((1.0 - kept_flags) * (1.0 - 0.5 * intersection.astype(jnp.float32))).reshape(
        -1, 1
    )
    local_counts = jnp.stack(
        [
            jnp.sum(patch_weight * (band_ids == band_level).astype(jnp.float32))
            for band_level in range(NB)
        ]
    )
    band_weight = lax.psum(local_counts, "dp")
    inverse = 1.0 / band_weight
    band_scale = jnp.zeros(band_ids.shape, jnp.float32)
    for band_level in range(NB):
        band_scale = band_scale + jnp.where(band_ids == band_level, inverse[band_level], 0.0)
    pixel_weight = patch_weight * band_scale
    image_rows = jnp.arange(images, dtype=jnp.int32)[:, None]
    flat_index = (kept_index + patch_count * image_rows).reshape(-1)
    kept_pixels = pixels[flat_index]
    enc_pos = jnp.take_along_axis(
        position_table(gsd_scale, D, GRID), kept_index[:, :, None], axis=1
    ).reshape(-1, D)
    token_rows = plain_dot(kept_pixels, embed_w) + pieces[0] + enc_pos
    enc_out, enc_saved = block_forward(token_rows, enc_attn_w, enc_mlp_w, pieces[1:5], images, DH)
    final_enc = layer_norm(enc_out, pieces[5], pieces[6]).astype(jnp.bfloat16)
    latent = plain_dot(final_enc, bridge_w)
    canvas = jnp.broadcast_to(pieces[7], (images, patch_count, E))
    canvas = canvas.at[image_rows, kept_index].set(latent.reshape(images, keep_count, E))
    dec_rows = (canvas + position_table(gsd_scale, E, GRID)).reshape(-1, E)
    dec_out, dec_saved = block_forward(dec_rows, dec_attn_w, dec_mlp_w, pieces[8:12], images, DDH)
    final_dec = layer_norm(dec_out, pieces[12], pieces[13]).astype(jnp.bfloat16)
    predicted = plain_dot(final_dec, predict_w) + pieces[14]
    mismatch = predicted - target.astype(jnp.float32)
    smooth = jnp.sqrt(mismatch * mismatch + EPS_C)
    loss_local = jnp.sum(pixel_weight * smooth)
    loss = lax.psum(loss_local, "dp")
    grad_pred = pixel_weight * mismatch / smooth
    grad_pred_low = grad_pred.astype(jnp.bfloat16)
    grad_pbias = jnp.sum(grad_pred, axis=0)
    grad_predict = contract_rows(final_dec, grad_pred_low)
    grad_final_dec = contract_cols(grad_pred_low, predict_w)
    _, dec_norm_back = jax.vjp(layer_norm, dec_out, pieces[12], pieces[13])
    grad_dec_out, grad_dec_fg, grad_dec_fb = dec_norm_back(grad_final_dec)
    grad_dec_rows, grad_dec_attn, grad_dec_mlp, dec_norm_grads = block_backward(
        grad_dec_out, dec_saved, dec_attn_w, dec_mlp_w, pieces[8:12], images, DDH
    )
    grad_canvas = grad_dec_rows.reshape(images, patch_count, E)
    grad_mask = jnp.sum(grad_canvas * (1.0 - kept_flags)[:, :, None], axis=(0, 1))
    grad_latent = grad_canvas[image_rows, kept_index].reshape(-1, E).astype(jnp.bfloat16)
    grad_bridge = contract_rows(final_enc, grad_latent)
    grad_final_enc = contract_cols(grad_latent, bridge_w)
    _, enc_norm_back = jax.vjp(layer_norm, enc_out, pieces[5], pieces[6])
    grad_enc_out, grad_enc_fg, grad_enc_fb = enc_norm_back(grad_final_enc)
    grad_tokens, grad_enc_attn, grad_enc_mlp, enc_norm_grads = block_backward(
        grad_enc_out, enc_saved, enc_attn_w, enc_mlp_w, pieces[1:5], images, DH
    )
    grad_ebias = jnp.sum(grad_tokens, axis=0)
    grad_embed = contract_rows(kept_pixels, grad_tokens.astype(jnp.bfloat16))
    grad_vectors = jnp.concatenate(
        [grad_ebias]
        + enc_norm_grads
        + [grad_enc_fg, grad_enc_fb, grad_mask]
        + dec_norm_grads
        + [grad_dec_fg, grad_dec_fb, grad_pbias]
    )
    reduced = (
        lax.psum_scatter(grad_enc_attn, "dp", scatter_dimension=1, tiled=True),
        lax.psum_scatter(grad_enc_mlp, "dp", scatter_dimension=1, tiled=True),
        lax.psum_scatter(grad_dec_attn, "dp", scatter_dimension=1, tiled=True),
        lax.psum_scatter(grad_dec_mlp, "dp", scatter_dimension=1, tiled=True),
        lax.psum_scatter(grad_embed, "dp", scatter_dimension=1, tiled=True),
        lax.psum_scatter(grad_bridge, "dp", scatter_dimension=0, tiled=True),
        lax.psum_scatter(grad_predict, "dp", scatter_dimension=0, tiled=True),
        lax.psum_scatter(grad_vectors, "dp", scatter_dimension=0, tiled=True),
    )
    shares = (1.0, 1.0, 1.0, 1.0, 0.5, 0.5, 0.5, 0.5)
    squares = jnp.zeros((), jnp.float32)
    for position, gradient in enumerate(reduced):
        squares = squares + shares[position] * jnp.sum(gradient * gradient)
    total_squares = lax.psum(squares, ("dp", "mp"))
    grad_norm = jnp.sqrt(total_squares)
    factor = CLIP / jnp.maximum(grad_norm, CLIP)
    news, new_firsts, new_seconds = ([], [], [])
    for position, master in enumerate(masters):
        is_vec = position == 7
        updated, first_new, second_new = adam_update(
            master,
            reduced[position] * factor,
            firsts[position],
            seconds[position],
            RATE_VEC if is_vec else RATE_MAT,
            0.0 if is_vec else DECAY_MAT,
        )
        news.append(updated)
        new_firsts.append(first_new)
        new_seconds.append(second_new)
    ema_attn = EMA_KEEP * ema_enc_attn + (1.0 - EMA_KEEP) * news[0]
    ema_mlp = EMA_KEEP * ema_enc_mlp + (1.0 - EMA_KEEP) * news[1]
    ema_embed = EMA_KEEP * ema_patch_embed + (1.0 - EMA_KEEP) * news[4]
    return (
        loss,
        band_weight,
        grad_norm,
        news[0],
        news[1],
        news[2],
        news[3],
        news[4],
        news[5],
        news[6],
        news[7],
        new_firsts[0],
        new_firsts[1],
        new_firsts[2],
        new_firsts[3],
        new_firsts[4],
        new_firsts[5],
        new_firsts[6],
        new_firsts[7],
        new_seconds[0],
        new_seconds[1],
        new_seconds[2],
        new_seconds[3],
        new_seconds[4],
        new_seconds[5],
        new_seconds[6],
        new_seconds[7],
        ema_attn,
        ema_mlp,
        ema_embed,
    )


def solution(mesh):
    return jax.shard_map(
        per_device,
        mesh=mesh,
        in_specs=(
            P("dp", None),
            P("dp", None),
            P("dp", None),
            P("dp", None),
            P("dp", None),
            P("dp"),
            P(None, "dp", "mp"),
            P(None, "dp", "mp"),
            P(None, "dp", "mp"),
            P(None, "dp", "mp"),
            P(None, "dp"),
            P("dp", None),
            P("dp", None),
            P("dp"),
            P(None, "dp", "mp"),
            P(None, "dp", "mp"),
            P(None, "dp", "mp"),
            P(None, "dp", "mp"),
            P(None, "dp"),
            P("dp", None),
            P("dp", None),
            P("dp"),
            P(None, "dp", "mp"),
            P(None, "dp", "mp"),
            P(None, "dp", "mp"),
            P(None, "dp", "mp"),
            P(None, "dp"),
            P("dp", None),
            P("dp", None),
            P("dp"),
            P(None, "dp", "mp"),
            P(None, "dp", "mp"),
            P(None, "dp"),
        ),
        out_specs=(
            P(),
            P(),
            P(),
            P(None, "dp", "mp"),
            P(None, "dp", "mp"),
            P(None, "dp", "mp"),
            P(None, "dp", "mp"),
            P(None, "dp"),
            P("dp", None),
            P("dp", None),
            P("dp"),
            P(None, "dp", "mp"),
            P(None, "dp", "mp"),
            P(None, "dp", "mp"),
            P(None, "dp", "mp"),
            P(None, "dp"),
            P("dp", None),
            P("dp", None),
            P("dp"),
            P(None, "dp", "mp"),
            P(None, "dp", "mp"),
            P(None, "dp", "mp"),
            P(None, "dp", "mp"),
            P(None, "dp"),
            P("dp", None),
            P("dp", None),
            P("dp"),
            P(None, "dp", "mp"),
            P(None, "dp", "mp"),
            P(None, "dp"),
        ),
        check_vma=False,
    )
```

profile of v0, /device:TPU:0, one launch (start us, length us, event | category | flops | bytes accessed | tf_op | source)
XLA Modules:
  0.0 2094.7 jit_solution(16820811554584692181)
XLA Ops:
  18.9 14.7 multiply_sine_fusion.1
  48.3 80.0 %all-reduce = bf16[11520]{0:T(1024)(128)(2,1)S(1)} all-reduce(bf16[11520]{0:T(1024)(128)(2,1)S(1)} %dynamic-update-slice), channel_id=1, replica_groups=mesh['dp'=16,'mp'=2] {'dp'}, use_global_device_ids=true, to_apply=%add | all-reduce | flops 11520 | bytes 46080
  132.3 18.2 all-gather.9.cloned.1.call-done
  179.1 17.3 all-reduce.12.cloned.1.call-done
  199.0 115.0 %all-gather.11.cloned.1.call-done = bf16[2,1024,2048]{2,1,0:T(8,128)(2,1)} async-done(((bf16[2,64,2048]{2,1,0:T(8,128)(2,1)}), bf16[2,1024,2048]{2,1,0:T(8,128)(2,1)}) %all-gather.11.cloned.1.call-update) | async-done | bytes 8388624 | tf_op jit(solution)/shard_map/all_gather | solution.py:295
  345.8 56.3 %all-gather.13.cloned.1.call-done = bf16[1024,512]{1,0:T(8,128)(2,1)} async-done(((bf16[64,512]{1,0:T(8,128)(2,1)}), bf16[1024,512]{1,0:T(8,128)(2,1)}) %all-gather.13.cloned.1.call-update) | async-done | bytes 1048592 | tf_op jit(solution)/shard_map/all_gather | solution.py:299
  407.5 63.9 %scatter_fusion = f32[8,256,512]{2,1,0:T(8,128)} fusion(f32[8,256,512]{2,1,0:T(8,128)} %broadcast_in_dim.57, s32[512]{0:T(512)S(1)} %reshape.670, f32[512,512]{1,0:T(8,128)} %fusion.139), kind=kCustom, calls=%fused_computation.3 | custom fusion | bytes 3149824 | tf_op jit(solution)/shard_map/scatter | solution.py:339
  521.1 19.3 all-reduce.16.cloned.1.call-done
  546.6 59.5 %all-gather.17.cloned.1.call-done = bf16[2,512,1024]{2,1,0:T(8,128)(2,1)} async-done(((bf16[2,32,1024]{2,1,0:T(8,128)(2,1)}), bf16[2,512,1024]{2,1,0:T(8,128)(2,1)}) %all-gather.17.cloned.1.call-update) | async-done | bytes 2097168 | tf_op jit(solution)/shard_map/all_gather | solution.py:297
  628.9 39.0 %psum.77 = f32[3]{0:T(128)S(1)} all-reduce(f32[3]{0:T(128)S(1)} %pad_maximum_fusion.5), channel_id=1, replica_groups=mesh['dp'=16,'mp'=2] {'dp'}, use_global_device_ids=true, to_apply=%region_4.0 | all-reduce | flops 3 | bytes 24 | tf_op jit(solution)/shard_map/psum | solution.py:322
  668.5 42.7 %all_gather.31 = bf16[512,768]{1,0:T(8,128)(2,1)} all-gather(bf16[32,768]{1,0:T(8,128)(2,1)S(1)} %convert_element_type.322), channel_id=1, replica_groups=mesh['dp'=16,'mp'=2] {'dp'}, dimensions={0}, use_global_device_ids=true | all-gather | bytes 835584 | tf_op jit(solution)/shard_map/all_gather | solution.py:300
  718.4 12.8 fusion.125
  750.1 19.0 all-reduce.20.cloned.1.call-done
  803.8 12.2 multiply_convert_fusion
  826.6 22.4 %all-reduce.22.cloned.1.call-done = bf16[2048,512]{1,0:T(8,128)(2,1)} async-done(((bf16[2048,512]{1,0:T(8,128)(2,1)}), bf16[2048,512]{1,0:T(8,128)(2,1)}) %all-reduce.22.cloned.1.call-update) | async-done | bytes 2097168 | tf_op jit(solution)/shard_map/psum | solution.py:80
  884.6 20.8 all-reduce.24.cloned.1.call-done
  1019.8 81.2 %reduce-scatter.20.cloned.1.call-done = f32[32,768]{1,0:T(8,128)} async-done(((f32[512,768]{1,0:T(8,128)}), f32[32,768]{1,0:T(8,128)}) %reduce-scatter.20.cloned.1.call-update) | async-done | bytes 98320 | tf_op jit(solution)/shard_map/reduce_scatter | solution.py:384
  1105.5 75.7 %all-reduce.2 = (f32[]{:T(128)}, f32[11520]{0:T(1024)S(1)}) all-reduce(f32[]{:T(128)} %get-tuple-element.106, f32[11520]{0:T(1024)S(1)} %constant_dynamic-update-slice_fusion), channel_id=1, replica_groups=mesh['dp'=16,'mp'=2] {'dp'}, use_global_device_ids=true, to_apply=%region_27.28 | all-reduce | flops 11521 | bytes 92168 | tf_op jit(solution)/shard_map/psum | solution.py:347
  1184.6 78.4 %reduce-scatter.18.cloned.1.call-done = f32[64,512]{1,0:T(8,128)} async-done(((f32[1024,512]{1,0:T(8,128)}), f32[64,512]{1,0:T(8,128)}) %reduce-scatter.18.cloned.1.call-update) | async-done | bytes 131088 | tf_op jit(solution)/shard_map/reduce_scatter | solution.py:383
  1265.1 91.9 %reduce-scatter.14.cloned.1.call-done = f32[2,32,1024]{2,1,0:T(8,128)} async-done(((f32[2,512,1024]{2,1,0:T(8,128)}), f32[2,32,1024]{2,1,0:T(8,128)}) %reduce-scatter.14.cloned.1.call-update) | async-done | bytes 262160 | tf_op jit(solution)/shard_map/reduce_scatter | solution.py:381
  1358.8 133.3 %reduce-scatter.16.cloned.1.call-done = f32[768,64]{0,1:T(8,128)} async-done(((f32[768,1024]{0,1:T(8,128)}), f32[768,64]{0,1:T(8,128)}) %reduce-scatter.16.cloned.1.call-update) | async-done | bytes 196624 | tf_op jit(solution)/shard_map/reduce_scatter | solution.py:382
  1494.3 176.9 %reduce-scatter.8.cloned.1.call-done = f32[4,64,512]{2,1,0:T(8,128)} async-done(((f32[4,1024,512]{2,1,0:T(8,128)}), f32[4,64,512]{2,1,0:T(8,128)}) %reduce-scatter.8.cloned.1.call-update) | async-done | bytes 524304 | tf_op jit(solution)/shard_map/reduce_scatter | solution.py:378
  1673.0 349.4 %reduce-scatter.10.cloned.1.call-done = f32[2,64,2048]{2,1,0:T(8,128)} async-done(((f32[2,1024,2048]{2,1,0:T(8,128)}), f32[2,64,2048]{2,1,0:T(8,128)}) %reduce-scatter.10.cloned.1.call-update) | async-done | bytes 1048592 | tf_op jit(solution)/shard_map/reduce_scatter | solution.py:379
  2027.1 44.4 %psum.87 = f32[]{:T(128)} all-reduce(f32[]{:T(128)S(6)} %add.524), channel_id=1, replica_groups=mesh['dp'=16,'mp'=2] {'dp','mp'}, use_global_device_ids=true, to_apply=%region_77.78 | all-reduce | flops 1 | bytes 8 | tf_op jit(solution)/shard_map/psum | solution.py:391
  (579 shorter events, 425.0 us)
Async XLA Ops:
  7.2 121.1 %all-gather.7.cloned.1.call-start = ((), (), s32[]{:S(2)}) async-start(), calls=%async_computation.7 | async-start | bytes 1671168 | tf_op jit(solution)/shard_map/all_gather | solution.py:298
  9.0 141.5 %all-gather.9.cloned.1.call-start = ((), (), s32[]{:S(2)}) async-start(), calls=%async_computation.8 | async-start | bytes 4456448 | tf_op jit(solution)/shard_map/all_gather | solution.py:294
  10.9 185.5 %all-reduce.12.cloned.1.call-start = ((), (), s32[]{:S(2)}) async-start(), calls=%async_computation.9 | async-start | bytes 2097152 | tf_op jit(solution)/shard_map/psum | solution.py:76
  178.1 135.8 %all-gather.11.cloned.1.call-start = ((), (), s32[]{:S(2)}) async-start(), calls=%async_computation.10 | async-start | bytes 8912896 | tf_op jit(solution)/shard_map/all_gather | solution.py:295
  179.0 163.4 %all-reduce.14.cloned.1.call-start = ((), (), s32[]{:S(2)}) async-start(), calls=%async_computation.11 | async-start | bytes 2097152 | tf_op jit(solution)/shard_map/psum | solution.py:76
  324.5 77.6 %all-gather.13.cloned.1.call-start = ((), (), s32[]{:S(2)}) async-start(), calls=%async_computation.12 | async-start | bytes 1114112 | tf_op jit(solution)/shard_map/all_gather | solution.py:299
  325.2 152.7 %all-gather.15.cloned.1.call-start = ((), (), s32[]{:S(2)}) async-start(), calls=%async_computation.13 | async-start | bytes 1114112 | tf_op jit(solution)/shard_map/all_gather | solution.py:296
  326.0 214.5 %all-reduce.16.cloned.1.call-start = ((), (), s32[]{:S(2)}) async-start(), calls=%async_computation.14 | async-start | bytes 4194304 | tf_op jit(solution)/shard_map/psum | solution.py:76
  520.1 86.0 %all-gather.17.cloned.1.call-start = ((), (), s32[]{:S(2)}) async-start(), calls=%async_computation.15 | async-start | bytes 2228224 | tf_op jit(solution)/shard_map/all_gather | solution.py:297
  520.9 190.4 %all-reduce.18.cloned.1.call-start = ((), (), s32[]{:S(2)}) async-start(), calls=%async_computation.16 | async-start | bytes 4194304 | tf_op jit(solution)/shard_map/psum | solution.py:76
  618.5 150.6 %all-reduce.20.cloned.1.call-start = ((), (), s32[]{:S(2)}) async-start(), calls=%async_computation.17 | async-start | bytes 4194304 | tf_op jit(solution)/shard_map/psum | solution.py:80
  750.1 99.0 %all-reduce.22.cloned.1.call-start = ((), (), s32[]{:S(2)}) async-start(), calls=%async_computation.18 | async-start | bytes 4194304 | tf_op jit(solution)/shard_map/psum | solution.py:80
  826.5 78.9 %all-reduce.24.cloned.1.call-start = ((), (), s32[]{:S(2)}) async-start(), calls=%async_computation.19 | async-start | bytes 2097152 | tf_op jit(solution)/shard_map/psum | solution.py:80
  884.5 99.9 %all-reduce.26.cloned.1.call-start = ((), (), s32[]{:S(2)}) async-start(), calls=%async_computation.24 | async-start | bytes 2097152 | tf_op jit(solution)/shard_map/psum | solution.py:80
  949.6 151.4 %reduce-scatter.20.cloned.1.call-start = ((), (), s32[]{:S(2)}) async-start(), calls=%async_computation.27 | async-start | bytes 1671168 | tf_op jit(solution)/shard_map/reduce_scatter | solution.py:384
  956.2 226.8 %reduce-scatter.12.cloned.1.call-start = ((), (), s32[]{:S(2)}) async-start(), calls=%async_computation.22 | async-start | bytes 2228224 | tf_op jit(solution)/shard_map/reduce_scatter | solution.py:380
  965.0 298.0 %reduce-scatter.18.cloned.1.call-start = ((), (), s32[]{:S(2)}) async-start(), calls=%async_computation.26 | async-start | bytes 2228224 | tf_op jit(solution)/shard_map/reduce_scatter | solution.py:383
  968.2 388.8 %reduce-scatter.14.cloned.1.call-start = ((), (), s32[]{:S(2)}) async-start(), calls=%async_computation.23 | async-start | bytes 4456448 | tf_op jit(solution)/shard_map/reduce_scatter | solution.py:381
  984.0 508.0 %reduce-scatter.16.cloned.1.call-start = ((), (), s32[]{:S(2)}) async-start(), calls=%async_computation.25 | async-start | bytes 3342336 | tf_op jit(solution)/shard_map/reduce_scatter | solution.py:382
  995.5 675.7 %reduce-scatter.8.cloned.1.call-start = ((), (), s32[]{:S(2)}) async-start(), calls=%async_computation.20 | async-start | bytes 8912896 | tf_op jit(solution)/shard_map/reduce_scatter | solution.py:378
  1004.8 1017.6 %reduce-scatter.10.cloned.1.call-start = ((), (), s32[]{:S(2)}) async-start(), calls=%async_computation.21 | async-start | bytes 17825792 | tf_op jit(solution)/shard_map/reduce_scatter | solution.py:379
  1019.0 1053.3 %copy-start.123 = (f32[720]{0:T(1024)S(1)}, f32[720]{0:T(1024)}, u32[]{:S(2)}) copy-start(f32[720]{0:T(1024)} %param.46) | copy-start | bytes 8644
  1019.0 1054.0 %copy-start.87 = (f32[32,768]{1,0:T(8,128)S(1)}, f32[32,768]{1,0:T(8,128)}, u32[]{:S(2)}) copy-start(f32[32,768]{1,0:T(8,128)} %param.45) | copy-start | bytes 294916
  1019.0 1055.7 %copy-start.83 = (f32[64,512]{1,0:T(8,128)S(1)}, f32[64,512]{1,0:T(8,128)}, u32[]{:S(2)}) copy-start(f32[64,512]{1,0:T(8,128)} %param.44) | copy-start | bytes 393220
  (150 other events, 15609.8 us)
Sparse Core Ops, SparseCore 0:
  11.4 60.7 all-gather.6
  75.5 75.0 all-gather.8
  178.2 18.1 all-reduce.11
  200.0 113.8 all-gather.10
  324.6 17.7 all-reduce.13
  345.6 56.4 all-gather.12
  405.4 53.7 all-gather.14
  520.2 20.1 all-reduce.15
  544.2 61.8 all-gather.16
  618.6 19.7 all-reduce.17
  750.2 18.8 all-reduce.19
  826.7 22.3 all-reduce.21
  884.7 20.7 all-reduce.23
  949.7 20.7 all-reduce.25
  975.2 125.7 reduce-scatter.19
  1103.1 79.8 reduce-scatter.11
  1185.1 77.7 reduce-scatter.17
  1265.1 91.9 reduce-scatter.13
  1362.1 129.9 reduce-scatter.15
  1494.2 177.0 reduce-scatter.7
  1673.6 348.7 reduce-scatter.9
where the time goes:
time: 2110 us; the launch traced here: 2090 us
  waiting for transfers between devices  1270 us (60%)
  blocking collectives  282 us (13%)
  matrix products  196 us (9%)
  other arithmetic  168 us (8%)
  local copies, waits for them, and re-layouts  155 us (7%)
  between operations  25.5 us (1%)
    reduce_scatter x1, waiting for transfers between devices, per_device(): lax.psum_scatter(grad_enc_mlp, 'dp', scatter_dimension=1, tiled=True)  349 us
    reduce_scatter x1, waiting for transfers between devices, per_device(): lax.psum_scatter(grad_enc_attn, 'dp', scatter_dimension=1, tiled=True)  177 us
    reduce_scatter x1, waiting for transfers between devices, per_device(): lax.psum_scatter(grad_embed, 'dp', scatter_dimension=1, tiled=True)  133 us
    all_gather x1, waiting for transfers between devices, per_device(): lax.all_gather(enc_mlp.astype(jnp.bfloat16), 'dp', axis=1, tiled=True)  115 us
    reduce_scatter x1, waiting for transfers between devices, per_device(): lax.psum_scatter(grad_dec_mlp, 'dp', scatter_dimension=1, tiled=True)  91.9 us
    reduce_scatter x1, waiting for transfers between devices, per_device(): lax.psum_scatter(grad_predict, 'dp', scatter_dimension=0, tiled=True)  81.2 us
    unnamed x1, blocking collectives  80 us
    reduce_scatter x1, waiting for transfers between devices, per_device(): lax.psum_scatter(grad_bridge, 'dp', scatter_dimension=0, tiled=True)  78.4 us
  transfers between devices with their start and end apart: 21, of which 17 were waited for; matrix products, arithmetic and copies ran while one was open for 11% of the time, Pallas kernels for 0%

commit v1 on v0

--- a/solution.py
+++ b/solution.py
@@ -73,11 +73,67 @@
 
 
 def mp_total(partial_rows):
-    return lax.psum(partial_rows.astype(jnp.bfloat16), "mp").astype(jnp.float32)
-
-
-def mp_back(partial_rows):
-    return lax.psum(partial_rows.astype(jnp.bfloat16), "mp").astype(jnp.float32)
+    low = partial_rows.astype(jnp.bfloat16)
+    other = lax.ppermute(low, "mp", [(0, 1), (1, 0)])
+    return low.astype(jnp.float32) + other.astype(jnp.float32)
+
+
+mp_back = mp_total
+
+
+def dp_bits():
+    return lax.axis_size("dp").bit_length() - 1
+
+
+def orders():
+    bits = dp_bits()
+    high = list(range(bits - 1, 1, -1))
+    return (high + [0, 1], high + [1, 0])
+
+
+def swap(block, bit):
+    size = lax.axis_size("dp")
+    return lax.ppermute(block, "dp", [(i, i ^ (1 << bit)) for i in range(size)])
+
+
+def my_bit(bit):
+    return (lax.axis_index("dp") >> bit) & 1
+
+
+def gather_dp(block, axis, order):
+    lead, rest = (block.shape[:axis], block.shape[axis:])
+    done = []
+    cur = block
+    for bit in order:
+        other = swap(cur, bit)
+        mine = my_bit(bit) == 1
+        place = axis + sum(1 for b in done if b > bit)
+        cur = jnp.stack([jnp.where(mine, other, cur), jnp.where(mine, cur, other)], axis=place)
+        done.append(bit)
+    return cur.reshape(lead + (rest[0] * lax.axis_size("dp"),) + rest[1:])
+
+
+def reduce_dp(block, axis, order, wire):
+    bits = dp_bits()
+    lead, rest = (block.shape[:axis], block.shape[axis:])
+    shard = rest[0] // lax.axis_size("dp")
+    cur = block.reshape(lead + (2,) * bits + (shard,) + rest[1:])
+    left = list(range(bits - 1, -1, -1))
+    for bit in reversed(order):
+        place = axis + left.index(bit)
+        mine = my_bit(bit)
+        keep = lax.dynamic_index_in_dim(cur, mine, place, keepdims=False)
+        give = lax.dynamic_index_in_dim(cur, 1 - mine, place, keepdims=False)
+        other = swap(give.astype(wire), bit)
+        cur = keep + other.astype(jnp.float32)
+        left.remove(bit)
+    return cur
+
+
+def total_dp(value):
+    for bit in range(dp_bits()):
+        value = value + swap(value, bit)
+    return value
 
 
 def block_forward(token_rows, attn_stack, mlp_stack, norms, sequences, head_dim):
@@ -218,7 +274,7 @@
     return (
         grad_rows + grad_after,
         grad_attn,
-        jnp.stack([grad_up, grad_down]),
+        [grad_up, grad_down],
         [grad_gain_a, grad_bias_a, grad_gain_b, grad_bias_b],
     )
 
@@ -290,19 +346,24 @@
         second_predict,
         second_vectors,
     )
-    gathered = (
-        lax.all_gather(enc_attn.astype(jnp.bfloat16), "dp", axis=1, tiled=True),
-        lax.all_gather(enc_mlp.astype(jnp.bfloat16), "dp", axis=1, tiled=True),
-        lax.all_gather(dec_attn.astype(jnp.bfloat16), "dp", axis=1, tiled=True),
-        lax.all_gather(dec_mlp.astype(jnp.bfloat16), "dp", axis=1, tiled=True),
-        lax.all_gather(patch_embed.astype(jnp.bfloat16), "dp", axis=1, tiled=True),
-        lax.all_gather(bridge.astype(jnp.bfloat16), "dp", axis=0, tiled=True),
-        lax.all_gather(predict.astype(jnp.bfloat16), "dp", axis=0, tiled=True),
-        lax.all_gather(vectors.astype(jnp.bfloat16), "dp", axis=0, tiled=True),
-    )
-    enc_attn_w, enc_mlp_w, dec_attn_w, dec_mlp_w, embed_w, bridge_w, predict_w, vector_low = (
-        gathered
-    )
+    order_a, order_b = orders()
+    low = jnp.bfloat16
+    embed_w = gather_dp(patch_embed.astype(low).T, 0, order_a).T
+    vector_low = gather_dp(vectors.astype(low).reshape(1, -1), 0, order_b).reshape(-1)
+    enc_attn_w = jnp.concatenate([
+        gather_dp(enc_attn[:2].astype(low), 1, order_a),
+        gather_dp(enc_attn[2:].astype(low), 1, order_b)])
+    enc_mlp_w = [
+        gather_dp(enc_mlp[0].astype(low), 0, order_a),
+        gather_dp(enc_mlp[1].astype(low), 0, order_b)]
+    bridge_w = gather_dp(bridge.astype(low), 0, order_a)
+    dec_attn_w = jnp.concatenate([
+        gather_dp(dec_attn[:2].astype(low), 1, order_a),
+        gather_dp(dec_attn[2:].astype(low), 1, order_b)])
+    dec_mlp_w = [
+        gather_dp(dec_mlp[0].astype(low), 0, order_a),
+        gather_dp(dec_mlp[1].astype(low), 0, order_b)]
+    predict_w = gather_dp(predict.astype(low), 0, order_b)
     pieces = split_vectors(vector_low.astype(jnp.float32), D, E)
     images, keep_count = kept_index.shape
     patch_count = intersection.shape[1]
@@ -319,7 +380,7 @@
             for band_level in range(NB)
         ]
     )
-    band_weight = lax.psum(local_counts, "dp")
+    band_weight = total_dp(local_counts)
     inverse = 1.0 / band_weight
     band_scale = jnp.zeros(band_ids.shape, jnp.float32)
     for band_level in range(NB):
@@ -336,7 +397,10 @@
     final_enc = layer_norm(enc_out, pieces[5], pieces[6]).astype(jnp.bfloat16)
     latent = plain_dot(final_enc, bridge_w)
     canvas = jnp.broadcast_to(pieces[7], (images, patch_count, E))
-    canvas = canvas.at[image_rows, kept_index].set(latent.reshape(images, keep_count, E))
+    place = jnp.argmax(kept_index[:, :, None] == patch_index[None, None, :], axis=1)
+    spread_rows = jnp.take_along_axis(
+        latent.reshape(images, keep_count, E), place[:, :, None], axis=1)
+    canvas = jnp.where(kept_flags[:, :, None] > 0.5, spread_rows, canvas)
     dec_rows = (canvas + position_table(gsd_scale, E, GRID)).reshape(-1, E)
     dec_out, dec_saved = block_forward(dec_rows, dec_attn_w, dec_mlp_w, pieces[8:12], images, DDH)
     final_dec = layer_norm(dec_out, pieces[12], pieces[13]).astype(jnp.bfloat16)
@@ -344,7 +408,7 @@
     mismatch = predicted - target.astype(jnp.float32)
     smooth = jnp.sqrt(mismatch * mismatch + EPS_C)
     loss_local = jnp.sum(pixel_weight * smooth)
-    loss = lax.psum(loss_local, "dp")
+    loss = total_dp(loss_local)
     grad_pred = pixel_weight * mismatch / smooth
     grad_pred_low = grad_pred.astype(jnp.bfloat16)
     grad_pbias = jnp.sum(grad_pred, axis=0)
@@ -375,20 +439,29 @@
         + [grad_dec_fg, grad_dec_fb, grad_pbias]
     )
     reduced = (
-        lax.psum_scatter(grad_enc_attn, "dp", scatter_dimension=1, tiled=True),
-        lax.psum_scatter(grad_enc_mlp, "dp", scatter_dimension=1, tiled=True),
-        lax.psum_scatter(grad_dec_attn, "dp", scatter_dimension=1, tiled=True),
-        lax.psum_scatter(grad_dec_mlp, "dp", scatter_dimension=1, tiled=True),
-        lax.psum_scatter(grad_embed, "dp", scatter_dimension=1, tiled=True),
-        lax.psum_scatter(grad_bridge, "dp", scatter_dimension=0, tiled=True),
-        lax.psum_scatter(grad_predict, "dp", scatter_dimension=0, tiled=True),
-        lax.psum_scatter(grad_vectors, "dp", scatter_dimension=0, tiled=True),
+        jnp.concatenate([
+            reduce_dp(grad_enc_attn[:2], 1, order_a, low),
+            reduce_dp(grad_enc_attn[2:], 1, order_b, low)]),
+        jnp.stack([
+            reduce_dp(grad_enc_mlp[0], 0, order_a, low),
+            reduce_dp(grad_enc_mlp[1], 0, order_b, low)]),
+        jnp.concatenate([
+            reduce_dp(grad_dec_attn[:2], 1, order_a, low),
+            reduce_dp(grad_dec_attn[2:], 1, order_b, low)]),
+        jnp.stack([
+            reduce_dp(grad_dec_mlp[0], 0, order_a, low),
+            reduce_dp(grad_dec_mlp[1], 0, order_b, low)]),
+        reduce_dp(grad_embed.T, 0, order_a, low).T,
+        reduce_dp(grad_bridge, 0, order_a, low),
+        reduce_dp(grad_predict, 0, order_b, low),
+        reduce_dp(grad_vectors, 0, order_b, jnp.float32),
     )
     shares = (1.0, 1.0, 1.0, 1.0, 0.5, 0.5, 0.5, 0.5)
     squares = jnp.zeros((), jnp.float32)
     for position, gradient in enumerate(reduced):
         squares = squares + shares[position] * jnp.sum(gradient * gradient)
-    total_squares = lax.psum(squares, ("dp", "mp"))
+    total_squares = total_dp(squares)
+    total_squares = total_squares + lax.ppermute(total_squares, "mp", [(0, 1), (1, 0)])
     grad_norm = jnp.sqrt(total_squares)
     factor = CLIP / jnp.maximum(grad_norm, CLIP)
     news, new_firsts, new_seconds = ([], [], [])

time: 2110 us -> 1070 us (0.51)
  waiting for transfers between devices: 1270 us -> 335 us
  blocking collectives: 282 us -> 0 us
  starting transfers between devices: 1.9 us -> 127 us
  other arithmetic: 168 us -> 233 us
  matrix products: 196 us -> 160 us
  local copies, waits for them, and re-layouts: 155 us -> 181 us
    reduce_scatter x7 -> x0, waiting for transfers between devices: 911 us -> none  [the longest x1 349 us: per_device(): lax.psum_scatter(grad_enc_mlp, 'dp', scatter_dimension=1, tiled=True)]
    ppermute x0 -> x117, waiting for transfers between devices: none -> 335 us  [the longest x108 335 us: swap(): return lax.ppermute(block, 'dp', [(i, i ^ 1 << bit) for i in range(size)])]
    all_gather x6 -> x0, waiting for transfers between devices: 249 us -> none  [the longest x1 115 us: per_device(): lax.all_gather(enc_mlp.astype(jnp.bfloat16), 'dp', axis=1, tiled=True)]
    psum x3 -> x0, blocking collectives: 159 us -> none  [the longest x1 75.7 us: per_device(): loss = lax.psum(loss_local, 'dp')]
    ppermute x0 -> x117, starting transfers between devices: none -> 127 us  [the longest x108 126 us: swap(): return lax.ppermute(block, 'dp', [(i, i ^ 1 << bit) for i in range(size)])]
    psum x8 -> x0, waiting for transfers between devices: 106 us -> none  [the longest x4 62.3 us: mp_back(): return lax.psum(partial_rows.astype(jnp.bfloat16), 'mp').astype(jnp.float32)]
    unnamed x1 -> x0, blocking collectives: 80 us -> none
    scatter x1 -> x0, local copies, waits for them, and re-layouts: 63.9 us -> none  [per_device(): canvas.at[image_rows, kept_index].set(latent.reshape(images, keep_count, E))]
  transfers between devices with their start and end apart: 21 -> 117, of which waited for: 17 -> 70; matrix products, arithmetic and copies ran while one was open for 11% -> 37% of each run, Pallas kernels for 0% -> 0%
where the time goes in v1:
time: 1070 us; the launch traced here: 1060 us
  waiting for transfers between devices  335 us (31%)
  other arithmetic  233 us (22%)
  local copies, waits for them, and re-layouts  181 us (17%)
  matrix products  160 us (15%)
  starting transfers between devices  127 us (12%)
  between operations  19.3 us (2%)
    ppermute x108, waiting for transfers between devices, swap(): return lax.ppermute(block, 'dp', [(i, i ^ 1 << bit) for i in range(size)])  335 us
    ppermute x108, starting transfers between devices, swap(): return lax.ppermute(block, 'dp', [(i, i ^ 1 << bit) for i in range(size)])  126 us
    dot_general x15, matrix products, plain_dot(): return jnp.dot(left, right, preferred_element_type=jnp.float32)  47.8 us
    unnamed x578, local copies, waits for them, and re-layouts  36.3 us
    sin x3, other arithmetic, position_table(): jnp.sin(row_arg)  32.2 us
    another operation x93, other arithmetic, gather_dp(): jnp.stack([jnp.where(mine, other, cur), jnp.where(mine, cur, other)], axi...  31.9 us
    gather x2, local copies, waits for them, and re-layouts, per_device(): jnp.take_along_axis(latent.reshape(images, keep_count, E), place[:, :, No...  30.5 us
    dot_general x14, matrix products, contract_cols(): lax.dot_general(left, right, (((1,), (1,)), ((), ())), preferred_element_...  30.3 us
  transfers between devices with their start and end apart: 117, of which 70 were waited for; matrix products, arithmetic and copies ran while one was open for 37% of the time, Pallas kernels for 0%

profile of v1, /device:TPU:0, one launch (start us, length us, event | category | flops | bytes accessed | tf_op | source)
XLA Modules:
  0.0 1055.5 jit_solution(9609662525536303088)
XLA Ops:
  26.9 8.7 multiply_sine_fusion.3
  35.6 14.7 %multiply_sine_fusion.1 = (f32[8,256,256]{2,1,0:T(8,128)S(1)}, f32[8,256,256]{2,1,0:T(8,128)S(1)}, f32[8,256,256]{2,1,0:T(8,128)S(1)}, f32[8,256,256]{2,1,0:T(8,128)S(1)}) fusion(f32[256]{0:T(256)S(1)} %multiply_exponential_fusion, f32[8,256]{1,0:T(8,128)S(1)} %get-tuple-element.270, f32[8,256]{1,0:T(8,128)S(1)} %get-tuple-element.280), kind=kLoop, calls=%fused_computation.91 | loop fusion | flops 1048576 | bytes 8406016 | tf_op jit(solution)/shard_map/sin | solution.py:44
  50.3 8.9 multiply_sine_fusion.5
  90.1 10.5 gather_fusion.2
  112.5 11.0 %collective-permute-done.47 = bf16[32,1024]{1,0:T(8,128)(2,1)S(1)} collective-permute-done((bf16[32,1024]{1,0:T(8,128)(2,1)S(1)}, bf16[32,1024]{1,0:T(8,128)(2,1)S(1)}, u32[]{:S(2)}, u32[]{:S(2)}) %collective-permute-start.47) | collective-permute-done | bytes 65568 | tf_op jit(solution)/shard_map/ppermute | solution.py:96
  123.6 13.8 %collective-permute-done.34 = bf16[2,32,256]{2,1,0:T(8,128)(2,1)S(1)} collective-permute-done((bf16[2,32,256]{2,1,0:T(8,128)(2,1)S(1)}, bf16[2,32,256]{2,1,0:T(8,128)(2,1)S(1)}, u32[]{:S(2)}, u32[]{:S(2)}) %collective-permute-start.34) | collective-permute-done | bytes 32800 | tf_op jit(solution)/shard_map/ppermute | solution.py:96
  228.3 14.4 %collective-permute-done.7 = bf16[2,2,2,64,768]{4,3,2,1,0:T(8,128)(2,1)S(1)} collective-permute-done((bf16[2,2,2,64,768]{4,3,2,1,0:T(8,128)(2,1)S(1)}, bf16[2,2,2,64,768]{4,3,2,1,0:T(8,128)(2,1)S(1)}, u32[]{:S(2)}, u32[]{:S(2)}) %collective-permute-start.7) | collective-permute-done | bytes 786464 | tf_op jit(solution)/shard_map/ppermute | solution.py:96
  246.1 18.9 %collective-permute-done.27 = bf16[2,2,64,2048]{3,2,0,1:T(8,128)(2,1)S(1)} collective-permute-done((bf16[2,2,64,2048]{3,2,0,1:T(8,128)(2,1)S(1)}, bf16[2,2,64,2048]{3,2,0,1:T(8,128)(2,1)S(1)}, u32[]{:S(2)}, u32[]{:S(2)}) %collective-permute-start.27) | collective-permute-done | bytes 1048608 | tf_op jit(solution)/shard_map/ppermute | solution.py:96
  268.0 8.3 collective-permute-done.19
  328.7 36.6 %collective-permute-done.24 = bf16[2,2,2,64,2048]{4,3,2,1,0:T(8,128)(2,1)S(1)} collective-permute-done((bf16[2,2,2,64,2048]{4,3,2,1,0:T(8,128)(2,1)S(1)}, bf16[2,2,2,64,2048]{4,3,2,1,0:T(8,128)(2,1)S(1)}, u32[]{:S(2)}, u32[]{:S(2)}) %collective-permute-start.24) | collective-permute-done | bytes 2097184 | tf_op jit(solution)/shard_map/ppermute | solution.py:96
  385.2 25.1 %gather_fusion.3 = f32[2048,512]{1,0:T(8,128)} fusion(f32[8,64,512]{2,1,0:T(8,128)S(1)} %fusion.225, s32[2048]{0:T(1024)S(1)} %bitcast.777), kind=kCustom, calls=%fused_computation.3 | custom fusion | bytes 8404992 | tf_op jit(solution)/shard_map/jit(take_along_axis)/gather | solution.py:401
  444.9 9.3 exponential_reduce_fusion
  454.2 8.6 fusion.43
  473.1 8.7 collective-permute-done.46
  546.8 11.3 %fusion.209 = (f32[768]{0:T(1024)}, bf16[2048,768]{1,0:T(8,128)(2,1)S(1)}, f32[]{:T(128)}) fusion(bf16[2048,768]{1,0:T(8,128)(2,1)S(1)} %copy-done.260, f32[768]{0:T(1024)S(1)} %slice.206, pred[2048,768]{1,0:T(32,128)(4,1)S(1)} %copy-done.121, f32[]{:T(128)} %bitcast.5, pred[2048,768]{1,0:T(32,128)(4,1)S(1)} %copy-done.120, f32[]{:T(128)} %bitcast.4, ...), kind=kOutput, calls=%fused_computation.701 | convolution fusion | flops 1642593536 | bytes 16025616 | tf_op jit(solution)/shard_map/dot_general | solution.py:60
  578.8 7.4 fusion.85
  586.2 8.0 fusion.7
  607.4 9.4 collective-permute-done.56
  679.5 8.6 fusion.44
  688.1 11.4 %multiply_reduce_fusion = (f32[8,8,256]{2,1,0:T(8,128)S(1)}, f32[8,8,256,256]{2,3,1,0:T(8,128)}) fusion(f32[8,8,256,256]{2,3,1,0:T(8,128)} %get-tuple-element.289, f32[8,8,256]{2,1,0:T(8,128)S(1)} %log_add_fusion, bf16[8,256,8,32]{1,0,3,2:T(8,128)(2,1)S(1)} %bitcast.790, bf16[8,256,8,32]{1,0,3,2:T(8,128)(2,1)S(1)} %bitcast.792), kind=kOutput, calls=%fused_computation.5 | convolution fusion | flops 285196288 | bytes 35782656 | tf_op jit(solution)/shard_map/bqhd,bkhd->bhqk/dot_general | solution.py:236
  699.5 12.0 %multiply_convert_fusion = bf16[8,8,256,256]{2,3,1,0:T(8,128)(2,1)S(1)} fusion(f32[8,8,256,256]{2,3,1,0:T(8,128)} %get-tuple-element.291, f32[8,8,256,256]{2,3,1,0:T(8,128)} %get-tuple-element.289, f32[8,8,256]{2,1,0:T(8,128)S(1)} %get-tuple-element.290, f32[8,8,256]{2,1,0:T(8,128)S(1)} %log_add_fusion), kind=kLoop, calls=%fused_computation.4 | loop fusion | flops 20971520 | bytes 42074112 | tf_op jit(solution)/shard_map/convert_element_type | solution.py:242
  890.9 16.7 %collective-permute-done.108 = f32[2,2,2,720]{3,2,1,0:T(2,128)S(1)} collective-permute-done((f32[2,2,2,720]{3,2,1,0:T(2,128)S(1)}, f32[2,2,2,720]{3,2,1,0:T(2,128)S(1)}, u32[]{:S(2)}, u32[]{:S(2)}) %collective-permute-start.108) | collective-permute-done | bytes 23072 | tf_op jit(solution)/shard_map/ppermute | solution.py:96
  909.2 18.9 %collective-permute-done.109 = f32[2,2,720]{2,1,0:T(2,128)S(1)} collective-permute-done((f32[2,2,720]{2,1,0:T(2,128)S(1)}, f32[2,2,720]{2,1,0:T(2,128)S(1)}, u32[]{:S(2)}, u32[]{:S(2)}) %collective-permute-start.109) | collective-permute-done | bytes 11552 | tf_op jit(solution)/shard_map/ppermute | solution.py:96
  973.4 11.5 %collective-permute-done.98 = bf16[2,64,768]{2,1,0:T(8,128)(2,1)S(1)} collective-permute-done((bf16[2,64,768]{2,1,0:T(8,128)(2,1)S(1)}, bf16[2,64,768]{2,1,0:T(8,128)(2,1)S(1)}, u32[]{:S(2)}, u32[]{:S(2)}) %collective-permute-start.98) | collective-permute-done | bytes 196640 | tf_op jit(solution)/shard_map/ppermute | solution.py:96
  (1209 shorter events, 723.7 us)
Async XLA Ops:
  1.5 68.3 %collective-permute-start.8 = (bf16[1,720]{1,0:T(2,128)(2,1)S(1)}, bf16[1,720]{1,0:T(2,128)(2,1)S(1)}, u32[]{:S(2)}, u32[]{:S(2)}) collective-permute-start(bf16[1,720]{1,0:T(2,128)(2,1)S(1)} %reshape.1552), channel_id=1, source_target_pairs={{0,16},{2,18},{4,20},{6,22},{8,24},{10,26},{12,28},{14,30},{16,0},... | collective-permute-start | bytes 4328 | tf_op jit(solution)/shard_map/ppermute | solution.py:96
  7.1 99.5 %collective-permute-start.52 = (bf16[32,768]{1,0:T(8,128)(2,1)}, bf16[32,768]{1,0:T(8,128)(2,1)}, u32[]{:S(2)}, u32[]{:S(2)}) collective-permute-start(bf16[32,768]{1,0:T(8,128)(2,1)} %convert_element_type.794), channel_id=1, source_target_pairs={{0,16},{2,18},{4,20},{6,22},{8,24},{10,26},{12,28},{14,30},{16,0},... | collective-permute-start | bytes 147464 | tf_op jit(solution)/shard_map/ppermute | solution.py:96
  8.7 94.4 %collective-permute-start.38 = (bf16[2,32,256]{2,1,0:T(8,128)(2,1)}, bf16[2,32,256]{2,1,0:T(8,128)(2,1)}, u32[]{:S(2)}, u32[]{:S(2)}) collective-permute-start(bf16[2,32,256]{2,1,0:T(8,128)(2,1)} %slice.197), channel_id=1, source_target_pairs={{0,16},{2,18},{4,20},{6,22},{8,24},{10,26},{12,28},{14,30},{16,0},... | collective-permute-start | bytes 98312 | tf_op jit(solution)/shard_map/ppermute | solution.py:96
  13.1 95.5 %collective-permute-start.30 = (bf16[64,512]{1,0:T(8,128)(2,1)}, bf16[64,512]{1,0:T(8,128)(2,1)}, u32[]{:S(2)}, u32[]{:S(2)}) collective-permute-start(bf16[64,512]{1,0:T(8,128)(2,1)} %convert_element_type.773), channel_id=1, source_target_pairs={{0,16},{2,18},{4,20},{6,22},{8,24},{10,26},{12,28},{14,30},{16,0},... | collective-permute-start | bytes 196616 | tf_op jit(solution)/shard_map/ppermute | solution.py:96
  14.8 127.5 %collective-permute-start.4 = (bf16[64,768]{1,0:T(8,128)(2,1)}, bf16[64,768]{1,0:T(8,128)(2,1)}, u32[]{:S(2)}, u32[]{:S(2)}) collective-permute-start(bf16[64,768]{1,0:T(8,128)(2,1)} %convert_bitcast_fusion.1), channel_id=1, source_target_pairs={{0,16},{2,18},{4,20},{6,22},{8,24},{10,26},{12,28},{14,30},{16,0},... | collective-permute-start | bytes 294920 | tf_op jit(solution)/shard_map/ppermute | solution.py:96
  108.6 74.0 %collective-permute-start.21 = (bf16[64,2048]{1,0:T(8,128)(2,1)S(1)}, bf16[64,2048]{1,0:T(8,128)(2,1)S(1)}, u32[]{:S(2)}, u32[]{:S(2)}) collective-permute-start(bf16[64,2048]{1,0:T(8,128)(2,1)S(1)} %copy-done.181), channel_id=1, source_target_pairs={{0,16},{2,18},{4,20},{6,22},{8,24},{10,26},{12,28},{14,30},{16,0},... | collective-permute-start | bytes 786440 | tf_op jit(solution)/shard_map/ppermute | solution.py:96
  112.1 72.6 %collective-permute-start.25 = (bf16[64,2048]{1,0:T(8,128)(2,1)S(1)}, bf16[64,2048]{1,0:T(8,128)(2,1)S(1)}, u32[]{:S(2)}, u32[]{:S(2)}) collective-permute-start(bf16[64,2048]{1,0:T(8,128)(2,1)S(1)} %copy-done.180), channel_id=1, source_target_pairs={{0,16},{2,18},{4,20},{6,22},{8,24},{10,26},{12,28},{14,30},{16,0},... | collective-permute-start | bytes 786440 | tf_op jit(solution)/shard_map/ppermute | solution.py:96
  141.7 366.9 %collective-permute-start = (f32[3]{0:T(128)}, f32[3]{0:T(128)}, u32[]{:S(2)}, u32[]{:S(2)}) collective-permute-start(f32[3]{0:T(128)} %pad_maximum_fusion.52), channel_id=1, source_target_pairs={{0,2},{2,0},{4,6},{6,4},{8,10},{10,8},{12,14},{14,12},{16,18},{18,... | collective-permute-start | bytes 44 | tf_op jit(solution)/shard_map/ppermute | solution.py:96
  147.3 320.7 %collective-permute-start.53 = (bf16[2,32,768]{2,1,0:T(8,128)(2,1)}, bf16[2,32,768]{2,1,0:T(8,128)(2,1)}, u32[]{:S(2)}, u32[]{:S(2)}) collective-permute-start(bf16[2,32,768]{2,1,0:T(8,128)(2,1)} %pad_maximum_fusion.46), channel_id=1, source_target_pairs={{0,8},{2,10},{4,12},{6,14},{8,0},{10,2},{12,4},{14,6},{16,24},{18,... | collective-permute-start | bytes 294920 | tf_op jit(solution)/shard_map/ppermute | solution.py:96
  219.1 45.9 %collective-permute-start.27 = (bf16[2,2,64,2048]{3,2,0,1:T(8,128)(2,1)S(1)}, bf16[2,2,64,2048]{3,2,0,1:T(8,128)(2,1)S(1)}, u32[]{:S(2)}, u32[]{:S(2)}) collective-permute-start(bf16[2,2,64,2048]{3,2,0,1:T(8,128)(2,1)S(1)} %pad_maximum_fusion.11), channel_id=1, source_target_pairs={{0,4},{2,6},{4,0},{6,2},{8,12},{10,14},{12,8},{14,10},{16,20},{18,... | collective-permute-start | bytes 3145736 | tf_op jit(solution)/shard_map/ppermute | solution.py:96
  225.8 89.5 %collective-permute-start.23 = (bf16[2,2,64,2048]{3,2,1,0:T(8,128)(2,1)}, bf16[2,2,64,2048]{3,2,1,0:T(8,128)(2,1)}, u32[]{:S(2)}, u32[]{:S(2)}) collective-permute-start(bf16[2,2,64,2048]{3,2,1,0:T(8,128)(2,1)} %pad_maximum_fusion.10), channel_id=1, source_target_pairs={{0,2},{2,0},{4,6},{6,4},{8,10},{10,8},{12,14},{14,12},{16,18},{18,... | collective-permute-start | bytes 3145736 | tf_op jit(solution)/shard_map/ppermute | solution.py:96
  276.3 48.2 %collective-permute-start.28 = (bf16[2,2,2,64,2048]{4,3,0,1,2:T(8,128)(2,1)}, bf16[2,2,2,64,2048]{4,3,0,1,2:T(8,128)(2,1)}, u32[]{:S(2)}, u32[]{:S(2)}) collective-permute-start(bf16[2,2,2,64,2048]{4,3,0,1,2:T(8,128)(2,1)} %pad_maximum_fusion.4), channel_id=1, source_target_pairs={{0,2},{2,0},{4,6},{6,4},{8,10},{10,8},{12,14},{14,12},{16,18},{18,... | collective-permute-start | bytes 6291464 | tf_op jit(solution)/shard_map/ppermute | solution.py:96
  316.9 48.5 %collective-permute-start.24 = (bf16[2,2,2,64,2048]{4,3,2,1,0:T(8,128)(2,1)S(1)}, bf16[2,2,2,64,2048]{4,3,2,1,0:T(8,128)(2,1)S(1)}, u32[]{:S(2)}, u32[]{:S(2)}) collective-permute-start(bf16[2,2,2,64,2048]{4,3,2,1,0:T(8,128)(2,1)S(1)} %pad_maximum_fusion.3), channel_id=1, source_target_pairs={{0,4},{2,6},{4,0},{6,2},{8,12},{10,14},{12,8},{14,10},{16,20},{18,... | collective-permute-start | bytes 6291464 | tf_op jit(solution)/shard_map/ppermute | solution.py:96
  319.3 53.8 %collective-permute-start.41 = (bf16[2,2,2,2,32,256]{5,4,0,1,2,3:T(8,128)(2,1)S(1)}, bf16[2,2,2,2,32,256]{5,4,0,1,2,3:T(8,128)(2,1)S(1)}, u32[]{:S(2)}, u32[]{:S(2)}) collective-permute-start(bf16[2,2,2,2,32,256]{5,4,0,1,2,3:T(8,128)(2,1)S(1)} %copy-done.178), channel_id=1, source_target_pairs={{0,4},{2,6},{4,0},{6,2},{8,12},{10,14},{12,8},{14,10},{16,20},{18,... | collective-permute-start | bytes 786440 | tf_op jit(solution)/shard_map/ppermute | solution.py:96
  324.5 50.2 %collective-permute-start.37 = (bf16[2,2,2,2,32,256]{5,4,3,2,1,0:T(8,128)(2,1)S(1)}, bf16[2,2,2,2,32,256]{5,4,3,2,1,0:T(8,128)(2,1)S(1)}, u32[]{:S(2)}, u32[]{:S(2)}) collective-permute-start(bf16[2,2,2,2,32,256]{5,4,3,2,1,0:T(8,128)(2,1)S(1)} %copy-done.179), channel_id=1, source_target_pairs={{0,2},{2,0},{4,6},{6,4},{8,10},{10,8},{12,14},{14,12},{16,18},{18,... | collective-permute-start | bytes 786440 | tf_op jit(solution)/shard_map/ppermute | solution.py:96
  374.7 91.1 %collective-permute-start.45 = (bf16[2,2,32,1024]{3,2,1,0:T(8,128)(2,1)}, bf16[2,2,32,1024]{3,2,1,0:T(8,128)(2,1)}, u32[]{:S(2)}, u32[]{:S(2)}) collective-permute-start(bf16[2,2,32,1024]{3,2,1,0:T(8,128)(2,1)} %pad_maximum_fusion.35), channel_id=1, source_target_pairs={{0,2},{2,0},{4,6},{6,4},{8,10},{10,8},{12,14},{14,12},{16,18},{18,... | collective-permute-start | bytes 786440 | tf_op jit(solution)/shard_map/ppermute | solution.py:96
  381.8 89.0 %collective-permute-start.50 = (bf16[2,2,2,32,1024]{4,3,0,1,2:T(8,128)(2,1)}, bf16[2,2,2,32,1024]{4,3,0,1,2:T(8,128)(2,1)}, u32[]{:S(2)}, u32[]{:S(2)}) collective-permute-start(bf16[2,2,2,32,1024]{4,3,0,1,2:T(8,128)(2,1)} %pad_maximum_fusion.24), channel_id=1, source_target_pairs={{0,2},{2,0},{4,6},{6,4},{8,10},{10,8},{12,14},{14,12},{16,18},{18,... | collective-permute-start | bytes 1572872 | tf_op jit(solution)/shard_map/ppermute | solution.py:96
  607.4 58.1 %collective-permute-start.60 = (bf16[2048,512]{0,1:T(8,128)(2,1)S(1)}, bf16[2048,512]{0,1:T(8,128)(2,1)}, u32[]{:S(2)}, u32[]{:S(2)}) collective-permute-start(bf16[2048,512]{0,1:T(8,128)(2,1)S(1)} %convolution_convert_fusion.1), channel_id=1, source_target_pairs={{0,1},{1,0},{2,3},{3,2},{4,5},{5,4},{6,7},{7,6},{8,9},{9,8},{10,11... | collective-permute-start | bytes 6291464 | tf_op jit(solution)/shard_map/ppermute | solution.py:77
  801.9 61.7 %collective-permute-start.75 = (bf16[2,2,2,64,2048]{4,3,0,1,2:T(8,128)(2,1)}, bf16[2,2,2,64,2048]{4,3,0,1,2:T(8,128)(2,1)}, u32[]{:S(2)}, u32[]{:S(2)}) collective-permute-start(bf16[2,2,2,64,2048]{4,3,0,1,2:T(8,128)(2,1)} %fusion.18), channel_id=1, source_target_pairs={{0,2},{2,0},{4,6},{6,4},{8,10},{10,8},{12,14},{14,12},{16,18},{18,... | collective-permute-start | bytes 6291464 | tf_op jit(solution)/shard_map/ppermute | solution.py:96
  807.4 63.3 %collective-permute-start.71 = (bf16[2,2,2,64,2048]{4,3,0,1,2:T(8,128)(2,1)}, bf16[2,2,2,64,2048]{4,3,0,1,2:T(8,128)(2,1)}, u32[]{:S(2)}, u32[]{:S(2)}) collective-permute-start(bf16[2,2,2,64,2048]{4,3,0,1,2:T(8,128)(2,1)} %fusion.17), channel_id=1, source_target_pairs={{0,4},{2,6},{4,0},{6,2},{8,12},{10,14},{12,8},{14,10},{16,20},{18,... | collective-permute-start | bytes 6291464 | tf_op jit(solution)/shard_map/ppermute | solution.py:96
  862.9 66.0 %collective-permute-start.63 = (bf16[2,2,2,2,64,512]{5,4,3,2,1,0:T(8,128)(2,1)}, bf16[2,2,2,2,64,512]{5,4,3,2,1,0:T(8,128)(2,1)}, u32[]{:S(2)}, u32[]{:S(2)}) collective-permute-start(bf16[2,2,2,2,64,512]{5,4,3,2,1,0:T(8,128)(2,1)} %fusion.62), channel_id=1, source_target_pairs={{0,4},{2,6},{4,0},{6,2},{8,12},{10,14},{12,8},{14,10},{16,20},{18,... | collective-permute-start | bytes 3145736 | tf_op jit(solution)/shard_map/ppermute | solution.py:96
  869.7 97.4 %collective-permute-start.76 = (bf16[2,2,64,2048]{3,2,0,1:T(8,128)(2,1)}, bf16[2,2,64,2048]{3,2,0,1:T(8,128)(2,1)}, u32[]{:S(2)}, u32[]{:S(2)}) collective-permute-start(bf16[2,2,64,2048]{3,2,0,1:T(8,128)(2,1)} %fusion.59), channel_id=1, source_target_pairs={{0,4},{2,6},{4,0},{6,2},{8,12},{10,14},{12,8},{14,10},{16,20},{18,... | collective-permute-start | bytes 3145736 | tf_op jit(solution)/shard_map/ppermute | solution.py:96
  874.4 97.4 %collective-permute-start.72 = (bf16[2,2,64,2048]{3,2,0,1:T(8,128)(2,1)}, bf16[2,2,64,2048]{3,2,0,1:T(8,128)(2,1)}, u32[]{:S(2)}, u32[]{:S(2)}) collective-permute-start(bf16[2,2,64,2048]{3,2,0,1:T(8,128)(2,1)} %fusion.58), channel_id=1, source_target_pairs={{0,2},{2,0},{4,6},{6,4},{8,10},{10,8},{12,14},{14,12},{16,18},{18,... | collective-permute-start | bytes 3145736 | tf_op jit(solution)/shard_map/ppermute | solution.py:96
  887.7 64.6 %collective-permute-start.96 = (bf16[2,2,2,64,768]{4,3,0,1,2:T(8,128)(2,1)}, bf16[2,2,2,64,768]{4,3,0,1,2:T(8,128)(2,1)}, u32[]{:S(2)}, u32[]{:S(2)}) collective-permute-start(bf16[2,2,2,64,768]{4,3,0,1,2:T(8,128)(2,1)} %fusion.86), channel_id=1, source_target_pairs={{0,4},{2,6},{4,0},{6,2},{8,12},{10,14},{12,8},{14,10},{16,20},{18,... | collective-permute-start | bytes 2359304 | tf_op jit(solution)/shard_map/ppermute | solution.py:96
  (366 other events, 4773.3 us)

commit v2 on v1

v2 whole, which is shorter than its diff:
```python
import functools
import math

import jax
import jax.numpy as jnp
from jax import lax
from jax.experimental import pallas as pl
from jax.experimental.pallas import tpu as pltpu
from jax.sharding import PartitionSpec as P

D = 1024
DH = 64
E = 512
DDH = 32
GRID = 16
NB = 3
STEP = 10


EPS_LN = 1e-06
EPS_C = 0.01
CLIP = 0.0002
BETA_ONE = 0.9
BETA_TWO = 0.999
ADAM_EPS = 1e-12
RATE_MAT = 0.06
RATE_VEC = 0.5
DECAY_MAT = 0.05
EMA_KEEP = 0.9
REF_GSD = 4.0


def split_vectors(flat_vec, enc_width, dec_width):
    lengths = [enc_width] * 7 + [dec_width] * 7
    pieces = []
    offset = 0
    for length in lengths:
        pieces.append(flat_vec[offset : offset + length])
        offset = offset + length
    pieces.append(flat_vec[offset:])
    return pieces


F32 = jnp.float32
BF16 = jnp.bfloat16
VMEM_LIMIT = 58 * 2**20
GELU_C = math.sqrt(2.0 / math.pi)


def dot_nn(left, right):
    return jnp.dot(left, right, preferred_element_type=F32)


def dot_nt(left, right):
    return lax.dot_general(left, right, (((1,), (1,)), ((), ())), preferred_element_type=F32)


def dot_tn(left, right):
    return lax.dot_general(left, right, (((0,), (0,)), ((), ())), preferred_element_type=F32)


def dot_exact(left, right):
    return jnp.dot(left, right, preferred_element_type=F32, precision=lax.Precision.HIGHEST)


def normalize(rows):
    centred = rows - jnp.mean(rows, axis=-1, keepdims=True)
    rstd = lax.rsqrt(jnp.mean(centred * centred, axis=-1, keepdims=True) + EPS_LN)
    return centred * rstd, rstd


def norm_back(grad, gain, unit, rstd):
    scaled = grad * gain
    mean_one = jnp.mean(scaled, axis=-1, keepdims=True)
    mean_two = jnp.mean(scaled * unit, axis=-1, keepdims=True)
    grad_in = rstd * (scaled - mean_one - unit * mean_two)
    return (
        grad_in,
        jnp.sum(grad * unit, axis=0, keepdims=True),
        jnp.sum(grad, axis=0, keepdims=True),
    )


def both(mine_ref, other_ref, rows):
    return mine_ref[rows, :].astype(F32) + other_ref[rows, :].astype(F32)


def gelu_parts(up):
    square = up * up
    bent = jnp.tanh(GELU_C * up * (1.0 + 0.044715 * square))
    half = 0.5 * (1.0 + bent)
    return square, bent, half


def group_mask(group, length):
    if group == length:
        return None
    row_image = lax.broadcasted_iota(jnp.int32, (group, group), 0) // length
    col_image = lax.broadcasted_iota(jnp.int32, (group, group), 1) // length
    return row_image == col_image


def attend(qkv_ref, mixed_ref, lse_ref, cols, width, head_dim, mask):
    scale = head_dim ** (-0.5)
    for head in range(width // head_dim):
        at = pl.ds(head * head_dim, head_dim)
        queries = qkv_ref[at, cols]
        keys = qkv_ref[pl.ds(width + head * head_dim, head_dim), cols]
        values = qkv_ref[pl.ds(2 * width + head * head_dim, head_dim), cols]
        scores = dot_tn(keys, queries) * scale
        if mask is not None:
            scores = jnp.where(mask, scores, -1e30)
        top = jnp.max(scores, axis=0, keepdims=True)
        weights = jnp.exp(scores - top)
        total = jnp.sum(weights, axis=0, keepdims=True)
        lse_ref[pl.ds(head, 1), cols] = top + jnp.log(total)
        soft = (weights * (1.0 / total)).astype(BF16)
        mixed_ref[at, cols] = dot_nn(values, soft).astype(BF16)


def attend_back(qkv_ref, grad_ref, lse_ref, out_ref, cols, width, head_dim, mask):
    scale = head_dim ** (-0.5)
    for head in range(width // head_dim):
        at = pl.ds(head * head_dim, head_dim)
        at_k = pl.ds(width + head * head_dim, head_dim)
        at_v = pl.ds(2 * width + head * head_dim, head_dim)
        queries, keys, values = qkv_ref[at, cols], qkv_ref[at_k, cols], qkv_ref[at_v, cols]
        grad = grad_ref[at, :]
        scores = dot_tn(keys, queries) * scale
        if mask is not None:
            scores = jnp.where(mask, scores, -1e30)
        soft = jnp.exp(scores - lse_ref[pl.ds(head, 1), cols])
        out_ref[at_v, cols] = dot_nt(grad, soft.astype(BF16)).astype(BF16)
        grad_soft = dot_tn(values, grad)
        inner = jnp.sum(soft * grad_soft, axis=0, keepdims=True)
        grad_scores = (soft * (grad_soft - inner)).astype(BF16)
        out_ref[at, cols] = (dot_nn(keys, grad_scores) * scale).astype(BF16)
        out_ref[at_k, cols] = (dot_nt(queries, grad_scores) * scale).astype(BF16)


def transposed_weights(attn_ref, flat_ref):
    width = attn_ref.shape[2]
    for part in range(4):
        flat_ref[pl.ds(part * width, width), :] = attn_ref[part].T


def attention_rows(unit, vec_ref, flat_ref, qkv_ref, mixed_ref, lse_ref, part_ref, rows, head_dim, mask, attn_ref):
    width = mixed_ref.shape[0]
    low = (unit * vec_ref[1:2, :] + vec_ref[2:3, :]).astype(BF16)
    qkv_ref[:, rows] = dot_nt(flat_ref[: 3 * width, :], low).astype(BF16)
    attend(qkv_ref, mixed_ref, lse_ref, rows, width, head_dim, mask)
    part_ref[rows, :] = dot_nt(mixed_ref[:, rows].T, attn_ref[3]).astype(BF16)


def enc_in_kernel(length, group, head_dim, pix_ref, kept_ref, table_ref, embed_ref, vec_ref, attn_ref,
                  x_ref, qkv_ref, mixed_ref, lse_ref, part_ref, pixk_ref, flat_ref):
    images, patches = table_ref.shape[0], pix_ref.shape[0] // table_ref.shape[0]
    side = table_ref.shape[1]
    transposed_weights(attn_ref, flat_ref)

    def pick(image, carry):
        rows = pl.ds(image * length, length)
        index = kept_ref[rows, :]
        hot = lax.broadcasted_iota(jnp.int32, (length, patches), 1) == index
        pixels = pix_ref[pl.ds(image * patches, patches), :]
        pixk_ref[rows, :] = dot_nn(hot.astype(BF16), pixels).astype(BF16)
        grid_at = lax.broadcasted_iota(jnp.int32, (length, side), 1)
        table = table_ref[image]
        half = table.shape[1]
        x_ref[rows, :half] = dot_exact((grid_at == index // side).astype(F32), table)
        x_ref[rows, half:] = dot_exact((grid_at == index % side).astype(F32), table)
        return carry

    lax.fori_loop(0, images, pick, 0)
    mask = group_mask(group, length)

    def step(number, carry):
        rows = pl.ds(pl.multiple_of(number * group, group), group)
        rows_x = dot_nt(pixk_ref[rows, :], embed_ref[...]) + vec_ref[0:1, :] + x_ref[rows, :]
        x_ref[rows, :] = rows_x
        unit, _ = normalize(rows_x)
        attention_rows(unit, vec_ref, flat_ref, qkv_ref, mixed_ref, lse_ref, part_ref, rows, head_dim, mask, attn_ref)
        return carry

    lax.fori_loop(0, x_ref.shape[0] // group, step, 0)


def dec_in_kernel(length, head_dim, x1_ref, mine_ref, other_ref, evec_ref, bridge_ref, kept_ref, hidden_ref,
                  table_ref, vec_ref, attn_ref,
                  x2_ref, final_ref, x_ref, qkv_ref, mixed_ref, lse_ref, part_ref, flat_ref, latent_ref):
    images, side, half = table_ref.shape
    patches = side * side
    transposed_weights(attn_ref, flat_ref)
    every = pl.ds(0, x1_ref.shape[0])
    out = x1_ref[...] + both(mine_ref, other_ref, every)
    x2_ref[...] = out
    unit, _ = normalize(out)
    final = (unit * evec_ref[5:6, :] + evec_ref[6:7, :]).astype(BF16)
    final_ref[...] = final
    latent_ref[...] = dot_nn(final, bridge_ref[...])

    def step(image, carry):
        rows = pl.ds(pl.multiple_of(image * patches, patches), patches)
        hot = lax.broadcasted_iota(jnp.int32, (patches, length), 0) == kept_ref[pl.ds(image, 1), :]
        latent = latent_ref[pl.ds(image * length, length), :]
        table = table_ref[image]
        by_row = jnp.broadcast_to(table[:, None, :], (side, side, half)).reshape(patches, half)
        by_col = jnp.broadcast_to(table[None, :, :], (side, side, half)).reshape(patches, half)
        place = jnp.concatenate([by_row, by_col], axis=1)
        rows_x = dot_exact(hot.astype(F32), latent) + hidden_ref[rows, :] * vec_ref[0:1, :] + place
        x_ref[rows, :] = rows_x
        unit, _ = normalize(rows_x)
        attention_rows(unit, vec_ref, flat_ref, qkv_ref, mixed_ref, lse_ref, part_ref, rows, head_dim, None, attn_ref)
        return carry

    lax.fori_loop(0, images, step, 0)


def mlp_kernel(tile, x_ref, mine_ref, other_ref, vec_ref, up_ref, down_ref, x1_ref, part_ref, low_ref, acc_ref):
    number = pl.program_id(0)
    count = x_ref.shape[0] // tile

    def first(step, carry):
        rows = pl.ds(pl.multiple_of(step * tile, tile), tile)
        after = x_ref[rows, :] + both(mine_ref, other_ref, rows)
        x1_ref[rows, :] = after
        unit, _ = normalize(after)
        low_ref[rows, :] = (unit * vec_ref[3:4, :] + vec_ref[4:5, :]).astype(BF16)
        return carry

    @pl.when(number == 0)
    def _():
        lax.fori_loop(0, count, first, 0)
        acc_ref[...] = jnp.zeros_like(acc_ref)

    def step(piece, carry):
        rows = pl.ds(pl.multiple_of(piece * tile, tile), tile)
        up = dot_nn(low_ref[rows, :], up_ref[...])
        _, _, half = gelu_parts(up)
        acc_ref[rows, :] += dot_nt((up * half).astype(BF16), down_ref[...])
        return carry

    lax.fori_loop(0, count, step, 0)

    @pl.when(number == pl.num_programs(0) - 1)
    def _():
        part_ref[...] = acc_ref[...].astype(BF16)


def head_kernel(core_ref, inverse_ref, x1_ref, mine_ref, other_ref, vec_ref, bias_ref, predict_ref, target_ref,
                band_ref, weight_ref, gy_ref, gpred_ref, gbias_ref, loss_ref, gain_ref, shift_ref, low_ref):
    number = pl.program_id(0)

    @pl.when(number == 0)
    def _():
        for ref in (gpred_ref, gbias_ref, loss_ref, gain_ref, shift_ref):
            ref[...] = jnp.zeros_like(ref)

    every = pl.ds(0, x1_ref.shape[0])
    unit, rstd = normalize(x1_ref[...] + both(mine_ref, other_ref, every))
    gain = vec_ref[5:6, :]
    final = (unit * gain + vec_ref[6:7, :]).astype(BF16)
    mismatch = dot_nn(final, predict_ref[...]) + bias_ref[...] - target_ref[...].astype(F32)
    band = band_ref[...]
    level = jnp.where(band == 0, inverse_ref[0], jnp.where(band == 1, inverse_ref[1], inverse_ref[2]))
    level = level * weight_ref[...]
    square = mismatch * mismatch + EPS_C
    root = lax.rsqrt(square)
    loss_ref[...] += jnp.sum(level * (square * root), axis=0, keepdims=True)
    grad = level * (mismatch * root)
    gbias_ref[...] += jnp.sum(grad, axis=0, keepdims=True)
    low_ref[...] = grad.astype(BF16)
    share = gpred_ref.shape[1]
    columns = pl.ds(pl.multiple_of(core_ref[0] * share, share), share)
    gpred_ref[...] += dot_tn(final, low_ref[:, columns])
    grad_final = dot_nt(low_ref[...], predict_ref[...])
    grad_in, gain_sum, shift_sum = norm_back(grad_final, gain, unit, rstd)
    gy_ref[...] = grad_in
    gain_ref[...] += gain_sum
    shift_ref[...] += shift_sum


def mlp_back_kernel(tile, gy_ref, x1_ref, vec_ref, up_ref, down_ref, gup_ref, gdown_ref, part_ref,
                    low_ref, lowt_ref, grad_ref, gradt_ref, gu_ref, z_ref, acc_ref):
    number = pl.program_id(0)
    count = x1_ref.shape[0] // tile

    def first(step, carry):
        rows = pl.ds(pl.multiple_of(step * tile, tile), tile)
        unit, _ = normalize(x1_ref[rows, :])
        low = (unit * vec_ref[3:4, :] + vec_ref[4:5, :]).astype(BF16)
        low_ref[rows, :] = low
        lowt_ref[:, rows] = low.T
        grad = gy_ref[rows, :].astype(BF16)
        grad_ref[rows, :] = grad
        gradt_ref[:, rows] = grad.T
        return carry

    @pl.when(number == 0)
    def _():
        lax.fori_loop(0, count, first, 0)
        acc_ref[...] = jnp.zeros_like(acc_ref)

    def step(piece, carry):
        rows = pl.ds(pl.multiple_of(piece * tile, tile), tile)
        up = dot_nn(low_ref[rows, :], up_ref[...])
        square, bent, half = gelu_parts(up)
        z_ref[rows, :] = (up * half).astype(BF16)
        slope = half + (0.5 * GELU_C) * up * (1.0 - bent * bent) * (1.0 + (3.0 * 0.044715) * square)
        grad_up = (dot_nn(grad_ref[rows, :], down_ref[...]) * slope).astype(BF16)
        gu_ref[rows, :] = grad_up
        acc_ref[rows, :] += dot_nt(grad_up, up_ref[...])
        return carry

    lax.fori_loop(0, count, step, 0)
    gup_ref[...] = dot_nn(lowt_ref[...], gu_ref[...]).astype(BF16)
    gdown_ref[...] = dot_nn(gradt_ref[...], z_ref[...]).astype(BF16)

    @pl.when(number == pl.num_programs(0) - 1)
    def _():
        part_ref[...] = acc_ref[...].astype(BF16)


def attn_back_kernel(length, group, head_dim, gy_ref, x1_ref, mine_ref, other_ref, x_ref, qkv_ref, mixed_ref, lse_ref,
                     vec_ref, attn_ref, gx_ref, gqk_ref, gvo_ref, gain_ref, shift_ref, part_ref,
                     flat_ref, lowt_ref, gradt_ref, gmix_ref, gqkv_ref):
    width = mixed_ref.shape[0]
    transposed_weights(attn_ref, flat_ref)
    gain_ref[...] = jnp.zeros_like(gain_ref)
    shift_ref[...] = jnp.zeros_like(shift_ref)
    mask = group_mask(group, length)

    def step(number, carry):
        rows = pl.ds(pl.multiple_of(number * group, group), group)
        unit, rstd = normalize(x1_ref[rows, :])
        grad_in, gain_sum, shift_sum = norm_back(both(mine_ref, other_ref, rows), vec_ref[3:4, :], unit, rstd)
        grad_in = grad_in + gy_ref[rows, :]
        gx_ref[rows, :] = grad_in
        gain_ref[...] += gain_sum
        shift_ref[...] += shift_sum
        low_grad = grad_in.astype(BF16)
        gradt_ref[:, rows] = low_grad.T
        gmix_ref[...] = dot_nt(flat_ref[3 * width :, :], low_grad).astype(BF16)
        attend_back(qkv_ref, gmix_ref, lse_ref, gqkv_ref, rows, width, head_dim, mask)
        part_ref[rows, :] = dot_nn(gqkv_ref[:, rows].T, flat_ref[: 3 * width, :]).astype(BF16)
        unit_a, _ = normalize(x_ref[rows, :])
        lowt_ref[:, rows] = (unit_a * vec_ref[1:2, :] + vec_ref[2:3, :]).astype(BF16).T
        return carry

    lax.fori_loop(0, x_ref.shape[0] // group, step, 0)
    gqk_ref[0] = dot_nt(lowt_ref[...], gqkv_ref[:width, :]).astype(BF16)
    gqk_ref[1] = dot_nt(lowt_ref[...], gqkv_ref[width : 2 * width, :]).astype(BF16)
    gvo_ref[0] = dot_nt(lowt_ref[...], gqkv_ref[2 * width :, :]).astype(BF16)
    gvo_ref[1] = dot_nt(gradt_ref[...], mixed_ref[...]).astype(BF16)


def between_kernel(length, core_ref, gx_ref, x_ref, mine_ref, other_ref, vec_ref, kept_ref, hidden_ref, final_ref, x2_ref,
                   evec_ref, bridge_ref, gain_ref, shift_ref, mask_ref, gbridge_ref, egain_ref, eshift_ref, gy_ref,
                   latent_ref):
    images = kept_ref.shape[0] // length
    patches = x_ref.shape[0] // images
    for ref in (gain_ref, shift_ref, mask_ref):
        ref[...] = jnp.zeros_like(ref)

    def step(image, carry):
        rows = pl.ds(pl.multiple_of(image * patches, patches), patches)
        unit, rstd = normalize(x_ref[rows, :])
        grad_in, gain_sum, shift_sum = norm_back(both(mine_ref, other_ref, rows), vec_ref[1:2, :], unit, rstd)
        grad_in = grad_in + gx_ref[rows, :]
        gain_ref[...] += gain_sum
        shift_ref[...] += shift_sum
        mask_ref[...] += jnp.sum(grad_in * hidden_ref[rows, :], axis=0, keepdims=True)
        kept_rows = pl.ds(pl.multiple_of(image * length, length), length)
        hot = lax.broadcasted_iota(jnp.int32, (length, patches), 1) == kept_ref[kept_rows, :]
        latent_ref[kept_rows, :] = dot_nn(hot.astype(BF16), grad_in.astype(BF16)).astype(BF16)
        return carry

    lax.fori_loop(0, images, step, 0)
    share = gbridge_ref.shape[1]
    columns = pl.ds(pl.multiple_of(core_ref[0] * share, share), share)
    gbridge_ref[...] = dot_tn(final_ref[...], latent_ref[:, columns]).astype(BF16)
    grad_final = dot_nt(latent_ref[...], bridge_ref[...])
    unit, rstd = normalize(x2_ref[...])
    gy_ref[...], egain_ref[...], eshift_ref[...] = norm_back(grad_final, evec_ref[5:6, :], unit, rstd)


def enc_out_kernel(core_ref, gx_ref, x_ref, mine_ref, other_ref, vec_ref, pixk_ref,
                   gain_ref, shift_ref, ebias_ref, gembed_ref):
    every = pl.ds(0, x_ref.shape[0])
    unit, rstd = normalize(x_ref[...])
    grad_in, gain_ref[...], shift_ref[...] = norm_back(both(mine_ref, other_ref, every), vec_ref[1:2, :], unit, rstd)
    grad_in = grad_in + gx_ref[...]
    ebias_ref[...] = jnp.sum(grad_in, axis=0, keepdims=True)
    share = gembed_ref.shape[1]
    columns = pl.ds(pl.multiple_of(core_ref[0] * share, share), share)
    gembed_ref[...] = dot_tn(grad_in.astype(BF16), pixk_ref[:, columns]).astype(BF16)


def shape(dims, dtype):
    return jax.ShapeDtypeStruct(dims, dtype)


def run(kernel, outs, scratch, args, flops, scalars=0):
    moved = sum(math.prod(a.shape) * a.dtype.itemsize for a in list(args) + list(outs))
    in_vmem = pl.BlockSpec(memory_space=pltpu.VMEM)
    return pl.pallas_call(
        kernel,
        out_shape=tuple(outs),
        in_specs=[pl.BlockSpec(memory_space=pltpu.SMEM)] * scalars + [in_vmem] * (len(args) - scalars),
        out_specs=tuple([in_vmem] * len(outs)),
        scratch_shapes=scratch,
        compiler_params=pltpu.CompilerParams(vmem_limit_bytes=VMEM_LIMIT),
        cost_estimate=pl.CostEstimate(flops=flops, bytes_accessed=moved, transcendentals=0),
    )(*args)


def other_core(block):
    return lax.ppermute(block, "mp", [(0, 1), (1, 0)])


def mlp_forward(x, mine, vec, up, down):
    rows, width = x.shape
    hidden = up.shape[1]
    block = min(hidden, 512)
    tile = min(rows, 512)
    other = other_core(mine)
    whole = pl.BlockSpec((rows, width), lambda i: (0, 0))
    cols = pl.BlockSpec((width, block), lambda i: (0, i))
    return pl.pallas_call(
        functools.partial(mlp_kernel, tile),
        out_shape=(shape((rows, width), F32), shape((rows, width), BF16)),
        grid=(hidden // block,),
        in_specs=[whole] * 3 + [pl.BlockSpec((8, width), lambda i: (0, 0)), cols, cols],
        out_specs=(whole, whole),
        scratch_shapes=[pltpu.VMEM((rows, width), BF16), pltpu.VMEM((rows, width), F32)],
        compiler_params=pltpu.CompilerParams(vmem_limit_bytes=VMEM_LIMIT),
        cost_estimate=pl.CostEstimate(flops=4 * rows * width * hidden, bytes_accessed=rows * width * 14 + width * hidden * 4,
                                      transcendentals=rows * hidden),
    )(x, mine, other, vec, up, down)


def mlp_backward(gy, x1, vec, up, down):
    rows, width = x1.shape
    hidden = up.shape[1]
    block = min(hidden, 512)
    tile = min(rows, 256)
    whole = pl.BlockSpec((rows, width), lambda i: (0, 0))
    cols = pl.BlockSpec((width, block), lambda i: (0, i))
    return pl.pallas_call(
        functools.partial(mlp_back_kernel, tile),
        out_shape=(shape((width, hidden), BF16), shape((width, hidden), BF16), shape((rows, width), BF16)),
        grid=(hidden // block,),
        in_specs=[whole] * 2 + [pl.BlockSpec((8, width), lambda i: (0, 0)), cols, cols],
        out_specs=(cols, cols, whole),
        scratch_shapes=[
            pltpu.VMEM((rows, width), BF16), pltpu.VMEM((width, rows), BF16),
            pltpu.VMEM((rows, width), BF16), pltpu.VMEM((width, rows), BF16),
            pltpu.VMEM((rows, block), BF16), pltpu.VMEM((rows, block), BF16),
            pltpu.VMEM((rows, width), F32)],
        compiler_params=pltpu.CompilerParams(vmem_limit_bytes=VMEM_LIMIT),
        cost_estimate=pl.CostEstimate(flops=10 * rows * width * hidden, bytes_accessed=rows * width * 10 + width * hidden * 8,
                                      transcendentals=rows * hidden),
    )(gy, x1, vec, up, down)


def head(core, inverse, x1, mine, vec, bias, predict, target, band, weight, patches):
    rows, width = x1.shape
    pixels = target.shape[1]
    share = pixels // 2
    other = other_core(mine)
    smem = pl.BlockSpec(memory_space=pltpu.SMEM)
    row_w = pl.BlockSpec((patches, width), lambda i: (i, 0))
    row_p = pl.BlockSpec((patches, pixels), lambda i: (i, 0))
    fix = lambda a, b: pl.BlockSpec((a, b), lambda i: (0, 0))
    return pl.pallas_call(
        head_kernel,
        out_shape=(shape((rows, width), F32), shape((width, share), F32), shape((1, pixels), F32),
                   shape((1, pixels), F32), shape((1, width), F32), shape((1, width), F32)),
        grid=(rows // patches,),
        in_specs=[smem, smem, row_w, row_w, row_w, fix(8, width), fix(1, pixels), fix(width, pixels), row_p, row_p,
                  pl.BlockSpec((patches, 1), lambda i: (i, 0))],
        out_specs=(row_w, fix(width, share), fix(1, pixels), fix(1, pixels), fix(1, width), fix(1, width)),
        scratch_shapes=[pltpu.VMEM((patches, pixels), BF16)],
        compiler_params=pltpu.CompilerParams(vmem_limit_bytes=VMEM_LIMIT),
        cost_estimate=pl.CostEstimate(flops=5 * rows * width * pixels, bytes_accessed=rows * (width * 12 + pixels * 6),
                                      transcendentals=rows * pixels),
    )(core, inverse, x1, mine, other, vec, bias, predict, target, band, weight)


def attn_backward(gy, x1, mine, x, saved, vec, attn, length, group, head_dim):
    qkv, mixed, lse = saved
    rows, width = x.shape
    local = mixed.shape[0]
    return run(
        functools.partial(attn_back_kernel, length, group, head_dim),
        [shape((rows, width), F32), shape((2, width, local), BF16), shape((2, width, local), BF16),
         shape((1, width), F32), shape((1, width), F32), shape((rows, width), BF16)],
        [pltpu.VMEM((4 * local, width), BF16), pltpu.VMEM((width, rows), BF16), pltpu.VMEM((width, rows), BF16),
         pltpu.VMEM((local, group), BF16), pltpu.VMEM((3 * local, rows), BF16)],
        (gy, x1, mine, other_core(mine), x, qkv, mixed, lse, vec, attn),
        18 * rows * width * local)


def sine_table(gsd_values, feature_width, grid_side):
    quarter = feature_width // 4
    frequency = jnp.exp(-jnp.log(10000.0) * jnp.arange(quarter).astype(F32) / quarter)
    gsd_ratio = gsd_values.astype(F32)[:, None, None] / REF_GSD
    line = jnp.arange(grid_side, dtype=jnp.int32).astype(F32)
    arg = line[None, :, None] * gsd_ratio * frequency
    return jnp.concatenate([jnp.sin(arg), jnp.cos(arg)], axis=-1)


def dp_bits():
    return lax.axis_size("dp").bit_length() - 1


def orders():
    bits = dp_bits()
    high = list(range(bits - 1, 1, -1))
    return (high + [0, 1], high + [1, 0])


def swap(block, bit):
    size = lax.axis_size("dp")
    return lax.ppermute(block, "dp", [(i, i ^ (1 << bit)) for i in range(size)])


def my_bit(bit):
    return (lax.axis_index("dp") >> bit) & 1


def gather_dp(block, axis, order):
    lead, rest = (block.shape[:axis], block.shape[axis:])
    done = []
    cur = block
    for bit in order:
        other = swap(cur, bit)
        mine = my_bit(bit) == 1
        place = axis + sum(1 for b in done if b > bit)
        cur = jnp.stack([jnp.where(mine, other, cur), jnp.where(mine, cur, other)], axis=place)
        done.append(bit)
    return cur.reshape(lead + (rest[0] * lax.axis_size("dp"),) + rest[1:])


def reduce_dp(block, axis, order, wire):
    bits = dp_bits()
    lead, rest = (block.shape[:axis], block.shape[axis:])
    shard = rest[0] // lax.axis_size("dp")
    cur = block.reshape(lead + (2,) * bits + (shard,) + rest[1:])
    left = list(range(bits - 1, -1, -1))
    for bit in reversed(order):
        place = axis + left.index(bit)
        mine = my_bit(bit)
        keep = lax.dynamic_index_in_dim(cur, mine, place, keepdims=False)
        give = lax.dynamic_index_in_dim(cur, 1 - mine, place, keepdims=False)
        other = swap(give.astype(wire), bit)
        cur = keep.astype(F32) + other.astype(F32)
        left.remove(bit)
    return cur


def join_cores(mine, core):
    other = other_core(mine)
    return jnp.concatenate([jnp.where(core == 0, mine, other), jnp.where(core == 0, other, mine)], axis=1)


def total_dp(value):
    for bit in range(dp_bits()):
        value = value + swap(value, bit)
    return value


def adam_update(master, gradient, first_old, second_old, step_rate, decay_rate):
    first_new = BETA_ONE * first_old + (1.0 - BETA_ONE) * gradient
    second_new = BETA_TWO * second_old + (1.0 - BETA_TWO) * gradient * gradient
    first_hat = first_new / (1.0 - BETA_ONE**STEP)
    second_hat = second_new / (1.0 - BETA_TWO**STEP)
    updated = master - step_rate * (
        first_hat / (jnp.sqrt(second_hat) + ADAM_EPS) + decay_rate * master
    )
    return (updated, first_new, second_new)


def per_device(
    pixels,
    target,
    band_ids,
    kept_index,
    intersection,
    gsd_scale,
    enc_attn,
    enc_mlp,
    dec_attn,
    dec_mlp,
    patch_embed,
    bridge,
    predict,
    vectors,
    first_enc_attn,
    first_enc_mlp,
    first_dec_attn,
    first_dec_mlp,
    first_patch_embed,
    first_bridge,
    first_predict,
    first_vectors,
    second_enc_attn,
    second_enc_mlp,
    second_dec_attn,
    second_dec_mlp,
    second_patch_embed,
    second_bridge,
    second_predict,
    second_vectors,
    ema_enc_attn,
    ema_enc_mlp,
    ema_patch_embed,
):
    masters = (enc_attn, enc_mlp, dec_attn, dec_mlp, patch_embed, bridge, predict, vectors)
    firsts = (
        first_enc_attn,
        first_enc_mlp,
        first_dec_attn,
        first_dec_mlp,
        first_patch_embed,
        first_bridge,
        first_predict,
        first_vectors,
    )
    seconds = (
        second_enc_attn,
        second_enc_mlp,
        second_dec_attn,
        second_dec_mlp,
        second_patch_embed,
        second_bridge,
        second_predict,
        second_vectors,
    )
    order_a, order_b = orders()
    low = jnp.bfloat16
    embed_w = gather_dp(patch_embed.astype(low).T, 0, order_a)
    vector_low = gather_dp(vectors.astype(low).reshape(1, -1), 0, order_b).reshape(-1)
    enc_attn_w = jnp.concatenate([
        gather_dp(enc_attn[:2].astype(low), 1, order_a),
        gather_dp(enc_attn[2:].astype(low), 1, order_b)])
    enc_mlp_w = [
        gather_dp(enc_mlp[0].astype(low), 0, order_a),
        gather_dp(enc_mlp[1].astype(low), 0, order_b)]
    bridge_w = gather_dp(bridge.astype(low), 0, order_a)
    dec_attn_w = jnp.concatenate([
        gather_dp(dec_attn[:2].astype(low), 1, order_a),
        gather_dp(dec_attn[2:].astype(low), 1, order_b)])
    dec_mlp_w = [
        gather_dp(dec_mlp[0].astype(low), 0, order_a),
        gather_dp(dec_mlp[1].astype(low), 0, order_b)]
    predict_w = gather_dp(predict.astype(low), 0, order_b)
    pieces = split_vectors(vector_low.astype(jnp.float32), D, E)
    images, keep_count = kept_index.shape
    patch_count = intersection.shape[1]
    patch_index = jnp.arange(patch_count, dtype=jnp.int32)
    kept_flags = jnp.any(kept_index[:, :, None] == patch_index[None, None, :], axis=1).astype(
        jnp.float32
    )
    patch_weight = ((1.0 - kept_flags) * (1.0 - 0.5 * intersection.astype(jnp.float32))).reshape(
        -1, 1
    )
    local_counts = jnp.stack(
        [
            jnp.sum(patch_weight * (band_ids == band_level).astype(jnp.float32))
            for band_level in range(NB)
        ]
    )
    band_weight = total_dp(local_counts)
    inverse = 1.0 / band_weight
    core = lax.axis_index("mp").astype(jnp.int32).reshape(1)
    hidden_rows = (1.0 - kept_flags).reshape(-1, 1)
    kept_column = kept_index.reshape(-1, 1)
    rows, rows_d = images * keep_count, images * patch_count
    local, local_d = enc_attn_w.shape[2], dec_attn_w.shape[2]
    pixel_count = pixels.shape[1]
    evec = jnp.stack(pieces[:7] + [jnp.zeros_like(pieces[0])])
    dvec = jnp.stack(pieces[7:14] + [jnp.zeros_like(pieces[7])])
    group = 2 * keep_count
    x0, *enc_saved, part, kept_pixels = run(
        functools.partial(enc_in_kernel, keep_count, group, DH),
        [shape((rows, D), F32), shape((3 * local, rows), BF16), shape((local, rows), BF16),
         shape((local // DH, rows), F32), shape((rows, D), BF16), shape((rows, pixel_count), BF16)],
        [pltpu.VMEM((4 * local, D), BF16)],
        (pixels, kept_column, sine_table(gsd_scale, D, GRID), embed_w, evec, enc_attn_w),
        rows * D * (2 * pixel_count + 8 * local))
    x1, part = mlp_forward(x0, part, evec, *enc_mlp_w)
    x2, final_enc, xd, *dec_saved, part = run(
        functools.partial(dec_in_kernel, keep_count, DDH),
        [shape((rows, D), F32), shape((rows, D), BF16), shape((rows_d, E), F32), shape((3 * local_d, rows_d), BF16),
         shape((local_d, rows_d), BF16), shape((local_d // DDH, rows_d), F32), shape((rows_d, E), BF16)],
        [pltpu.VMEM((4 * local_d, E), BF16), pltpu.VMEM((rows, E), F32)],
        (x1, part, other_core(part), evec, bridge_w, kept_index, hidden_rows, sine_table(gsd_scale, E, GRID), dvec,
         dec_attn_w),
        rows_d * E * 8 * local_d + 2 * rows * D * E)
    xd1, part = mlp_forward(xd, part, dvec, *dec_mlp_w)
    gyd, grad_predict, grad_pbias, loss_parts, grad_dec_fg, grad_dec_fb = head(
        core, inverse, xd1, part, dvec, pieces[14].reshape(1, -1), predict_w, target, band_ids, patch_weight, patch_count)
    loss = total_dp(jnp.sum(loss_parts))
    grad_dec_up, grad_dec_down, part = mlp_backward(gyd, xd1, dvec, *dec_mlp_w)
    gxd, grad_dec_qk, grad_dec_vo, grad_dec_gb, grad_dec_bb, part = attn_backward(
        gyd, xd1, part, xd, dec_saved, dvec, dec_attn_w, patch_count, patch_count, DDH)
    one_d, one_e = shape((1, D), F32), shape((1, E), F32)
    grad_dec_ga, grad_dec_ba, grad_mask, grad_bridge, grad_enc_fg, grad_enc_fb, gye = run(
        functools.partial(between_kernel, keep_count),
        [one_e, one_e, one_e, shape((D, E // 2), BF16), one_d, one_d, shape((rows, D), F32)],
        [pltpu.VMEM((rows, E), BF16)],
        (core, gxd, xd, part, other_core(part), dvec, kept_column, hidden_rows, final_enc, x2, evec, bridge_w),
        3 * rows * D * E, 1)
    grad_enc_up, grad_enc_down, part = mlp_backward(gye, x1, evec, *enc_mlp_w)
    gxe, grad_enc_qk, grad_enc_vo, grad_enc_gb, grad_enc_bb, part = attn_backward(
        gye, x1, part, x0, enc_saved, evec, enc_attn_w, keep_count, group, DH)
    grad_enc_ga, grad_enc_ba, grad_ebias, grad_embed = run(
        enc_out_kernel,
        [one_d, one_d, one_d, shape((D, pixel_count // 2), BF16)],
        [], (core, gxe, x0, part, other_core(part), evec, kept_pixels), rows * D * pixel_count, 1)
    grad_vectors = jnp.concatenate(
        [grad_ebias, grad_enc_ga, grad_enc_ba, grad_enc_gb, grad_enc_bb, grad_enc_fg, grad_enc_fb, grad_mask,
         grad_dec_ga, grad_dec_ba, grad_dec_gb, grad_dec_bb, grad_dec_fg, grad_dec_fb, grad_pbias], axis=1).reshape(-1)
    reduced = (
        jnp.concatenate([
            reduce_dp(grad_enc_qk, 1, order_a, low),
            reduce_dp(grad_enc_vo, 1, order_b, low)]),
        jnp.stack([
            reduce_dp(grad_enc_up, 0, order_a, low),
            reduce_dp(grad_enc_down, 0, order_b, low)]),
        jnp.concatenate([
            reduce_dp(grad_dec_qk, 1, order_a, low),
            reduce_dp(grad_dec_vo, 1, order_b, low)]),
        jnp.stack([
            reduce_dp(grad_dec_up, 0, order_a, low),
            reduce_dp(grad_dec_down, 0, order_b, low)]),
        join_cores(reduce_dp(grad_embed, 0, order_a, low), core).T,
        join_cores(reduce_dp(grad_bridge, 0, order_a, low), core),
        join_cores(reduce_dp(grad_predict, 0, order_b, low), core),
        reduce_dp(grad_vectors, 0, order_b, F32),
    )
    shares = (1.0, 1.0, 1.0, 1.0, 0.5, 0.5, 0.5, 0.5)
    squares = jnp.zeros((), jnp.float32)
    for position, gradient in enumerate(reduced):
        squares = squares + shares[position] * jnp.sum(gradient * gradient)
    total_squares = total_dp(squares)
    total_squares = total_squares + lax.ppermute(total_squares, "mp", [(0, 1), (1, 0)])
    grad_norm = jnp.sqrt(total_squares)
    factor = CLIP / jnp.maximum(grad_norm, CLIP)
    news, new_firsts, new_seconds = ([], [], [])
    for position, master in enumerate(masters):
        is_vec = position == 7
        updated, first_new, second_new = adam_update(
            master,
            reduced[position] * factor,
            firsts[position],
            seconds[position],
            RATE_VEC if is_vec else RATE_MAT,
            0.0 if is_vec else DECAY_MAT,
        )
        news.append(updated)
        new_firsts.append(first_new)
        new_seconds.append(second_new)
    ema_attn = EMA_KEEP * ema_enc_attn + (1.0 - EMA_KEEP) * news[0]
    ema_mlp = EMA_KEEP * ema_enc_mlp + (1.0 - EMA_KEEP) * news[1]
    ema_embed = EMA_KEEP * ema_patch_embed + (1.0 - EMA_KEEP) * news[4]
    return (
        loss,
        band_weight,
        grad_norm,
        news[0],
        news[1],
        news[2],
        news[3],
        news[4],
        news[5],
        news[6],
        news[7],
        new_firsts[0],
        new_firsts[1],
        new_firsts[2],
        new_firsts[3],
        new_firsts[4],
        new_firsts[5],
        new_firsts[6],
        new_firsts[7],
        new_seconds[0],
        new_seconds[1],
        new_seconds[2],
        new_seconds[3],
        new_seconds[4],
        new_seconds[5],
        new_seconds[6],
        new_seconds[7],
        ema_attn,
        ema_mlp,
        ema_embed,
    )


def solution(mesh):
    return jax.shard_map(
        per_device,
        mesh=mesh,
        in_specs=(
            P("dp", None),
            P("dp", None),
            P("dp", None),
            P("dp", None),
            P("dp", None),
            P("dp"),
            P(None, "dp", "mp"),
            P(None, "dp", "mp"),
            P(None, "dp", "mp"),
            P(None, "dp", "mp"),
            P(None, "dp"),
            P("dp", None),
            P("dp", None),
            P("dp"),
            P(None, "dp", "mp"),
            P(None, "dp", "mp"),
            P(None, "dp", "mp"),
            P(None, "dp", "mp"),
            P(None, "dp"),
            P("dp", None),
            P("dp", None),
            P("dp"),
            P(None, "dp", "mp"),
            P(None, "dp", "mp"),
            P(None, "dp", "mp"),
            P(None, "dp", "mp"),
            P(None, "dp"),
            P("dp", None),
            P("dp", None),
            P("dp"),
            P(None, "dp", "mp"),
            P(None, "dp", "mp"),
            P(None, "dp"),
        ),
        out_specs=(
            P(),
            P(),
            P(),
            P(None, "dp", "mp"),
            P(None, "dp", "mp"),
            P(None, "dp", "mp"),
            P(None, "dp", "mp"),
            P(None, "dp"),
            P("dp", None),
            P("dp", None),
            P("dp"),
            P(None, "dp", "mp"),
            P(None, "dp", "mp"),
            P(None, "dp", "mp"),
            P(None, "dp", "mp"),
            P(None, "dp"),
            P("dp", None),
            P("dp", None),
            P("dp"),
            P(None, "dp", "mp"),
            P(None, "dp", "mp"),
            P(None, "dp", "mp"),
            P(None, "dp", "mp"),
            P(None, "dp"),
            P("dp", None),
            P("dp", None),
            P("dp"),
            P(None, "dp", "mp"),
            P(None, "dp", "mp"),
            P(None, "dp"),
        ),
        check_vma=False,
    )
```

time: 1070 us -> 855 us (0.80)
  Pallas kernels: 0 us -> 248 us
  matrix products: 160 us -> 0 us
  other arithmetic: 233 us -> 78.7 us
  local copies, waits for them, and re-layouts: 181 us -> 56.3 us
  waiting for transfers between devices: 335 us -> 315 us
    pallas_call x0 -> x11, Pallas kernels: none -> 248 us  [the longest x6 157 us: run(): pl.pallas_call(kernel, out_shape=tuple(outs), in_specs=[pl.BlockSpec(memo...]
    dot_general x56 -> x0, matrix products: 160 us -> none  [the longest x15 47.8 us: plain_dot(): return jnp.dot(left, right, preferred_element_type=jnp.float32)]
    reduce_sum x26 -> x1, other arithmetic: 60.7 us -> 1.3 us  [per_device(): loss = total_dp(jnp.sum(loss_parts))]
    gather x6 -> x0, local copies, waits for them, and re-layouts: 51.3 us -> none  [the longest x2 30.5 us: per_device(): jnp.take_along_axis(latent.reshape(images, keep_count, E), place[:, :, No...]
    reshape x18 -> x2, local copies, waits for them, and re-layouts: 34.9 us -> 1.49 us  [the longest x1 0.9 us: per_device(): kept_column = kept_index.reshape(-1, 1)]
    sin x3 -> x2, other arithmetic: 32.2 us -> 0.84 us  [sine_table(): return jnp.concatenate([jnp.sin(arg), jnp.cos(arg)], axis=-1)]
    convert_element_type x12 -> x1, other arithmetic: 23.2 us -> 0.01 us  [sine_table(): line = jnp.arange(grid_side, dtype=jnp.int32).astype(F32)]
    ppermute x108, waiting for transfers between devices: 335 us -> 314 us  [swap(): return lax.ppermute(block, 'dp', [(i, i ^ 1 << bit) for i in range(size)])]
  transfers between devices with their start and end apart: 117 -> 120, of which waited for: 70 -> 65; matrix products, arithmetic and copies ran while one was open for 37% -> 13% of each run, Pallas kernels for 0% -> 27%
where the time goes in v2:
time: 855 us; the launch traced here: 845 us
  waiting for transfers between devices  315 us (37%)
  Pallas kernels  248 us (29%)
  starting transfers between devices  130 us (15%)
  other arithmetic  78.7 us (9%)
  local copies, waits for them, and re-layouts  56.3 us (7%)
  between operations  17.5 us (2%)
    ppermute x108, waiting for transfers between devices, swap(): return lax.ppermute(block, 'dp', [(i, i ^ 1 << bit) for i in range(size)])  314 us
    pallas_call x6, Pallas kernels, run(): pl.pallas_call(kernel, out_shape=tuple(outs), in_specs=[pl.BlockSpec(memo...  157 us
    ppermute x108, starting transfers between devices, swap(): return lax.ppermute(block, 'dp', [(i, i ^ 1 << bit) for i in range(size)])  128 us
    pallas_call x2, Pallas kernels, mlp_backward(): pl.pallas_call(functools.partial(mlp_back_kernel, tile), out_shape=(shape...  47.3 us
    pallas_call x2, Pallas kernels, mlp_forward(): pl.pallas_call(functools.partial(mlp_kernel, tile), out_shape=(shape((row...  27.4 us
    add x43, other arithmetic, reduce_dp(): cur = keep.astype(F32) + other.astype(F32)  19.1 us
  transfers between devices with their start and end apart: 120, of which 65 were waited for; matrix products, arithmetic and copies ran while one was open for 13% of the time, Pallas kernels for 27%

profile of v2, /device:TPU:0, one launch (start us, length us, event | category | flops | bytes accessed | tf_op | source)
XLA Modules:
  0.0 845.3 jit_solution(12703508578177258204)
XLA Ops:
  36.0 7.8 collective-permute-done.47
  46.8 9.3 %collective-permute-done.38 = bf16[2,32,256]{2,1,0:T(8,128)(2,1)S(1)} collective-permute-done((bf16[2,32,256]{2,1,0:T(8,128)(2,1)S(1)}, bf16[2,32,256]{2,1,0:T(8,128)(2,1)S(1)}, u32[]{:S(2)}, u32[]{:S(2)}) %collective-permute-start.38) | collective-permute-done | bytes 32800 | tf_op jit(solution)/shard_map/ppermute | solution.py:525
  69.4 8.1 collective-permute-done.31
  137.5 15.1 %collective-permute-done.7 = bf16[2,2,2,64,768]{4,3,0,1,2:T(8,128)(2,1)S(1)} collective-permute-done((bf16[2,2,2,64,768]{4,3,0,1,2:T(8,128)(2,1)S(1)}, bf16[2,2,2,64,768]{4,3,0,1,2:T(8,128)(2,1)S(1)}, u32[]{:S(2)}, u32[]{:S(2)}) %collective-permute-start.7) | collective-permute-done | bytes 786464 | tf_op jit(solution)/shard_map/ppermute | solution.py:525
  157.7 17.4 %collective-permute-done.27 = bf16[2,2,64,2048]{3,2,0,1:T(8,128)(2,1)S(1)} collective-permute-done((bf16[2,2,64,2048]{3,2,0,1:T(8,128)(2,1)S(1)}, bf16[2,2,64,2048]{3,2,0,1:T(8,128)(2,1)S(1)}, u32[]{:S(2)}, u32[]{:S(2)}) %collective-permute-start.27) | collective-permute-done | bytes 1048608 | tf_op jit(solution)/shard_map/ppermute | solution.py:525
  178.3 19.2 %collective-permute-done.15 = bf16[2,2,2,2,64,512]{5,4,0,1,2,3:T(8,128)(2,1)S(1)} collective-permute-done((bf16[2,2,2,2,64,512]{5,4,0,1,2,3:T(8,128)(2,1)S(1)}, bf16[2,2,2,2,64,512]{5,4,0,1,2,3:T(8,128)(2,1)S(1)}, u32[]{:S(2)}, u32[]{:S(2)}) %collective-permute-start.15) | collective-permute-done | bytes 1048608 | tf_op jit(solution)/shard_map/ppermute | solution.py:525
  202.9 27.3 %shard_map.544 = (f32[512,1024]{1,0:T(8,128)}, bf16[1536,512]{1,0:T(8,128)(2,1)}, bf16[512,512]{1,0:T(8,128)(2,1)}, f32[8,512]{1,0:T(8,128)}, bf16[512,1024]{1,0:T(8,128)(2,1)}, /*index=5*/bf16[512,768]{1,0:T(8,128)(2,1)}) custom-call(bf16[2048,768]{1,0:T(8,128)(2,1)} %pix_ref.1, s32[512,1]{1,0:T(8,128)} %reshape.310.kept_ref, ...), custom_call_target="tpu_custom_call" | custom-call | flops 2952790016 | bytes 15255552 | tf_op jit(solution)/shard_map/pallas_call | solution.py:406
  230.2 10.9 %collective-permute-done.24 = bf16[2,2,2,64,2048]{4,3,0,1,2:T(8,128)(2,1)} collective-permute-done((bf16[2,2,2,64,2048]{4,3,0,1,2:T(8,128)(2,1)}, bf16[2,2,2,64,2048]{4,3,0,1,2:T(8,128)(2,1)}, u32[]{:S(2)}, u32[]{:S(2)}) %collective-permute-start.24) | collective-permute-done | bytes 2097184 | tf_op jit(solution)/shard_map/ppermute | solution.py:525
  252.2 11.5 %shard_map.545 = (f32[512,1024]{1,0:T(8,128)}, bf16[512,1024]{1,0:T(8,128)(2,1)}) custom-call(f32[512,1024]{1,0:T(8,128)} %get-tuple-element.82.x_ref, bf16[512,1024]{1,0:T(8,128)(2,1)} %get-tuple-element.83.mine_ref, bf16[512,1024]{1,0:T(8,128)(2,1)} %copy-done.77, f32[8,1024]{1,0:T(8,128)} %stack.545.vec_ref.evec_ref, bf16[1024,2048]{1,0:T(8,128)(2,1)} %bitcast.537, ...), custom_call_target="tpu_custom_call" | custom-call | flops 4294967296 | bytes 15728640 | tf_op jit(solution)/shard_map/pallas_call | solution.py:429
  269.4 39.5 %shard_map.546 = (f32[512,1024]{1,0:T(8,128)}, bf16[512,1024]{1,0:T(8,128)(2,1)}, f32[2048,512]{1,0:T(8,128)}, bf16[768,2048]{1,0:T(8,128)(2,1)}, bf16[256,2048]...) custom-call(f32[512,1024]{1,0:T(8,128)} %get-tuple-element.84.x1_ref, ...), custom_call_target="tpu_custom_call" | custom-call | flops 2684354560 | bytes 20178944 | tf_op jit(solution)/shard_map/pallas_call | solution.py:406
  328.2 15.9 %shard_map.547 = (f32[2048,512]{1,0:T(8,128)}, bf16[2048,512]{1,0:T(8,128)(2,1)}) custom-call(f32[2048,512]{1,0:T(8,128)} %get-tuple-element.86.x_ref, bf16[2048,512]{1,0:T(8,128)(2,1)} %get-tuple-element.87.mine_ref, bf16[2048,512]{1,0:T(8,128)(2,1)} %copy-done.74, f32[8,512]{1,0:T(8,128)} %stack.613.vec_ref, bf16[512,1024]{1,0:T(8,128)(2,1)} %bitcast.549, ...), custom_call_target="tpu_custom_call" | custom-call | flops 4294967296 | bytes 16777216 | tf_op jit(solution)/shard_map/pallas_call | solution.py:429
  372.3 16.0 %shard_map.548 = (f32[2048,512]{1,0:T(8,128)}, f32[512,384]{1,0:T(8,128)}, f32[1,768]{1,0:T(1,128)}, f32[1,768]{1,0:T(1,128)}, f32[1,512]{1,0:T(1,128)}, /*index=5*/f32[1,512]{1,0:T(1,128)}) custom-call(s32[1]{0:T(128)} %bitcast.core_ref, f32[3]{0:T(128)} %get-tuple-element.168.inverse_ref, f32[2048,512]{1,0:T(8,128)} %get-tuple-element.88.x1_ref, ...), custom_call_target="tpu_custom_call" | custom-call | flops 4026531840 | bytes 22020096 | tf_op jit(solution)/shard_map/pallas_call | solution.py:475
  401.9 26.6 %shard_map.549 = (bf16[512,1024]{1,0:T(8,128)(2,1)}, bf16[512,1024]{1,0:T(8,128)(2,1)}, bf16[2048,512]{1,0:T(8,128)(2,1)}) custom-call(f32[2048,512]{1,0:T(8,128)} %get-tuple-element.91.gy_ref, f32[2048,512]{1,0:T(8,128)} %get-tuple-element.88.x1_ref, f32[8,512]{1,0:T(8,128)} %stack.613.vec_ref, bf16[512,1024]{1,0:T(8,128)(2,1)} %bitcast.550, ...), custom_call_target="tpu_custom_call" | custom-call | flops 10737418240 | bytes 14680064 | tf_op jit(solution)/shard_map/pallas_call | solution.py:449
  436.8 10.7 %collective-permute-start.57 = (f32[]{:T(128)}, f32[]{:T(128)}, u32[]{:S(2)}, u32[]{:S(2)}) collective-permute-start(f32[]{:T(128)} %add.489), channel_id=1, source_target_pairs={{0,4},{2,6},{4,0},{6,2},{8,12},{10,14},{12,8},{14,10},{16,20},{18,... | collective-permute-start | bytes 20 | tf_op jit(solution)/shard_map/ppermute | solution.py:525
  480.6 42.5 %shard_map.550 = (f32[2048,512]{1,0:T(8,128)}, bf16[2,512,256]{2,1,0:T(8,128)(2,1)}, bf16[2,512,256]{2,1,0:T(8,128)(2,1)}, f32[1,512]{1,0:T(1,128)}, f32[1,512]{1,0:T(1,128)}, /*index=5*/bf16[2048,512]{1,0:T(8,128)(2,1)}) custom-call(f32[2048,512]{1,0:T(8,128)} %get-tuple-element.91.gy_ref, f32[2048,512]{1,0:T(8,128)} %get-tuple-element.88.x1_ref, ...), custom_call_target="tpu_custom_call" | custom-call | flops 4831838208 | bytes 29446144 | tf_op jit(solution)/shard_map/pallas_call | solution.py:406
  547.7 13.9 %shard_map.551 = (f32[1,512]{1,0:T(1,128)}, f32[1,512]{1,0:T(1,128)}, f32[1,512]{1,0:T(1,128)}, bf16[1024,256]{1,0:T(8,128)(2,1)}, f32[1,1024]{1,0:T(1,128)}, /*index=5*/f32[1,1024]{1,0:T(1,128)}, f32[512,1024]{1,0:T(8,128)}) custom-call(s32[1]{0:T(128)} %bitcast.core_ref, f32[2048,512]{1,0:T(8,128)} %get-tuple-element.96.gx_ref, ...), custom_call_target="tpu_custom_call" | custom-call | flops 805306368 | bytes 19472388 | tf_op jit(solution)/shard_map/pallas_call | solution.py:406
  570.3 20.7 %shard_map.552 = (bf16[1024,2048]{1,0:T(8,128)(2,1)}, bf16[1024,2048]{1,0:T(8,128)(2,1)}, bf16[512,1024]{1,0:T(8,128)(2,1)}) custom-call(f32[512,1024]{1,0:T(8,128)} %get-tuple-element.100.gy_ref, f32[512,1024]{1,0:T(8,128)} %get-tuple-element.84.x1_ref, f32[8,1024]{1,0:T(8,128)} %stack.545.vec_ref.evec_ref, bf16[1024,2048]{1,0:T(8,128)(2,1)} %bitcast.538, ...), custom_call_target="tpu_custom_call" | custom-call | flops 10737418240 | bytes 22020096 | tf_op jit(solution)/shard_map/pallas_call | solution.py:449
  607.4 27.6 %shard_map.553 = (f32[512,1024]{1,0:T(8,128)}, bf16[2,1024,512]{2,1,0:T(8,128)(2,1)}, bf16[2,1024,512]{2,1,0:T(8,128)(2,1)}, f32[1,1024]{1,0:T(1,128)}, f32[1,1024]{1,0:T(1,128)}, /*index=5*/bf16[512,1024]{1,0:T(8,128)(2,1)}) custom-call(f32[512,1024]{1,0:T(8,128)} %get-tuple-element.100.gy_ref, f32[512,1024]{1,0:T(8,128)} %get-tuple-element.84.x1_ref, ...), custom_call_target="tpu_custom_call" | custom-call | flops 4831838208 | bytes 22077440 | tf_op jit(solution)/shard_map/pallas_call | solution.py:406
  672.3 17.3 %collective-permute-done.111 = f32[2,2,2,720]{3,2,1,0:T(2,128)S(1)} collective-permute-done((f32[2,2,2,720]{3,2,1,0:T(2,128)S(1)}, f32[2,2,2,720]{3,2,1,0:T(2,128)S(1)}, u32[]{:S(2)}, u32[]{:S(2)}) %collective-permute-start.111) | collective-permute-done | bytes 23072 | tf_op jit(solution)/shard_map/ppermute | solution.py:525
  691.7 15.4 %collective-permute-done.112 = f32[2,2,720]{2,1,0:T(2,128)S(1)} collective-permute-done((f32[2,2,720]{2,1,0:T(2,128)S(1)}, f32[2,2,720]{2,1,0:T(2,128)S(1)}, u32[]{:S(2)}, u32[]{:S(2)}) %collective-permute-start.112) | collective-permute-done | bytes 11552 | tf_op jit(solution)/shard_map/ppermute | solution.py:525
  722.5 8.7 %collective-permute-done.97 = bf16[2,2,64,384]{3,2,0,1:T(8,128)(2,1)S(1)} collective-permute-done((bf16[2,2,64,384]{3,2,0,1:T(8,128)(2,1)S(1)}, bf16[2,2,64,384]{3,2,0,1:T(8,128)(2,1)S(1)}, u32[]{:S(2)}, u32[]{:S(2)}) %collective-permute-start.97) | collective-permute-done | bytes 196640 | tf_op jit(solution)/shard_map/ppermute | solution.py:525
  765.0 11.0 %collective-permute-done.77 = bf16[2,64,2048]{2,1,0:T(8,128)(2,1)S(1)} collective-permute-done((bf16[2,64,2048]{2,1,0:T(8,128)(2,1)S(1)}, bf16[2,64,2048]{2,1,0:T(8,128)(2,1)S(1)}, u32[]{:S(2)}, u32[]{:S(2)}) %collective-permute-start.77) | collective-permute-done | bytes 524320 | tf_op jit(solution)/shard_map/ppermute | solution.py:525
  776.2 15.7 %collective-permute-done.73 = bf16[2,64,2048]{2,1,0:T(8,128)(2,1)S(1)} collective-permute-done((bf16[2,64,2048]{2,1,0:T(8,128)(2,1)S(1)}, bf16[2,64,2048]{2,1,0:T(8,128)(2,1)S(1)}, u32[]{:S(2)}, u32[]{:S(2)}) %collective-permute-start.73) | collective-permute-done | bytes 524320 | tf_op jit(solution)/shard_map/ppermute | solution.py:525
  792.4 12.8 %collective-permute-done.74 = bf16[64,2048]{1,0:T(8,128)(2,1)S(1)} collective-permute-done((bf16[64,2048]{1,0:T(8,128)(2,1)S(1)}, bf16[64,2048]{1,0:T(8,128)(2,1)S(1)}, u32[]{:S(2)}, u32[]{:S(2)}) %collective-permute-start.74) | collective-permute-done | bytes 262176 | tf_op jit(solution)/shard_map/ppermute | solution.py:525
  (679 shorter events, 406.6 us)
Async XLA Ops:
  6.4 337.8 %collective-permute-start.52 = (bf16[32,768]{1,0:T(8,128)(2,1)S(1)}, bf16[32,768]{1,0:T(8,128)(2,1)S(1)}, u32[]{:S(2)}, u32[]{:S(2)}) collective-permute-start(bf16[32,768]{1,0:T(8,128)(2,1)S(1)} %convert_element_type.492), channel_id=1, source_target_pairs={{0,16},{2,18},{4,20},{6,22},{8,24},{10,26},{12,28},{14,30},{16,0},... | collective-permute-start | bytes 147464 | tf_op jit(solution)/shard_map/ppermute | solution.py:525
  12.3 48.9 %collective-permute-start.4 = (bf16[64,768]{1,0:T(8,128)(2,1)S(1)}, bf16[64,768]{1,0:T(8,128)(2,1)S(1)}, u32[]{:S(2)}, u32[]{:S(2)}) collective-permute-start(bf16[64,768]{1,0:T(8,128)(2,1)S(1)} %convert_bitcast_fusion), channel_id=1, source_target_pairs={{0,16},{2,18},{4,20},{6,22},{8,24},{10,26},{12,28},{14,30},{16,0},... | collective-permute-start | bytes 294920 | tf_op jit(solution)/shard_map/ppermute | solution.py:525
  35.6 33.7 %collective-permute-start.12 = (bf16[2,64,512]{2,1,0:T(8,128)(2,1)S(1)}, bf16[2,64,512]{2,1,0:T(8,128)(2,1)S(1)}, u32[]{:S(2)}, u32[]{:S(2)}) collective-permute-start(bf16[2,64,512]{2,1,0:T(8,128)(2,1)S(1)} %slice.107), channel_id=1, source_target_pairs={{0,16},{2,18},{4,20},{6,22},{8,24},{10,26},{12,28},{14,30},{16,0},... | collective-permute-start | bytes 393224 | tf_op jit(solution)/shard_map/ppermute | solution.py:525
  43.8 53.2 %collective-permute-start.25 = (bf16[64,2048]{1,0:T(8,128)(2,1)}, bf16[64,2048]{1,0:T(8,128)(2,1)S(1)}, u32[]{:S(2)}, u32[]{:S(2)}) collective-permute-start(bf16[64,2048]{1,0:T(8,128)(2,1)} %get-tuple-element.238), channel_id=1, source_target_pairs={{0,16},{2,18},{4,20},{6,22},{8,24},{10,26},{12,28},{14,30},{16,0},... | collective-permute-start | bytes 786440 | tf_op jit(solution)/shard_map/ppermute | solution.py:525
  60.4 37.4 %collective-permute-start.21 = (bf16[64,2048]{1,0:T(8,128)(2,1)}, bf16[64,2048]{1,0:T(8,128)(2,1)S(1)}, u32[]{:S(2)}, u32[]{:S(2)}) collective-permute-start(bf16[64,2048]{1,0:T(8,128)(2,1)} %get-tuple-element.239), channel_id=1, source_target_pairs={{0,16},{2,18},{4,20},{6,22},{8,24},{10,26},{12,28},{14,30},{16,0},... | collective-permute-start | bytes 786440 | tf_op jit(solution)/shard_map/ppermute | solution.py:525
  97.1 211.9 %collective-permute-start.45 = (bf16[2,2,32,1024]{3,2,0,1:T(8,128)(2,1)}, bf16[2,2,32,1024]{3,2,0,1:T(8,128)(2,1)}, u32[]{:S(2)}, u32[]{:S(2)}) collective-permute-start(bf16[2,2,32,1024]{3,2,0,1:T(8,128)(2,1)} %pad_maximum_fusion.37), channel_id=1, source_target_pairs={{0,2},{2,0},{4,6},{6,4},{8,10},{10,8},{12,14},{14,12},{16,18},{18,... | collective-permute-start | bytes 786440 | tf_op jit(solution)/shard_map/ppermute | solution.py:525
  135.8 39.3 %collective-permute-start.27 = (bf16[2,2,64,2048]{3,2,0,1:T(8,128)(2,1)S(1)}, bf16[2,2,64,2048]{3,2,0,1:T(8,128)(2,1)S(1)}, u32[]{:S(2)}, u32[]{:S(2)}) collective-permute-start(bf16[2,2,64,2048]{3,2,0,1:T(8,128)(2,1)S(1)} %pad_maximum_fusion.11), channel_id=1, source_target_pairs={{0,4},{2,6},{4,0},{6,2},{8,12},{10,14},{12,8},{14,10},{16,20},{18,... | collective-permute-start | bytes 3145736 | tf_op jit(solution)/shard_map/ppermute | solution.py:525
  152.6 44.9 %collective-permute-start.15 = (bf16[2,2,2,2,64,512]{5,4,0,1,2,3:T(8,128)(2,1)S(1)}, bf16[2,2,2,2,64,512]{5,4,0,1,2,3:T(8,128)(2,1)S(1)}, u32[]{:S(2)}, u32[]{:S(2)}) collective-permute-start(bf16[2,2,2,2,64,512]{5,4,0,1,2,3:T(8,128)(2,1)S(1)} %pad_maximum_fusion.8), channel_id=1, source_target_pairs={{0,4},{2,6},{4,0},{6,2},{8,12},{10,14},{12,8},{14,10},{16,20},{18,... | collective-permute-start | bytes 3145736 | tf_op jit(solution)/shard_map/ppermute | solution.py:525
  155.7 42.7 %collective-permute-start.19 = (bf16[2,2,2,2,64,512]{5,4,0,1,2,3:T(8,128)(2,1)S(1)}, bf16[2,2,2,2,64,512]{5,4,0,1,2,3:T(8,128)(2,1)S(1)}, u32[]{:S(2)}, u32[]{:S(2)}) collective-permute-start(bf16[2,2,2,2,64,512]{5,4,0,1,2,3:T(8,128)(2,1)S(1)} %pad_maximum_fusion.9), channel_id=1, source_target_pairs={{0,2},{2,0},{4,6},{6,4},{8,10},{10,8},{12,14},{14,12},{16,18},{18,... | collective-permute-start | bytes 3145736 | tf_op jit(solution)/shard_map/ppermute | solution.py:525
  175.1 66.0 %collective-permute-start.24 = (bf16[2,2,2,64,2048]{4,3,0,1,2:T(8,128)(2,1)}, bf16[2,2,2,64,2048]{4,3,0,1,2:T(8,128)(2,1)}, u32[]{:S(2)}, u32[]{:S(2)}) collective-permute-start(bf16[2,2,2,64,2048]{4,3,0,1,2:T(8,128)(2,1)} %pad_maximum_fusion.5), channel_id=1, source_target_pairs={{0,4},{2,6},{4,0},{6,2},{8,12},{10,14},{12,8},{14,10},{16,20},{18,... | collective-permute-start | bytes 6291464 | tf_op jit(solution)/shard_map/ppermute | solution.py:525
  197.6 48.1 %collective-permute-start.28 = (bf16[2,2,2,64,2048]{4,3,0,1,2:T(8,128)(2,1)}, bf16[2,2,2,64,2048]{4,3,0,1,2:T(8,128)(2,1)}, u32[]{:S(2)}, u32[]{:S(2)}) collective-permute-start(bf16[2,2,2,64,2048]{4,3,0,1,2:T(8,128)(2,1)} %pad_maximum_fusion.6), channel_id=1, source_target_pairs={{0,2},{2,0},{4,6},{6,4},{8,10},{10,8},{12,14},{14,12},{16,18},{18,... | collective-permute-start | bytes 6291464 | tf_op jit(solution)/shard_map/ppermute | solution.py:525
  198.4 65.3 %collective-permute-start.37 = (bf16[2,2,2,2,32,256]{5,4,0,1,2,3:T(8,128)(2,1)}, bf16[2,2,2,2,32,256]{5,4,0,1,2,3:T(8,128)(2,1)}, u32[]{:S(2)}, u32[]{:S(2)}) collective-permute-start(bf16[2,2,2,2,32,256]{5,4,0,1,2,3:T(8,128)(2,1)} %pad_maximum_fusion.35), channel_id=1, source_target_pairs={{0,4},{2,6},{4,0},{6,2},{8,12},{10,14},{12,8},{14,10},{16,20},{18,... | collective-permute-start | bytes 786440 | tf_op jit(solution)/shard_map/ppermute | solution.py:525
  264.8 46.4 %collective-permute-start.49 = (bf16[2,2,32,1024]{3,2,0,1:T(8,128)(2,1)S(1)}, bf16[2,2,32,1024]{3,2,0,1:T(8,128)(2,1)S(1)}, u32[]{:S(2)}, u32[]{:S(2)}) collective-permute-start(bf16[2,2,32,1024]{3,2,0,1:T(8,128)(2,1)S(1)} %pad_maximum_fusion.38), channel_id=1, source_target_pairs={{0,4},{2,6},{4,0},{6,2},{8,12},{10,14},{12,8},{14,10},{16,20},{18,... | collective-permute-start | bytes 786440 | tf_op jit(solution)/shard_map/ppermute | solution.py:525
  398.3 37.2 %collective-permute-start.56 = (f32[]{:T(128)}, f32[]{:T(128)}, u32[]{:S(2)}, u32[]{:S(2)}) collective-permute-start(f32[]{:T(128)} %reduce_sum.111), channel_id=1, source_target_pairs={{0,2},{2,0},{4,6},{6,4},{8,10},{10,8},{12,14},{14,12},{16,18},{18,... | collective-permute-start | bytes 20 | tf_op jit(solution)/shard_map/ppermute | solution.py:525
  430.9 30.4 %collective-permute-start.91 = (bf16[2,2,2,32,1024]{4,3,0,1,2:T(8,128)(2,1)}, bf16[2,2,2,32,1024]{4,3,0,1,2:T(8,128)(2,1)}, u32[]{:S(2)}, u32[]{:S(2)}) collective-permute-start(bf16[2,2,2,32,1024]{4,3,0,1,2:T(8,128)(2,1)} %bitcast.521), channel_id=1, source_target_pairs={{0,2},{2,0},{4,6},{6,4},{8,10},{10,8},{12,14},{14,12},{16,18},{18,... | collective-permute-start | bytes 1572872 | tf_op jit(solution)/shard_map/ppermute | solution.py:525
  435.4 45.2 %collective-permute-start.60 = (bf16[2048,512]{1,0:T(8,128)(2,1)S(1)}, bf16[2048,512]{1,0:T(8,128)(2,1)}, u32[]{:S(2)}, u32[]{:S(2)}) collective-permute-start(bf16[2048,512]{1,0:T(8,128)(2,1)S(1)} %copy-done.9), channel_id=1, source_target_pairs={{0,1},{1,0},{2,3},{3,2},{4,5},{5,4},{6,7},{7,6},{8,9},{9,8},{10,11... | collective-permute-start | bytes 6291464 | tf_op jit(solution)/shard_map/ppermute | solution.py:418
  477.1 48.2 %collective-permute-start.90 = (bf16[32,1024]{1,0:T(8,128)(2,1)S(1)}, bf16[32,1024]{1,0:T(8,128)(2,1)S(1)}, u32[]{:S(2)}, u32[]{:S(2)}) collective-permute-start(bf16[32,1024]{1,0:T(8,128)(2,1)S(1)} %fusion.38), channel_id=1, source_target_pairs={{0,16},{2,18},{4,20},{6,22},{8,24},{10,26},{12,28},{14,30},{16,0},... | collective-permute-start | bytes 196616 | tf_op jit(solution)/shard_map/ppermute | solution.py:525
  563.9 40.3 %collective-permute-start.86 = (bf16[2,32,256]{2,1,0:T(8,128)(2,1)S(1)}, bf16[2,32,256]{2,1,0:T(8,128)(2,1)S(1)}, u32[]{:S(2)}, u32[]{:S(2)}) collective-permute-start(bf16[2,32,256]{2,1,0:T(8,128)(2,1)S(1)} %fusion.44), channel_id=1, source_target_pairs={{0,16},{2,18},{4,20},{6,22},{8,24},{10,26},{12,28},{14,30},{16,0},... | collective-permute-start | bytes 98312 | tf_op jit(solution)/shard_map/ppermute | solution.py:525
  595.9 48.4 %collective-permute-start.75 = (bf16[2,2,2,64,2048]{4,3,0,1,2:T(8,128)(2,1)}, bf16[2,2,2,64,2048]{4,3,0,1,2:T(8,128)(2,1)}, u32[]{:S(2)}, u32[]{:S(2)}) collective-permute-start(bf16[2,2,2,64,2048]{4,3,0,1,2:T(8,128)(2,1)} %bitcast.517), channel_id=1, source_target_pairs={{0,2},{2,0},{4,6},{6,4},{8,10},{10,8},{12,14},{14,12},{16,18},{18,... | collective-permute-start | bytes 6291464 | tf_op jit(solution)/shard_map/ppermute | solution.py:525
  603.0 48.8 %collective-permute-start.71 = (bf16[2,2,2,64,2048]{4,3,0,1,2:T(8,128)(2,1)}, bf16[2,2,2,64,2048]{4,3,0,1,2:T(8,128)(2,1)}, u32[]{:S(2)}, u32[]{:S(2)}) collective-permute-start(bf16[2,2,2,64,2048]{4,3,0,1,2:T(8,128)(2,1)} %bitcast.518), channel_id=1, source_target_pairs={{0,4},{2,6},{4,0},{6,2},{8,12},{10,14},{12,8},{14,10},{16,20},{18,... | collective-permute-start | bytes 6291464 | tf_op jit(solution)/shard_map/ppermute | solution.py:525
  641.9 66.4 %collective-permute-start.63 = (bf16[2,2,2,2,64,512]{5,4,0,1,2,3:T(8,128)(2,1)}, bf16[2,2,2,2,64,512]{5,4,0,1,2,3:T(8,128)(2,1)}, u32[]{:S(2)}, u32[]{:S(2)}) collective-permute-start(bf16[2,2,2,2,64,512]{5,4,0,1,2,3:T(8,128)(2,1)} %bitcast.520), channel_id=1, source_target_pairs={{0,4},{2,6},{4,0},{6,2},{8,12},{10,14},{12,8},{14,10},{16,20},{18,... | collective-permute-start | bytes 3145736 | tf_op jit(solution)/shard_map/ppermute | solution.py:525
  647.8 110.9 %collective-permute-start.76 = (bf16[2,2,64,2048]{3,2,0,1:T(8,128)(2,1)}, bf16[2,2,64,2048]{3,2,0,1:T(8,128)(2,1)}, u32[]{:S(2)}, u32[]{:S(2)}) collective-permute-start(bf16[2,2,64,2048]{3,2,0,1:T(8,128)(2,1)} %fusion.2), channel_id=1, source_target_pairs={{0,4},{2,6},{4,0},{6,2},{8,12},{10,14},{12,8},{14,10},{16,20},{18,... | collective-permute-start | bytes 3145736 | tf_op jit(solution)/shard_map/ppermute | solution.py:525
  656.5 104.8 %collective-permute-start.72 = (bf16[2,2,64,2048]{3,2,0,1:T(8,128)(2,1)}, bf16[2,2,64,2048]{3,2,0,1:T(8,128)(2,1)}, u32[]{:S(2)}, u32[]{:S(2)}) collective-permute-start(bf16[2,2,64,2048]{3,2,0,1:T(8,128)(2,1)} %fusion.1), channel_id=1, source_target_pairs={{0,2},{2,0},{4,6},{6,4},{8,10},{10,8},{12,14},{14,12},{16,18},{18,... | collective-permute-start | bytes 3145736 | tf_op jit(solution)/shard_map/ppermute | solution.py:525
  671.2 49.9 %collective-permute-start.68 = (bf16[2,2,2,64,512]{4,3,0,1,2:T(8,128)(2,1)}, bf16[2,2,2,64,512]{4,3,0,1,2:T(8,128)(2,1)}, u32[]{:S(2)}, u32[]{:S(2)}) collective-permute-start(bf16[2,2,2,64,512]{4,3,0,1,2:T(8,128)(2,1)} %fusion.5), channel_id=1, source_target_pairs={{0,4},{2,6},{4,0},{6,2},{8,12},{10,14},{12,8},{14,10},{16,20},{18,... | collective-permute-start | bytes 1572872 | tf_op jit(solution)/shard_map/ppermute | solution.py:525
  (174 other events, 2033.4 us)

commit v3 on v2

--- a/solution.py
+++ b/solution.py
@@ -139,9 +139,10 @@
 
 
 def transposed_weights(attn_ref, flat_ref):
-    width = attn_ref.shape[2]
+    width = attn_ref.shape[1] // 4
     for part in range(4):
-        flat_ref[pl.ds(part * width, width), :] = attn_ref[part].T
+        at = pl.ds(part * width, width)
+        flat_ref[at, :] = attn_ref[:, at].T
 
 
 def attention_rows(unit, vec_ref, flat_ref, qkv_ref, mixed_ref, lse_ref, part_ref, rows, head_dim, mask, attn_ref):
@@ -149,7 +150,7 @@
     low = (unit * vec_ref[1:2, :] + vec_ref[2:3, :]).astype(BF16)
     qkv_ref[:, rows] = dot_nt(flat_ref[: 3 * width, :], low).astype(BF16)
     attend(qkv_ref, mixed_ref, lse_ref, rows, width, head_dim, mask)
-    part_ref[rows, :] = dot_nt(mixed_ref[:, rows].T, attn_ref[3]).astype(BF16)
+    part_ref[rows, :] = dot_nt(mixed_ref[:, rows].T, attn_ref[:, 3 * width :]).astype(BF16)
 
 
 def enc_in_kernel(length, group, head_dim, pix_ref, kept_ref, table_ref, embed_ref, vec_ref, attn_ref,
@@ -176,7 +177,9 @@
 
     def step(number, carry):
         rows = pl.ds(pl.multiple_of(number * group, group), group)
-        rows_x = dot_nt(pixk_ref[rows, :], embed_ref[...]) + vec_ref[0:1, :] + x_ref[rows, :]
+        share = embed_ref.shape[2]
+        rows_x = dot_nt(pixk_ref[rows, :share], embed_ref[0]) + dot_nt(pixk_ref[rows, share:], embed_ref[1])
+        rows_x = rows_x + vec_ref[0:1, :] + x_ref[rows, :]
         x_ref[rows, :] = rows_x
         unit, _ = normalize(rows_x)
         attention_rows(unit, vec_ref, flat_ref, qkv_ref, mixed_ref, lse_ref, part_ref, rows, head_dim, mask, attn_ref)
@@ -197,7 +200,9 @@
     unit, _ = normalize(out)
     final = (unit * evec_ref[5:6, :] + evec_ref[6:7, :]).astype(BF16)
     final_ref[...] = final
-    latent_ref[...] = dot_nn(final, bridge_ref[...])
+    share = bridge_ref.shape[2]
+    latent_ref[:, :share] = dot_nn(final, bridge_ref[0])
+    latent_ref[:, share:] = dot_nn(final, bridge_ref[1])
 
     def step(image, carry):
         rows = pl.ds(pl.multiple_of(image * patches, patches), patches)
@@ -248,7 +253,7 @@
 
 
 def head_kernel(core_ref, inverse_ref, x1_ref, mine_ref, other_ref, vec_ref, bias_ref, predict_ref, target_ref,
-                band_ref, weight_ref, gy_ref, gpred_ref, gbias_ref, loss_ref, gain_ref, shift_ref, low_ref):
+                band_ref, weight_ref, gy_ref, glow_ref, gbias_ref, loss_ref, gain_ref, shift_ref, low_ref, gpred_ref):
     number = pl.program_id(0)
 
     @pl.when(number == 0)
@@ -260,7 +265,9 @@
     unit, rstd = normalize(x1_ref[...] + both(mine_ref, other_ref, every))
     gain = vec_ref[5:6, :]
     final = (unit * gain + vec_ref[6:7, :]).astype(BF16)
-    mismatch = dot_nn(final, predict_ref[...]) + bias_ref[...] - target_ref[...].astype(F32)
+    share = gpred_ref.shape[1]
+    predicted = jnp.concatenate([dot_nn(final, predict_ref[0]), dot_nn(final, predict_ref[1])], axis=1)
+    mismatch = predicted + bias_ref[...] - target_ref[...].astype(F32)
     band = band_ref[...]
     level = jnp.where(band == 0, inverse_ref[0], jnp.where(band == 1, inverse_ref[1], inverse_ref[2]))
     level = level * weight_ref[...]
@@ -270,14 +277,17 @@
     grad = level * (mismatch * root)
     gbias_ref[...] += jnp.sum(grad, axis=0, keepdims=True)
     low_ref[...] = grad.astype(BF16)
-    share = gpred_ref.shape[1]
     columns = pl.ds(pl.multiple_of(core_ref[0] * share, share), share)
     gpred_ref[...] += dot_tn(final, low_ref[:, columns])
-    grad_final = dot_nt(low_ref[...], predict_ref[...])
+    grad_final = dot_nt(low_ref[:, :share], predict_ref[0]) + dot_nt(low_ref[:, share:], predict_ref[1])
     grad_in, gain_sum, shift_sum = norm_back(grad_final, gain, unit, rstd)
     gy_ref[...] = grad_in
     gain_ref[...] += gain_sum
     shift_ref[...] += shift_sum
+
+    @pl.when(number == pl.num_programs(0) - 1)
+    def _():
+        glow_ref[...] = gpred_ref[...].astype(BF16)
 
 
 def mlp_back_kernel(tile, gy_ref, x1_ref, vec_ref, up_ref, down_ref, gup_ref, gdown_ref, part_ref,
@@ -322,7 +332,7 @@
 
 
 def attn_back_kernel(length, group, head_dim, gy_ref, x1_ref, mine_ref, other_ref, x_ref, qkv_ref, mixed_ref, lse_ref,
-                     vec_ref, attn_ref, gx_ref, gqk_ref, gvo_ref, gain_ref, shift_ref, part_ref,
+                     vec_ref, attn_ref, gx_ref, grad_ref, gain_ref, shift_ref, part_ref,
                      flat_ref, lowt_ref, gradt_ref, gmix_ref, gqkv_ref):
     width = mixed_ref.shape[0]
     transposed_weights(attn_ref, flat_ref)
@@ -348,10 +358,8 @@
         return carry
 
     lax.fori_loop(0, x_ref.shape[0] // group, step, 0)
-    gqk_ref[0] = dot_nt(lowt_ref[...], gqkv_ref[:width, :]).astype(BF16)
-    gqk_ref[1] = dot_nt(lowt_ref[...], gqkv_ref[width : 2 * width, :]).astype(BF16)
-    gvo_ref[0] = dot_nt(lowt_ref[...], gqkv_ref[2 * width :, :]).astype(BF16)
-    gvo_ref[1] = dot_nt(gradt_ref[...], mixed_ref[...]).astype(BF16)
+    grad_ref[:, : 3 * width] = dot_nt(lowt_ref[...], gqkv_ref[...]).astype(BF16)
+    grad_ref[:, 3 * width :] = dot_nt(gradt_ref[...], mixed_ref[...]).astype(BF16)
 
 
 def between_kernel(length, core_ref, gx_ref, x_ref, mine_ref, other_ref, vec_ref, kept_ref, hidden_ref, final_ref, x2_ref,
@@ -379,7 +387,7 @@
     share = gbridge_ref.shape[1]
     columns = pl.ds(pl.multiple_of(core_ref[0] * share, share), share)
     gbridge_ref[...] = dot_tn(final_ref[...], latent_ref[:, columns]).astype(BF16)
-    grad_final = dot_nt(latent_ref[...], bridge_ref[...])
+    grad_final = dot_nt(latent_ref[:, :share], bridge_ref[0]) + dot_nt(latent_ref[:, share:], bridge_ref[1])
     unit, rstd = normalize(x2_ref[...])
     gy_ref[...], egain_ref[...], eshift_ref[...] = norm_back(grad_final, evec_ref[5:6, :], unit, rstd)
 
@@ -418,39 +426,41 @@
     return lax.ppermute(block, "mp", [(0, 1), (1, 0)])
 
 
-def mlp_forward(x, mine, vec, up, down):
+def mlp_forward(x, mine, vec, stack):
     rows, width = x.shape
-    hidden = up.shape[1]
+    hidden = stack.shape[1] // 2
     block = min(hidden, 512)
     tile = min(rows, 512)
     other = other_core(mine)
     whole = pl.BlockSpec((rows, width), lambda i: (0, 0))
     cols = pl.BlockSpec((width, block), lambda i: (0, i))
+    later = pl.BlockSpec((width, block), lambda i: (0, i + hidden // block))
     return pl.pallas_call(
         functools.partial(mlp_kernel, tile),
         out_shape=(shape((rows, width), F32), shape((rows, width), BF16)),
         grid=(hidden // block,),
-        in_specs=[whole] * 3 + [pl.BlockSpec((8, width), lambda i: (0, 0)), cols, cols],
+        in_specs=[whole] * 3 + [pl.BlockSpec((8, width), lambda i: (0, 0)), cols, later],
         out_specs=(whole, whole),
         scratch_shapes=[pltpu.VMEM((rows, width), BF16), pltpu.VMEM((rows, width), F32)],
         compiler_params=pltpu.CompilerParams(vmem_limit_bytes=VMEM_LIMIT),
         cost_estimate=pl.CostEstimate(flops=4 * rows * width * hidden, bytes_accessed=rows * width * 14 + width * hidden * 4,
                                       transcendentals=rows * hidden),
-    )(x, mine, other, vec, up, down)
-
-
-def mlp_backward(gy, x1, vec, up, down):
+    )(x, mine, other, vec, stack, stack)
+
+
+def mlp_backward(gy, x1, vec, stack):
     rows, width = x1.shape
-    hidden = up.shape[1]
+    hidden = stack.shape[1] // 2
     block = min(hidden, 512)
     tile = min(rows, 256)
     whole = pl.BlockSpec((rows, width), lambda i: (0, 0))
     cols = pl.BlockSpec((width, block), lambda i: (0, i))
+    later = pl.BlockSpec((width, block), lambda i: (0, i + hidden // block))
     return pl.pallas_call(
         functools.partial(mlp_back_kernel, tile),
         out_shape=(shape((width, hidden), BF16), shape((width, hidden), BF16), shape((rows, width), BF16)),
         grid=(hidden // block,),
-        in_specs=[whole] * 2 + [pl.BlockSpec((8, width), lambda i: (0, 0)), cols, cols],
+        in_specs=[whole] * 2 + [pl.BlockSpec((8, width), lambda i: (0, 0)), cols, later],
         out_specs=(cols, cols, whole),
         scratch_shapes=[
             pltpu.VMEM((rows, width), BF16), pltpu.VMEM((width, rows), BF16),
@@ -460,7 +470,7 @@
         compiler_params=pltpu.CompilerParams(vmem_limit_bytes=VMEM_LIMIT),
         cost_estimate=pl.CostEstimate(flops=10 * rows * width * hidden, bytes_accessed=rows * width * 10 + width * hidden * 8,
                                       transcendentals=rows * hidden),
-    )(gy, x1, vec, up, down)
+    )(gy, x1, vec, stack, stack)
 
 
 def head(core, inverse, x1, mine, vec, bias, predict, target, band, weight, patches):
@@ -474,13 +484,13 @@
     fix = lambda a, b: pl.BlockSpec((a, b), lambda i: (0, 0))
     return pl.pallas_call(
         head_kernel,
-        out_shape=(shape((rows, width), F32), shape((width, share), F32), shape((1, pixels), F32),
+        out_shape=(shape((rows, width), F32), shape((width, share), BF16), shape((1, pixels), F32),
                    shape((1, pixels), F32), shape((1, width), F32), shape((1, width), F32)),
         grid=(rows // patches,),
-        in_specs=[smem, smem, row_w, row_w, row_w, fix(8, width), fix(1, pixels), fix(width, pixels), row_p, row_p,
+        in_specs=[smem, smem, row_w, row_w, row_w, fix(8, width), fix(1, pixels), pl.BlockSpec((2, width, share), lambda i: (0, 0, 0)), row_p, row_p,
                   pl.BlockSpec((patches, 1), lambda i: (i, 0))],
         out_specs=(row_w, fix(width, share), fix(1, pixels), fix(1, pixels), fix(1, width), fix(1, width)),
-        scratch_shapes=[pltpu.VMEM((patches, pixels), BF16)],
+        scratch_shapes=[pltpu.VMEM((patches, pixels), BF16), pltpu.VMEM((width, share), F32)],
         compiler_params=pltpu.CompilerParams(vmem_limit_bytes=VMEM_LIMIT),
         cost_estimate=pl.CostEstimate(flops=5 * rows * width * pixels, bytes_accessed=rows * (width * 12 + pixels * 6),
                                       transcendentals=rows * pixels),
@@ -493,7 +503,7 @@
     local = mixed.shape[0]
     return run(
         functools.partial(attn_back_kernel, length, group, head_dim),
-        [shape((rows, width), F32), shape((2, width, local), BF16), shape((2, width, local), BF16),
+        [shape((rows, width), F32), shape((width, 4 * local), BF16),
          shape((1, width), F32), shape((1, width), F32), shape((rows, width), BF16)],
         [pltpu.VMEM((4 * local, width), BF16), pltpu.VMEM((width, rows), BF16), pltpu.VMEM((width, rows), BF16),
          pltpu.VMEM((local, group), BF16), pltpu.VMEM((3 * local, rows), BF16)],
@@ -568,6 +578,294 @@
     for bit in range(dp_bits()):
         value = value + swap(value, bit)
     return value
+
+
+def place_of():
+    index = lax.axis_index("dp")
+    core = lax.axis_index("mp")
+    low, high = lax.rem(index, 4), index // 4
+    bit_x, bit_y = lax.rem(low, 2), low // 2
+    low_x, low_y = low + 1 - 2 * bit_x, low + 2 - 4 * bit_y
+    return core, low, high, low_x, low_y
+
+
+def greet(partners):
+    barrier = pltpu.get_barrier_semaphore()
+    for partner in partners:
+        pl.semaphore_signal(barrier, inc=1, device_id=partner, device_id_type=pl.DeviceIdType.MESH)
+    pl.semaphore_wait(barrier, len(partners))
+
+
+def blocks_of(widths, limit):
+    found = []
+    for number, width in enumerate(widths):
+        start = 0
+        while start < width:
+            size = min(limit, width - start)
+            found.append((number, start, size))
+            start += size
+    return found
+
+
+def gather_kernel(highs, shared, groups, count, *refs):
+    shards, fulls = refs[:count], refs[count : 2 * count]
+    own_sem, zs_sem, zr_sem, cs_sem, cr_sem, fs_sem, fr_sem, ms_sem, mr_sem = refs[2 * count :]
+    core, low, high, low_x, low_y = place_of()
+    at_x, at_y = (high * 4 + low_x, core), (high * 4 + low_y, core)
+    at_high = [(lax.rem(high + k, highs) * 4 + low, core) for k in range(1, highs)]
+    sibling = (high * 4 + low, 1 - core)
+    greet([at_x, at_y, sibling] + at_high)
+
+    def full(group):
+        number, start, size = group
+        ref = fulls[number].at[core] if shared[number] else fulls[number]
+        return ref, pl.ds(start, size)
+
+    def remote(source, target, send, receive, device):
+        return pltpu.make_async_remote_copy(
+            src_ref=source, dst_ref=target, send_sem=send, recv_sem=receive,
+            device_id=device, device_id_type=pl.DeviceIdType.MESH)
+
+    def first(at):
+        ref, cols = full(groups[at])
+        shard = shards[groups[at][0]].at[:, cols]
+        mine = ref.at[high, low, :, cols]
+        copies = [pltpu.make_async_copy(shard, mine, own_sem.at[at])]
+        for k in range(1, highs):
+            copies.append(remote(shard, mine, zs_sem.at[at, k - 1], zr_sem.at[at, k - 1], at_high[k - 1]))
+        return copies
+
+    def column(at):
+        ref, cols = full(groups[at])
+        part = ref.at[:, low, :, cols]
+        return [remote(part, part, cs_sem.at[at, 0], cr_sem.at[at, 0], at_x),
+                remote(part, part, cs_sem.at[at, 1], cr_sem.at[at, 1], at_y)]
+
+    def forward(at):
+        ref, cols = full(groups[at])
+        if at % 2 == 0:
+            part = ref.at[:, low_x, :, cols]
+            return remote(part, part, fs_sem.at[at], fr_sem.at[at], at_y)
+        part = ref.at[:, low_y, :, cols]
+        return remote(part, part, fs_sem.at[at], fr_sem.at[at], at_x)
+
+    total = len(groups)
+    pairs = (total + 1) // 2
+    in_pair = lambda pair: [at for at in (2 * pair, 2 * pair + 1) if at < total]
+    for step in range(pairs + 2):
+        if step < pairs:
+            for at in in_pair(step):
+                for copy in first(at):
+                    copy.start()
+        if 0 <= step - 1 < pairs:
+            for at in in_pair(step - 1):
+                for copy in first(at):
+                    copy.wait()
+                for copy in column(at):
+                    copy.start()
+        if 0 <= step - 2 < pairs:
+            for at in in_pair(step - 2):
+                column(at)[at % 2].wait()
+                forward(at).start()
+    swaps = []
+    for at in range(total):
+        column(at)[1 - at % 2].wait()
+        forward(at).wait()
+    for number in range(count):
+        if shared[number]:
+            part = fulls[number].at[core]
+            swap = remote(part, part, ms_sem.at[number], mr_sem.at[number], sibling)
+            swap.start()
+            swaps.append(swap)
+    for swap in swaps:
+        swap.wait()
+
+
+def gather_all(shards, shared):
+    size = lax.axis_size("dp")
+    if any(a.shape[0] % 16 for a in shards if a.dtype == BF16):
+        order_a, order_b = orders()
+        fulls = []
+        for number, shard in enumerate(shards):
+            full = gather_dp(shard, 0, (order_a, order_b)[number % 2])
+            if shared[number]:
+                other, zero = other_core(full), lax.axis_index("mp") == 0
+                full = jnp.stack([jnp.where(zero, full, other), jnp.where(zero, other, full)])
+            fulls.append(full)
+        return fulls
+    highs = size // 4
+    count = len(shards)
+    groups = blocks_of([a.shape[1] for a in shards], 1024)
+    outs = []
+    for shard, split in zip(shards, shared):
+        dims = (highs, 4) + shard.shape
+        outs.append(shape((2,) + dims if split else dims, shard.dtype))
+    dma = pltpu.SemaphoreType.DMA
+    total = len(groups)
+    any_space = pl.BlockSpec(memory_space=pl.ANY)
+    fulls = pl.pallas_call(
+        functools.partial(gather_kernel, highs, shared, groups, count),
+        out_shape=tuple(outs),
+        in_specs=[any_space] * count,
+        out_specs=tuple([any_space] * count),
+        scratch_shapes=[dma((total,)), dma((total, highs - 1)), dma((total, highs - 1)), dma((total, 2)), dma((total, 2)),
+                        dma((total,)), dma((total,)), dma((count,)), dma((count,))],
+        compiler_params=pltpu.CompilerParams(collective_id=0, has_side_effects=True),
+        cost_estimate=pl.CostEstimate(flops=0, bytes_accessed=sum(a.size * a.dtype.itemsize * size for a in shards),
+                                      transcendentals=0),
+    )(*shards)
+    return [full.reshape(((2,) if split else ()) + (size * shard.shape[0], shard.shape[1]))
+            for full, split, shard in zip(fulls, shared, shards)]
+
+
+def reduce_kernel(highs, weights, groups, count, loss_ref, *refs):
+    grads, outs, sums_ref = refs[:count], refs[count : 2 * count], refs[2 * count]
+    refs = refs[2 * count + 1 :]
+    total = len(groups)
+    buffers, refs = refs[: 6 * total], refs[6 * total :]
+    plane_ref, norm_ref, near_ref, far_ref = refs[:4]
+    load_sem, as_sem, ar_sem, bs_sem, br_sem, zs_sem, zr_sem, ns_sem, nr_sem, hs_sem, hr_sem = refs[4:]
+    core, low, high, low_x, low_y = place_of()
+    low_d = 3 - low
+    spot = low * 2 + core
+    dev_x, dev_y = (high * 4 + low_x, core), (high * 4 + low_y, core)
+    at_high = [(lax.rem(high + k, highs) * 4 + low, core) for k in range(1, highs)]
+    near = [(high * 4 + lax.rem(spot + k, 8) // 2, lax.rem(lax.rem(spot + k, 8), 2)) for k in range(1, 8)]
+    greet(near + at_high)
+
+    def remote(source, target, send, receive, device):
+        return pltpu.make_async_remote_copy(
+            src_ref=source, dst_ref=target, send_sem=send, recv_sem=receive,
+            device_id=device, device_id_type=pl.DeviceIdType.MESH)
+
+    def route(at):
+        if at % 2 == 0:
+            return low_y, dev_y, low_x, dev_x
+        return low_x, dev_x, low_y, dev_y
+
+    def grad(at, which):
+        number, start, size = groups[at]
+        return grads[number].at[:, which, :, pl.ds(start, size)]
+
+    def loads(at):
+        _, _, low_two, _ = route(at)
+        return [pltpu.make_async_copy(grad(at, low_two), buffers[6 * at], load_sem.at[at, 0]),
+                pltpu.make_async_copy(grad(at, low), buffers[6 * at + 1], load_sem.at[at, 1])]
+
+    def one(at):
+        low_one, dev_one, _, _ = route(at)
+        return [remote(grad(at, low_d), buffers[6 * at + 2], as_sem.at[at, 0], ar_sem.at[at, 0], dev_one),
+                remote(grad(at, low_one), buffers[6 * at + 3], as_sem.at[at, 1], ar_sem.at[at, 1], dev_one)]
+
+    def two(at):
+        return remote(buffers[6 * at], buffers[6 * at + 4], bs_sem.at[at], br_sem.at[at], route(at)[3])
+
+    def three(at):
+        return [remote(buffers[6 * at + 1].at[lax.rem(high + k, highs)], buffers[6 * at + 5].at[k - 1],
+                       zs_sem.at[at, k - 1], zr_sem.at[at, k - 1], at_high[k - 1]) for k in range(1, highs)]
+
+    pairs = (total + 1) // 2
+    in_pair = lambda pair: [at for at in (2 * pair, 2 * pair + 1) if at < total]
+    norm_ref[...] = jnp.zeros_like(norm_ref)
+    kept = {}
+    for step in range(pairs + 3):
+        if step < pairs:
+            for at in in_pair(step):
+                for copy in one(at) + loads(at):
+                    copy.start()
+        if 0 <= step - 1 < pairs:
+            for at in in_pair(step - 1):
+                mine = buffers[6 * at]
+                loads(at)[0].wait()
+                one(at)[0].wait()
+                mine[...] = (mine[...].astype(F32) + buffers[6 * at + 2][...].astype(F32)).astype(mine.dtype)
+                two(at).start()
+        if 0 <= step - 2 < pairs:
+            for at in in_pair(step - 2):
+                number, start, size = groups[at]
+                mine = buffers[6 * at + 1]
+                loads(at)[1].wait()
+                one(at)[1].wait()
+                two(at).wait()
+                rows = mine.shape[1]
+                plane = plane_ref.at[at % 4, :, :rows, :size]
+                plane[...] = (mine[...].astype(F32) + buffers[6 * at + 3][...].astype(F32)
+                              + buffers[6 * at + 4][...].astype(F32))
+                outs[number][:, pl.ds(start, size)] = plane[high]
+                mine[...] = plane[...].astype(mine.dtype)
+                for copy in three(at):
+                    copy.start()
+        if 0 <= step - 3 < pairs:
+            for at in in_pair(step - 3):
+                number, start, size = groups[at]
+                for copy in three(at):
+                    copy.wait()
+                cols = pl.ds(start, size)
+                done = outs[number][:, cols]
+                for k in range(highs - 1):
+                    done = done + buffers[6 * at + 5][k].astype(F32)
+                outs[number][:, cols] = done
+                norm_ref[0:1, 0:1] += weights[number] * jnp.sum(done * done, keepdims=True)
+    norm_ref[1:2, 0:1] = jnp.sum(loss_ref[...], keepdims=True)
+    near_ref[spot] = norm_ref[...]
+    copies = [remote(norm_ref, near_ref.at[spot], ns_sem.at[k], nr_sem.at[k], near[k]) for k in range(7)]
+    for copy in copies:
+        copy.start()
+    for copy in copies:
+        copy.wait()
+    local = near_ref[0]
+    for k in range(1, 8):
+        local = local + near_ref[k]
+    norm_ref[...] = local
+    far_ref[high] = local
+    copies = [remote(norm_ref, far_ref.at[high], hs_sem.at[k], hr_sem.at[k], at_high[k]) for k in range(highs - 1)]
+    for copy in copies:
+        copy.start()
+    for copy in copies:
+        copy.wait()
+    every = far_ref[0]
+    for k in range(1, highs):
+        every = every + far_ref[k]
+    sums_ref[...] = every
+
+
+def reduce_all(grads, weights, loss_parts):
+    size = lax.axis_size("dp")
+    highs = size // 4
+    if any((a.shape[0] // size) % 16 for a in grads if a.dtype == BF16):
+        order_a, order_b = orders()
+        outs = [reduce_dp(a, 0, (order_a, order_b)[number % 2], a.dtype) for number, a in enumerate(grads)]
+        sums = jnp.stack([sum(w * jnp.sum(a * a) for w, a in zip(weights, outs)), jnp.sum(loss_parts)])
+        sums = total_dp(sums)
+        sums = sums + other_core(sums)
+        return outs, sums[0], 0.5 * sums[1]
+    count = len(grads)
+    groups = blocks_of([a.shape[1] for a in grads], 512)
+    shards = [a.shape[0] // size for a in grads]
+    total = len(groups)
+    buffers = []
+    for number, _, width in groups:
+        piece = pltpu.VMEM((highs, shards[number], width), grads[number].dtype)
+        buffers += [piece] * 5 + [pltpu.VMEM((highs - 1, shards[number], width), grads[number].dtype)]
+    dma = pltpu.SemaphoreType.DMA
+    small = (8, 128)
+    in_vmem = pl.BlockSpec(memory_space=pltpu.VMEM)
+    any_space = pl.BlockSpec(memory_space=pl.ANY)
+    result = pl.pallas_call(
+        functools.partial(reduce_kernel, highs, weights, groups, count),
+        out_shape=tuple([shape((rows, a.shape[1]), F32) for rows, a in zip(shards, grads)] + [shape(small, F32)]),
+        in_specs=[in_vmem] + [any_space] * count,
+        out_specs=tuple([in_vmem] * (count + 1)),
+        scratch_shapes=buffers + [
+            pltpu.VMEM((4, highs, max(shards), max(g[2] for g in groups)), F32), pltpu.VMEM(small, F32),
+            pltpu.VMEM((8,) + small, F32), pltpu.VMEM((highs,) + small, F32),
+            dma((total, 2)), dma((total, 2)), dma((total, 2)), dma((total,)), dma((total,)),
+            dma((total, highs - 1)), dma((total, highs - 1)), dma((7,)), dma((7,)), dma((highs - 1,)), dma((highs - 1,))],
+        compiler_params=pltpu.CompilerParams(collective_id=1, has_side_effects=True, vmem_limit_bytes=VMEM_LIMIT),
+        cost_estimate=pl.CostEstimate(flops=0, bytes_accessed=sum(a.size * a.dtype.itemsize for a in grads),
+                                      transcendentals=0),
+    )(loss_parts, *[a.reshape(highs, 4, rows, a.shape[1]) for rows, a in zip(shards, grads)])
+    return list(result[:count]), result[count][0, 0], 0.5 * result[count][1, 0]
 
 
 def adam_update(master, gradient, first_old, second_old, step_rate, decay_rate):
@@ -637,25 +935,6 @@
         second_predict,
         second_vectors,
     )
-    order_a, order_b = orders()
-    low = jnp.bfloat16
-    embed_w = gather_dp(patch_embed.astype(low).T, 0, order_a)
-    vector_low = gather_dp(vectors.astype(low).reshape(1, -1), 0, order_b).reshape(-1)
-    enc_attn_w = jnp.concatenate([
-        gather_dp(enc_attn[:2].astype(low), 1, order_a),
-        gather_dp(enc_attn[2:].astype(low), 1, order_b)])
-    enc_mlp_w = [
-        gather_dp(enc_mlp[0].astype(low), 0, order_a),
-        gather_dp(enc_mlp[1].astype(low), 0, order_b)]
-    bridge_w = gather_dp(bridge.astype(low), 0, order_a)
-    dec_attn_w = jnp.concatenate([
-        gather_dp(dec_attn[:2].astype(low), 1, order_a),
-        gather_dp(dec_attn[2:].astype(low), 1, order_b)])
-    dec_mlp_w = [
-        gather_dp(dec_mlp[0].astype(low), 0, order_a),
-        gather_dp(dec_mlp[1].astype(low), 0, order_b)]
-    predict_w = gather_dp(predict.astype(low), 0, order_b)
-    pieces = split_vectors(vector_low.astype(jnp.float32), D, E)
     images, keep_count = kept_index.shape
     patch_count = intersection.shape[1]
     patch_index = jnp.arange(patch_count, dtype=jnp.int32)
@@ -671,13 +950,33 @@
             for band_level in range(NB)
         ]
     )
-    band_weight = total_dp(local_counts)
+    core_at = lax.axis_index("mp")
+    size = lax.axis_size("dp")
+    low = jnp.bfloat16
+
+    def flat(stack):
+        return jnp.concatenate([part.astype(low) for part in stack], axis=1)
+
+    def core_half(block):
+        return lax.dynamic_slice_in_dim(block, core_at * (block.shape[1] // 2), block.shape[1] // 2, 1).astype(low)
+
+    vec_shard = vectors.shape[0]
+    vec_room = -(-(vec_shard + NB) // 1024) * 1024
+    vec_rows = jnp.concatenate([lax.reduce_precision(vectors, 8, 7), local_counts,
+                                jnp.zeros((vec_room - vec_shard - NB,), F32)]).reshape(-1, 128)
+    enc_attn_w, enc_mlp_w, dec_attn_w, dec_mlp_w, embed_w, bridge_w, predict_w, vec_full = gather_all(
+        [flat(enc_attn), flat(enc_mlp), flat(dec_attn), flat(dec_mlp), core_half(patch_embed.T), core_half(bridge),
+         core_half(predict), vec_rows],
+        (False, False, False, False, True, True, True, False))
+    vec_full = vec_full.reshape(size, vec_room)
+    pieces = split_vectors(vec_full[:, :vec_shard].reshape(-1), D, E)
+    band_weight = jnp.sum(vec_full[:, vec_shard : vec_shard + NB], axis=0)
     inverse = 1.0 / band_weight
     core = lax.axis_index("mp").astype(jnp.int32).reshape(1)
     hidden_rows = (1.0 - kept_flags).reshape(-1, 1)
     kept_column = kept_index.reshape(-1, 1)
     rows, rows_d = images * keep_count, images * patch_count
-    local, local_d = enc_attn_w.shape[2], dec_attn_w.shape[2]
+    local, local_d = enc_attn_w.shape[1] // 4, dec_attn_w.shape[1] // 4
     pixel_count = pixels.shape[1]
     evec = jnp.stack(pieces[:7] + [jnp.zeros_like(pieces[0])])
     dvec = jnp.stack(pieces[7:14] + [jnp.zeros_like(pieces[7])])
@@ -689,7 +988,7 @@
         [pltpu.VMEM((4 * local, D), BF16)],
         (pixels, kept_column, sine_table(gsd_scale, D, GRID), embed_w, evec, enc_attn_w),
         rows * D * (2 * pixel_count + 8 * local))
-    x1, part = mlp_forward(x0, part, evec, *enc_mlp_w)
+    x1, part = mlp_forward(x0, part, evec, enc_mlp_w)
     x2, final_enc, xd, *dec_saved, part = run(
         functools.partial(dec_in_kernel, keep_count, DDH),
         [shape((rows, D), F32), shape((rows, D), BF16), shape((rows_d, E), F32), shape((3 * local_d, rows_d), BF16),
@@ -698,12 +997,11 @@
         (x1, part, other_core(part), evec, bridge_w, kept_index, hidden_rows, sine_table(gsd_scale, E, GRID), dvec,
          dec_attn_w),
         rows_d * E * 8 * local_d + 2 * rows * D * E)
-    xd1, part = mlp_forward(xd, part, dvec, *dec_mlp_w)
+    xd1, part = mlp_forward(xd, part, dvec, dec_mlp_w)
     gyd, grad_predict, grad_pbias, loss_parts, grad_dec_fg, grad_dec_fb = head(
         core, inverse, xd1, part, dvec, pieces[14].reshape(1, -1), predict_w, target, band_ids, patch_weight, patch_count)
-    loss = total_dp(jnp.sum(loss_parts))
-    grad_dec_up, grad_dec_down, part = mlp_backward(gyd, xd1, dvec, *dec_mlp_w)
-    gxd, grad_dec_qk, grad_dec_vo, grad_dec_gb, grad_dec_bb, part = attn_backward(
+    grad_dec_up, grad_dec_down, part = mlp_backward(gyd, xd1, dvec, dec_mlp_w)
+    gxd, grad_dec_attn, grad_dec_gb, grad_dec_bb, part = attn_backward(
         gyd, xd1, part, xd, dec_saved, dvec, dec_attn_w, patch_count, patch_count, DDH)
     one_d, one_e = shape((1, D), F32), shape((1, E), F32)
     grad_dec_ga, grad_dec_ba, grad_mask, grad_bridge, grad_enc_fg, grad_enc_fb, gye = run(
@@ -712,8 +1010,8 @@
         [pltpu.VMEM((rows, E), BF16)],
         (core, gxd, xd, part, other_core(part), dvec, kept_column, hidden_rows, final_enc, x2, evec, bridge_w),
         3 * rows * D * E, 1)
-    grad_enc_up, grad_enc_down, part = mlp_backward(gye, x1, evec, *enc_mlp_w)
-    gxe, grad_enc_qk, grad_enc_vo, grad_enc_gb, grad_enc_bb, part = attn_backward(
+    grad_enc_up, grad_enc_down, part = mlp_backward(gye, x1, evec, enc_mlp_w)
+    gxe, grad_enc_attn, grad_enc_gb, grad_enc_bb, part = attn_backward(
         gye, x1, part, x0, enc_saved, evec, enc_attn_w, keep_count, group, DH)
     grad_enc_ga, grad_enc_ba, grad_ebias, grad_embed = run(
         enc_out_kernel,
@@ -722,30 +1020,21 @@
     grad_vectors = jnp.concatenate(
         [grad_ebias, grad_enc_ga, grad_enc_ba, grad_enc_gb, grad_enc_bb, grad_enc_fg, grad_enc_fb, grad_mask,
          grad_dec_ga, grad_dec_ba, grad_dec_gb, grad_dec_bb, grad_dec_fg, grad_dec_fb, grad_pbias], axis=1).reshape(-1)
+    vec_grads = jnp.pad(grad_vectors.reshape(size, vec_shard), ((0, 0), (0, vec_room - vec_shard)))
+    sums, total_squares, loss = reduce_all(
+        [grad_enc_attn, grad_enc_up, grad_enc_down, grad_dec_attn, grad_dec_up, grad_dec_down, grad_embed, grad_bridge,
+         grad_predict, vec_grads.reshape(-1, 128)],
+        (1.0,) * 9 + (0.5,), loss_parts)
     reduced = (
-        jnp.concatenate([
-            reduce_dp(grad_enc_qk, 1, order_a, low),
-            reduce_dp(grad_enc_vo, 1, order_b, low)]),
-        jnp.stack([
-            reduce_dp(grad_enc_up, 0, order_a, low),
-            reduce_dp(grad_enc_down, 0, order_b, low)]),
-        jnp.concatenate([
-            reduce_dp(grad_dec_qk, 1, order_a, low),
-            reduce_dp(grad_dec_vo, 1, order_b, low)]),
-        jnp.stack([
-            reduce_dp(grad_dec_up, 0, order_a, low),
-            reduce_dp(grad_dec_down, 0, order_b, low)]),
-        join_cores(reduce_dp(grad_embed, 0, order_a, low), core).T,
-        join_cores(reduce_dp(grad_bridge, 0, order_a, low), core),
-        join_cores(reduce_dp(grad_predict, 0, order_b, low), core),
-        reduce_dp(grad_vectors, 0, order_b, F32),
+        jnp.stack(jnp.split(sums[0], 4, axis=1)),
+        jnp.stack(sums[1:3]),
+        jnp.stack(jnp.split(sums[3], 4, axis=1)),
+        jnp.stack(sums[4:6]),
+        join_cores(sums[6], core).T,
+        join_cores(sums[7], core),
+        join_cores(sums[8], core),
+        sums[9].reshape(-1)[:vec_shard],
     )
-    shares = (1.0, 1.0, 1.0, 1.0, 0.5, 0.5, 0.5, 0.5)
-    squares = jnp.zeros((), jnp.float32)
-    for position, gradient in enumerate(reduced):
-        squares = squares + shares[position] * jnp.sum(gradient * gradient)
-    total_squares = total_dp(squares)
-    total_squares = total_squares + lax.ppermute(total_squares, "mp", [(0, 1), (1, 0)])
     grad_norm = jnp.sqrt(total_squares)
     factor = CLIP / jnp.maximum(grad_norm, CLIP)
     news, new_firsts, new_seconds = ([], [], [])

time: 855 us -> 695 us (0.81)
  Pallas kernels: 248 us -> 598 us
  waiting for transfers between devices: 315 us -> 22.3 us
  starting transfers between devices: 130 us -> 2.35 us
  other arithmetic: 78.7 us -> 28.7 us
  local copies, waits for them, and re-layouts: 56.3 us -> 29.1 us
  between operations: 17.5 us -> 5.54 us
    pallas_call x0 -> x2, Pallas kernels: none -> 349 us  [the longest x1 178 us: gather_all(): pl.pallas_call(functools.partial(gather_kernel, highs, shared, groups, co...]
    ppermute x109 -> x0, waiting for transfers between devices: 315 us -> none  [the longest x108 314 us: swap(): return lax.ppermute(block, 'dp', [(i, i ^ 1 << bit) for i in range(size)])]
    ppermute x109 -> x0, starting transfers between devices: 129 us -> none  [the longest x108 128 us: swap(): return lax.ppermute(block, 'dp', [(i, i ^ 1 << bit) for i in range(size)])]
    add x46 -> x0, other arithmetic: 23.1 us -> none  [the longest x43 19.1 us: reduce_dp(): cur = keep.astype(F32) + other.astype(F32)]
    ppermute x11, waiting for transfers between devices: 0.58 us -> 22.3 us  [other_core(): return lax.ppermute(block, 'mp', [(0, 1), (1, 0)])]
    dynamic_slice x24 -> x0, local copies, waits for them, and re-layouts: 20.4 us -> none  [the longest x13 12.6 us: reduce_dp(): keep = lax.dynamic_index_in_dim(cur, mine, place, keepdims=False)]
    another operation x100 -> x4, other arithmetic: 21 us -> 3.29 us  [the longest x91 16.8 us: gather_dp(): jnp.stack([jnp.where(mine, other, cur), jnp.where(mine, cur, other)], axi...]
    another operation x12 -> x3, local copies, waits for them, and re-layouts: 10.6 us -> 2.04 us  [the longest x1 1.13 us: per_device(): jnp.stack(jnp.split(sums[0], 4, axis=1))]
  transfers between devices with their start and end apart: 120 -> 11, of which waited for: 65 -> 7; matrix products, arithmetic and copies ran while one was open for 13% -> 3% of each run, Pallas kernels for 27% -> 0%
where the time goes in v3:
time: 695 us; the launch traced here: 686 us
  Pallas kernels  598 us (86%)
  local copies, waits for them, and re-layouts  29.1 us (4%)
  other arithmetic  28.7 us (4%)
  waiting for transfers between devices  22.3 us (3%)
    pallas_call x1, Pallas kernels, gather_all(): pl.pallas_call(functools.partial(gather_kernel, highs, shared, groups, co...  178 us
    pallas_call x1, Pallas kernels, reduce_all(): pl.pallas_call(functools.partial(reduce_kernel, highs, weights, groups, c...  171 us
    pallas_call x6, Pallas kernels, run(): pl.pallas_call(kernel, out_shape=tuple(outs), in_specs=[pl.BlockSpec(memo...  158 us
    pallas_call x2, Pallas kernels, mlp_backward(): pl.pallas_call(functools.partial(mlp_back_kernel, tile), out_shape=(shape...  47 us
    pallas_call x2, Pallas kernels, mlp_forward(): pl.pallas_call(functools.partial(mlp_kernel, tile), out_shape=(shape((row...  27.2 us
    ppermute x11, waiting for transfers between devices, other_core(): return lax.ppermute(block, 'mp', [(0, 1), (1, 0)])  22.3 us
    pallas_call x1, Pallas kernels, head(): pl.pallas_call(head_kernel, out_shape=(shape((rows, width), F32), shape((...  17 us
    unnamed x122, local copies, waits for them, and re-layouts  15.8 us
  transfers between devices with their start and end apart: 11, of which 7 were waited for; matrix products, arithmetic and copies ran while one was open for 3% of the time, Pallas kernels for 0%

profile of v3, /device:TPU:0, one launch (start us, length us, event | category | flops | bytes accessed | tf_op | source)
XLA Modules:
  0.0 686.1 jit_solution(16125422741028408172)
XLA Ops:
  10.9 4.7 select_reduce_fusion
  19.1 2.6 concatenate.37
  21.7 178.3 %shard_map.544 = (bf16[4,4,64,2048]{3,2,1,0:T(8,128)(2,1)}, bf16[4,4,64,4096]{3,2,1,0:T(8,128)(2,1)}, bf16[4,4,32,1024]{3,2,1,0:T(8,128)(2,1)}, bf16[4,4,32,2048...) custom-call(bf16[64,2048]{1,0:T(8,128)(2,1)} %pad_maximum_fusion.1.r, ...), custom_call_target="tpu_custom_call" | custom-call | bytes 17498112 | tf_op jit(solution)/shard_map/pallas_call | solution.py:706
  203.1 27.0 %shard_map.545 = (f32[512,1024]{1,0:T(8,128)}, bf16[1536,512]{1,0:T(8,128)(2,1)}, bf16[512,512]{1,0:T(8,128)(2,1)}, f32[8,512]{1,0:T(8,128)}, bf16[512,1024]{1,0:T(8,128)(2,1)}, /*index=5*/bf16[512,768]{1,0:T(8,128)(2,1)}) custom-call(bf16[2048,768]{1,0:T(8,128)(2,1)} %pix_ref.1, s32[512,1]{1,0:T(8,128)} %reshape.238.kept_ref, ...), custom_call_target="tpu_custom_call" | custom-call | flops 2952790016 | bytes 15255552 | tf_op jit(solution)/shard_map/pallas_call | solution.py:414
  230.5 2.5 collective-permute-done.other_ref
  234.0 11.4 %shard_map.546 = (f32[512,1024]{1,0:T(8,128)}, bf16[512,1024]{1,0:T(8,128)(2,1)}) custom-call(f32[512,1024]{1,0:T(8,128)} %get-tuple-element.102.x_ref, bf16[512,1024]{1,0:T(8,128)(2,1)} %get-tuple-element.103.mine_ref, bf16[512,1024]{1,0:T(8,128)(2,1)} %copy-done.8, f32[8,1024]{1,0:T(8,128)} %stack.115.vec_ref.evec_ref, bf16[1024,4096]{1,0:T(8,128)(2,1)} %bitcast.115, ...), custom_call_target="tpu_custom_call" | custom-call | flops 4294967296 | bytes 15728640 | tf_op jit(solution)/shard_map/pallas_call | solution.py:438
  249.7 39.9 %shard_map.547 = (f32[512,1024]{1,0:T(8,128)}, bf16[512,1024]{1,0:T(8,128)(2,1)}, f32[2048,512]{1,0:T(8,128)}, bf16[768,2048]{1,0:T(8,128)(2,1)}, bf16[256,2048]...) custom-call(f32[512,1024]{1,0:T(8,128)} %get-tuple-element.105.x1_ref, ...), custom_call_target="tpu_custom_call" | custom-call | flops 2684354560 | bytes 20178944 | tf_op jit(solution)/shard_map/pallas_call | solution.py:414
  289.8 4.2 collective-permute-done.2.other_ref
  295.3 15.8 %shard_map.548 = (f32[2048,512]{1,0:T(8,128)}, bf16[2048,512]{1,0:T(8,128)(2,1)}) custom-call(f32[2048,512]{1,0:T(8,128)} %get-tuple-element.109.x_ref, bf16[2048,512]{1,0:T(8,128)(2,1)} %get-tuple-element.110.mine_ref, bf16[2048,512]{1,0:T(8,128)(2,1)} %copy-done.46, f32[8,512]{1,0:T(8,128)} %stack.123.vec_ref, bf16[512,2048]{1,0:T(8,128)(2,1)} %bitcast.165, ...), custom_call_target="tpu_custom_call" | custom-call | flops 4294967296 | bytes 16777216 | tf_op jit(solution)/shard_map/pallas_call | solution.py:438
  313.8 1.7 collective-permute-done.3.other_ref
  316.9 17.0 %shard_map.549 = (f32[2048,512]{1,0:T(8,128)}, bf16[512,384]{1,0:T(8,128)(2,1)}, f32[1,768]{1,0:T(1,128)}, f32[1,768]{1,0:T(1,128)}, f32[1,512]{1,0:T(1,128)}, /*index=5*/f32[1,512]{1,0:T(1,128)}) custom-call(s32[1]{0:T(128)} %bitcast.core_ref, f32[3]{0:T(128)} %broadcast_divide_fusion.inverse_ref, f32[2048,512]{1,0:T(8,128)} %get-tuple-element.112.x1_ref, ...), custom_call_target="tpu_custom_call" | custom-call | flops 4026531840 | bytes 22020096 | tf_op jit(solution)/shard_map/pallas_call | solution.py:485
  333.9 26.5 %shard_map.550 = (bf16[512,1024]{1,0:T(8,128)(2,1)}, bf16[512,1024]{1,0:T(8,128)(2,1)}, bf16[2048,512]{1,0:T(8,128)(2,1)}) custom-call(f32[2048,512]{1,0:T(8,128)} %get-tuple-element.116.gy_ref, f32[2048,512]{1,0:T(8,128)} %get-tuple-element.112.x1_ref, f32[8,512]{1,0:T(8,128)} %stack.123.vec_ref, bf16[512,2048]{1,0:T(8,128)(2,1)} %bitcast.167, ...), custom_call_target="tpu_custom_call" | custom-call | flops 10737418240 | bytes 14680064 | tf_op jit(solution)/shard_map/pallas_call | solution.py:459
  360.6 4.2 collective-permute-done.4.other_ref
  366.2 42.4 %shard_map.551 = (f32[2048,512]{1,0:T(8,128)}, bf16[512,1024]{1,0:T(8,128)(2,1)}, f32[1,512]{1,0:T(1,128)}, f32[1,512]{1,0:T(1,128)}, bf16[2048,512]{1,0:T(8,128)(2,1)}) custom-call(f32[2048,512]{1,0:T(8,128)} %get-tuple-element.116.gy_ref, f32[2048,512]{1,0:T(8,128)} %get-tuple-element.112.x1_ref, bf16[2048,512]{1,0:T(8,128)(2,1)} %get-tuple-element.117.mine_ref, ...), custom_call_target="tpu_custom_call" | custom-call | flops 4831838208 | bytes 29446144 | tf_op jit(solution)/shard_map/pallas_call | solution.py:414
  408.7 4.2 collective-permute-done.5.other_ref
  414.3 14.1 %shard_map.552 = (f32[1,512]{1,0:T(1,128)}, f32[1,512]{1,0:T(1,128)}, f32[1,512]{1,0:T(1,128)}, bf16[1024,256]{1,0:T(8,128)(2,1)}, f32[1,1024]{1,0:T(1,128)}, /*index=5*/f32[1,1024]{1,0:T(1,128)}, f32[512,1024]{1,0:T(8,128)}) custom-call(s32[1]{0:T(128)} %bitcast.core_ref, f32[2048,512]{1,0:T(8,128)} %get-tuple-element.121.gx_ref, ...), custom_call_target="tpu_custom_call" | custom-call | flops 805306368 | bytes 19472388 | tf_op jit(solution)/shard_map/pallas_call | solution.py:414
  428.4 20.5 %shard_map.553 = (bf16[1024,2048]{1,0:T(8,128)(2,1)}, bf16[1024,2048]{1,0:T(8,128)(2,1)}, bf16[512,1024]{1,0:T(8,128)(2,1)}) custom-call(f32[512,1024]{1,0:T(8,128)} %get-tuple-element.125.gy_ref, f32[512,1024]{1,0:T(8,128)} %get-tuple-element.105.x1_ref, f32[8,1024]{1,0:T(8,128)} %stack.115.vec_ref.evec_ref, bf16[1024,4096]{1,0:T(8,128)(2,1)} %bitcast.117, ...), custom_call_target="tpu_custom_call" | custom-call | flops 10737418240 | bytes 22020096 | tf_op jit(solution)/shard_map/pallas_call | solution.py:459
  449.1 2.7 collective-permute-done.6.other_ref
  452.8 28.3 %shard_map.554 = (f32[512,1024]{1,0:T(8,128)}, bf16[1024,2048]{1,0:T(8,128)(2,1)}, f32[1,1024]{1,0:T(1,128)}, f32[1,1024]{1,0:T(1,128)}, bf16[512,1024]{1,0:T(8,128)(2,1)}) custom-call(f32[512,1024]{1,0:T(8,128)} %get-tuple-element.125.gy_ref, f32[512,1024]{1,0:T(8,128)} %get-tuple-element.105.x1_ref, bf16[512,1024]{1,0:T(8,128)(2,1)} %get-tuple-element.126.mine_ref, ...), custom_call_target="tpu_custom_call" | custom-call | flops 4831838208 | bytes 22077440 | tf_op jit(solution)/shard_map/pallas_call | solution.py:414
  481.2 2.7 collective-permute-done.7.other_ref
  485.0 6.1 shard_map.555
  494.3 170.8 %shard_map.556 = (f32[64,2048]{1,0:T(8,128)}, f32[64,2048]{1,0:T(8,128)}, f32[64,2048]{1,0:T(8,128)}, f32[32,1024]{1,0:T(8,128)}, f32[32,1024]{1,0:T(8,128)}, /*...) custom-call(f32[1,768]{1,0:T(1,128)} %get-tuple-element.115.loss_ref, ...), custom_call_target="tpu_custom_call" | custom-call | bytes 17498112 | tf_op jit(solution)/shard_map/pallas_call | solution.py:854
  669.8 2.4 multiply_subtract_fusion.2
  672.3 4.4 multiply_add_fusion
  (193 shorter events, 46.0 us)
Async XLA Ops:
  0.7 10.2 %copy-start.9 = (f32[2,32,1024]{2,1,0:T(8,128)S(1)}, f32[2,32,1024]{2,1,0:T(8,128)}, u32[]{:S(2)}) copy-start(f32[2,32,1024]{2,1,0:T(8,128)} %param.42) | copy-start | bytes 786436
  15.7 185.4 %copy-start.49 = (s32[8]{0:T(128)S(1)}, s32[8]{0:T(128)}, u32[]{:S(2)}) copy-start(s32[8]{0:T(128)} %param.38) | copy-start | bytes 100
  230.1 2.9 collective-permute-start
  245.4 3.4 collective-permute-start.1
  289.6 4.4 collective-permute-start.2
  311.1 4.4 collective-permute-start.3
  313.3 20.6 %copy-start.45 = (f32[3]{0:T(128)}, f32[3]{0:T(128)S(1)}, u32[]{:S(2)}) copy-start(f32[3]{0:T(128)S(1)} %slice_reduce_fusion) | copy-start | bytes 40
  360.4 4.4 collective-permute-start.4
  408.6 4.4 collective-permute-start.5
  448.9 2.9 collective-permute-start.6
  481.1 2.9 collective-permute-start.7
  484.9 8.3 %copy-start.34 = (f32[1,1024]{1,0:T(1,128)S(1)}, f32[1,1024]{1,0:T(1,128)}, u32[]{:S(2)}) copy-start(f32[1,1024]{1,0:T(1,128)} %get-tuple-element.147) | copy-start | bytes 12292
  484.9 8.3 %copy-start.33 = (f32[1,1024]{1,0:T(1,128)S(1)}, f32[1,1024]{1,0:T(1,128)}, u32[]{:S(2)}) copy-start(f32[1,1024]{1,0:T(1,128)} %get-tuple-element.148) | copy-start | bytes 12292
  484.9 8.3 %copy-start.44 = (f32[1,512]{1,0:T(1,128)S(1)}, f32[1,512]{1,0:T(1,128)}, u32[]{:S(2)}) copy-start(f32[1,512]{1,0:T(1,128)} %get-tuple-element.149) | copy-start | bytes 6148
  485.0 8.3 %copy-start.43 = (f32[1,512]{1,0:T(1,128)S(1)}, f32[1,512]{1,0:T(1,128)}, u32[]{:S(2)}) copy-start(f32[1,512]{1,0:T(1,128)} %get-tuple-element.150) | copy-start | bytes 6148
  485.0 8.3 %copy-start.42 = (f32[1,512]{1,0:T(1,128)S(1)}, f32[1,512]{1,0:T(1,128)}, u32[]{:S(2)}) copy-start(f32[1,512]{1,0:T(1,128)} %get-tuple-element.151) | copy-start | bytes 6148
  485.0 8.3 %copy-start.41 = (f32[1,512]{1,0:T(1,128)S(1)}, f32[1,512]{1,0:T(1,128)}, u32[]{:S(2)}) copy-start(f32[1,512]{1,0:T(1,128)} %get-tuple-element.152) | copy-start | bytes 6148
  485.0 8.3 %copy-start.40 = (f32[1,512]{1,0:T(1,128)S(1)}, f32[1,512]{1,0:T(1,128)}, u32[]{:S(2)}) copy-start(f32[1,512]{1,0:T(1,128)} %get-tuple-element.153) | copy-start | bytes 6148
  485.0 8.4 %copy-start.39 = (f32[1,512]{1,0:T(1,128)S(1)}, f32[1,512]{1,0:T(1,128)}, u32[]{:S(2)}) copy-start(f32[1,512]{1,0:T(1,128)} %get-tuple-element.154) | copy-start | bytes 6148
  485.0 8.4 %copy-start.38 = (f32[1,512]{1,0:T(1,128)S(1)}, f32[1,512]{1,0:T(1,128)}, u32[]{:S(2)}) copy-start(f32[1,512]{1,0:T(1,128)} %get-tuple-element.155) | copy-start | bytes 6148
  485.0 8.4 %copy-start.37 = (f32[1,768]{1,0:T(1,128)S(1)}, f32[1,768]{1,0:T(1,128)}, u32[]{:S(2)}) copy-start(f32[1,768]{1,0:T(1,128)} %get-tuple-element.156) | copy-start | bytes 9220
  667.2 13.5 %collective-permute-start.10 = (f32[32,384]{1,0:T(8,128)}, f32[32,384]{1,0:T(8,128)S(1)}, u32[]{:S(2)}, u32[]{:S(2)}) collective-permute-start(f32[32,384]{1,0:T(8,128)} %get-tuple-element.166), channel_id=1, source_target_pairs={{0,1},{1,0},{2,3},{3,2},{4,5},{5,4},{6,7},{7,6},{8,9},{9,8},{10,11... | collective-permute-start | bytes 147464 | tf_op jit(solution)/shard_map/ppermute | solution.py:426
  667.3 14.2 %collective-permute-start.9 = (f32[64,256]{1,0:T(8,128)}, f32[64,256]{1,0:T(8,128)S(1)}, u32[]{:S(2)}, u32[]{:S(2)}) collective-permute-start(f32[64,256]{1,0:T(8,128)} %get-tuple-element.165), channel_id=1, source_target_pairs={{0,1},{1,0},{2,3},{3,2},{4,5},{5,4},{6,7},{7,6},{8,9},{9,8},{10,11... | collective-permute-start | bytes 196616 | tf_op jit(solution)/shard_map/ppermute | solution.py:426
  667.8 14.6 %collective-permute-start.8 = (f32[64,384]{1,0:T(8,128)}, f32[64,384]{1,0:T(8,128)S(1)}, u32[]{:S(2)}, u32[]{:S(2)}) collective-permute-start(f32[64,384]{1,0:T(8,128)} %get-tuple-element.164), channel_id=1, source_target_pairs={{0,1},{1,0},{2,3},{3,2},{4,5},{5,4},{6,7},{7,6},{8,9},{9,8},{10,11... | collective-permute-start | bytes 294920 | tf_op jit(solution)/shard_map/ppermute | solution.py:426
  (37 other events, 149.4 us)

commit v4 on v3

--- a/solution.py
+++ b/solution.py
@@ -607,27 +607,72 @@
     return found
 
 
-def gather_kernel(highs, shared, groups, count, *refs):
-    shards, fulls = refs[:count], refs[count : 2 * count]
-    own_sem, zs_sem, zr_sem, cs_sem, cr_sem, fs_sem, fr_sem, ms_sem, mr_sem = refs[2 * count :]
+def remote(source, target, send, receive, device):
+    return pltpu.make_async_remote_copy(
+        src_ref=source, dst_ref=target, send_sem=send, recv_sem=receive,
+        device_id=device, device_id_type=pl.DeviceIdType.MESH)
+
+
+def small_gather_kernel(size, part_ref, full_ref, send_sem, receive_sem):
+    index, core = lax.axis_index("dp"), lax.axis_index("mp")
+    peers = [(lax.rem(index + k, size), core) for k in range(1, size)]
+    greet(peers)
+    full_ref[index] = part_ref[...]
+    copies = [remote(part_ref, full_ref.at[index], send_sem.at[k], receive_sem.at[k], peers[k])
+              for k in range(size - 1)]
+    for copy in copies:
+        copy.start()
+    for copy in copies:
+        copy.wait()
+
+
+def small_gather(part):
+    size = lax.axis_size("dp")
+    in_vmem = pl.BlockSpec(memory_space=pltpu.VMEM)
+    dma = pltpu.SemaphoreType.DMA
+    return pl.pallas_call(
+        functools.partial(small_gather_kernel, size),
+        out_shape=shape((size,) + part.shape, part.dtype),
+        in_specs=[in_vmem],
+        out_specs=in_vmem,
+        scratch_shapes=[dma((size - 1,)), dma((size - 1,))],
+        compiler_params=pltpu.CompilerParams(collective_id=2, has_side_effects=True),
+    )(part)
+
+
+def total_blocks(block_ref, near_ref, far_ref, sems, low, high, core, highs, stage):
+    send, receive = sems
+    if stage == 0:
+        spots = [(high * 4 + lax.rem(low + k, 4), core) for k in range(1, 4)]
+        return [remote(block_ref, near_ref.at[low], send.at[k], receive.at[k], spots[k]) for k in range(3)]
+    spots = [(lax.rem(high + k, highs) * 4 + low, core) for k in range(1, highs)]
+    return [remote(block_ref, far_ref.at[high], send.at[3 + k], receive.at[3 + k], spots[k]) for k in range(highs - 1)]
+
+
+def forward_kernel(highs, shared, groups, count, length, group, head_dim, *refs):
+    shards, refs = refs[:count], refs[count:]
+    pix_ref, band_ref, weight_ref, kept_ref, table_ref, vec_ref = refs[:6]
+    fulls, refs = refs[6 : 6 + count], refs[6 + count :]
+    x_ref, qkv_ref, mixed_ref, lse_ref, pixk_ref, x1_ref, last_ref, far_out_ref, counts_ref = refs[:9]
+    refs = refs[9:]
+    (bands_v, embed_v, attn_v, mlp_v, flat_ref, part_ref, other_ref, low_ref, acc_ref, block_ref, near_ref,
+     far_ref) = refs[:12]
+    (own_sem, zs_sem, zr_sem, cs_sem, cr_sem, fs_sem, fr_sem, ms_sem, mr_sem, load_sem, xs_sem, xr_sem, ts_sem,
+     tr_sem) = refs[12:]
     core, low, high, low_x, low_y = place_of()
     at_x, at_y = (high * 4 + low_x, core), (high * 4 + low_y, core)
     at_high = [(lax.rem(high + k, highs) * 4 + low, core) for k in range(1, highs)]
     sibling = (high * 4 + low, 1 - core)
-    greet([at_x, at_y, sibling] + at_high)
-
-    def full(group):
-        number, start, size = group
+    near = [(high * 4 + lax.rem(low + k, 4), core) for k in range(1, 4)]
+    greet([sibling] + near + at_high)
+
+    def full(at):
+        number, start, size = groups[at]
         ref = fulls[number].at[core] if shared[number] else fulls[number]
         return ref, pl.ds(start, size)
 
-    def remote(source, target, send, receive, device):
-        return pltpu.make_async_remote_copy(
-            src_ref=source, dst_ref=target, send_sem=send, recv_sem=receive,
-            device_id=device, device_id_type=pl.DeviceIdType.MESH)
-
     def first(at):
-        ref, cols = full(groups[at])
+        ref, cols = full(at)
         shard = shards[groups[at][0]].at[:, cols]
         mine = ref.at[high, low, :, cols]
         copies = [pltpu.make_async_copy(shard, mine, own_sem.at[at])]
@@ -636,23 +681,96 @@
         return copies
 
     def column(at):
-        ref, cols = full(groups[at])
+        ref, cols = full(at)
         part = ref.at[:, low, :, cols]
         return [remote(part, part, cs_sem.at[at, 0], cr_sem.at[at, 0], at_x),
                 remote(part, part, cs_sem.at[at, 1], cr_sem.at[at, 1], at_y)]
 
     def forward(at):
-        ref, cols = full(groups[at])
-        if at % 2 == 0:
-            part = ref.at[:, low_x, :, cols]
-            return remote(part, part, fs_sem.at[at], fr_sem.at[at], at_y)
-        part = ref.at[:, low_y, :, cols]
-        return remote(part, part, fs_sem.at[at], fr_sem.at[at], at_x)
+        ref, cols = full(at)
+        which, device = (low_x, at_y) if at % 2 == 0 else (low_y, at_x)
+        part = ref.at[:, which, :, cols]
+        return remote(part, part, fs_sem.at[at], fr_sem.at[at], device)
+
+    def swap(number):
+        part = fulls[number].at[core]
+        return remote(part, part, ms_sem.at[number], mr_sem.at[number], sibling)
+
+    def exchange(at, source, target):
+        return remote(source, target, xs_sem.at[at], xr_sem.at[at], sibling)
 
     total = len(groups)
     pairs = (total + 1) // 2
     in_pair = lambda pair: [at for at in (2 * pair, 2 * pair + 1) if at < total]
-    for step in range(pairs + 2):
+    pair_of = lambda number: max(at for at in range(total) if groups[at][0] == number) // 2
+    images, side = table_ref.shape[0], table_ref.shape[1]
+    patches = pix_ref.shape[0] // images
+    width = mixed_ref.shape[0]
+    mask = group_mask(group, length)
+
+    def pick(image, carry):
+        rows = pl.ds(image * length, length)
+        index = kept_ref[rows, :]
+        hot = lax.broadcasted_iota(jnp.int32, (length, patches), 1) == index
+        pixels = pix_ref[pl.ds(image * patches, patches), :]
+        pixk_ref[rows, :] = dot_nn(hot.astype(BF16), pixels).astype(BF16)
+        grid_at = lax.broadcasted_iota(jnp.int32, (length, side), 1)
+        table = table_ref[image]
+        half = table.shape[1]
+        x_ref[rows, :half] = dot_exact((grid_at == index // side).astype(F32), table)
+        x_ref[rows, half:] = dot_exact((grid_at == index % side).astype(F32), table)
+        return carry
+
+    def tally(image, carry):
+        rows = pl.ds(image * patches, patches)
+        band, weight = bands_v[rows, :], weight_ref[rows, :]
+        for level in range(NB):
+            row = jnp.sum(jnp.where(band == level, weight, 0.0), axis=0, keepdims=True)
+            for start in range(0, row.shape[1], 128):
+                block_ref[level : level + 1, :] += row[:, start : start + 128]
+        return carry
+
+    def rows_step(number, carry):
+        rows = pl.ds(pl.multiple_of(number * group, group), group)
+        share = embed_v.shape[-1]
+        embed = lambda half: embed_v[half].reshape(-1, share)
+        rows_x = dot_nt(pixk_ref[rows, :share], embed(0)) + dot_nt(pixk_ref[rows, share:], embed(1))
+        rows_x = rows_x + vec_ref[0:1, :] + x_ref[rows, :]
+        x_ref[rows, :] = rows_x
+        unit, _ = normalize(rows_x)
+        low_a = (unit * vec_ref[1:2, :] + vec_ref[2:3, :]).astype(BF16)
+        qkv_ref[:, rows] = dot_nt(flat_ref[: 3 * width, :], low_a).astype(BF16)
+        attend(qkv_ref, mixed_ref, lse_ref, rows, width, head_dim, mask)
+        part_ref[rows, :] = dot_nn(mixed_ref[:, rows].T, flat_ref[3 * width :, :]).astype(BF16)
+        return carry
+
+    def mlp_first():
+        after = x_ref[...] + both(part_ref, other_ref, pl.ds(0, x_ref.shape[0]))
+        x1_ref[...] = after
+        unit, _ = normalize(after)
+        low_ref[...] = (unit * vec_ref[3:4, :] + vec_ref[4:5, :]).astype(BF16)
+        acc_ref[...] = jnp.zeros_like(acc_ref)
+
+    def mlp_block(piece, carry):
+        size = 512
+        hidden = mlp_v.shape[-1] // 2
+        start = pl.multiple_of(piece * size, size)
+        wide = x_ref.shape[1]
+        up = dot_nn(low_ref[...], mlp_v[:, :, :, pl.ds(start, size)].reshape(wide, size))
+        _, _, half = gelu_parts(up)
+        down = mlp_v[:, :, :, pl.ds(pl.multiple_of(hidden + start, size), size)].reshape(wide, size)
+        acc_ref[...] += dot_nt((up * half).astype(BF16), down)
+        return carry
+
+    load_bands = pltpu.make_async_copy(band_ref, bands_v, load_sem.at[0])
+    load_attn = pltpu.make_async_copy(fulls[1], attn_v, load_sem.at[1])
+    load_embed = pltpu.make_async_copy(fulls[0], embed_v, load_sem.at[2])
+    load_mlp = pltpu.make_async_copy(fulls[2], mlp_v, load_sem.at[3])
+    stages = functools.partial(total_blocks, block_ref, near_ref, far_ref, (ts_sem, tr_sem), low, high, core, highs)
+    embed_at, attn_at, mlp_at = pair_of(0) + 3, pair_of(1) + 3, pair_of(2) + 3
+    row_groups = x_ref.shape[0] // group
+    swapped = set()
+    for step in range(pairs + 3):
         if step < pairs:
             for at in in_pair(step):
                 for copy in first(at):
@@ -667,55 +785,120 @@
             for at in in_pair(step - 2):
                 column(at)[at % 2].wait()
                 forward(at).start()
-    swaps = []
-    for at in range(total):
-        column(at)[1 - at % 2].wait()
-        forward(at).wait()
-    for number in range(count):
+        if 0 <= step - 3 < pairs:
+            for at in in_pair(step - 3):
+                column(at)[1 - at % 2].wait()
+                forward(at).wait()
+        for number in range(count):
+            if shared[number] and number not in swapped and pair_of(number) + 3 <= step:
+                swap(number).start()
+                swapped.add(number)
+        if step == 0:
+            load_bands.start()
+            lax.fori_loop(0, images, pick, 0)
+            block_ref[...] = jnp.zeros_like(block_ref)
+            load_bands.wait()
+            lax.fori_loop(0, images, tally, 0)
+            near_ref[low] = block_ref[...]
+            for copy in stages(0):
+                copy.start()
+        if step == 1:
+            for copy in stages(0):
+                copy.wait()
+            block_ref[...] = (near_ref[0] + near_ref[1]) + (near_ref[2] + near_ref[3])
+            far_ref[high] = block_ref[...]
+            for copy in stages(1):
+                copy.start()
+        if step == 2:
+            for copy in stages(1):
+                copy.wait()
+            counts = far_ref[0]
+            for k in range(1, highs):
+                counts = counts + far_ref[k]
+            counts_ref[...] = counts
+        if step == attn_at:
+            swap(0).wait()
+            load_attn.start()
+            load_embed.start()
+            load_attn.wait()
+            for part in range(4):
+                at = pl.ds(part * width, width)
+                flat_ref[at, :] = attn_v[:, :, :, at].reshape(-1, width).T
+            load_embed.wait()
+        if attn_at <= step < mlp_at - 1:
+            share = -(-row_groups // (mlp_at - 1 - attn_at))
+            start, stop = (step - attn_at) * share, min((step - attn_at + 1) * share, row_groups)
+            if start < stop:
+                lax.fori_loop(start, stop, rows_step, 0)
+                if stop == row_groups:
+                    exchange(0, part_ref, other_ref).start()
+        if step == mlp_at:
+            load_mlp.start()
+            exchange(0, part_ref, other_ref).wait()
+            mlp_first()
+            load_mlp.wait()
+            lax.fori_loop(0, mlp_v.shape[-1] // 1024, mlp_block, 0)
+            last_ref[...] = acc_ref[...].astype(BF16)
+            exchange(1, last_ref, far_out_ref).start()
+    exchange(1, last_ref, far_out_ref).wait()
+    for number in range(1, count):
         if shared[number]:
-            part = fulls[number].at[core]
-            swap = remote(part, part, ms_sem.at[number], mr_sem.at[number], sibling)
-            swap.start()
-            swaps.append(swap)
-    for swap in swaps:
-        swap.wait()
-
-
-def gather_all(shards, shared):
+            swap(number).wait()
+
+
+def forward_all(shards, shared, pixels, band_ids, patch_weight, kept_column, table, evec):
     size = lax.axis_size("dp")
-    if any(a.shape[0] % 16 for a in shards if a.dtype == BF16):
-        order_a, order_b = orders()
-        fulls = []
-        for number, shard in enumerate(shards):
-            full = gather_dp(shard, 0, (order_a, order_b)[number % 2])
-            if shared[number]:
-                other, zero = other_core(full), lax.axis_index("mp") == 0
-                full = jnp.stack([jnp.where(zero, full, other), jnp.where(zero, other, full)])
-            fulls.append(full)
-        return fulls
     highs = size // 4
     count = len(shards)
-    groups = blocks_of([a.shape[1] for a in shards], 1024)
-    outs = []
+    groups = blocks_of([a.shape[1] for a in shards], 512)
+    total = len(groups)
+    rows, wide, local = kept_column.shape[0], evec.shape[1], shards[1].shape[1] // 4
+    images = table.shape[0]
+    length = rows // images
+    group = 2 * length
+    fulls = []
     for shard, split in zip(shards, shared):
         dims = (highs, 4) + shard.shape
-        outs.append(shape((2,) + dims if split else dims, shard.dtype))
+        fulls.append(shape((2,) + dims if split else dims, shard.dtype))
+    outs = [shape((rows, wide), F32), shape((3 * local, rows), BF16), shape((local, rows), BF16),
+            shape((local // DH, rows), F32), shape((rows, pixels.shape[1]), BF16), shape((rows, wide), F32),
+            shape((rows, wide), BF16), shape((rows, wide), BF16), shape((8, 128), F32)]
     dma = pltpu.SemaphoreType.DMA
-    total = len(groups)
+    small = (8, 128)
+    in_vmem = pl.BlockSpec(memory_space=pltpu.VMEM)
     any_space = pl.BlockSpec(memory_space=pl.ANY)
-    fulls = pl.pallas_call(
-        functools.partial(gather_kernel, highs, shared, groups, count),
-        out_shape=tuple(outs),
-        in_specs=[any_space] * count,
-        out_specs=tuple([any_space] * count),
-        scratch_shapes=[dma((total,)), dma((total, highs - 1)), dma((total, highs - 1)), dma((total, 2)), dma((total, 2)),
-                        dma((total,)), dma((total,)), dma((count,)), dma((count,))],
-        compiler_params=pltpu.CompilerParams(collective_id=0, has_side_effects=True),
+    result = pl.pallas_call(
+        functools.partial(forward_kernel, highs, shared, groups, count, length, group, DH),
+        out_shape=tuple(fulls + outs),
+        in_specs=[any_space] * count + [in_vmem, any_space] + [in_vmem] * 4,
+        out_specs=tuple([any_space] * count + [in_vmem] * len(outs)),
+        scratch_shapes=[
+            pltpu.VMEM(band_ids.shape, jnp.int32), pltpu.VMEM(fulls[0].shape, BF16), pltpu.VMEM(fulls[1].shape, BF16),
+            pltpu.VMEM(fulls[2].shape, BF16), pltpu.VMEM((4 * local, wide), BF16), pltpu.VMEM((rows, wide), BF16),
+            pltpu.VMEM((rows, wide), BF16), pltpu.VMEM((rows, wide), BF16), pltpu.VMEM((rows, wide), F32),
+            pltpu.VMEM(small, F32), pltpu.VMEM((4,) + small, F32), pltpu.VMEM((highs,) + small, F32),
+            dma((total,)), dma((total, highs - 1)), dma((total, highs - 1)), dma((total, 2)), dma((total, 2)),
+            dma((total,)), dma((total,)), dma((count,)), dma((count,)), dma((4,)), dma((2,)), dma((2,)),
+            dma((highs + 2,)), dma((highs + 2,))],
+        compiler_params=pltpu.CompilerParams(collective_id=0, has_side_effects=True, vmem_limit_bytes=VMEM_LIMIT),
         cost_estimate=pl.CostEstimate(flops=0, bytes_accessed=sum(a.size * a.dtype.itemsize * size for a in shards),
                                       transcendentals=0),
-    )(*shards)
-    return [full.reshape(((2,) if split else ()) + (size * shard.shape[0], shard.shape[1]))
-            for full, split, shard in zip(fulls, shared, shards)]
+    )(*shards, pixels, band_ids, patch_weight, kept_column, table, evec)
+    weights = [full.reshape(((2,) if split else ()) + (size * shard.shape[0], shard.shape[1]))
+               for full, split, shard in zip(result[:count], shared, shards)]
+    return weights, result[count:]
+
+
+def gather_all(shards, shared):
+    order_a, order_b = orders()
+    fulls = []
+    for number, shard in enumerate(shards):
+        full = gather_dp(shard, 0, (order_a, order_b)[number % 2])
+        if shared[number]:
+            other, zero = other_core(full), lax.axis_index("mp") == 0
+            full = jnp.stack([jnp.where(zero, full, other), jnp.where(zero, other, full)])
+        fulls.append(full)
+    return fulls
 
 
 def reduce_kernel(highs, weights, groups, count, loss_ref, *refs):
@@ -732,11 +915,6 @@
     at_high = [(lax.rem(high + k, highs) * 4 + low, core) for k in range(1, highs)]
     near = [(high * 4 + lax.rem(spot + k, 8) // 2, lax.rem(lax.rem(spot + k, 8), 2)) for k in range(1, 8)]
     greet(near + at_high)
-
-    def remote(source, target, send, receive, device):
-        return pltpu.make_async_remote_copy(
-            src_ref=source, dst_ref=target, send_sem=send, recv_sem=receive,
-            device_id=device, device_id_type=pl.DeviceIdType.MESH)
 
     def route(at):
         if at % 2 == 0:
@@ -944,12 +1122,6 @@
     patch_weight = ((1.0 - kept_flags) * (1.0 - 0.5 * intersection.astype(jnp.float32))).reshape(
         -1, 1
     )
-    local_counts = jnp.stack(
-        [
-            jnp.sum(patch_weight * (band_ids == band_level).astype(jnp.float32))
-            for band_level in range(NB)
-        ]
-    )
     core_at = lax.axis_index("mp")
     size = lax.axis_size("dp")
     low = jnp.bfloat16
@@ -961,40 +1133,51 @@
         return lax.dynamic_slice_in_dim(block, core_at * (block.shape[1] // 2), block.shape[1] // 2, 1).astype(low)
 
     vec_shard = vectors.shape[0]
-    vec_room = -(-(vec_shard + NB) // 1024) * 1024
-    vec_rows = jnp.concatenate([lax.reduce_precision(vectors, 8, 7), local_counts,
-                                jnp.zeros((vec_room - vec_shard - NB,), F32)]).reshape(-1, 128)
-    enc_attn_w, enc_mlp_w, dec_attn_w, dec_mlp_w, embed_w, bridge_w, predict_w, vec_full = gather_all(
-        [flat(enc_attn), flat(enc_mlp), flat(dec_attn), flat(dec_mlp), core_half(patch_embed.T), core_half(bridge),
-         core_half(predict), vec_rows],
-        (False, False, False, False, True, True, True, False))
-    vec_full = vec_full.reshape(size, vec_room)
-    pieces = split_vectors(vec_full[:, :vec_shard].reshape(-1), D, E)
-    band_weight = jnp.sum(vec_full[:, vec_shard : vec_shard + NB], axis=0)
+    vec_room = -(-vec_shard // 1024) * 1024
+    vec_rows = jnp.pad(lax.reduce_precision(vectors, 8, 7), (0, vec_room - vec_shard)).reshape(-1, 128)
+    whole_tiles = patch_embed.shape[1] % 16 == 0 and dec_attn.shape[1] % 16 == 0
+    vec_full = small_gather(vec_rows) if whole_tiles else gather_dp(vec_rows, 0, orders()[0])
+    pieces = split_vectors(vec_full.reshape(size, vec_room)[:, :vec_shard].reshape(-1), D, E)
+    evec = jnp.stack(pieces[:7] + [jnp.zeros_like(pieces[0])])
+    dvec = jnp.stack(pieces[7:14] + [jnp.zeros_like(pieces[7])])
+    kept_column = kept_index.reshape(-1, 1)
+    rows, rows_d = images * keep_count, images * patch_count
+    pixel_count = pixels.shape[1]
+    group = 2 * keep_count
+    shards = [core_half(patch_embed.T), flat(enc_attn), flat(enc_mlp), flat(dec_attn), flat(dec_mlp), core_half(bridge),
+              core_half(predict)]
+    shared = (True, False, False, False, False, True, True)
+    enc_table = sine_table(gsd_scale, D, GRID)
+    if whole_tiles:
+        weights, results = forward_all(shards, shared, pixels, band_ids, patch_weight, kept_column, enc_table, evec)
+        embed_w, enc_attn_w, enc_mlp_w, dec_attn_w, dec_mlp_w, bridge_w, predict_w = weights
+        x0, *enc_saved, kept_pixels, x1, part, other, counts = results
+        band_weight = jnp.sum(counts[:NB], axis=1)
+    else:
+        weights = gather_all(shards, shared)
+        embed_w, enc_attn_w, enc_mlp_w, dec_attn_w, dec_mlp_w, bridge_w, predict_w = weights
+        local = enc_attn_w.shape[1] // 4
+        band_weight = total_dp(jnp.stack([
+            jnp.sum(jnp.where(band_ids == level, patch_weight, 0.0)) for level in range(NB)]))
+        x0, *enc_saved, part, kept_pixels = run(
+            functools.partial(enc_in_kernel, keep_count, group, DH),
+            [shape((rows, D), F32), shape((3 * local, rows), BF16), shape((local, rows), BF16),
+             shape((local // DH, rows), F32), shape((rows, D), BF16), shape((rows, pixel_count), BF16)],
+            [pltpu.VMEM((4 * local, D), BF16)],
+            (pixels, kept_column, enc_table, embed_w, evec, enc_attn_w),
+            rows * D * (2 * pixel_count + 8 * local))
+        x1, part = mlp_forward(x0, part, evec, enc_mlp_w)
+        other = other_core(part)
     inverse = 1.0 / band_weight
     core = lax.axis_index("mp").astype(jnp.int32).reshape(1)
     hidden_rows = (1.0 - kept_flags).reshape(-1, 1)
-    kept_column = kept_index.reshape(-1, 1)
-    rows, rows_d = images * keep_count, images * patch_count
-    local, local_d = enc_attn_w.shape[1] // 4, dec_attn_w.shape[1] // 4
-    pixel_count = pixels.shape[1]
-    evec = jnp.stack(pieces[:7] + [jnp.zeros_like(pieces[0])])
-    dvec = jnp.stack(pieces[7:14] + [jnp.zeros_like(pieces[7])])
-    group = 2 * keep_count
-    x0, *enc_saved, part, kept_pixels = run(
-        functools.partial(enc_in_kernel, keep_count, group, DH),
-        [shape((rows, D), F32), shape((3 * local, rows), BF16), shape((local, rows), BF16),
-         shape((local // DH, rows), F32), shape((rows, D), BF16), shape((rows, pixel_count), BF16)],
-        [pltpu.VMEM((4 * local, D), BF16)],
-        (pixels, kept_column, sine_table(gsd_scale, D, GRID), embed_w, evec, enc_attn_w),
-        rows * D * (2 * pixel_count + 8 * local))
-    x1, part = mlp_forward(x0, part, evec, enc_mlp_w)
+    local_d = dec_attn_w.shape[1] // 4
     x2, final_enc, xd, *dec_saved, part = run(
         functools.partial(dec_in_kernel, keep_count, DDH),
         [shape((rows, D), F32), shape((rows, D), BF16), shape((rows_d, E), F32), shape((3 * local_d, rows_d), BF16),
          shape((local_d, rows_d), BF16), shape((local_d // DDH, rows_d), F32), shape((rows_d, E), BF16)],
         [pltpu.VMEM((4 * local_d, E), BF16), pltpu.VMEM((rows, E), F32)],
-        (x1, part, other_core(part), evec, bridge_w, kept_index, hidden_rows, sine_table(gsd_scale, E, GRID), dvec,
+        (x1, part, other, evec, bridge_w, kept_index, hidden_rows, sine_table(gsd_scale, E, GRID), dvec,
          dec_attn_w),
         rows_d * E * 8 * local_d + 2 * rows * D * E)
     xd1, part = mlp_forward(xd, part, dvec, dec_mlp_w)

time: 695 us -> 638 us (0.918)
  Pallas kernels: 598 us -> 559 us
  other arithmetic: 28.7 us -> 20.8 us
    pallas_call x6 -> x5, Pallas kernels: 158 us -> 131 us  [run(): pl.pallas_call(kernel, out_shape=tuple(outs), in_specs=[pl.BlockSpec(memo...]
    pallas_call x2 -> x1, Pallas kernels: 27.2 us -> 15.8 us  [mlp_forward(): pl.pallas_call(functools.partial(mlp_kernel, tile), out_shape=(shape((row...]
    pallas_call x1 -> x2, Pallas kernels: 178 us -> 182 us  [the longest x1 171 us: forward_all(): pl.pallas_call(functools.partial(forward_kernel, highs, shared, groups, c...]
    ppermute x11 -> x9, waiting for transfers between devices: 22.3 us -> 19.8 us  [other_core(): return lax.ppermute(block, 'mp', [(0, 1), (1, 0)])]
    unnamed x122 -> x123, local copies, waits for them, and re-layouts: 15.8 us -> 14 us
  transfers between devices with their start and end apart: 11 -> 9, of which waited for: 7 -> 6; matrix products, arithmetic and copies ran while one was open for 3% -> 2% of each run, Pallas kernels for 0% -> 0%
where the time goes in v4:
time: 638 us; the launch traced here: 634 us
  Pallas kernels  559 us (88%)
  local copies, waits for them, and re-layouts  26 us (4%)
  other arithmetic  20.8 us (3%)
  waiting for transfers between devices  19.8 us (3%)
    pallas_call x1, Pallas kernels, forward_all(): pl.pallas_call(functools.partial(forward_kernel, highs, shared, groups, c...  171 us
    pallas_call x1, Pallas kernels, reduce_all(): pl.pallas_call(functools.partial(reduce_kernel, highs, weights, groups, c...  166 us
    pallas_call x5, Pallas kernels, run(): pl.pallas_call(kernel, out_shape=tuple(outs), in_specs=[pl.BlockSpec(memo...  131 us
    pallas_call x2, Pallas kernels, mlp_backward(): pl.pallas_call(functools.partial(mlp_back_kernel, tile), out_shape=(shape...  47 us
    ppermute x9, waiting for transfers between devices, other_core(): return lax.ppermute(block, 'mp', [(0, 1), (1, 0)])  19.8 us
    pallas_call x1, Pallas kernels, head(): pl.pallas_call(head_kernel, out_shape=(shape((rows, width), F32), shape((...  17 us
    pallas_call x1, Pallas kernels, mlp_forward(): pl.pallas_call(functools.partial(mlp_kernel, tile), out_shape=(shape((row...  15.8 us
    unnamed x123, local copies, waits for them, and re-layouts  14 us
  transfers between devices with their start and end apart: 9, of which 6 were waited for; matrix products, arithmetic and copies ran while one was open for 2% of the time, Pallas kernels for 0%

profile of v4, /device:TPU:0, one launch (start us, length us, event | category | flops | bytes accessed | tf_op | source)
XLA Modules:
  0.0 634.2 jit_solution(8630818585312250762)
XLA Ops:
  1.7 1.6 reshape.238.refs_10_.kept_ref
  4.5 11.0 %shard_map.544 = f32[16,8,128]{2,1,0:T(8,128)} custom-call(f32[8,128]{1,0:T(8,128)} %pad_bitcast_fusion.1.part_ref), custom_call_target="tpu_custom_call" | custom-call | tf_op jit(solution)/shard_map/pallas_call | solution.py:633
  16.6 1.5 fusion.9.refs_0_
  24.6 1.5 dynamic-slice_convert_fusion.1.refs_5_
  31.6 171.1 %shard_map.545 = (bf16[2,4,4,64,384]{4,3,2,1,0:T(8,128)(2,1)}, bf16[4,4,64,2048]{3,2,1,0:T(8,128)(2,1)}, bf16[4,4,64,4096]{3,2,1,0:T(8,128)(2,1)}, bf16[4,4,32,1...) custom-call(bf16[64,384]{1,0:T(8,128)(2,1)} %fusion.9.refs_0_, ...), custom_call_target="tpu_custom_call" | custom-call | bytes 17432576 | tf_op jit(solution)/shard_map/pallas_call | solution.py:870
  202.7 39.7 %shard_map.546 = (f32[512,1024]{1,0:T(8,128)}, bf16[512,1024]{1,0:T(8,128)(2,1)}, f32[2048,512]{1,0:T(8,128)}, bf16[768,2048]{1,0:T(8,128)(2,1)}, bf16[256,2048]...) custom-call(f32[512,1024]{1,0:T(8,128)} %get-tuple-element.99.x1_ref, ...), custom_call_target="tpu_custom_call" | custom-call | flops 2684354560 | bytes 20178944 | tf_op jit(solution)/shard_map/pallas_call | solution.py:414
  242.7 4.0 collective-permute-done.other_ref
  248.1 15.8 %shard_map.547 = (f32[2048,512]{1,0:T(8,128)}, bf16[2048,512]{1,0:T(8,128)(2,1)}) custom-call(f32[2048,512]{1,0:T(8,128)} %get-tuple-element.104.x_ref, bf16[2048,512]{1,0:T(8,128)(2,1)} %get-tuple-element.105.mine_ref, bf16[2048,512]{1,0:T(8,128)(2,1)} %copy-done.48, f32[8,512]{1,0:T(8,128)} %stack.111.vec_ref, bf16[512,2048]{1,0:T(8,128)(2,1)} %bitcast.153, ...), custom_call_target="tpu_custom_call" | custom-call | flops 4294967296 | bytes 16777216 | tf_op jit(solution)/shard_map/pallas_call | solution.py:438
  265.5 2.8 collective-permute-done.1.other_ref
  269.7 17.0 %shard_map.548 = (f32[2048,512]{1,0:T(8,128)}, bf16[512,384]{1,0:T(8,128)(2,1)}, f32[1,768]{1,0:T(1,128)}, f32[1,768]{1,0:T(1,128)}, f32[1,512]{1,0:T(1,128)}, /*index=5*/f32[1,512]{1,0:T(1,128)}) custom-call(s32[1]{0:T(128)} %bitcast.core_ref, f32[3]{0:T(128)} %broadcast_divide_fusion.inverse_ref, f32[2048,512]{1,0:T(8,128)} %get-tuple-element.107.x1_ref, ...), custom_call_target="tpu_custom_call" | custom-call | flops 4026531840 | bytes 22020096 | tf_op jit(solution)/shard_map/pallas_call | solution.py:485
  286.8 26.5 %shard_map.549 = (bf16[512,1024]{1,0:T(8,128)(2,1)}, bf16[512,1024]{1,0:T(8,128)(2,1)}, bf16[2048,512]{1,0:T(8,128)(2,1)}) custom-call(f32[2048,512]{1,0:T(8,128)} %get-tuple-element.111.gy_ref, f32[2048,512]{1,0:T(8,128)} %get-tuple-element.107.x1_ref, f32[8,512]{1,0:T(8,128)} %stack.111.vec_ref, bf16[512,2048]{1,0:T(8,128)(2,1)} %bitcast.155, ...), custom_call_target="tpu_custom_call" | custom-call | flops 10737418240 | bytes 14680064 | tf_op jit(solution)/shard_map/pallas_call | solution.py:459
  313.7 4.0 collective-permute-done.2.other_ref
  319.0 42.7 %shard_map.550 = (f32[2048,512]{1,0:T(8,128)}, bf16[512,1024]{1,0:T(8,128)(2,1)}, f32[1,512]{1,0:T(1,128)}, f32[1,512]{1,0:T(1,128)}, bf16[2048,512]{1,0:T(8,128)(2,1)}) custom-call(f32[2048,512]{1,0:T(8,128)} %get-tuple-element.111.gy_ref, f32[2048,512]{1,0:T(8,128)} %get-tuple-element.107.x1_ref, bf16[2048,512]{1,0:T(8,128)(2,1)} %get-tuple-element.112.mine_ref, ...), custom_call_target="tpu_custom_call" | custom-call | flops 4831838208 | bytes 29446144 | tf_op jit(solution)/shard_map/pallas_call | solution.py:414
  362.1 4.0 collective-permute-done.3.other_ref
  367.4 14.2 %shard_map.551 = (f32[1,512]{1,0:T(1,128)}, f32[1,512]{1,0:T(1,128)}, f32[1,512]{1,0:T(1,128)}, bf16[1024,256]{1,0:T(8,128)(2,1)}, f32[1,1024]{1,0:T(1,128)}, /*index=5*/f32[1,1024]{1,0:T(1,128)}, f32[512,1024]{1,0:T(8,128)}) custom-call(s32[1]{0:T(128)} %bitcast.core_ref, f32[2048,512]{1,0:T(8,128)} %get-tuple-element.116.gx_ref, ...), custom_call_target="tpu_custom_call" | custom-call | flops 805306368 | bytes 19472388 | tf_op jit(solution)/shard_map/pallas_call | solution.py:414
  381.6 20.5 %shard_map.552 = (bf16[1024,2048]{1,0:T(8,128)(2,1)}, bf16[1024,2048]{1,0:T(8,128)(2,1)}, bf16[512,1024]{1,0:T(8,128)(2,1)}) custom-call(f32[512,1024]{1,0:T(8,128)} %get-tuple-element.120.gy_ref, f32[512,1024]{1,0:T(8,128)} %get-tuple-element.99.x1_ref, f32[8,1024]{1,0:T(8,128)} %stack.103.refs_12_.evec_ref.vec_ref, bf16[1024,4096]{1,0:T(8,128)(2,1)} %bitcast.150, ...), custom_call_target="tpu_custom_call" | custom-call | flops 10737418240 | bytes 22020096 | tf_op jit(solution)/shard_map/pallas_call | solution.py:459
  402.5 2.5 collective-permute-done.4.other_ref
  406.0 28.5 %shard_map.553 = (f32[512,1024]{1,0:T(8,128)}, bf16[1024,2048]{1,0:T(8,128)(2,1)}, f32[1,1024]{1,0:T(1,128)}, f32[1,1024]{1,0:T(1,128)}, bf16[512,1024]{1,0:T(8,128)(2,1)}) custom-call(f32[512,1024]{1,0:T(8,128)} %get-tuple-element.120.gy_ref, f32[512,1024]{1,0:T(8,128)} %get-tuple-element.99.x1_ref, bf16[512,1024]{1,0:T(8,128)(2,1)} %get-tuple-element.122.mine_ref, ...), custom_call_target="tpu_custom_call" | custom-call | flops 4831838208 | bytes 22077440 | tf_op jit(solution)/shard_map/pallas_call | solution.py:414
  434.8 2.5 collective-permute-done.5.other_ref
  438.4 6.1 shard_map.554
  447.7 166.2 %shard_map.555 = (f32[64,2048]{1,0:T(8,128)}, f32[64,2048]{1,0:T(8,128)}, f32[64,2048]{1,0:T(8,128)}, f32[32,1024]{1,0:T(8,128)}, f32[32,1024]{1,0:T(8,128)}, /*...) custom-call(f32[1,768]{1,0:T(1,128)} %get-tuple-element.110.loss_ref, ...), custom_call_target="tpu_custom_call" | custom-call | bytes 17498112 | tf_op jit(solution)/shard_map/pallas_call | solution.py:1032
  618.6 2.3 multiply_subtract_fusion.2
  621.0 4.1 multiply_add_fusion
  626.0 1.7 multiply_add_fusion.2
  (187 shorter events, 37.2 us)
Async XLA Ops:
  0.7 20.0 %copy-start.13 = (f32[4,32,256]{2,1,0:T(8,128)S(1)}, f32[4,32,256]{2,1,0:T(8,128)}, u32[]{:S(2)}) copy-start(f32[4,32,256]{2,1,0:T(8,128)} %param.41) | copy-start | bytes 393220
  0.7 20.0 %copy-start.50 = (s32[8]{0:T(128)S(1)}, s32[8]{0:T(128)}, u32[]{:S(2)}) copy-start(s32[8]{0:T(128)} %param.38) | copy-start | bytes 100
  0.7 20.0 %copy-start = (f32[2,64,2048]{2,1,0:T(8,128)S(1)}, f32[2,64,2048]{2,1,0:T(8,128)}, u32[]{:S(2)}) copy-start(f32[2,64,2048]{2,1,0:T(8,128)} %param.40) | copy-start | bytes 3145732
  242.4 4.4 collective-permute-start
  248.1 16.8 %copy-start.46 = (f32[8,128]{1,0:T(8,128)S(1)}, f32[8,128]{1,0:T(8,128)}, u32[]{:S(2)}) copy-start(f32[8,128]{1,0:T(8,128)} %get-tuple-element.98) | copy-start | bytes 12292
  263.9 4.4 collective-permute-start.1
  265.0 21.8 %copy-start.47 = (f32[3]{0:T(128)}, f32[3]{0:T(128)S(1)}, u32[]{:S(2)}) copy-start(f32[3]{0:T(128)S(1)} %slice_reduce_fusion) | copy-start | bytes 40
  313.3 4.4 collective-permute-start.2
  361.7 4.4 collective-permute-start.3
  402.1 2.9 collective-permute-start.4
  434.5 2.9 collective-permute-start.5
  438.3 8.3 %copy-start.35 = (f32[1,1024]{1,0:T(1,128)S(1)}, f32[1,1024]{1,0:T(1,128)}, u32[]{:S(2)}) copy-start(f32[1,1024]{1,0:T(1,128)} %get-tuple-element.145) | copy-start | bytes 12292
  438.3 8.3 %copy-start.34 = (f32[1,1024]{1,0:T(1,128)S(1)}, f32[1,1024]{1,0:T(1,128)}, u32[]{:S(2)}) copy-start(f32[1,1024]{1,0:T(1,128)} %get-tuple-element.146) | copy-start | bytes 12292
  438.3 8.3 %copy-start.45 = (f32[1,512]{1,0:T(1,128)S(1)}, f32[1,512]{1,0:T(1,128)}, u32[]{:S(2)}) copy-start(f32[1,512]{1,0:T(1,128)} %get-tuple-element.147) | copy-start | bytes 6148
  438.3 8.3 %copy-start.44 = (f32[1,512]{1,0:T(1,128)S(1)}, f32[1,512]{1,0:T(1,128)}, u32[]{:S(2)}) copy-start(f32[1,512]{1,0:T(1,128)} %get-tuple-element.148) | copy-start | bytes 6148
  438.4 8.3 %copy-start.43 = (f32[1,512]{1,0:T(1,128)S(1)}, f32[1,512]{1,0:T(1,128)}, u32[]{:S(2)}) copy-start(f32[1,512]{1,0:T(1,128)} %get-tuple-element.149) | copy-start | bytes 6148
  438.4 8.3 %copy-start.42 = (f32[1,512]{1,0:T(1,128)S(1)}, f32[1,512]{1,0:T(1,128)}, u32[]{:S(2)}) copy-start(f32[1,512]{1,0:T(1,128)} %get-tuple-element.150) | copy-start | bytes 6148
  438.4 8.3 %copy-start.41 = (f32[1,512]{1,0:T(1,128)S(1)}, f32[1,512]{1,0:T(1,128)}, u32[]{:S(2)}) copy-start(f32[1,512]{1,0:T(1,128)} %get-tuple-element.151) | copy-start | bytes 6148
  438.4 8.4 %copy-start.40 = (f32[1,512]{1,0:T(1,128)S(1)}, f32[1,512]{1,0:T(1,128)}, u32[]{:S(2)}) copy-start(f32[1,512]{1,0:T(1,128)} %get-tuple-element.152) | copy-start | bytes 6148
  438.4 8.4 %copy-start.39 = (f32[1,512]{1,0:T(1,128)S(1)}, f32[1,512]{1,0:T(1,128)}, u32[]{:S(2)}) copy-start(f32[1,512]{1,0:T(1,128)} %get-tuple-element.153) | copy-start | bytes 6148
  438.4 8.4 %copy-start.38 = (f32[1,768]{1,0:T(1,128)S(1)}, f32[1,768]{1,0:T(1,128)}, u32[]{:S(2)}) copy-start(f32[1,768]{1,0:T(1,128)} %get-tuple-element.154) | copy-start | bytes 9220
  616.0 13.1 %collective-permute-start.8 = (f32[32,384]{1,0:T(8,128)}, f32[32,384]{1,0:T(8,128)S(1)}, u32[]{:S(2)}, u32[]{:S(2)}) collective-permute-start(f32[32,384]{1,0:T(8,128)} %get-tuple-element.164), channel_id=1, source_target_pairs={{0,1},{1,0},{2,3},{3,2},{4,5},{5,4},{6,7},{7,6},{8,9},{9,8},{10,11... | collective-permute-start | bytes 147464 | tf_op jit(solution)/shard_map/ppermute | solution.py:426
  616.1 13.8 %collective-permute-start.7 = (f32[64,256]{1,0:T(8,128)}, f32[64,256]{1,0:T(8,128)S(1)}, u32[]{:S(2)}, u32[]{:S(2)}) collective-permute-start(f32[64,256]{1,0:T(8,128)} %get-tuple-element.163), channel_id=1, source_target_pairs={{0,1},{1,0},{2,3},{3,2},{4,5},{5,4},{6,7},{7,6},{8,9},{9,8},{10,11... | collective-permute-start | bytes 196616 | tf_op jit(solution)/shard_map/ppermute | solution.py:426
  616.6 14.2 %collective-permute-start.6 = (f32[64,384]{1,0:T(8,128)}, f32[64,384]{1,0:T(8,128)S(1)}, u32[]{:S(2)}, u32[]{:S(2)}) collective-permute-start(f32[64,384]{1,0:T(8,128)} %get-tuple-element.162), channel_id=1, source_target_pairs={{0,1},{1,0},{2,3},{3,2},{4,5},{5,4},{6,7},{7,6},{8,9},{9,8},{10,11... | collective-permute-start | bytes 294920 | tf_op jit(solution)/shard_map/ppermute | solution.py:426
  (36 other events, 124.3 us)

commit v5 on v4

--- a/solution.py
+++ b/solution.py
@@ -653,12 +653,12 @@
     shards, refs = refs[:count], refs[count:]
     pix_ref, band_ref, weight_ref, kept_ref, table_ref, vec_ref = refs[:6]
     fulls, refs = refs[6 : 6 + count], refs[6 + count :]
-    x_ref, qkv_ref, mixed_ref, lse_ref, pixk_ref, x1_ref, last_ref, far_out_ref, counts_ref = refs[:9]
-    refs = refs[9:]
-    (bands_v, embed_v, attn_v, mlp_v, flat_ref, part_ref, other_ref, low_ref, acc_ref, block_ref, near_ref,
-     far_ref) = refs[:12]
+    x_ref, qkv_ref, mixed_ref, lse_ref, pixk_ref, x1_ref, last_ref, far_out_ref, counts_ref, flat_ref = refs[:10]
+    refs = refs[10:]
+    (bands_v, embed_v, attn_v, mlp_v, part_ref, other_ref, low_ref, acc_ref, block_ref, near_ref,
+     far_ref) = refs[:11]
     (own_sem, zs_sem, zr_sem, cs_sem, cr_sem, fs_sem, fr_sem, ms_sem, mr_sem, load_sem, xs_sem, xr_sem, ts_sem,
-     tr_sem) = refs[12:]
+     tr_sem) = refs[11:]
     core, low, high, low_x, low_y = place_of()
     at_x, at_y = (high * 4 + low_x, core), (high * 4 + low_y, core)
     at_high = [(lax.rem(high + k, highs) * 4 + low, core) for k in range(1, highs)]
@@ -862,7 +862,7 @@
         fulls.append(shape((2,) + dims if split else dims, shard.dtype))
     outs = [shape((rows, wide), F32), shape((3 * local, rows), BF16), shape((local, rows), BF16),
             shape((local // DH, rows), F32), shape((rows, pixels.shape[1]), BF16), shape((rows, wide), F32),
-            shape((rows, wide), BF16), shape((rows, wide), BF16), shape((8, 128), F32)]
+            shape((rows, wide), BF16), shape((rows, wide), BF16), shape((8, 128), F32), shape((4 * local, wide), BF16)]
     dma = pltpu.SemaphoreType.DMA
     small = (8, 128)
     in_vmem = pl.BlockSpec(memory_space=pltpu.VMEM)
@@ -874,7 +874,7 @@
         out_specs=tuple([any_space] * count + [in_vmem] * len(outs)),
         scratch_shapes=[
             pltpu.VMEM(band_ids.shape, jnp.int32), pltpu.VMEM(fulls[0].shape, BF16), pltpu.VMEM(fulls[1].shape, BF16),
-            pltpu.VMEM(fulls[2].shape, BF16), pltpu.VMEM((4 * local, wide), BF16), pltpu.VMEM((rows, wide), BF16),
+            pltpu.VMEM(fulls[2].shape, BF16), pltpu.VMEM((rows, wide), BF16),
             pltpu.VMEM((rows, wide), BF16), pltpu.VMEM((rows, wide), BF16), pltpu.VMEM((rows, wide), F32),
             pltpu.VMEM(small, F32), pltpu.VMEM((4,) + small, F32), pltpu.VMEM((highs,) + small, F32),
             dma((total,)), dma((total, highs - 1)), dma((total, highs - 1)), dma((total, 2)), dma((total, 2)),
@@ -901,102 +901,305 @@
     return fulls
 
 
-def reduce_kernel(highs, weights, groups, count, loss_ref, *refs):
-    grads, outs, sums_ref = refs[:count], refs[count : 2 * count], refs[2 * count]
-    refs = refs[2 * count + 1 :]
+class Reducer:
+    def __init__(self, highs, groups, weights, grads, outs, near, second, far, load_two, load_own, plane, norm, sems):
+        self.highs, self.groups, self.weights = highs, groups, weights
+        self.grads, self.outs = grads, outs
+        self.near, self.second, self.far = near, second, far
+        self.load_two, self.load_own, self.plane, self.norm = load_two, load_own, plane, norm
+        self.load_sem, self.as_sem, self.ar_sem, self.bs_sem, self.br_sem, self.zs_sem, self.zr_sem = sems
+        self.core, self.low, self.high, self.low_x, self.low_y = place_of()
+        self.dev_x, self.dev_y = (self.high * 4 + self.low_x, self.core), (self.high * 4 + self.low_y, self.core)
+        self.at_high = [(lax.rem(self.high + k, highs) * 4 + self.low, self.core) for k in range(1, highs)]
+        self.pairs = (len(groups) + 1) // 2
+
+    def in_pair(self, pair):
+        return [at for at in (2 * pair, 2 * pair + 1) if 0 <= at < len(self.groups)] if 0 <= pair < self.pairs else []
+
+    def route(self, at):
+        if at % 2 == 0:
+            return self.low_y, self.dev_y, self.low_x, self.dev_x
+        return self.low_x, self.dev_x, self.low_y, self.dev_y
+
+    def grad(self, at, which):
+        number, start, size = self.groups[at]
+        return self.grads[number].at[:, which, :, pl.ds(start, size)]
+
+    def slot(self, ref, at, count):
+        number, _, size = self.groups[at]
+        return ref.at[at % count, :, pl.ds(0, self.outs[number].shape[0]), pl.ds(0, size)]
+
+    def two_ref(self, at):
+        return self.slot(self.load_two, at, 6)
+
+    def own_ref(self, at):
+        return self.slot(self.load_own, at, 8)
+
+    def loads(self, at):
+        return [pltpu.make_async_copy(self.grad(at, self.route(at)[2]), self.two_ref(at), self.load_sem.at[at, 0]),
+                pltpu.make_async_copy(self.grad(at, self.low), self.own_ref(at), self.load_sem.at[at, 1])]
+
+    def one(self, at):
+        low_one, dev_one, _, _ = self.route(at)
+        return [remote(self.grad(at, 3 - self.low), self.near[2 * at], self.as_sem.at[at, 0], self.ar_sem.at[at, 0], dev_one),
+                remote(self.grad(at, low_one), self.near[2 * at + 1], self.as_sem.at[at, 1], self.ar_sem.at[at, 1], dev_one)]
+
+    def two(self, at):
+        return remote(self.two_ref(at), self.second[at], self.bs_sem.at[at], self.br_sem.at[at], self.route(at)[3])
+
+    def three(self, at):
+        return [remote(self.own_ref(at).at[lax.rem(self.high + k, self.highs)], self.far[at].at[k - 1],
+                       self.zs_sem.at[at, k - 1], self.zr_sem.at[at, k - 1], self.at_high[k - 1])
+                for k in range(1, self.highs)]
+
+    def step(self, step):
+        for at in self.in_pair(step):
+            for copy in self.one(at) + self.loads(at):
+                copy.start()
+        for at in self.in_pair(step - 1):
+            mine = self.two_ref(at)
+            self.loads(at)[0].wait()
+            self.one(at)[0].wait()
+            mine[...] = (mine[...].astype(F32) + self.near[2 * at][...].astype(F32)).astype(BF16)
+            self.two(at).start()
+        for at in self.in_pair(step - 2):
+            number, start, size = self.groups[at]
+            mine = self.own_ref(at)
+            self.loads(at)[1].wait()
+            self.one(at)[1].wait()
+            self.two(at).wait()
+            plane = self.slot(self.plane, at, 2)
+            plane[...] = (mine[...].astype(F32) + self.near[2 * at + 1][...].astype(F32)
+                          + self.second[at][...].astype(F32))
+            self.outs[number][:, pl.ds(start, size)] = plane[self.high]
+            mine[...] = plane[...].astype(BF16)
+            for copy in self.three(at):
+                copy.start()
+        for at in self.in_pair(step - 3):
+            number, start, size = self.groups[at]
+            for copy in self.three(at):
+                copy.wait()
+            cols = pl.ds(start, size)
+            done = self.outs[number][:, cols]
+            for k in range(self.highs - 1):
+                done = done + self.far[at][k].astype(F32)
+            self.outs[number][:, cols] = done
+            self.norm[0:1, 0:1] += self.weights[number] * jnp.sum(done * done, keepdims=True)
+
+
+def reducer_scratch(highs, groups, shards):
+    piece = lambda lead, group: pltpu.VMEM((lead, shards[group[0]], group[2]), BF16)
+    near = [piece(highs, group) for group in groups for _ in range(2)]
+    second = [piece(highs, group) for group in groups]
+    far = [piece(highs - 1, group) for group in groups]
+    slot = (highs, max(shards), max(group[2] for group in groups))
+    loads = [pltpu.VMEM((6,) + slot, BF16), pltpu.VMEM((8,) + slot, BF16), pltpu.VMEM((2,) + slot, F32)]
+    dma, total = pltpu.SemaphoreType.DMA, len(groups)
+    sems = [dma((total, 2)), dma((total, 2)), dma((total, 2)), dma((total,)), dma((total,)),
+            dma((total, highs - 1)), dma((total, highs - 1))]
+    return near + second + far + loads + sems
+
+
+def make_reducer(highs, groups, weights, grads, outs, norm, refs):
     total = len(groups)
-    buffers, refs = refs[: 6 * total], refs[6 * total :]
-    plane_ref, norm_ref, near_ref, far_ref = refs[:4]
-    load_sem, as_sem, ar_sem, bs_sem, br_sem, zs_sem, zr_sem, ns_sem, nr_sem, hs_sem, hr_sem = refs[4:]
-    core, low, high, low_x, low_y = place_of()
-    low_d = 3 - low
+    near, second, far, refs = refs[: 2 * total], refs[2 * total : 3 * total], refs[3 * total : 4 * total], refs[4 * total :]
+    return Reducer(highs, groups, weights, grads, outs, near, second, far, *refs[:3], norm, refs[3:10]), refs[10:]
+
+
+def backward_kernel(highs, weights, groups, ready, count, length, group, head_dim, *refs):
+    given = count - 4
+    gy_ref, x1_ref, vec_ref, vgrad_ref, loss_ref, lse_ref = refs[:6]
+    x_any, qkv_any, mixed_any, flat_any, pixk_any, mlp_any = refs[6:12]
+    refs = refs[12:]
+    grads, refs = refs[:given], refs[given:]
+    outs, sums_ref, vsum_ref, refs = refs[:count], refs[count], refs[count + 1], refs[count + 2 :]
+    made, refs = refs[:4], refs[4:]
+    grads = tuple(grads) + tuple(made)
+    (x_ref, qkv_ref, mixed_ref, flat_ref, pixk_ref, wmlp_ref, low_ref, lowt_ref, grad_ref, gradt_ref, acc_ref, part_ref,
+     other_ref, last_ref, gmix_ref, gqkv_ref, stage_ref, norm_ref, spots_ref, far_ref, vnear_ref, vfar_ref) = refs[:22]
+    (load_sem, wload_sem, store_sem, xs_sem, xr_sem, ns_sem, nr_sem, hs_sem, hr_sem, ts_sem, tr_sem) = refs[22:33]
+    red, _ = make_reducer(highs, groups, weights, grads, outs, norm_ref, refs[33:])
+    core, low, high = red.core, red.low, red.high
     spot = low * 2 + core
-    dev_x, dev_y = (high * 4 + low_x, core), (high * 4 + low_y, core)
-    at_high = [(lax.rem(high + k, highs) * 4 + low, core) for k in range(1, highs)]
+    sibling = (high * 4 + low, 1 - core)
     near = [(high * 4 + lax.rem(spot + k, 8) // 2, lax.rem(lax.rem(spot + k, 8), 2)) for k in range(1, 8)]
-    greet(near + at_high)
-
-    def route(at):
-        if at % 2 == 0:
-            return low_y, dev_y, low_x, dev_x
-        return low_x, dev_x, low_y, dev_y
-
-    def grad(at, which):
-        number, start, size = groups[at]
-        return grads[number].at[:, which, :, pl.ds(start, size)]
-
-    def loads(at):
-        _, _, low_two, _ = route(at)
-        return [pltpu.make_async_copy(grad(at, low_two), buffers[6 * at], load_sem.at[at, 0]),
-                pltpu.make_async_copy(grad(at, low), buffers[6 * at + 1], load_sem.at[at, 1])]
-
-    def one(at):
-        low_one, dev_one, _, _ = route(at)
-        return [remote(grad(at, low_d), buffers[6 * at + 2], as_sem.at[at, 0], ar_sem.at[at, 0], dev_one),
-                remote(grad(at, low_one), buffers[6 * at + 3], as_sem.at[at, 1], ar_sem.at[at, 1], dev_one)]
-
-    def two(at):
-        return remote(buffers[6 * at], buffers[6 * at + 4], bs_sem.at[at], br_sem.at[at], route(at)[3])
-
-    def three(at):
-        return [remote(buffers[6 * at + 1].at[lax.rem(high + k, highs)], buffers[6 * at + 5].at[k - 1],
-                       zs_sem.at[at, k - 1], zr_sem.at[at, k - 1], at_high[k - 1]) for k in range(1, highs)]
-
-    pairs = (total + 1) // 2
-    in_pair = lambda pair: [at for at in (2 * pair, 2 * pair + 1) if at < total]
+    greet(near + red.at_high)
+    rows, wide = x_ref.shape
+    width = mixed_ref.shape[0]
+    hidden = mlp_any.shape[-1] // 2
+    size = 512
+    tiles = hidden // size
+    mask = group_mask(group, length)
+
+    late = [pltpu.make_async_copy(source, target, load_sem.at[at]) for at, (source, target) in enumerate(
+        ((x_any, x_ref), (qkv_any, qkv_ref), (mixed_any, mixed_ref), (flat_any, flat_ref), (pixk_any, pixk_ref)))]
+
+    def weight_loads(tile):
+        return [pltpu.make_async_copy(mlp_any.at[:, :, :, pl.ds(half * hidden + tile * size, size)],
+                                      wmlp_ref.at[tile % 2, half], wload_sem.at[tile % 2, half]) for half in range(2)]
+
+    def store(slot, target, start, columns=512):
+        return pltpu.make_async_copy(stage_ref.at[slot, :, :, :, pl.ds(0, columns)],
+                                     target.at[:, :, :, pl.ds(start, columns)], store_sem.at[slot])
+
+    def exchange(at, target):
+        return remote(part_ref, target, xs_sem.at[at], xr_sem.at[at], sibling)
+
+    def staged(slot, value):
+        columns = value.shape[1]
+        stage_ref[slot, :, :, :, :columns] = value.astype(BF16).reshape(stage_ref.shape[1:4] + (columns,))
+
+    def mlp_first():
+        unit, _ = normalize(x1_ref[...])
+        value = (unit * vec_ref[3:4, :] + vec_ref[4:5, :]).astype(BF16)
+        low_ref[...] = value
+        lowt_ref[...] = value.T
+        value = gy_ref[...].astype(BF16)
+        grad_ref[...] = value
+        gradt_ref[...] = value.T
+        acc_ref[...] = jnp.zeros_like(acc_ref)
+
+    def mlp_block(tile):
+        for copy in weight_loads(tile):
+            copy.wait()
+        if tile + 1 < tiles:
+            for copy in weight_loads(tile + 1):
+                copy.start()
+        w_up = wmlp_ref[tile % 2, 0].reshape(wide, size)
+        w_down = wmlp_ref[tile % 2, 1].reshape(wide, size)
+        up = dot_nn(low_ref[...], w_up)
+        square, bent, half = gelu_parts(up)
+        mid = (up * half).astype(BF16)
+        slope = half + (0.5 * GELU_C) * up * (1.0 - bent * bent) * (1.0 + (3.0 * 0.044715) * square)
+        grad_up = (dot_nn(grad_ref[...], w_down) * slope).astype(BF16)
+        acc_ref[...] += dot_nt(grad_up, w_up)
+        slot = 2 * (tile % 2)
+        if tile >= 2:
+            store(slot, made[0], (tile - 2) * size).wait()
+            store(slot + 1, made[1], (tile - 2) * size).wait()
+        staged(slot, dot_nn(lowt_ref[...], grad_up))
+        store(slot, made[0], tile * size).start()
+        staged(slot + 1, dot_nn(gradt_ref[...], mid))
+        store(slot + 1, made[1], tile * size).start()
+
+    def mlp_last():
+        part_ref[...] = acc_ref[...].astype(BF16)
+        exchange(0, other_ref).start()
+
+    def stores_done(tile):
+        slot = 2 * (tile % 2)
+        store(slot, made[0], tile * size).wait()
+        store(slot + 1, made[1], tile * size).wait()
+
+    def rows_step(number, carry):
+        at = pl.ds(pl.multiple_of(number * group, group), group)
+        unit, rstd = normalize(x1_ref[at, :])
+        grad_in, gain_sum, shift_sum = norm_back(both(part_ref, other_ref, at), vec_ref[3:4, :], unit, rstd)
+        grad_in = grad_in + gy_ref[at, :]
+        gy_ref[at, :] = grad_in
+        vsum_ref[3:4, :] += gain_sum
+        vsum_ref[4:5, :] += shift_sum
+        low_grad = grad_in.astype(BF16)
+        gradt_ref[:, at] = low_grad.T
+        gmix_ref[...] = dot_nt(flat_ref[3 * width :, :], low_grad).astype(BF16)
+        attend_back(qkv_ref, gmix_ref, lse_ref, gqkv_ref, at, width, head_dim, mask)
+        part_ref[at, :] = dot_nn(gqkv_ref[:, at].T, flat_ref[: 3 * width, :]).astype(BF16)
+        unit_a, _ = normalize(x_ref[at, :])
+        lowt_ref[:, at] = (unit_a * vec_ref[1:2, :] + vec_ref[2:3, :]).astype(BF16).T
+        return carry
+
+    def attn_grads():
+        for slot in range(4):
+            if slot < 3:
+                value = dot_nt(lowt_ref[...], gqkv_ref[pl.ds(slot * width, width), :])
+            else:
+                value = dot_nt(gradt_ref[...], mixed_ref[...])
+            staged(slot, value)
+            store(slot, made[2], slot * width, width).start()
+
+    def enc_out():
+        unit, rstd = normalize(x_ref[...])
+        grad_in, gain_sum, shift_sum = norm_back(both(part_ref, last_ref, pl.ds(0, rows)), vec_ref[1:2, :], unit, rstd)
+        grad_in = grad_in + gy_ref[...]
+        vsum_ref[0:1, :] = jnp.sum(grad_in, axis=0, keepdims=True)
+        vsum_ref[1:2, :] = gain_sum
+        vsum_ref[2:3, :] = shift_sum
+        share = made[3].shape[-1]
+        columns = pl.ds(pl.multiple_of(core * share, share), share)
+        staged(0, dot_tn(grad_in.astype(BF16), pixk_ref[:, columns]))
+        store(0, made[3], 0, share).start()
+
+    stages = functools.partial(total_blocks, vsum_ref, vnear_ref, vfar_ref, (ts_sem, tr_sem), low, high, core, highs)
+    mlp_ready, attn_ready, embed_ready = ready
+    row_groups = rows // group
     norm_ref[...] = jnp.zeros_like(norm_ref)
-    kept = {}
-    for step in range(pairs + 3):
-        if step < pairs:
-            for at in in_pair(step):
-                for copy in one(at) + loads(at):
-                    copy.start()
-        if 0 <= step - 1 < pairs:
-            for at in in_pair(step - 1):
-                mine = buffers[6 * at]
-                loads(at)[0].wait()
-                one(at)[0].wait()
-                mine[...] = (mine[...].astype(F32) + buffers[6 * at + 2][...].astype(F32)).astype(mine.dtype)
-                two(at).start()
-        if 0 <= step - 2 < pairs:
-            for at in in_pair(step - 2):
-                number, start, size = groups[at]
-                mine = buffers[6 * at + 1]
-                loads(at)[1].wait()
-                one(at)[1].wait()
-                two(at).wait()
-                rows = mine.shape[1]
-                plane = plane_ref.at[at % 4, :, :rows, :size]
-                plane[...] = (mine[...].astype(F32) + buffers[6 * at + 3][...].astype(F32)
-                              + buffers[6 * at + 4][...].astype(F32))
-                outs[number][:, pl.ds(start, size)] = plane[high]
-                mine[...] = plane[...].astype(mine.dtype)
-                for copy in three(at):
-                    copy.start()
-        if 0 <= step - 3 < pairs:
-            for at in in_pair(step - 3):
-                number, start, size = groups[at]
-                for copy in three(at):
+    vsum_ref[...] = vgrad_ref[...]
+    for copy in weight_loads(0):
+        copy.start()
+    for step in range(red.pairs + 3):
+        if tiles - 2 <= step - mlp_ready < tiles:
+            stores_done(step - mlp_ready)
+        if step == attn_ready:
+            for slot in range(4):
+                store(slot, made[2], slot * width, width).wait()
+        if step == embed_ready:
+            store(0, made[3], 0, made[3].shape[-1]).wait()
+        red.step(step)
+        if step == 0:
+            for copy in late:
+                copy.start()
+            mlp_first()
+        if step < tiles:
+            mlp_block(step)
+            if step == tiles - 1:
+                mlp_last()
+        if tiles <= step < attn_ready - 1:
+            if step == tiles:
+                for copy in late:
                     copy.wait()
-                cols = pl.ds(start, size)
-                done = outs[number][:, cols]
-                for k in range(highs - 1):
-                    done = done + buffers[6 * at + 5][k].astype(F32)
-                outs[number][:, cols] = done
-                norm_ref[0:1, 0:1] += weights[number] * jnp.sum(done * done, keepdims=True)
+                exchange(0, other_ref).wait()
+            share = -(-row_groups // (attn_ready - 1 - tiles))
+            start, stop = (step - tiles) * share, min((step - tiles + 1) * share, row_groups)
+            if start < stop:
+                lax.fori_loop(start, stop, rows_step, 0)
+                if stop == row_groups:
+                    exchange(1, last_ref).start()
+        if step == attn_ready - 1:
+            attn_grads()
+        if step == embed_ready - 1:
+            exchange(1, last_ref).wait()
+            enc_out()
+            vnear_ref[low] = vsum_ref[...]
+            for copy in stages(0):
+                copy.start()
+        if step == embed_ready:
+            for copy in stages(0):
+                copy.wait()
+            vsum_ref[...] = (vnear_ref[0] + vnear_ref[1]) + (vnear_ref[2] + vnear_ref[3])
+            vfar_ref[high] = vsum_ref[...]
+            for copy in stages(1):
+                copy.start()
+        if step == embed_ready + 1:
+            for copy in stages(1):
+                copy.wait()
+            every = vfar_ref[0]
+            for k in range(1, highs):
+                every = every + vfar_ref[k]
+            vsum_ref[...] = every
+            norm_ref[0:1, 0:1] += jnp.sum(every * every, keepdims=True) * (1.0 / (8 * highs))
     norm_ref[1:2, 0:1] = jnp.sum(loss_ref[...], keepdims=True)
-    near_ref[spot] = norm_ref[...]
-    copies = [remote(norm_ref, near_ref.at[spot], ns_sem.at[k], nr_sem.at[k], near[k]) for k in range(7)]
+    spots_ref[spot] = norm_ref[...]
+    copies = [remote(norm_ref, spots_ref.at[spot], ns_sem.at[k], nr_sem.at[k], near[k]) for k in range(7)]
     for copy in copies:
         copy.start()
     for copy in copies:
         copy.wait()
-    local = near_ref[0]
+    local = spots_ref[0]
     for k in range(1, 8):
-        local = local + near_ref[k]
+        local = local + spots_ref[k]
     norm_ref[...] = local
     far_ref[high] = local
-    copies = [remote(norm_ref, far_ref.at[high], hs_sem.at[k], hr_sem.at[k], at_high[k]) for k in range(highs - 1)]
+    copies = [remote(norm_ref, far_ref.at[high], hs_sem.at[k], hr_sem.at[k], red.at_high[k]) for k in range(highs - 1)]
     for copy in copies:
         copy.start()
     for copy in copies:
@@ -1007,43 +1210,64 @@
     sums_ref[...] = every
 
 
-def reduce_all(grads, weights, loss_parts):
+def backward_all(gy, x1, evec, vec_grads, loss_parts, enc_saved, x0, flat, pixk, mlp, grads, length, head_dim):
     size = lax.axis_size("dp")
     highs = size // 4
-    if any((a.shape[0] // size) % 16 for a in grads if a.dtype == BF16):
-        order_a, order_b = orders()
-        outs = [reduce_dp(a, 0, (order_a, order_b)[number % 2], a.dtype) for number, a in enumerate(grads)]
-        sums = jnp.stack([sum(w * jnp.sum(a * a) for w, a in zip(weights, outs)), jnp.sum(loss_parts)])
-        sums = total_dp(sums)
-        sums = sums + other_core(sums)
-        return outs, sums[0], 0.5 * sums[1]
-    count = len(grads)
-    groups = blocks_of([a.shape[1] for a in grads], 512)
-    shards = [a.shape[0] // size for a in grads]
-    total = len(groups)
-    buffers = []
-    for number, _, width in groups:
-        piece = pltpu.VMEM((highs, shards[number], width), grads[number].dtype)
-        buffers += [piece] * 5 + [pltpu.VMEM((highs - 1, shards[number], width), grads[number].dtype)]
+    qkv, mixed, lse = enc_saved
+    rows, wide = x1.shape
+    width = mixed.shape[0]
+    hidden = mlp.shape[1] // 2
+    group = 2 * length
+    shard = wide // size
+    lead = (highs, 4, shard)
+    fresh = [lead + (hidden,), lead + (hidden,), lead + (4 * width,), lead + (pixk.shape[1] // 2,)]
+    widths = [a.shape[1] for a in grads] + [dims[-1] for dims in fresh]
+    shards = [a.shape[0] // size for a in grads] + [shard] * 4
+    count, given = len(widths), len(grads)
+    blocks = blocks_of(widths, 512)
+    first = [b for b in blocks if b[0] < given]
+    if len(first) % 2:
+        raise ValueError("odd blocks")
+    middle = [b for at in range(0, hidden, 512) for b in ((given, at, 512), (given + 1, at, 512))]
+    attn = [b for b in blocks if b[0] == given + 2]
+    groups = first + middle + attn + [b for b in blocks if b[0] == given + 3]
+    ready = (len(first) // 2, (len(first) + len(middle)) // 2, (len(first) + len(middle) + len(attn)) // 2)
     dma = pltpu.SemaphoreType.DMA
-    small = (8, 128)
+    small, vec_block = (8, 128), vec_grads.shape
     in_vmem = pl.BlockSpec(memory_space=pltpu.VMEM)
     any_space = pl.BlockSpec(memory_space=pl.ANY)
     result = pl.pallas_call(
-        functools.partial(reduce_kernel, highs, weights, groups, count),
-        out_shape=tuple([shape((rows, a.shape[1]), F32) for rows, a in zip(shards, grads)] + [shape(small, F32)]),
-        in_specs=[in_vmem] + [any_space] * count,
-        out_specs=tuple([in_vmem] * (count + 1)),
-        scratch_shapes=buffers + [
-            pltpu.VMEM((4, highs, max(shards), max(g[2] for g in groups)), F32), pltpu.VMEM(small, F32),
-            pltpu.VMEM((8,) + small, F32), pltpu.VMEM((highs,) + small, F32),
-            dma((total, 2)), dma((total, 2)), dma((total, 2)), dma((total,)), dma((total,)),
-            dma((total, highs - 1)), dma((total, highs - 1)), dma((7,)), dma((7,)), dma((highs - 1,)), dma((highs - 1,))],
-        compiler_params=pltpu.CompilerParams(collective_id=1, has_side_effects=True, vmem_limit_bytes=VMEM_LIMIT),
-        cost_estimate=pl.CostEstimate(flops=0, bytes_accessed=sum(a.size * a.dtype.itemsize for a in grads),
-                                      transcendentals=0),
-    )(loss_parts, *[a.reshape(highs, 4, rows, a.shape[1]) for rows, a in zip(shards, grads)])
-    return list(result[:count]), result[count][0, 0], 0.5 * result[count][1, 0]
+        functools.partial(backward_kernel, highs, (1.0,) * count, groups, ready, count, length, group, head_dim),
+        out_shape=tuple([shape((r, w), F32) for r, w in zip(shards, widths)] + [shape(small, F32), shape(vec_block, F32)]
+                        + [shape(dims, BF16) for dims in fresh]),
+        in_specs=[in_vmem] * 6 + [any_space] * (6 + given),
+        out_specs=tuple([in_vmem] * (count + 2) + [any_space] * 4),
+        scratch_shapes=[
+            pltpu.VMEM((rows, wide), F32), pltpu.VMEM(qkv.shape, BF16), pltpu.VMEM(mixed.shape, BF16),
+            pltpu.VMEM(flat.shape, BF16), pltpu.VMEM(pixk.shape, BF16), pltpu.VMEM((2, 2) + lead + (512,), BF16),
+            pltpu.VMEM((rows, wide), BF16), pltpu.VMEM((wide, rows), BF16), pltpu.VMEM((rows, wide), BF16),
+            pltpu.VMEM((wide, rows), BF16), pltpu.VMEM((rows, wide), F32), pltpu.VMEM((rows, wide), BF16),
+            pltpu.VMEM((rows, wide), BF16), pltpu.VMEM((rows, wide), BF16), pltpu.VMEM((width, group), BF16),
+            pltpu.VMEM((3 * width, rows), BF16), pltpu.VMEM((4,) + lead + (512,), BF16), pltpu.VMEM(small, F32),
+            pltpu.VMEM((8,) + small, F32), pltpu.VMEM((highs,) + small, F32), pltpu.VMEM((4,) + vec_block, F32),
+            pltpu.VMEM((highs,) + vec_block, F32),
+            dma((5,)), dma((2, 2)), dma((4,)), dma((2,)), dma((2,)), dma((7,)), dma((7,)), dma((highs - 1,)),
+            dma((highs - 1,)), dma((highs + 2,)), dma((highs + 2,))] + reducer_scratch(highs, groups, shards),
+        compiler_params=pltpu.CompilerParams(collective_id=1, has_side_effects=True, vmem_limit_bytes=62 * 2**20),
+        cost_estimate=pl.CostEstimate(flops=0, bytes_accessed=sum(a.size * 2 for a in grads), transcendentals=0),
+    )(gy, x1, evec, vec_grads, loss_parts, lse, x0, qkv, mixed, flat, pixk, mlp.reshape(lead + (2 * hidden,)),
+      *[a.reshape(highs, 4, r, a.shape[1]) for r, a in zip(shards, grads)])
+    return list(result[:count]), result[count][0, 0], 0.5 * result[count][1, 0], result[count + 1]
+
+
+def reduce_plain(grads, loss_parts, vec_grads):
+    order_a, order_b = orders()
+    outs = [reduce_dp(a, 0, (order_a, order_b)[number % 2], a.dtype) for number, a in enumerate(grads)]
+    vec_sums = total_dp(vec_grads)
+    sums = jnp.stack([sum(jnp.sum(a * a) for a in outs), jnp.sum(loss_parts)])
+    sums = total_dp(sums)
+    sums = sums + other_core(sums)
+    return outs, sums[0] + jnp.sum(vec_sums * vec_sums), 0.5 * sums[1], vec_sums
 
 
 def adam_update(master, gradient, first_old, second_old, step_rate, decay_rate):
@@ -1151,7 +1375,7 @@
     if whole_tiles:
         weights, results = forward_all(shards, shared, pixels, band_ids, patch_weight, kept_column, enc_table, evec)
         embed_w, enc_attn_w, enc_mlp_w, dec_attn_w, dec_mlp_w, bridge_w, predict_w = weights
-        x0, *enc_saved, kept_pixels, x1, part, other, counts = results
+        x0, *enc_saved, kept_pixels, x1, part, other, counts, enc_flat = results
         band_weight = jnp.sum(counts[:NB], axis=1)
     else:
         weights = gather_all(shards, shared)
@@ -1193,30 +1417,37 @@
         [pltpu.VMEM((rows, E), BF16)],
         (core, gxd, xd, part, other_core(part), dvec, kept_column, hidden_rows, final_enc, x2, evec, bridge_w),
         3 * rows * D * E, 1)
-    grad_enc_up, grad_enc_down, part = mlp_backward(gye, x1, evec, enc_mlp_w)
-    gxe, grad_enc_attn, grad_enc_gb, grad_enc_bb, part = attn_backward(
-        gye, x1, part, x0, enc_saved, evec, enc_attn_w, keep_count, group, DH)
-    grad_enc_ga, grad_enc_ba, grad_ebias, grad_embed = run(
-        enc_out_kernel,
-        [one_d, one_d, one_d, shape((D, pixel_count // 2), BF16)],
-        [], (core, gxe, x0, part, other_core(part), evec, kept_pixels), rows * D * pixel_count, 1)
-    grad_vectors = jnp.concatenate(
-        [grad_ebias, grad_enc_ga, grad_enc_ba, grad_enc_gb, grad_enc_bb, grad_enc_fg, grad_enc_fb, grad_mask,
-         grad_dec_ga, grad_dec_ba, grad_dec_gb, grad_dec_bb, grad_dec_fg, grad_dec_fb, grad_pbias], axis=1).reshape(-1)
-    vec_grads = jnp.pad(grad_vectors.reshape(size, vec_shard), ((0, 0), (0, vec_room - vec_shard)))
-    sums, total_squares, loss = reduce_all(
-        [grad_enc_attn, grad_enc_up, grad_enc_down, grad_dec_attn, grad_dec_up, grad_dec_down, grad_embed, grad_bridge,
-         grad_predict, vec_grads.reshape(-1, 128)],
-        (1.0,) * 9 + (0.5,), loss_parts)
+    wide_row = lambda row: jnp.pad(row, ((0, 0), (0, D - row.shape[1])))
+    no_row = jnp.zeros((1, D), F32)
+    late_rows = [grad_enc_fg, grad_enc_fb] + [wide_row(row) for row in (
+        grad_mask, grad_dec_ga, grad_dec_ba, grad_dec_gb, grad_dec_bb, grad_dec_fg, grad_dec_fb, grad_pbias)] + [no_row]
+    dec_grads = [grad_predict, grad_dec_up, grad_dec_down, grad_dec_attn, grad_bridge]
+    if whole_tiles:
+        sums, total_squares, loss, vec_sums = backward_all(
+            gye, x1, evec, jnp.concatenate([no_row] * 5 + late_rows), loss_parts, enc_saved, x0, enc_flat, kept_pixels,
+            enc_mlp_w, dec_grads, keep_count, DH)
+    else:
+        grad_enc_up, grad_enc_down, part = mlp_backward(gye, x1, evec, enc_mlp_w)
+        gxe, grad_enc_attn, grad_enc_gb, grad_enc_bb, part = attn_backward(
+            gye, x1, part, x0, enc_saved, evec, enc_attn_w, keep_count, group, DH)
+        grad_enc_ga, grad_enc_ba, grad_ebias, grad_embed = run(
+            enc_out_kernel,
+            [one_d, one_d, one_d, shape((D, pixel_count // 2), BF16)],
+            [], (core, gxe, x0, part, other_core(part), evec, kept_pixels), rows * D * pixel_count, 1)
+        vec_grads = jnp.concatenate([grad_ebias, grad_enc_ga, grad_enc_ba, grad_enc_gb, grad_enc_bb] + late_rows)
+        sums, total_squares, loss, vec_sums = reduce_plain(
+            dec_grads + [grad_enc_up, grad_enc_down, grad_enc_attn, grad_embed], loss_parts, vec_grads)
+    vec_grad = jnp.concatenate([vec_sums[:7].reshape(-1), vec_sums[7:14, :E].reshape(-1), vec_sums[14, :pixel_count]])
+    vec_grad = lax.dynamic_slice_in_dim(vec_grad, lax.axis_index("dp") * vec_shard, vec_shard)
     reduced = (
-        jnp.stack(jnp.split(sums[0], 4, axis=1)),
+        jnp.stack(jnp.split(sums[7], 4, axis=1)),
+        jnp.stack(sums[5:7]),
+        jnp.stack(jnp.split(sums[3], 4, axis=1)),
         jnp.stack(sums[1:3]),
-        jnp.stack(jnp.split(sums[3], 4, axis=1)),
-        jnp.stack(sums[4:6]),
-        join_cores(sums[6], core).T,
-        join_cores(sums[7], core),
-        join_cores(sums[8], core),
-        sums[9].reshape(-1)[:vec_shard],
+        join_cores(sums[8], core).T,
+        join_cores(sums[4], core),
+        join_cores(sums[0], core),
+        vec_grad,
     )
     grad_norm = jnp.sqrt(total_squares)
     factor = CLIP / jnp.maximum(grad_norm, CLIP)

time: 638 us -> 593 us (0.929)
  Pallas kernels: 559 us -> 520 us
    pallas_call x5 -> x3, Pallas kernels: 131 us -> 96.4 us  [run(): pl.pallas_call(kernel, out_shape=tuple(outs), in_specs=[pl.BlockSpec(memo...]
    pallas_call x2 -> x1, Pallas kernels: 47 us -> 26.5 us  [mlp_backward(): pl.pallas_call(functools.partial(mlp_back_kernel, tile), out_shape=(shape...]
    pallas_call x1, Pallas kernels: 166 us -> 181 us  [backward_all(): pl.pallas_call(functools.partial(backward_kernel, highs, (1.0,) * count,...]
    ppermute x9 -> x7, waiting for transfers between devices: 19.8 us -> 13.5 us  [other_core(): return lax.ppermute(block, 'mp', [(0, 1), (1, 0)])]
    unnamed x123 -> x85, local copies, waits for them, and re-layouts: 14 us -> 7.84 us
  transfers between devices with their start and end apart: 9 -> 7, of which waited for: 6 -> 4; matrix products, arithmetic and copies ran while one was open for 2% -> 3% of each run, Pallas kernels for 0% -> 0%
where the time goes in v5:
time: 593 us; the launch traced here: 589 us
  Pallas kernels  520 us (88%)
  local copies, waits for them, and re-layouts  27.5 us (5%)
  other arithmetic  20.4 us (3%)
  waiting for transfers between devices  13.5 us (2%)
    pallas_call x1, Pallas kernels, backward_all(): pl.pallas_call(functools.partial(backward_kernel, highs, (1.0,) * count,...  181 us
    pallas_call x1, Pallas kernels, forward_all(): pl.pallas_call(functools.partial(forward_kernel, highs, shared, groups, c...  173 us
    pallas_call x3, Pallas kernels, run(): pl.pallas_call(kernel, out_shape=tuple(outs), in_specs=[pl.BlockSpec(memo...  96.4 us
    pallas_call x1, Pallas kernels, mlp_backward(): pl.pallas_call(functools.partial(mlp_back_kernel, tile), out_shape=(shape...  26.5 us
    pallas_call x1, Pallas kernels, head(): pl.pallas_call(head_kernel, out_shape=(shape((rows, width), F32), shape((...  17 us
    pallas_call x1, Pallas kernels, mlp_forward(): pl.pallas_call(functools.partial(mlp_kernel, tile), out_shape=(shape((row...  15.8 us
    ppermute x7, waiting for transfers between devices, other_core(): return lax.ppermute(block, 'mp', [(0, 1), (1, 0)])  13.5 us
  transfers between devices with their start and end apart: 7, of which 4 were waited for; matrix products, arithmetic and copies ran while one was open for 3% of the time, Pallas kernels for 0%

profile of v5, /device:TPU:0, one launch (start us, length us, event | category | flops | bytes accessed | tf_op | source)
XLA Modules:
  0.0 589.4 jit_solution(4689873298711911560)
XLA Ops:
  1.7 1.6 reshape.218.refs_10_.kept_ref
  4.5 11.0 %shard_map.544 = f32[16,8,128]{2,1,0:T(8,128)} custom-call(f32[8,128]{1,0:T(8,128)} %pad_bitcast_fusion.part_ref), custom_call_target="tpu_custom_call" | custom-call | tf_op jit(solution)/shard_map/pallas_call | solution.py:633
  16.6 1.5 fusion.9.refs_0_
  18.1 1.4 dynamic-slice_convert_fusion.2.refs_6_
  20.9 1.3 copy.76
  24.6 1.5 dynamic-slice_convert_fusion.1.refs_5_
  31.6 172.6 %shard_map.545 = (bf16[2,4,4,64,384]{4,3,2,1,0:T(8,128)(2,1)}, bf16[4,4,64,2048]{3,2,1,0:T(8,128)(2,1)}, bf16[4,4,64,4096]{3,2,1,0:T(8,128)(2,1)}, bf16[4,4,32,1...) custom-call(bf16[64,384]{1,0:T(8,128)(2,1)} %fusion.9.refs_0_, ...), custom_call_target="tpu_custom_call" | custom-call | bytes 17432576 | tf_op jit(solution)/shard_map/pallas_call | solution.py:870
  204.1 39.8 %shard_map.546 = (f32[512,1024]{1,0:T(8,128)}, bf16[512,1024]{1,0:T(8,128)(2,1)}, f32[2048,512]{1,0:T(8,128)}, bf16[768,2048]{1,0:T(8,128)(2,1)}, bf16[256,2048]...) custom-call(f32[512,1024]{1,0:T(8,128)} %get-tuple-element.87.x1_ref.refs_1_, ...), custom_call_target="tpu_custom_call" | custom-call | flops 2684354560 | bytes 20178944 | tf_op jit(solution)/shard_map/pallas_call | solution.py:414
  244.4 4.0 collective-permute-done.other_ref
  248.4 1.4 copy-done.38
  249.7 15.8 %shard_map.547 = (f32[2048,512]{1,0:T(8,128)}, bf16[2048,512]{1,0:T(8,128)(2,1)}) custom-call(f32[2048,512]{1,0:T(8,128)} %get-tuple-element.92.x_ref, bf16[2048,512]{1,0:T(8,128)(2,1)} %get-tuple-element.93.mine_ref, bf16[2048,512]{1,0:T(8,128)(2,1)} %copy-done.38, f32[8,512]{1,0:T(8,128)} %stack.111.vec_ref, bf16[512,2048]{1,0:T(8,128)(2,1)} %bitcast.133, ...), custom_call_target="tpu_custom_call" | custom-call | flops 4294967296 | bytes 16777216 | tf_op jit(solution)/shard_map/pallas_call | solution.py:438
  267.1 2.8 collective-permute-done.1.other_ref
  269.9 1.4 copy-done.1
  271.3 17.0 %shard_map.548 = (f32[2048,512]{1,0:T(8,128)}, bf16[512,384]{1,0:T(8,128)(2,1)}, f32[1,768]{1,0:T(1,128)}, f32[1,768]{1,0:T(1,128)}, f32[1,512]{1,0:T(1,128)}, /*index=5*/f32[1,512]{1,0:T(1,128)}) custom-call(s32[1]{0:T(128)} %bitcast.core_ref, f32[3]{0:T(128)} %broadcast_divide_fusion.inverse_ref, f32[2048,512]{1,0:T(8,128)} %get-tuple-element.95.x1_ref, ...), custom_call_target="tpu_custom_call" | custom-call | flops 4026531840 | bytes 22020096 | tf_op jit(solution)/shard_map/pallas_call | solution.py:485
  288.3 26.5 %shard_map.549 = (bf16[512,1024]{1,0:T(8,128)(2,1)}, bf16[512,1024]{1,0:T(8,128)(2,1)}, bf16[2048,512]{1,0:T(8,128)(2,1)}) custom-call(f32[2048,512]{1,0:T(8,128)} %get-tuple-element.98.gy_ref, f32[2048,512]{1,0:T(8,128)} %get-tuple-element.95.x1_ref, f32[8,512]{1,0:T(8,128)} %stack.111.vec_ref, bf16[512,2048]{1,0:T(8,128)(2,1)} %bitcast.135, ...), custom_call_target="tpu_custom_call" | custom-call | flops 10737418240 | bytes 14680064 | tf_op jit(solution)/shard_map/pallas_call | solution.py:459
  315.2 4.0 collective-permute-done.2.other_ref
  320.5 42.3 %shard_map.550 = (f32[2048,512]{1,0:T(8,128)}, bf16[512,1024]{1,0:T(8,128)(2,1)}, f32[1,512]{1,0:T(1,128)}, f32[1,512]{1,0:T(1,128)}, bf16[2048,512]{1,0:T(8,128)(2,1)}) custom-call(f32[2048,512]{1,0:T(8,128)} %get-tuple-element.98.gy_ref, f32[2048,512]{1,0:T(8,128)} %get-tuple-element.95.x1_ref, bf16[2048,512]{1,0:T(8,128)(2,1)} %get-tuple-element.99.mine_ref, ...), custom_call_target="tpu_custom_call" | custom-call | flops 4831838208 | bytes 29446144 | tf_op jit(solution)/shard_map/pallas_call | solution.py:414
  364.6 2.7 collective-permute-done.3.other_ref
  367.3 14.3 %shard_map.551 = (f32[1,512]{1,0:T(1,128)}, f32[1,512]{1,0:T(1,128)}, f32[1,512]{1,0:T(1,128)}, bf16[1024,256]{1,0:T(8,128)(2,1)}, f32[1,1024]{1,0:T(1,128)}, /*index=5*/f32[1,1024]{1,0:T(1,128)}, f32[512,1024]{1,0:T(8,128)}) custom-call(s32[1]{0:T(128)} %bitcast.core_ref, f32[2048,512]{1,0:T(8,128)} %get-tuple-element.103.gx_ref, ...), custom_call_target="tpu_custom_call" | custom-call | flops 805306368 | bytes 19472388 | tf_op jit(solution)/shard_map/pallas_call | solution.py:414
  383.7 2.0 concatenate.43.refs_3_
  385.7 181.2 %shard_map.552 = (f32[32,384]{1,0:T(8,128)}, f32[32,1024]{1,0:T(8,128)}, f32[32,1024]{1,0:T(8,128)}, f32[32,1024]{1,0:T(8,128)}, f32[64,256]{1,0:T(8,128)}, /*in...) custom-call(f32[512,1024]{1,0:T(8,128)} %get-tuple-element.107.refs_, ...), custom_call_target="tpu_custom_call" | custom-call | bytes 4063232 | tf_op jit(solution)/shard_map/pallas_call | solution.py:1239
  574.0 2.0 multiply_subtract_fusion.2
  576.0 4.1 multiply_add_fusion
  581.0 1.7 multiply_add_fusion.2
  (154 shorter events, 30.3 us)
Async XLA Ops:
  0.7 20.0 %copy-start.11 = (f32[4,32,256]{2,1,0:T(8,128)S(1)}, f32[4,32,256]{2,1,0:T(8,128)}, u32[]{:S(2)}) copy-start(f32[4,32,256]{2,1,0:T(8,128)} %param.41) | copy-start | bytes 393220
  0.7 20.0 %copy-start.39 = (s32[8]{0:T(128)S(1)}, s32[8]{0:T(128)}, u32[]{:S(2)}) copy-start(s32[8]{0:T(128)} %param.38) | copy-start | bytes 100
  0.7 20.0 %copy-start = (f32[2,64,2048]{2,1,0:T(8,128)S(1)}, f32[2,64,2048]{2,1,0:T(8,128)}, u32[]{:S(2)}) copy-start(f32[2,64,2048]{2,1,0:T(8,128)} %param.40) | copy-start | bytes 3145732
  244.0 4.4 collective-permute-start
  249.7 16.7 %copy-start.36 = (f32[8,128]{1,0:T(8,128)S(1)}, f32[8,128]{1,0:T(8,128)}, u32[]{:S(2)}) copy-start(f32[8,128]{1,0:T(8,128)} %get-tuple-element.86) | copy-start | bytes 12292
  265.5 4.4 collective-permute-start.1
  266.6 21.7 %copy-start.37 = (f32[3]{0:T(128)}, f32[3]{0:T(128)S(1)}, u32[]{:S(2)}) copy-start(f32[3]{0:T(128)S(1)} %slice_reduce_fusion.1) | copy-start | bytes 40
  314.8 4.4 collective-permute-start.2
  320.5 42.7 %copy-start.35 = (f32[1,512]{1,0:T(1,128)S(1)}, f32[1,512]{1,0:T(1,128)}, u32[]{:S(2)}) copy-start(f32[1,512]{1,0:T(1,128)} %get-tuple-element.115) | copy-start | bytes 6148
  320.5 42.7 %copy-start.34 = (f32[1,512]{1,0:T(1,128)S(1)}, f32[1,512]{1,0:T(1,128)}, u32[]{:S(2)}) copy-start(f32[1,512]{1,0:T(1,128)} %get-tuple-element.116) | copy-start | bytes 6148
  320.5 42.7 %copy-start.33 = (f32[1,768]{1,0:T(1,128)S(1)}, f32[1,768]{1,0:T(1,128)}, u32[]{:S(2)}) copy-start(f32[1,768]{1,0:T(1,128)} %get-tuple-element.117) | copy-start | bytes 9220
  362.8 4.5 collective-permute-start.3
  385.7 188.2 %copy-start.13 = (f32[2,32,1024]{2,1,0:T(8,128)S(1)}, f32[2,32,1024]{2,1,0:T(8,128)}, u32[]{:S(2)}) copy-start(f32[2,32,1024]{2,1,0:T(8,128)} %param.50) | copy-start | bytes 786436
  385.7 188.3 %copy-start.14 = (f32[2,32,1024]{2,1,0:T(8,128)S(1)}, f32[2,32,1024]{2,1,0:T(8,128)}, u32[]{:S(2)}) copy-start(f32[2,32,1024]{2,1,0:T(8,128)} %param.58) | copy-start | bytes 786436
  566.9 9.0 %copy-start.4 = (f32[2,64,2048]{2,1,0:T(8,128)S(1)}, f32[2,64,2048]{2,1,0:T(8,128)}, u32[]{:S(2)}) copy-start(f32[2,64,2048]{2,1,0:T(8,128)} %param.64) | copy-start | bytes 3145732
  571.3 4.6 copy-start.5
  571.3 4.6 copy-start.6
  571.3 12.8 %collective-permute-start.6 = (f32[32,384]{1,0:T(8,128)}, f32[32,384]{1,0:T(8,128)S(1)}, u32[]{:S(2)}, u32[]{:S(2)}) collective-permute-start(f32[32,384]{1,0:T(8,128)} %get-tuple-element.140), channel_id=1, source_target_pairs={{0,1},{1,0},{2,3},{3,2},{4,5},{5,4},{6,7},{7,6},{8,9},{9,8},{10,11... | collective-permute-start | bytes 147464 | tf_op jit(solution)/shard_map/ppermute | solution.py:426
  571.4 13.6 %collective-permute-start.5 = (f32[64,256]{1,0:T(8,128)}, f32[64,256]{1,0:T(8,128)S(1)}, u32[]{:S(2)}, u32[]{:S(2)}) collective-permute-start(f32[64,256]{1,0:T(8,128)} %get-tuple-element.139), channel_id=1, source_target_pairs={{0,1},{1,0},{2,3},{3,2},{4,5},{5,4},{6,7},{7,6},{8,9},{9,8},{10,11... | collective-permute-start | bytes 196616 | tf_op jit(solution)/shard_map/ppermute | solution.py:426
  571.9 13.9 %collective-permute-start.4 = (f32[64,384]{1,0:T(8,128)}, f32[64,384]{1,0:T(8,128)S(1)}, u32[]{:S(2)}, u32[]{:S(2)}) collective-permute-start(f32[64,384]{1,0:T(8,128)} %get-tuple-element.138), channel_id=1, source_target_pairs={{0,1},{1,0},{2,3},{3,2},{4,5},{5,4},{6,7},{7,6},{8,9},{9,8},{10,11... | collective-permute-start | bytes 294920 | tf_op jit(solution)/shard_map/ppermute | solution.py:426
  576.0 4.9 copy-start.3
  576.0 4.9 copy-start.8
  576.0 4.9 copy-start.9
  576.0 4.9 copy-start.10
  (23 other events, 65.0 us)

commit v6 on v5

--- a/solution.py
+++ b/solution.py
@@ -901,6 +901,255 @@
     return fulls
 
 
+def decoder_kernel(length, head_dim, inverse_ref, x1e_ref, mine_ref, other_ref, evec_ref, kept_ref, column_ref, rows_ref,
+                   table_ref, vec_ref, bias_ref, target_any, band_any, attn_any, mlp_any, bridge_any, predict_any,
+                   gy_out, gattn_ref, gup_ref, gdown_ref, gpred_ref, gbridge_ref, loss_ref, gbias_ref, sums_ref, esums_ref,
+                   final_ref, glat_ref, x_ref, x1_ref, gy_ref, qkv_ref, mixed_ref, lse_ref, part_ref, from_ref,
+                   lowt_ref, gradt_ref, z_ref, gu_ref, flat_ref, mlp_ref, bridge_ref, predict_ref, target_ref,
+                   band_ref, gp_ref, gpred_acc, gmix_ref, load_sem, stream_sem, send_sem, receive_sem):
+    core, index = lax.axis_index("mp"), lax.axis_index("dp")
+    sibling = (index, 1 - core)
+    greet([sibling])
+    images, side, half = table_ref.shape
+    patches = side * side
+    width = mixed_ref.shape[0]
+    hidden = z_ref.shape[1]
+    share = predict_ref.shape[2]
+    attn_ref = z_ref.at[pl.ds(0, attn_any.shape[0]), pl.ds(0, 4 * width)]
+
+    loads = [pltpu.make_async_copy(source, target, load_sem.at[at]) for at, (source, target) in enumerate(
+        ((attn_any, attn_ref), (bridge_any, bridge_ref), (mlp_any, mlp_ref), (predict_any, predict_ref)))]
+    for copy in loads:
+        copy.start()
+
+    def rows_of(image):
+        return pl.ds(pl.multiple_of(image * patches, patches), patches)
+
+    def exchange(phase, image):
+        rows = rows_of(image)
+        return remote(part_ref.at[phase % 2, rows, :], from_ref.at[phase % 2, rows, :], send_sem.at[phase, image],
+                      receive_sem.at[phase, image], sibling)
+
+    def summed(phase, rows):
+        return part_ref[phase % 2, rows, :].astype(F32) + from_ref[phase % 2, rows, :].astype(F32)
+
+    def give(phase, image, value):
+        part_ref[phase % 2, rows_of(image), :] = value.astype(BF16)
+        exchange(phase, image).start()
+
+    def stream(image):
+        rows, slot = rows_of(image), lax.rem(image, 2)
+        return [pltpu.make_async_copy(target_any.at[rows, :], target_ref.at[slot], stream_sem.at[0, slot]),
+                pltpu.make_async_copy(band_any.at[rows, :], band_ref.at[slot], stream_sem.at[1, slot])]
+
+    sums_ref[...] = jnp.zeros_like(sums_ref)
+    loss_ref[...] = jnp.zeros_like(loss_ref)
+    gbias_ref[...] = jnp.zeros_like(gbias_ref)
+    gpred_acc[...] = jnp.zeros_like(gpred_acc)
+    for copy in stream(0):
+        copy.start()
+    loads[0].wait()
+    for part in range(4):
+        at = pl.ds(part * width, width)
+        flat_ref[at, :] = attn_ref[:, at].T
+    loads[1].wait()
+    ends = bridge_ref.shape[2]
+    latent_ref = gy_ref
+
+    def ends_rows(step):
+        return pl.ds(pl.multiple_of(step * 128, 128), 128)
+
+    def enc_end(step, carry):
+        rows = ends_rows(step)
+        out = x1e_ref[rows, :] + both(mine_ref, other_ref, rows)
+        gy_out[rows, :] = out
+        unit, _ = normalize(out)
+        final = (unit * evec_ref[5:6, :] + evec_ref[6:7, :]).astype(BF16)
+        final_ref[rows, :] = final
+        latent_ref[rows, :ends] = dot_nn(final, bridge_ref[0])
+        latent_ref[rows, ends:] = dot_nn(final, bridge_ref[1])
+        return carry
+
+    lax.fori_loop(0, x1e_ref.shape[0] // 128, enc_end, 0)
+
+    def phase_a(image, carry):
+        rows = rows_of(image)
+        hot = lax.broadcasted_iota(jnp.int32, (patches, length), 0) == kept_ref[pl.ds(image, 1), :]
+        latent = latent_ref[pl.ds(pl.multiple_of(image * length, length), length), :]
+        table = table_ref[image]
+        by_row = jnp.broadcast_to(table[:, None, :], (side, side, half)).reshape(patches, half)
+        by_col = jnp.broadcast_to(table[None, :, :], (side, side, half)).reshape(patches, half)
+        place = jnp.concatenate([by_row, by_col], axis=1)
+        rows_x = dot_exact(hot.astype(F32), latent) + rows_ref[rows, 0:1] * vec_ref[0:1, :] + place
+        x_ref[rows, :] = rows_x
+        unit, _ = normalize(rows_x)
+        low = (unit * vec_ref[1:2, :] + vec_ref[2:3, :]).astype(BF16)
+        qkv_ref[:, rows] = dot_nt(flat_ref[: 3 * width, :], low).astype(BF16)
+        attend(qkv_ref, mixed_ref, lse_ref, rows, width, head_dim, None)
+        give(0, image, dot_nn(mixed_ref[:, rows].T, flat_ref[3 * width :, :]))
+        return carry
+
+    lax.fori_loop(0, images, phase_a, 0)
+    loads[2].wait()
+    loads[3].wait()
+
+    def phase_b(image, carry):
+        rows = rows_of(image)
+        exchange(0, image).wait()
+        after = x_ref[rows, :] + summed(0, rows)
+        x1_ref[rows, :] = after
+        unit, _ = normalize(after)
+        low = (unit * vec_ref[3:4, :] + vec_ref[4:5, :]).astype(BF16)
+        lowt_ref[:, rows] = low.T
+        up = dot_nn(low, mlp_ref[:, :hidden])
+        square, bent, rise = gelu_parts(up)
+        mid = (up * rise).astype(BF16)
+        z_ref[rows, :] = mid
+        slope = rise + (0.5 * GELU_C) * up * (1.0 - bent * bent) * (1.0 + (3.0 * 0.044715) * square)
+        gu_ref[rows, :] = slope.astype(BF16)
+        give(1, image, dot_nt(mid, mlp_ref[:, hidden:]))
+        return carry
+
+    lax.fori_loop(0, images, phase_b, 0)
+
+    def phase_c(image, carry):
+        rows, slot = rows_of(image), lax.rem(image, 2)
+
+        @pl.when(image + 1 < images)
+        def _():
+            for copy in stream(image + 1):
+                copy.start()
+
+        exchange(1, image).wait()
+        unit, rstd = normalize(x1_ref[rows, :] + summed(1, rows))
+        gain = vec_ref[5:6, :]
+        final = (unit * gain + vec_ref[6:7, :]).astype(BF16)
+        for copy in stream(image):
+            copy.wait()
+        predicted = jnp.concatenate([dot_nn(final, predict_ref[0]), dot_nn(final, predict_ref[1])], axis=1)
+        mismatch = predicted + bias_ref[...] - target_ref[slot].astype(F32)
+        band = band_ref[slot]
+        level = jnp.where(band == 0, inverse_ref[0], jnp.where(band == 1, inverse_ref[1], inverse_ref[2]))
+        level = level * rows_ref[rows, 1:2]
+        square = mismatch * mismatch + EPS_C
+        root = lax.rsqrt(square)
+        loss_ref[...] += jnp.sum(level * (square * root), axis=0, keepdims=True)
+        grad = level * (mismatch * root)
+        gbias_ref[...] += jnp.sum(grad, axis=0, keepdims=True)
+        gp_ref[...] = grad.astype(BF16)
+        columns = pl.ds(pl.multiple_of(core * share, share), share)
+        gpred_acc[...] += dot_tn(final, gp_ref[:, columns])
+        grad_final = dot_nt(gp_ref[:, :share], predict_ref[0]) + dot_nt(gp_ref[:, share:], predict_ref[1])
+        grad_in, gain_sum, shift_sum = norm_back(grad_final, gain, unit, rstd)
+        gy_ref[rows, :] = grad_in
+        sums_ref[5:6, :] += gain_sum
+        sums_ref[6:7, :] += shift_sum
+        low = grad_in.astype(BF16)
+        gradt_ref[:, rows] = low.T
+        grad_up = (dot_nn(low, mlp_ref[:, hidden:]) * gu_ref[rows, :].astype(F32)).astype(BF16)
+        gu_ref[rows, :] = grad_up
+        give(2, image, dot_nt(grad_up, mlp_ref[:, :hidden]))
+        return carry
+
+    lax.fori_loop(0, images, phase_c, 0)
+    gpred_ref[...] = gpred_acc[...].astype(BF16)
+    tile = 256
+    for start in range(0, hidden, tile):
+        at = pl.ds(start, tile)
+        gup_ref[:, at] = dot_nn(lowt_ref[...], gu_ref[:, at]).astype(BF16)
+        gdown_ref[:, at] = dot_nn(gradt_ref[...], z_ref[:, at]).astype(BF16)
+
+    def phase_d(image, carry):
+        rows = rows_of(image)
+        exchange(2, image).wait()
+        unit, rstd = normalize(x1_ref[rows, :])
+        grad_in, gain_sum, shift_sum = norm_back(summed(2, rows), vec_ref[3:4, :], unit, rstd)
+        grad_in = grad_in + gy_ref[rows, :]
+        gy_ref[rows, :] = grad_in
+        sums_ref[3:4, :] += gain_sum
+        sums_ref[4:5, :] += shift_sum
+        low = grad_in.astype(BF16)
+        gradt_ref[:, rows] = low.T
+        gmix_ref[...] = dot_nt(flat_ref[3 * width :, :], low).astype(BF16)
+        attend_back(qkv_ref, gmix_ref, lse_ref, qkv_ref, rows, width, head_dim, None)
+        unit_a, _ = normalize(x_ref[rows, :])
+        lowt_ref[:, rows] = (unit_a * vec_ref[1:2, :] + vec_ref[2:3, :]).astype(BF16).T
+        give(3, image, dot_nn(qkv_ref[:, rows].T, flat_ref[: 3 * width, :]))
+        return carry
+
+    lax.fori_loop(0, images, phase_d, 0)
+    for part in range(3):
+        at = pl.ds(part * width, width)
+        gattn_ref[:, at] = dot_nt(lowt_ref[...], qkv_ref[at, :]).astype(BF16)
+    gattn_ref[:, 3 * width :] = dot_nt(gradt_ref[...], mixed_ref[...]).astype(BF16)
+
+    def phase_e(image, carry):
+        rows = rows_of(image)
+        exchange(3, image).wait()
+        unit, rstd = normalize(x_ref[rows, :])
+        grad_in, gain_sum, shift_sum = norm_back(summed(3, rows), vec_ref[1:2, :], unit, rstd)
+        grad_in = grad_in + gy_ref[rows, :]
+        sums_ref[1:2, :] += gain_sum
+        sums_ref[2:3, :] += shift_sum
+        sums_ref[0:1, :] += jnp.sum(grad_in * rows_ref[rows, 0:1], axis=0, keepdims=True)
+        kept_rows = pl.ds(pl.multiple_of(image * length, length), length)
+        hot = lax.broadcasted_iota(jnp.int32, (length, patches), 1) == column_ref[kept_rows, :]
+        glat_ref[kept_rows, :] = dot_nn(hot.astype(BF16), grad_in.astype(BF16)).astype(BF16)
+        return carry
+
+    lax.fori_loop(0, images, phase_e, 0)
+    columns = pl.ds(pl.multiple_of(core * ends, ends), ends)
+    gbridge_ref[...] = dot_tn(final_ref[...], glat_ref[:, columns]).astype(BF16)
+    esums_ref[...] = jnp.zeros_like(esums_ref)
+
+    def enc_start(step, carry):
+        rows = ends_rows(step)
+        grad_final = dot_nt(glat_ref[rows, :ends], bridge_ref[0]) + dot_nt(glat_ref[rows, ends:], bridge_ref[1])
+        unit, rstd = normalize(gy_out[rows, :])
+        grad_in, gain_sum, shift_sum = norm_back(grad_final, evec_ref[5:6, :], unit, rstd)
+        gy_out[rows, :] = grad_in
+        esums_ref[0:1, :] += gain_sum
+        esums_ref[1:2, :] += shift_sum
+        return carry
+
+    lax.fori_loop(0, x1e_ref.shape[0] // 128, enc_start, 0)
+
+
+def decoder_all(inverse, x1e, mine, other, evec, kept_index, kept_column, row_values, table, dvec, bias, target, band,
+                attn, mlp, bridge, predict):
+    rows_e, wide = x1e.shape
+    images, length = kept_index.shape
+    rows, pixel_count = target.shape
+    patches = rows // images
+    low_wide = dvec.shape[1]
+    width, hidden, share, ends = attn.shape[1] // 4, mlp.shape[1] // 2, predict.shape[2], bridge.shape[2]
+    in_vmem = pl.BlockSpec(memory_space=pltpu.VMEM)
+    any_space = pl.BlockSpec(memory_space=pl.ANY)
+    dma = pltpu.SemaphoreType.DMA
+    vm = pltpu.VMEM
+    return pl.pallas_call(
+        functools.partial(decoder_kernel, length, DDH),
+        out_shape=(
+            shape((rows_e, wide), F32), shape((low_wide, 4 * width), BF16), shape((low_wide, hidden), BF16),
+            shape((low_wide, hidden), BF16), shape((low_wide, share), BF16), shape((wide, ends), BF16),
+            shape((1, pixel_count), F32), shape((1, pixel_count), F32), shape((8, low_wide), F32), shape((8, wide), F32)),
+        in_specs=[pl.BlockSpec(memory_space=pltpu.SMEM)] + [in_vmem] * 10 + [any_space] * 6,
+        out_specs=tuple([in_vmem] * 10),
+        scratch_shapes=[
+            vm((rows_e, wide), BF16), vm((rows_e, low_wide), BF16), vm((rows, low_wide), F32),
+            vm((rows, low_wide), F32), vm((rows, low_wide), F32), vm((3 * width, rows), BF16), vm((width, rows), BF16),
+            vm((width // DDH, rows), F32), vm((2, rows, low_wide), BF16), vm((2, rows, low_wide), BF16),
+            vm((low_wide, rows), BF16), vm((low_wide, rows), BF16), vm((rows, hidden), BF16), vm((rows, hidden), BF16),
+            vm((4 * width, low_wide), BF16), vm(mlp.shape, BF16), vm(bridge.shape, BF16),
+            vm(predict.shape, BF16), vm((2, patches, pixel_count), BF16), vm((2, patches, pixel_count), jnp.int32),
+            vm((patches, pixel_count), BF16), vm((low_wide, share), F32), vm((width, patches), BF16),
+            dma((4,)), dma((2, 2)), dma((4, images)), dma((4, images))],
+        compiler_params=pltpu.CompilerParams(collective_id=3, has_side_effects=True, vmem_limit_bytes=62 * 2**20),
+        cost_estimate=pl.CostEstimate(flops=0, bytes_accessed=2**25, transcendentals=0),
+    )(inverse, x1e, mine, other, evec, kept_index, kept_column, row_values, table, dvec, bias, target, band, attn, mlp,
+      bridge, predict)
+
+
 class Reducer:
     def __init__(self, highs, groups, weights, grads, outs, near, second, far, load_two, load_own, plane, norm, sems):
         self.highs, self.groups, self.weights = highs, groups, weights
@@ -1395,28 +1644,38 @@
     inverse = 1.0 / band_weight
     core = lax.axis_index("mp").astype(jnp.int32).reshape(1)
     hidden_rows = (1.0 - kept_flags).reshape(-1, 1)
-    local_d = dec_attn_w.shape[1] // 4
-    x2, final_enc, xd, *dec_saved, part = run(
-        functools.partial(dec_in_kernel, keep_count, DDH),
-        [shape((rows, D), F32), shape((rows, D), BF16), shape((rows_d, E), F32), shape((3 * local_d, rows_d), BF16),
-         shape((local_d, rows_d), BF16), shape((local_d // DDH, rows_d), F32), shape((rows_d, E), BF16)],
-        [pltpu.VMEM((4 * local_d, E), BF16), pltpu.VMEM((rows, E), F32)],
-        (x1, part, other, evec, bridge_w, kept_index, hidden_rows, sine_table(gsd_scale, E, GRID), dvec,
-         dec_attn_w),
-        rows_d * E * 8 * local_d + 2 * rows * D * E)
-    xd1, part = mlp_forward(xd, part, dvec, dec_mlp_w)
-    gyd, grad_predict, grad_pbias, loss_parts, grad_dec_fg, grad_dec_fb = head(
-        core, inverse, xd1, part, dvec, pieces[14].reshape(1, -1), predict_w, target, band_ids, patch_weight, patch_count)
-    grad_dec_up, grad_dec_down, part = mlp_backward(gyd, xd1, dvec, dec_mlp_w)
-    gxd, grad_dec_attn, grad_dec_gb, grad_dec_bb, part = attn_backward(
-        gyd, xd1, part, xd, dec_saved, dvec, dec_attn_w, patch_count, patch_count, DDH)
     one_d, one_e = shape((1, D), F32), shape((1, E), F32)
-    grad_dec_ga, grad_dec_ba, grad_mask, grad_bridge, grad_enc_fg, grad_enc_fb, gye = run(
-        functools.partial(between_kernel, keep_count),
-        [one_e, one_e, one_e, shape((D, E // 2), BF16), one_d, one_d, shape((rows, D), F32)],
-        [pltpu.VMEM((rows, E), BF16)],
-        (core, gxd, xd, part, other_core(part), dvec, kept_column, hidden_rows, final_enc, x2, evec, bridge_w),
-        3 * rows * D * E, 1)
+    dec_table = sine_table(gsd_scale, E, GRID)
+    if whole_tiles:
+        (gye, grad_dec_attn, grad_dec_up, grad_dec_down, grad_predict, grad_bridge, loss_parts, grad_pbias, dec_sums,
+         enc_sums) = decoder_all(
+            inverse, x1, part, other, evec, kept_index, kept_column, jnp.concatenate([hidden_rows, patch_weight], axis=1),
+            dec_table, dvec, pieces[14].reshape(1, -1), target, band_ids, dec_attn_w, dec_mlp_w, bridge_w, predict_w)
+        grad_mask, grad_dec_ga, grad_dec_ba, grad_dec_gb, grad_dec_bb, grad_dec_fg, grad_dec_fb = [
+            dec_sums[i : i + 1] for i in range(7)]
+        grad_enc_fg, grad_enc_fb = enc_sums[0:1], enc_sums[1:2]
+    else:
+        local_d = dec_attn_w.shape[1] // 4
+        x2, final_enc, xd, *dec_saved, part = run(
+            functools.partial(dec_in_kernel, keep_count, DDH),
+            [shape((rows, D), F32), shape((rows, D), BF16), shape((rows_d, E), F32), shape((3 * local_d, rows_d), BF16),
+             shape((local_d, rows_d), BF16), shape((local_d // DDH, rows_d), F32), shape((rows_d, E), BF16)],
+            [pltpu.VMEM((4 * local_d, E), BF16), pltpu.VMEM((rows, E), F32)],
+            (x1, part, other, evec, bridge_w, kept_index, hidden_rows, dec_table, dvec,
+             dec_attn_w),
+            rows_d * E * 8 * local_d + 2 * rows * D * E)
+        xd1, part = mlp_forward(xd, part, dvec, dec_mlp_w)
+        gyd, grad_predict, grad_pbias, loss_parts, grad_dec_fg, grad_dec_fb = head(
+            core, inverse, xd1, part, dvec, pieces[14].reshape(1, -1), predict_w, target, band_ids, patch_weight, patch_count)
+        grad_dec_up, grad_dec_down, part = mlp_backward(gyd, xd1, dvec, dec_mlp_w)
+        gxd, grad_dec_attn, grad_dec_gb, grad_dec_bb, part = attn_backward(
+            gyd, xd1, part, xd, dec_saved, dvec, dec_attn_w, patch_count, patch_count, DDH)
+        grad_dec_ga, grad_dec_ba, grad_mask, grad_bridge, grad_enc_fg, grad_enc_fb, gye = run(
+            functools.partial(between_kernel, keep_count),
+            [one_e, one_e, one_e, shape((D, E // 2), BF16), one_d, one_d, shape((rows, D), F32)],
+            [pltpu.VMEM((rows, E), BF16)],
+            (core, gxd, xd, part, other_core(part), dvec, kept_column, hidden_rows, final_enc, x2, evec, bridge_w),
+            3 * rows * D * E, 1)
     wide_row = lambda row: jnp.pad(row, ((0, 0), (0, D - row.shape[1])))
     no_row = jnp.zeros((1, D), F32)
     late_rows = [grad_enc_fg, grad_enc_fb] + [wide_row(row) for row in (

time: 593 us -> 543 us (0.916)
  Pallas kernels: 520 us -> 483 us
  waiting for transfers between devices: 13.5 us -> 0.01 us
  other arithmetic: 20.4 us -> 26.6 us
    pallas_call x6 -> x1, Pallas kernels: 156 us -> 118 us  [decoder_all(): pl.pallas_call(functools.partial(decoder_kernel, length, DDH), out_shape=...]
    ppermute x7 -> x3, waiting for transfers between devices: 13.5 us -> 0.01 us  [other_core(): return lax.ppermute(block, 'mp', [(0, 1), (1, 0)])]
    unnamed x85 -> x67, local copies, waits for them, and re-layouts: 7.84 us -> 1.04 us
  transfers between devices with their start and end apart: 7 -> 3, of which waited for: 4 -> 0; matrix products, arithmetic and copies ran while one was open for 3% -> 4% of each run, Pallas kernels for 0% -> 0%
where the time goes in v6:
time: 543 us; the launch traced here: 540 us
  Pallas kernels  483 us (89%)
  other arithmetic  26.6 us (5%)
  local copies, waits for them, and re-layouts  24.1 us (4%)
    pallas_call x1, Pallas kernels, backward_all(): pl.pallas_call(functools.partial(backward_kernel, highs, (1.0,) * count,...  181 us
    pallas_call x1, Pallas kernels, forward_all(): pl.pallas_call(functools.partial(forward_kernel, highs, shared, groups, c...  173 us
    pallas_call x1, Pallas kernels, decoder_all(): pl.pallas_call(functools.partial(decoder_kernel, length, DDH), out_shape=...  118 us
    pallas_call x1, Pallas kernels, small_gather(): pl.pallas_call(functools.partial(small_gather_kernel, size), out_shape=sh...  11 us
  transfers between devices with their start and end apart: 3, of which 0 were waited for; matrix products, arithmetic and copies ran while one was open for 4% of the time, Pallas kernels for 0%

profile of v6, /device:TPU:0, one launch (start us, length us, event | category | flops | bytes accessed | tf_op | source)
XLA Modules:
  0.0 539.7 jit_solution(9286664376475396543)
XLA Ops:
  2.1 11.0 %shard_map.544 = f32[16,8,128]{2,1,0:T(8,128)} custom-call(f32[8,128]{1,0:T(8,128)} %pad_bitcast_fusion.part_ref), custom_call_target="tpu_custom_call" | custom-call | tf_op jit(solution)/shard_map/pallas_call | solution.py:633
  13.2 0.9 copy.80
  15.0 1.6 reshape.217.refs_10_.column_ref
  18.0 1.3 copy.72.refs_9_
  19.4 1.4 dynamic-slice_convert_fusion.2.refs_6_
  20.8 1.5 fusion.9.refs_0_
  22.9 0.9 convert.22
  23.8 1.0 convert.23
  25.9 1.3 copy.75.rows_ref
  27.3 1.5 dynamic-slice_convert_fusion.1.refs_5_
  33.0 172.7 %shard_map.545 = (bf16[2,4,4,64,384]{4,3,2,1,0:T(8,128)(2,1)}, bf16[4,4,64,2048]{3,2,1,0:T(8,128)(2,1)}, bf16[4,4,64,4096]{3,2,1,0:T(8,128)(2,1)}, bf16[4,4,32,1...) custom-call(bf16[64,384]{1,0:T(8,128)(2,1)} %fusion.9.refs_0_, ...), custom_call_target="tpu_custom_call" | custom-call | bytes 17432576 | tf_op jit(solution)/shard_map/pallas_call | solution.py:870
  208.4 118.1 %shard_map.546 = (f32[512,1024]{1,0:T(8,128)}, bf16[512,1024]{1,0:T(8,128)(2,1)}, bf16[512,1024]{1,0:T(8,128)(2,1)}, bf16[512,1024]{1,0:T(8,128)(2,1)}, bf16[512...) custom-call(f32[3]{0:T(128)} %broadcast_divide_fusion.inverse_ref, ...), custom_call_target="tpu_custom_call" | custom-call | bytes 33554432 | tf_op jit(solution)/shard_map/pallas_call | solution.py:1130
  327.9 1.0 fusion.25
  329.0 1.3 concatenate.47.refs_3_
  330.3 181.3 %shard_map.547 = (f32[32,384]{1,0:T(8,128)}, f32[32,1024]{1,0:T(8,128)}, f32[32,1024]{1,0:T(8,128)}, f32[32,1024]{1,0:T(8,128)}, f32[64,256]{1,0:T(8,128)}, /*in...) custom-call(f32[512,1024]{1,0:T(8,128)} %get-tuple-element.74.refs_0, ...), custom_call_target="tpu_custom_call" | custom-call | bytes 4063232 | tf_op jit(solution)/shard_map/pallas_call | solution.py:1488
  512.3 1.3 slice_reduce_fusion
  515.1 1.3 fusion.26
  518.4 1.4 slice_bitcast_fusion.15
  519.8 1.1 slice_bitcast_fusion.5
  520.9 2.2 multiply_subtract_fusion.2
  523.2 4.7 multiply_add_fusion
  528.9 1.7 multiply_add_fusion.2
  535.3 0.9 broadcast_select_fusion.1
  536.3 1.0 multiply_add_fusion.5
  (128 shorter events, 22.1 us)
Async XLA Ops:
  0.7 25.1 %copy-start.1 = (f32[4,64,512]{2,1,0:T(8,128)S(1)}, f32[4,64,512]{2,1,0:T(8,128)}, u32[]{:S(2)}) copy-start(f32[4,64,512]{2,1,0:T(8,128)} %param.39) | copy-start | bytes 1572868
  0.7 25.1 %copy-start = (f32[2,64,2048]{2,1,0:T(8,128)S(1)}, f32[2,64,2048]{2,1,0:T(8,128)}, u32[]{:S(2)}) copy-start(f32[2,64,2048]{2,1,0:T(8,128)} %param.40) | copy-start | bytes 3145732
  330.3 190.6 %copy-start.3 = (f32[2,32,1024]{2,1,0:T(8,128)S(1)}, f32[2,32,1024]{2,1,0:T(8,128)}, u32[]{:S(2)}) copy-start(f32[2,32,1024]{2,1,0:T(8,128)} %param.42) | copy-start | bytes 786436
  511.6 11.5 %copy-start.2 = (f32[2,64,2048]{2,1,0:T(8,128)S(1)}, f32[2,64,2048]{2,1,0:T(8,128)}, u32[]{:S(2)}) copy-start(f32[2,64,2048]{2,1,0:T(8,128)} %param.64) | copy-start | bytes 3145732
  511.6 20.4 %collective-permute-start.2 = (f32[32,384]{1,0:T(8,128)}, f32[32,384]{1,0:T(8,128)}, u32[]{:S(2)}, u32[]{:S(2)}) collective-permute-start(f32[32,384]{1,0:T(8,128)} %get-tuple-element.100), channel_id=1, source_target_pairs={{0,1},{1,0},{2,3},{3,2},{4,5},{5,4},{6,7},{7,6},{8,9},{9,8},{10,11... | collective-permute-start | bytes 147464 | tf_op jit(solution)/shard_map/ppermute | solution.py:426
  511.7 21.9 %collective-permute-start.1 = (f32[64,256]{1,0:T(8,128)}, f32[64,256]{1,0:T(8,128)}, u32[]{:S(2)}, u32[]{:S(2)}) collective-permute-start(f32[64,256]{1,0:T(8,128)} %get-tuple-element.99), channel_id=1, source_target_pairs={{0,1},{1,0},{2,3},{3,2},{4,5},{5,4},{6,7},{7,6},{8,9},{9,8},{10,11... | collective-permute-start | bytes 196616 | tf_op jit(solution)/shard_map/ppermute | solution.py:426
  512.2 23.1 %collective-permute-start = (f32[64,384]{1,0:T(8,128)}, f32[64,384]{1,0:T(8,128)}, u32[]{:S(2)}, u32[]{:S(2)}) collective-permute-start(f32[64,384]{1,0:T(8,128)} %get-tuple-element.98), channel_id=1, source_target_pairs={{0,1},{1,0},{2,3},{3,2},{4,5},{5,4},{6,7},{7,6},{8,9},{9,8},{10,11... | collective-permute-start | bytes 294920 | tf_op jit(solution)/shard_map/ppermute | solution.py:426
  523.1 4.9 copy-start.15
  523.1 4.9 copy-start.18
  523.2 5.7 %copy-start.4 = (f32[4,64,512]{2,1,0:T(8,128)S(1)}, f32[4,64,512]{2,1,0:T(8,128)}, u32[]{:S(2)}) copy-start(f32[4,64,512]{2,1,0:T(8,128)} %param.63) | copy-start | bytes 1572868
  523.2 5.7 %copy-start.5 = (f32[4,64,512]{2,1,0:T(8,128)S(1)}, f32[4,64,512]{2,1,0:T(8,128)}, u32[]{:S(2)}) copy-start(f32[4,64,512]{2,1,0:T(8,128)} %param.47) | copy-start | bytes 1572868
  523.2 5.7 %copy-start.6 = (f32[4,64,512]{2,1,0:T(8,128)S(1)}, f32[4,64,512]{2,1,0:T(8,128)}, u32[]{:S(2)}) copy-start(f32[4,64,512]{2,1,0:T(8,128)} %param.55) | copy-start | bytes 1572868
  527.9 4.9 copy-start.13
  528.0 4.9 copy-start.21
  528.0 4.9 copy-start.22
  528.0 5.6 %copy-start.25 = (f32[64,256]{1,0:T(8,128)S(1)}, f32[64,256]{1,0:T(8,128)}, u32[]{:S(2)}) copy-start(f32[64,256]{1,0:T(8,128)} %get-tuple-element.99) | copy-start | bytes 196612
  528.8 5.6 %copy-start.9 = (f32[64,512]{1,0:T(8,128)S(1)}, f32[64,512]{1,0:T(8,128)}, u32[]{:S(2)}) copy-start(f32[64,512]{1,0:T(8,128)} %param.44) | copy-start | bytes 393220
  528.8 5.6 %copy-start.16 = (f32[64,512]{1,0:T(8,128)S(1)}, f32[64,512]{1,0:T(8,128)}, u32[]{:S(2)}) copy-start(f32[64,512]{1,0:T(8,128)} %param.52) | copy-start | bytes 393220
  528.9 5.6 %copy-start.17 = (f32[64,512]{1,0:T(8,128)S(1)}, f32[64,512]{1,0:T(8,128)}, u32[]{:S(2)}) copy-start(f32[64,512]{1,0:T(8,128)} %param.60) | copy-start | bytes 393220
  528.9 6.4 %copy-start.23 = (f32[64,384]{1,0:T(8,128)S(1)}, f32[64,384]{1,0:T(8,128)}, u32[]{:S(2)}) copy-start(f32[64,384]{1,0:T(8,128)} %get-tuple-element.98) | copy-start | bytes 294916
  528.9 7.3 %copy-start.8 = (f32[768,64]{0,1:T(8,128)S(1)}, f32[768,64]{0,1:T(8,128)}, u32[]{:S(2)}) copy-start(f32[768,64]{0,1:T(8,128)} %param.43) | copy-start | bytes 589828
  528.9 7.3 %copy-start.10 = (f32[768,64]{0,1:T(8,128)S(1)}, f32[768,64]{0,1:T(8,128)}, u32[]{:S(2)}) copy-start(f32[768,64]{0,1:T(8,128)} %param.65) | copy-start | bytes 589828
  528.9 7.3 %copy-start.11 = (f32[768,64]{0,1:T(8,128)S(1)}, f32[768,64]{0,1:T(8,128)}, u32[]{:S(2)}) copy-start(f32[768,64]{0,1:T(8,128)} %param.51) | copy-start | bytes 589828
  528.9 7.3 %copy-start.12 = (f32[768,64]{0,1:T(8,128)S(1)}, f32[768,64]{0,1:T(8,128)}, u32[]{:S(2)}) copy-start(f32[768,64]{0,1:T(8,128)} %param.59) | copy-start | bytes 589828
  (11 other events, 36.1 us)

commit v7 on v6

--- a/solution.py
+++ b/solution.py
@@ -613,33 +613,6 @@
         device_id=device, device_id_type=pl.DeviceIdType.MESH)
 
 
-def small_gather_kernel(size, part_ref, full_ref, send_sem, receive_sem):
-    index, core = lax.axis_index("dp"), lax.axis_index("mp")
-    peers = [(lax.rem(index + k, size), core) for k in range(1, size)]
-    greet(peers)
-    full_ref[index] = part_ref[...]
-    copies = [remote(part_ref, full_ref.at[index], send_sem.at[k], receive_sem.at[k], peers[k])
-              for k in range(size - 1)]
-    for copy in copies:
-        copy.start()
-    for copy in copies:
-        copy.wait()
-
-
-def small_gather(part):
-    size = lax.axis_size("dp")
-    in_vmem = pl.BlockSpec(memory_space=pltpu.VMEM)
-    dma = pltpu.SemaphoreType.DMA
-    return pl.pallas_call(
-        functools.partial(small_gather_kernel, size),
-        out_shape=shape((size,) + part.shape, part.dtype),
-        in_specs=[in_vmem],
-        out_specs=in_vmem,
-        scratch_shapes=[dma((size - 1,)), dma((size - 1,))],
-        compiler_params=pltpu.CompilerParams(collective_id=2, has_side_effects=True),
-    )(part)
-
-
 def total_blocks(block_ref, near_ref, far_ref, sems, low, high, core, highs, stage):
     send, receive = sems
     if stage == 0:
@@ -650,21 +623,31 @@
 
 
 def forward_kernel(highs, shared, groups, count, length, group, head_dim, *refs):
+    masters, refs = refs[:count], refs[count:]
+    pix_any, band_ref, kept_ref, inter_ref, table_ref, placed_ref = refs[:6]
+    fulls, refs = refs[6 : 6 + count], refs[6 + count :]
+    (x_ref, qkv_ref, mixed_ref, lse_ref, pixk_ref, x1_ref, last_ref, far_out_ref, counts_ref, flat_ref, vec_ref, rows_ref,
+     column_ref) = refs[:13]
+    refs = refs[13:]
     shards, refs = refs[:count], refs[count:]
-    pix_ref, band_ref, weight_ref, kept_ref, table_ref, vec_ref = refs[:6]
-    fulls, refs = refs[6 : 6 + count], refs[6 + count :]
-    x_ref, qkv_ref, mixed_ref, lse_ref, pixk_ref, x1_ref, last_ref, far_out_ref, counts_ref, flat_ref = refs[:10]
-    refs = refs[10:]
-    (bands_v, embed_v, attn_v, mlp_v, part_ref, other_ref, low_ref, acc_ref, block_ref, near_ref,
-     far_ref) = refs[:11]
+    (pix_ref, bands_v, embed_v, attn_v, mlp_v, part_ref, other_ref, low_ref, acc_ref, block_ref, near_ref,
+     far_ref) = refs[:12]
     (own_sem, zs_sem, zr_sem, cs_sem, cr_sem, fs_sem, fr_sem, ms_sem, mr_sem, load_sem, xs_sem, xr_sem, ts_sem,
-     tr_sem) = refs[11:]
+     tr_sem) = refs[12:]
     core, low, high, low_x, low_y = place_of()
     at_x, at_y = (high * 4 + low_x, core), (high * 4 + low_y, core)
     at_high = [(lax.rem(high + k, highs) * 4 + low, core) for k in range(1, highs)]
     sibling = (high * 4 + low, 1 - core)
     near = [(high * 4 + lax.rem(low + k, 4), core) for k in range(1, 4)]
     greet([sibling] + near + at_high)
+    for master, shard, split in zip(masters, shards, shared):
+        if len(master.shape) == 3:
+            wide = master.shape[2]
+            for part in range(master.shape[0]):
+                shard[:, part * wide : (part + 1) * wide] = master[part].astype(BF16)
+        else:
+            share = shard.shape[1]
+            shard[...] = master[:, pl.ds(pl.multiple_of(core * share, share), share)].astype(BF16)
 
     def full(at):
         number, start, size = groups[at]
@@ -704,15 +687,20 @@
     in_pair = lambda pair: [at for at in (2 * pair, 2 * pair + 1) if at < total]
     pair_of = lambda number: max(at for at in range(total) if groups[at][0] == number) // 2
     images, side = table_ref.shape[0], table_ref.shape[1]
-    patches = pix_ref.shape[0] // images
+    patches = side * side
     width = mixed_ref.shape[0]
     mask = group_mask(group, length)
 
+    def lane_of(image, flipped):
+        lanes = lax.broadcasted_iota(jnp.int32, flipped.shape, 1)
+        return jnp.sum(jnp.where(lanes == image, flipped, 0.0), axis=1, keepdims=True)
+
     def pick(image, carry):
-        rows = pl.ds(image * length, length)
-        index = kept_ref[rows, :]
+        rows = pl.ds(pl.multiple_of(image * length, length), length)
+        index = lane_of(image, kept_ref[...].astype(F32).T).astype(jnp.int32)
+        column_ref[rows, :] = index
         hot = lax.broadcasted_iota(jnp.int32, (length, patches), 1) == index
-        pixels = pix_ref[pl.ds(image * patches, patches), :]
+        pixels = pix_ref[pl.ds(pl.multiple_of(image * patches, patches), patches), :]
         pixk_ref[rows, :] = dot_nn(hot.astype(BF16), pixels).astype(BF16)
         grid_at = lax.broadcasted_iota(jnp.int32, (length, side), 1)
         table = table_ref[image]
@@ -722,12 +710,17 @@
         return carry
 
     def tally(image, carry):
-        rows = pl.ds(image * patches, patches)
-        band, weight = bands_v[rows, :], weight_ref[rows, :]
+        rows = pl.ds(pl.multiple_of(image * patches, patches), patches)
+        hot = lax.broadcasted_iota(jnp.int32, (patches, length), 0) == kept_ref[pl.ds(image, 1), :]
+        hidden = 1.0 - jnp.max(jnp.where(hot, 1.0, 0.0), axis=1, keepdims=True)
+        weight = hidden * (1.0 - 0.5 * lane_of(image, inter_ref[...].astype(F32).T))
+        rows_ref[rows, 0:1] = hidden
+        rows_ref[rows, 1:2] = weight
+        band = bands_v[rows, :]
         for level in range(NB):
             row = jnp.sum(jnp.where(band == level, weight, 0.0), axis=0, keepdims=True)
             for start in range(0, row.shape[1], 128):
-                block_ref[level : level + 1, :] += row[:, start : start + 128]
+                block_ref[24 + level : 25 + level, 0:128] += row[:, start : start + 128]
         return carry
 
     def rows_step(number, carry):
@@ -763,6 +756,7 @@
         return carry
 
     load_bands = pltpu.make_async_copy(band_ref, bands_v, load_sem.at[0])
+    load_pixels = pltpu.make_async_copy(pix_any, pix_ref, load_sem.at[4])
     load_attn = pltpu.make_async_copy(fulls[1], attn_v, load_sem.at[1])
     load_embed = pltpu.make_async_copy(fulls[0], embed_v, load_sem.at[2])
     load_mlp = pltpu.make_async_copy(fulls[2], mlp_v, load_sem.at[3])
@@ -795,8 +789,9 @@
                 swapped.add(number)
         if step == 0:
             load_bands.start()
-            lax.fori_loop(0, images, pick, 0)
+            load_pixels.start()
             block_ref[...] = jnp.zeros_like(block_ref)
+            block_ref[:24, :] = placed_ref[...]
             load_bands.wait()
             lax.fori_loop(0, images, tally, 0)
             near_ref[low] = block_ref[...]
@@ -809,6 +804,8 @@
             far_ref[high] = block_ref[...]
             for copy in stages(1):
                 copy.start()
+            load_pixels.wait()
+            lax.fori_loop(0, images, pick, 0)
         if step == 2:
             for copy in stages(1):
                 copy.wait()
@@ -816,6 +813,10 @@
             for k in range(1, highs):
                 counts = counts + far_ref[k]
             counts_ref[...] = counts
+            vec_ref[...] = jnp.zeros_like(vec_ref)
+            for piece in range(7):
+                vec_ref[piece : piece + 1, :512] = counts[2 * piece : 2 * piece + 1, :]
+                vec_ref[piece : piece + 1, 512:] = counts[2 * piece + 1 : 2 * piece + 2, :]
         if step == attn_at:
             swap(0).wait()
             load_attn.start()
@@ -846,46 +847,52 @@
             swap(number).wait()
 
 
-def forward_all(shards, shared, pixels, band_ids, patch_weight, kept_column, table, evec):
+def forward_all(masters, shared, pixels, band_ids, kept_index, intersection, table, placed):
     size = lax.axis_size("dp")
     highs = size // 4
-    count = len(shards)
-    groups = blocks_of([a.shape[1] for a in shards], 512)
+    count = len(masters)
+    dims_of = []
+    for master, split in zip(masters, shared):
+        if master.ndim == 3:
+            dims_of.append((master.shape[1], master.shape[0] * master.shape[2]))
+        else:
+            dims_of.append((master.shape[0], master.shape[1] // 2))
+    groups = blocks_of([dims[1] for dims in dims_of], 512)
     total = len(groups)
-    rows, wide, local = kept_column.shape[0], evec.shape[1], shards[1].shape[1] // 4
-    images = table.shape[0]
-    length = rows // images
+    images, length = kept_index.shape
+    rows, wide, local = images * length, D, dims_of[1][1] // 4
+    rows_d = pixels.shape[0]
     group = 2 * length
     fulls = []
-    for shard, split in zip(shards, shared):
-        dims = (highs, 4) + shard.shape
-        fulls.append(shape((2,) + dims if split else dims, shard.dtype))
+    for dims, split in zip(dims_of, shared):
+        dims = (highs, 4) + dims
+        fulls.append(shape((2,) + dims if split else dims, BF16))
+    block = (32, 512)
     outs = [shape((rows, wide), F32), shape((3 * local, rows), BF16), shape((local, rows), BF16),
             shape((local // DH, rows), F32), shape((rows, pixels.shape[1]), BF16), shape((rows, wide), F32),
-            shape((rows, wide), BF16), shape((rows, wide), BF16), shape((8, 128), F32), shape((4 * local, wide), BF16)]
+            shape((rows, wide), BF16), shape((rows, wide), BF16), shape(block, F32), shape((4 * local, wide), BF16),
+            shape((8, wide), F32), shape((rows_d, 2), F32), shape((rows, 1), jnp.int32)]
     dma = pltpu.SemaphoreType.DMA
-    small = (8, 128)
     in_vmem = pl.BlockSpec(memory_space=pltpu.VMEM)
     any_space = pl.BlockSpec(memory_space=pl.ANY)
     result = pl.pallas_call(
         functools.partial(forward_kernel, highs, shared, groups, count, length, group, DH),
         out_shape=tuple(fulls + outs),
-        in_specs=[any_space] * count + [in_vmem, any_space] + [in_vmem] * 4,
+        in_specs=[in_vmem] * count + [any_space] * 2 + [in_vmem] * 4,
         out_specs=tuple([any_space] * count + [in_vmem] * len(outs)),
-        scratch_shapes=[
-            pltpu.VMEM(band_ids.shape, jnp.int32), pltpu.VMEM(fulls[0].shape, BF16), pltpu.VMEM(fulls[1].shape, BF16),
-            pltpu.VMEM(fulls[2].shape, BF16), pltpu.VMEM((rows, wide), BF16),
+        scratch_shapes=[pltpu.VMEM(dims, BF16) for dims in dims_of] + [
+            pltpu.VMEM(pixels.shape, BF16), pltpu.VMEM(band_ids.shape, jnp.int32), pltpu.VMEM(fulls[0].shape, BF16),
+            pltpu.VMEM(fulls[1].shape, BF16), pltpu.VMEM(fulls[2].shape, BF16), pltpu.VMEM((rows, wide), BF16),
             pltpu.VMEM((rows, wide), BF16), pltpu.VMEM((rows, wide), BF16), pltpu.VMEM((rows, wide), F32),
-            pltpu.VMEM(small, F32), pltpu.VMEM((4,) + small, F32), pltpu.VMEM((highs,) + small, F32),
+            pltpu.VMEM(block, F32), pltpu.VMEM((4,) + block, F32), pltpu.VMEM((highs,) + block, F32),
             dma((total,)), dma((total, highs - 1)), dma((total, highs - 1)), dma((total, 2)), dma((total, 2)),
-            dma((total,)), dma((total,)), dma((count,)), dma((count,)), dma((4,)), dma((2,)), dma((2,)),
+            dma((total,)), dma((total,)), dma((count,)), dma((count,)), dma((5,)), dma((2,)), dma((2,)),
             dma((highs + 2,)), dma((highs + 2,))],
-        compiler_params=pltpu.CompilerParams(collective_id=0, has_side_effects=True, vmem_limit_bytes=VMEM_LIMIT),
-        cost_estimate=pl.CostEstimate(flops=0, bytes_accessed=sum(a.size * a.dtype.itemsize * size for a in shards),
-                                      transcendentals=0),
-    )(*shards, pixels, band_ids, patch_weight, kept_column, table, evec)
-    weights = [full.reshape(((2,) if split else ()) + (size * shard.shape[0], shard.shape[1]))
-               for full, split, shard in zip(result[:count], shared, shards)]
+        compiler_params=pltpu.CompilerParams(collective_id=0, has_side_effects=True, vmem_limit_bytes=62 * 2**20),
+        cost_estimate=pl.CostEstimate(flops=0, bytes_accessed=2**25, transcendentals=0),
+    )(*masters, pixels, band_ids, kept_index, intersection, table, placed)
+    weights = [full.reshape(((2,) if split else ()) + (size * dims[0], dims[1]))
+               for full, split, dims in zip(result[:count], shared, dims_of)]
     return weights, result[count:]
 
 
@@ -901,12 +908,12 @@
     return fulls
 
 
-def decoder_kernel(length, head_dim, inverse_ref, x1e_ref, mine_ref, other_ref, evec_ref, kept_ref, column_ref, rows_ref,
-                   table_ref, vec_ref, bias_ref, target_any, band_any, attn_any, mlp_any, bridge_any, predict_any,
-                   gy_out, gattn_ref, gup_ref, gdown_ref, gpred_ref, gbridge_ref, loss_ref, gbias_ref, sums_ref, esums_ref,
-                   final_ref, glat_ref, x_ref, x1_ref, gy_ref, qkv_ref, mixed_ref, lse_ref, part_ref, from_ref,
+def decoder_kernel(length, head_dim, x1e_ref, mine_ref, other_ref, evec_ref, kept_ref, column_ref, rows_ref,
+                   table_ref, totals_ref, target_any, band_any, attn_any, mlp_any, bridge_any, predict_any,
+                   gy_out, gattn_ref, gup_ref, gdown_ref, gpred_ref, gbridge_ref, loss_ref, vgrad_ref,
+                   gbias_ref, sums_ref, esums_ref, final_ref, glat_ref, x_ref, x1_ref, gy_ref, qkv_ref, mixed_ref, lse_ref, part_ref, from_ref,
                    lowt_ref, gradt_ref, z_ref, gu_ref, flat_ref, mlp_ref, bridge_ref, predict_ref, target_ref,
-                   band_ref, gp_ref, gpred_acc, gmix_ref, load_sem, stream_sem, send_sem, receive_sem):
+                   band_ref, gp_ref, gpred_acc, gmix_ref, vec_ref, load_sem, stream_sem, send_sem, receive_sem):
     core, index = lax.axis_index("mp"), lax.axis_index("dp")
     sibling = (index, 1 - core)
     greet([sibling])
@@ -915,6 +922,9 @@
     width = mixed_ref.shape[0]
     hidden = z_ref.shape[1]
     share = predict_ref.shape[2]
+    vec_ref[...] = totals_ref[14:22, :]
+    bias = jnp.concatenate([totals_ref[21:22, :], totals_ref[22:23, : 2 * share - totals_ref.shape[1]]], axis=1)
+    inverse = [1.0 / jnp.sum(totals_ref[24 + level : 25 + level, :], axis=1, keepdims=True) for level in range(NB)]
     attn_ref = z_ref.at[pl.ds(0, attn_any.shape[0]), pl.ds(0, 4 * width)]
 
     loads = [pltpu.make_async_copy(source, target, load_sem.at[at]) for at, (source, target) in enumerate(
@@ -1027,9 +1037,9 @@
         for copy in stream(image):
             copy.wait()
         predicted = jnp.concatenate([dot_nn(final, predict_ref[0]), dot_nn(final, predict_ref[1])], axis=1)
-        mismatch = predicted + bias_ref[...] - target_ref[slot].astype(F32)
+        mismatch = predicted + bias - target_ref[slot].astype(F32)
         band = band_ref[slot]
-        level = jnp.where(band == 0, inverse_ref[0], jnp.where(band == 1, inverse_ref[1], inverse_ref[2]))
+        level = jnp.where(band == 0, inverse[0], jnp.where(band == 1, inverse[1], inverse[2]))
         level = level * rows_ref[rows, 1:2]
         square = mismatch * mismatch + EPS_C
         root = lax.rsqrt(square)
@@ -1113,15 +1123,19 @@
         return carry
 
     lax.fori_loop(0, x1e_ref.shape[0] // 128, enc_start, 0)
-
-
-def decoder_all(inverse, x1e, mine, other, evec, kept_index, kept_column, row_values, table, dvec, bias, target, band,
+    vgrad_ref[...] = jnp.zeros_like(vgrad_ref)
+    vgrad_ref[5:7, :] = esums_ref[0:2, :]
+    vgrad_ref[7:14, : sums_ref.shape[1]] = sums_ref[0:7, :]
+    vgrad_ref[14:15, : gbias_ref.shape[1]] = gbias_ref[...]
+
+
+def decoder_all(x1e, mine, other, evec, kept_index, kept_column, row_values, table, totals, target, band,
                 attn, mlp, bridge, predict):
     rows_e, wide = x1e.shape
     images, length = kept_index.shape
     rows, pixel_count = target.shape
     patches = rows // images
-    low_wide = dvec.shape[1]
+    low_wide = mlp.shape[0]
     width, hidden, share, ends = attn.shape[1] // 4, mlp.shape[1] // 2, predict.shape[2], bridge.shape[2]
     in_vmem = pl.BlockSpec(memory_space=pltpu.VMEM)
     any_space = pl.BlockSpec(memory_space=pl.ANY)
@@ -1132,10 +1146,11 @@
         out_shape=(
             shape((rows_e, wide), F32), shape((low_wide, 4 * width), BF16), shape((low_wide, hidden), BF16),
             shape((low_wide, hidden), BF16), shape((low_wide, share), BF16), shape((wide, ends), BF16),
-            shape((1, pixel_count), F32), shape((1, pixel_count), F32), shape((8, low_wide), F32), shape((8, wide), F32)),
-        in_specs=[pl.BlockSpec(memory_space=pltpu.SMEM)] + [in_vmem] * 10 + [any_space] * 6,
-        out_specs=tuple([in_vmem] * 10),
+            shape((1, pixel_count), F32), shape((16, wide), F32)),
+        in_specs=[in_vmem] * 9 + [any_space] * 6,
+        out_specs=tuple([in_vmem] * 8),
         scratch_shapes=[
+            vm((1, pixel_count), F32), vm((8, low_wide), F32), vm((8, wide), F32),
             vm((rows_e, wide), BF16), vm((rows_e, low_wide), BF16), vm((rows, low_wide), F32),
             vm((rows, low_wide), F32), vm((rows, low_wide), F32), vm((3 * width, rows), BF16), vm((width, rows), BF16),
             vm((width // DDH, rows), F32), vm((2, rows, low_wide), BF16), vm((2, rows, low_wide), BF16),
@@ -1143,11 +1158,11 @@
             vm((4 * width, low_wide), BF16), vm(mlp.shape, BF16), vm(bridge.shape, BF16),
             vm(predict.shape, BF16), vm((2, patches, pixel_count), BF16), vm((2, patches, pixel_count), jnp.int32),
             vm((patches, pixel_count), BF16), vm((low_wide, share), F32), vm((width, patches), BF16),
+            vm((8, low_wide), F32),
             dma((4,)), dma((2, 2)), dma((4, images)), dma((4, images))],
         compiler_params=pltpu.CompilerParams(collective_id=3, has_side_effects=True, vmem_limit_bytes=62 * 2**20),
         cost_estimate=pl.CostEstimate(flops=0, bytes_accessed=2**25, transcendentals=0),
-    )(inverse, x1e, mine, other, evec, kept_index, kept_column, row_values, table, dvec, bias, target, band, attn, mlp,
-      bridge, predict)
+    )(x1e, mine, other, evec, kept_index, kept_column, row_values, table, totals, target, band, attn, mlp, bridge, predict)
 
 
 class Reducer:
@@ -1255,19 +1270,23 @@
     return Reducer(highs, groups, weights, grads, outs, near, second, far, *refs[:3], norm, refs[3:10]), refs[10:]
 
 
-def backward_kernel(highs, weights, groups, ready, count, length, group, head_dim, *refs):
+def backward_kernel(highs, weights, groups, ready, count, shared, length, group, head_dim, *refs):
     given = count - 4
     gy_ref, x1_ref, vec_ref, vgrad_ref, loss_ref, lse_ref = refs[:6]
     x_any, qkv_any, mixed_any, flat_any, pixk_any, mlp_any = refs[6:12]
     refs = refs[12:]
     grads, refs = refs[:given], refs[given:]
-    outs, sums_ref, vsum_ref, refs = refs[:count], refs[count], refs[count + 1], refs[count + 2 :]
+    outs, sums_ref, vflat_ref, refs = refs[:count], refs[count], refs[count + 1], refs[count + 2 :]
     made, refs = refs[:4], refs[4:]
     grads = tuple(grads) + tuple(made)
     (x_ref, qkv_ref, mixed_ref, flat_ref, pixk_ref, wmlp_ref, low_ref, lowt_ref, grad_ref, gradt_ref, acc_ref, part_ref,
-     other_ref, last_ref, gmix_ref, gqkv_ref, stage_ref, norm_ref, spots_ref, far_ref, vnear_ref, vfar_ref) = refs[:22]
-    (load_sem, wload_sem, store_sem, xs_sem, xr_sem, ns_sem, nr_sem, hs_sem, hr_sem, ts_sem, tr_sem) = refs[22:33]
-    red, _ = make_reducer(highs, groups, weights, grads, outs, norm_ref, refs[33:])
+     other_ref, last_ref, gmix_ref, gqkv_ref, stage_ref, norm_ref, spots_ref, far_ref, vnear_ref, vfar_ref,
+     vsum_ref) = refs[:23]
+    (load_sem, wload_sem, store_sem, xs_sem, xr_sem, ns_sem, nr_sem, hs_sem, hr_sem, ts_sem, tr_sem, js_sem,
+     jr_sem) = refs[23:36]
+    core_at = lax.axis_index("mp")
+    views = [ref.at[core_at] if split else ref for ref, split in zip(outs, shared)]
+    red, _ = make_reducer(highs, groups, weights, grads, views, norm_ref, refs[36:])
     core, low, high = red.core, red.low, red.high
     spot = low * 2 + core
     sibling = (high * 4 + low, 1 - core)
@@ -1434,8 +1453,17 @@
             every = vfar_ref[0]
             for k in range(1, highs):
                 every = every + vfar_ref[k]
-            vsum_ref[...] = every
+            for row in range(7):
+                vflat_ref[2 * row : 2 * row + 1, :] = every[row : row + 1, :512]
+                vflat_ref[2 * row + 1 : 2 * row + 2, :] = every[row : row + 1, 512:]
+            vflat_ref[14:22, :] = every[7:15, :512]
+            vflat_ref[22:23, :] = every[14:15, 512:]
+            vflat_ref[23:24, :] = jnp.zeros_like(vflat_ref[23:24, :])
             norm_ref[0:1, 0:1] += jnp.sum(every * every, keepdims=True) * (1.0 / (8 * highs))
+    joins = [remote(view, view, js_sem.at[at], jr_sem.at[at], sibling)
+             for at, (view, split) in enumerate(zip(views, shared)) if split]
+    for copy in joins:
+        copy.start()
     norm_ref[1:2, 0:1] = jnp.sum(loss_ref[...], keepdims=True)
     spots_ref[spot] = norm_ref[...]
     copies = [remote(norm_ref, spots_ref.at[spot], ns_sem.at[k], nr_sem.at[k], near[k]) for k in range(7)]
@@ -1457,9 +1485,11 @@
     for k in range(1, highs):
         every = every + far_ref[k]
     sums_ref[...] = every
-
-
-def backward_all(gy, x1, evec, vec_grads, loss_parts, enc_saved, x0, flat, pixk, mlp, grads, length, head_dim):
+    for copy in joins:
+        copy.wait()
+
+
+def backward_all(gy, x1, evec, vec_grads, loss_parts, enc_saved, x0, flat, pixk, mlp, grads, shared, length, head_dim):
     size = lax.axis_size("dp")
     highs = size // 4
     qkv, mixed, lse = enc_saved
@@ -1486,8 +1516,9 @@
     in_vmem = pl.BlockSpec(memory_space=pltpu.VMEM)
     any_space = pl.BlockSpec(memory_space=pl.ANY)
     result = pl.pallas_call(
-        functools.partial(backward_kernel, highs, (1.0,) * count, groups, ready, count, length, group, head_dim),
-        out_shape=tuple([shape((r, w), F32) for r, w in zip(shards, widths)] + [shape(small, F32), shape(vec_block, F32)]
+        functools.partial(backward_kernel, highs, (1.0,) * count, groups, ready, count, shared, length, group, head_dim),
+        out_shape=tuple([shape((2, r, w) if split else (r, w), F32) for r, w, split in zip(shards, widths, shared)]
+                        + [shape(small, F32), shape((24, 512), F32)]
                         + [shape(dims, BF16) for dims in fresh]),
         in_specs=[in_vmem] * 6 + [any_space] * (6 + given),
         out_specs=tuple([in_vmem] * (count + 2) + [any_space] * 4),
@@ -1499,14 +1530,14 @@
             pltpu.VMEM((rows, wide), BF16), pltpu.VMEM((rows, wide), BF16), pltpu.VMEM((width, group), BF16),
             pltpu.VMEM((3 * width, rows), BF16), pltpu.VMEM((4,) + lead + (512,), BF16), pltpu.VMEM(small, F32),
             pltpu.VMEM((8,) + small, F32), pltpu.VMEM((highs,) + small, F32), pltpu.VMEM((4,) + vec_block, F32),
-            pltpu.VMEM((highs,) + vec_block, F32),
+            pltpu.VMEM((highs,) + vec_block, F32), pltpu.VMEM(vec_block, F32),
             dma((5,)), dma((2, 2)), dma((4,)), dma((2,)), dma((2,)), dma((7,)), dma((7,)), dma((highs - 1,)),
-            dma((highs - 1,)), dma((highs + 2,)), dma((highs + 2,))] + reducer_scratch(highs, groups, shards),
+            dma((highs - 1,)), dma((highs + 2,)), dma((highs + 2,)), dma((count,)), dma((count,))] + reducer_scratch(highs, groups, shards),
         compiler_params=pltpu.CompilerParams(collective_id=1, has_side_effects=True, vmem_limit_bytes=62 * 2**20),
         cost_estimate=pl.CostEstimate(flops=0, bytes_accessed=sum(a.size * 2 for a in grads), transcendentals=0),
     )(gy, x1, evec, vec_grads, loss_parts, lse, x0, qkv, mixed, flat, pixk, mlp.reshape(lead + (2 * hidden,)),
       *[a.reshape(highs, 4, r, a.shape[1]) for r, a in zip(shards, grads)])
-    return list(result[:count]), result[count][0, 0], 0.5 * result[count][1, 0], result[count + 1]
+    return list(result[:count]), result[count], result[count + 1]
 
 
 def reduce_plain(grads, loss_parts, vec_grads):
@@ -1528,6 +1559,134 @@
         first_hat / (jnp.sqrt(second_hat) + ADAM_EPS) + decay_rate * master
     )
     return (updated, first_new, second_new)
+
+
+def adam_kernel(count, averaged, sums_ref, *refs):
+    sources, refs = refs[: count + 2], refs[count + 2 :]
+    masters, firsts, seconds, refs = refs[:count], refs[count : 2 * count], refs[2 * count : 3 * count], refs[3 * count :]
+    means, refs = refs[:averaged], refs[averaged:]
+    news, new_firsts, new_seconds, new_means = (
+        refs[:count], refs[count : 2 * count], refs[2 * count : 3 * count], refs[3 * count :])
+    factor = CLIP / jnp.maximum(jnp.sqrt(sums_ref[0:1, 0:1]), CLIP)
+
+    def update(number, at, gradient):
+        new, first, second = adam_update(masters[number][at], gradient * factor, firsts[number][at], seconds[number][at],
+                                         RATE_MAT, DECAY_MAT)
+        news[number][at] = new
+        new_firsts[number][at] = first
+        new_seconds[number][at] = second
+        mean = {0: 0, 1: 1, 4: 2}.get(number)
+        if mean is not None:
+            new_means[mean][at] = EMA_KEEP * means[mean][at] + (1.0 - EMA_KEEP) * new
+
+    enc_attn, enc_up, enc_down, dec_attn, dec_up, dec_down, embed, bridge, predict = sources
+    for number, source in ((0, enc_attn), (2, dec_attn)):
+        wide = source.shape[1] // 4
+        for part in range(4):
+            update(number, part, source[:, part * wide : (part + 1) * wide])
+    for number, pair in ((1, (enc_up, enc_down)), (3, (dec_up, dec_down))):
+        for part, source in enumerate(pair):
+            update(number, part, source[...])
+    for number, source in ((4, embed), (5, bridge), (6, predict)):
+        share = source.shape[2]
+        for half in range(2):
+            update(number, (slice(None), pl.ds(half * share, share)), source[half])
+
+
+def adam_all(sums, sources, masters, firsts, seconds, means):
+    like = lambda arrays: [shape(a.shape, F32) for a in arrays]
+    outs = like(masters) * 3 + like(means)
+    count = len(masters)
+    result = run(functools.partial(adam_kernel, count, len(means)), outs, [],
+                 (sums, *sources, *masters, *firsts, *seconds, *means), 0)
+    return (result[:count], result[count : 2 * count], result[2 * count : 3 * count], result[3 * count :])
+
+
+def plain_step(pixels, target, band_ids, kept_index, intersection, gsd_scale, masters, enc_table, dec_table):
+    enc_attn, enc_mlp, dec_attn, dec_mlp, patch_embed, bridge, predict, vectors = masters
+    images, keep_count = kept_index.shape
+    patch_count = intersection.shape[1]
+    patch_index = jnp.arange(patch_count, dtype=jnp.int32)
+    kept_flags = jnp.any(kept_index[:, :, None] == patch_index[None, None, :], axis=1).astype(F32)
+    patch_weight = ((1.0 - kept_flags) * (1.0 - 0.5 * intersection.astype(F32))).reshape(-1, 1)
+    hidden_rows = (1.0 - kept_flags).reshape(-1, 1)
+    core = lax.axis_index("mp").astype(jnp.int32).reshape(1)
+    size = lax.axis_size("dp")
+
+    def flat(stack):
+        return jnp.concatenate([part.astype(BF16) for part in stack], axis=1)
+
+    def core_half(block):
+        half = block.shape[1] // 2
+        return lax.dynamic_slice_in_dim(block, lax.axis_index("mp") * half, half, 1).astype(BF16)
+
+    vec_shard = vectors.shape[0]
+    vec_room = -(-vec_shard // 1024) * 1024
+    vec_rows = jnp.pad(lax.reduce_precision(vectors, 8, 7), (0, vec_room - vec_shard)).reshape(-1, 128)
+    vec_full = gather_dp(vec_rows, 0, orders()[0])
+    pieces = split_vectors(vec_full.reshape(size, vec_room)[:, :vec_shard].reshape(-1), D, E)
+    evec = jnp.stack(pieces[:7] + [jnp.zeros_like(pieces[0])])
+    dvec = jnp.stack(pieces[7:14] + [jnp.zeros_like(pieces[7])])
+    kept_column = kept_index.reshape(-1, 1)
+    rows, rows_d = images * keep_count, images * patch_count
+    pixel_count = pixels.shape[1]
+    group = 2 * keep_count
+    shards = [core_half(patch_embed.T), flat(enc_attn), flat(enc_mlp), flat(dec_attn), flat(dec_mlp), core_half(bridge),
+              core_half(predict)]
+    weights = gather_all(shards, (True, False, False, False, False, True, True))
+    embed_w, enc_attn_w, enc_mlp_w, dec_attn_w, dec_mlp_w, bridge_w, predict_w = weights
+    local = enc_attn_w.shape[1] // 4
+    band_weight = total_dp(jnp.stack([jnp.sum(jnp.where(band_ids == level, patch_weight, 0.0)) for level in range(NB)]))
+    inverse = 1.0 / band_weight
+    x0, *enc_saved, part, kept_pixels = run(
+        functools.partial(enc_in_kernel, keep_count, group, DH),
+        [shape((rows, D), F32), shape((3 * local, rows), BF16), shape((local, rows), BF16),
+         shape((local // DH, rows), F32), shape((rows, D), BF16), shape((rows, pixel_count), BF16)],
+        [pltpu.VMEM((4 * local, D), BF16)],
+        (pixels, kept_column, enc_table, embed_w, evec, enc_attn_w),
+        rows * D * (2 * pixel_count + 8 * local))
+    x1, part = mlp_forward(x0, part, evec, enc_mlp_w)
+    other = other_core(part)
+    one_d, one_e = shape((1, D), F32), shape((1, E), F32)
+    local_d = dec_attn_w.shape[1] // 4
+    x2, final_enc, xd, *dec_saved, part = run(
+        functools.partial(dec_in_kernel, keep_count, DDH),
+        [shape((rows, D), F32), shape((rows, D), BF16), shape((rows_d, E), F32), shape((3 * local_d, rows_d), BF16),
+         shape((local_d, rows_d), BF16), shape((local_d // DDH, rows_d), F32), shape((rows_d, E), BF16)],
+        [pltpu.VMEM((4 * local_d, E), BF16), pltpu.VMEM((rows, E), F32)],
+        (x1, part, other, evec, bridge_w, kept_index, hidden_rows, dec_table, dvec,
+         dec_attn_w),
+        rows_d * E * 8 * local_d + 2 * rows * D * E)
+    xd1, part = mlp_forward(xd, part, dvec, dec_mlp_w)
+    gyd, grad_predict, grad_pbias, loss_parts, grad_dec_fg, grad_dec_fb = head(
+        core, inverse, xd1, part, dvec, pieces[14].reshape(1, -1), predict_w, target, band_ids, patch_weight, patch_count)
+    grad_dec_up, grad_dec_down, part = mlp_backward(gyd, xd1, dvec, dec_mlp_w)
+    gxd, grad_dec_attn, grad_dec_gb, grad_dec_bb, part = attn_backward(
+        gyd, xd1, part, xd, dec_saved, dvec, dec_attn_w, patch_count, patch_count, DDH)
+    grad_dec_ga, grad_dec_ba, grad_mask, grad_bridge, grad_enc_fg, grad_enc_fb, gye = run(
+        functools.partial(between_kernel, keep_count),
+        [one_e, one_e, one_e, shape((D, E // 2), BF16), one_d, one_d, shape((rows, D), F32)],
+        [pltpu.VMEM((rows, E), BF16)],
+        (core, gxd, xd, part, other_core(part), dvec, kept_column, hidden_rows, final_enc, x2, evec, bridge_w),
+        3 * rows * D * E, 1)
+    wide_row = lambda row: jnp.pad(row, ((0, 0), (0, D - row.shape[1])))
+    no_row = jnp.zeros((1, D), F32)
+    late_rows = [grad_enc_fg, grad_enc_fb] + [wide_row(row) for row in (
+        grad_mask, grad_dec_ga, grad_dec_ba, grad_dec_gb, grad_dec_bb, grad_dec_fg, grad_dec_fb, grad_pbias)] + [no_row]
+    dec_grads = [grad_predict, grad_dec_up, grad_dec_down, grad_dec_attn, grad_bridge]
+    grad_enc_up, grad_enc_down, part = mlp_backward(gye, x1, evec, enc_mlp_w)
+    gxe, grad_enc_attn, grad_enc_gb, grad_enc_bb, part = attn_backward(
+        gye, x1, part, x0, enc_saved, evec, enc_attn_w, keep_count, group, DH)
+    grad_enc_ga, grad_enc_ba, grad_ebias, grad_embed = run(
+        enc_out_kernel,
+        [one_d, one_d, one_d, shape((D, pixel_count // 2), BF16)],
+        [], (core, gxe, x0, part, other_core(part), evec, kept_pixels), rows * D * pixel_count, 1)
+    vec_grads = jnp.concatenate([grad_ebias, grad_enc_ga, grad_enc_ba, grad_enc_gb, grad_enc_bb] + late_rows)
+    sums, total_squares, loss, vec_sums = reduce_plain(
+        dec_grads + [grad_enc_up, grad_enc_down, grad_enc_attn, grad_embed], loss_parts, vec_grads)
+    sums = [jnp.stack([jnp.where(core == 0, a, b), jnp.where(core == 0, b, a)]) if at in (0, 4, 8) else a
+            for at, a in enumerate(sums) for b in ([other_core(a)] if at in (0, 4, 8) else [a])]
+    return sums, total_squares, loss, vec_sums, band_weight
 
 
 def per_device(
@@ -1586,147 +1745,46 @@
         second_predict,
         second_vectors,
     )
-    images, keep_count = kept_index.shape
-    patch_count = intersection.shape[1]
-    patch_index = jnp.arange(patch_count, dtype=jnp.int32)
-    kept_flags = jnp.any(kept_index[:, :, None] == patch_index[None, None, :], axis=1).astype(
-        jnp.float32
-    )
-    patch_weight = ((1.0 - kept_flags) * (1.0 - 0.5 * intersection.astype(jnp.float32))).reshape(
-        -1, 1
-    )
-    core_at = lax.axis_index("mp")
-    size = lax.axis_size("dp")
-    low = jnp.bfloat16
-
-    def flat(stack):
-        return jnp.concatenate([part.astype(low) for part in stack], axis=1)
-
-    def core_half(block):
-        return lax.dynamic_slice_in_dim(block, core_at * (block.shape[1] // 2), block.shape[1] // 2, 1).astype(low)
-
+    averages = (ema_enc_attn, ema_enc_mlp, ema_patch_embed)
+    enc_table, dec_table = sine_table(gsd_scale, D, GRID), sine_table(gsd_scale, E, GRID)
     vec_shard = vectors.shape[0]
-    vec_room = -(-vec_shard // 1024) * 1024
-    vec_rows = jnp.pad(lax.reduce_precision(vectors, 8, 7), (0, vec_room - vec_shard)).reshape(-1, 128)
-    whole_tiles = patch_embed.shape[1] % 16 == 0 and dec_attn.shape[1] % 16 == 0
-    vec_full = small_gather(vec_rows) if whole_tiles else gather_dp(vec_rows, 0, orders()[0])
-    pieces = split_vectors(vec_full.reshape(size, vec_room)[:, :vec_shard].reshape(-1), D, E)
-    evec = jnp.stack(pieces[:7] + [jnp.zeros_like(pieces[0])])
-    dvec = jnp.stack(pieces[7:14] + [jnp.zeros_like(pieces[7])])
-    kept_column = kept_index.reshape(-1, 1)
-    rows, rows_d = images * keep_count, images * patch_count
-    pixel_count = pixels.shape[1]
-    group = 2 * keep_count
-    shards = [core_half(patch_embed.T), flat(enc_attn), flat(enc_mlp), flat(dec_attn), flat(dec_mlp), core_half(bridge),
-              core_half(predict)]
-    shared = (True, False, False, False, False, True, True)
-    enc_table = sine_table(gsd_scale, D, GRID)
-    if whole_tiles:
-        weights, results = forward_all(shards, shared, pixels, band_ids, patch_weight, kept_column, enc_table, evec)
+    vec_start = lax.axis_index("dp") * vec_shard
+    if patch_embed.shape[1] % 16 == 0 and dec_attn.shape[1] % 16 == 0:
+        placed = lax.dynamic_update_slice(
+            jnp.zeros((24 * 512,), F32), lax.reduce_precision(vectors, 8, 7), (vec_start,)).reshape(24, 512)
+        weights, results = forward_all(
+            [patch_embed.T, enc_attn, enc_mlp, dec_attn, dec_mlp, bridge, predict],
+            (True, False, False, False, False, True, True), pixels, band_ids, kept_index, intersection, enc_table, placed)
         embed_w, enc_attn_w, enc_mlp_w, dec_attn_w, dec_mlp_w, bridge_w, predict_w = weights
-        x0, *enc_saved, kept_pixels, x1, part, other, counts, enc_flat = results
-        band_weight = jnp.sum(counts[:NB], axis=1)
+        x0, *enc_saved, kept_pixels, x1, part, other, totals, enc_flat, evec, row_values, kept_column = results
+        band_weight = jnp.sum(totals[24 : 24 + NB], axis=1)
+        gye, grad_dec_attn, grad_dec_up, grad_dec_down, grad_predict, grad_bridge, loss_parts, vec_grads = decoder_all(
+            x1, part, other, evec, kept_index, kept_column, row_values, dec_table, totals, target, band_ids, dec_attn_w,
+            dec_mlp_w, bridge_w, predict_w)
+        sums, norms, vec_grad = backward_all(
+            gye, x1, evec, vec_grads, loss_parts, enc_saved, x0, enc_flat, kept_pixels, enc_mlp_w,
+            [grad_predict, grad_dec_up, grad_dec_down, grad_dec_attn, grad_bridge],
+            (True, False, False, False, True, False, False, False, True), kept_index.shape[1], DH)
+        total_squares, loss = norms[0, 0], 0.5 * norms[1, 0]
     else:
-        weights = gather_all(shards, shared)
-        embed_w, enc_attn_w, enc_mlp_w, dec_attn_w, dec_mlp_w, bridge_w, predict_w = weights
-        local = enc_attn_w.shape[1] // 4
-        band_weight = total_dp(jnp.stack([
-            jnp.sum(jnp.where(band_ids == level, patch_weight, 0.0)) for level in range(NB)]))
-        x0, *enc_saved, part, kept_pixels = run(
-            functools.partial(enc_in_kernel, keep_count, group, DH),
-            [shape((rows, D), F32), shape((3 * local, rows), BF16), shape((local, rows), BF16),
-             shape((local // DH, rows), F32), shape((rows, D), BF16), shape((rows, pixel_count), BF16)],
-            [pltpu.VMEM((4 * local, D), BF16)],
-            (pixels, kept_column, enc_table, embed_w, evec, enc_attn_w),
-            rows * D * (2 * pixel_count + 8 * local))
-        x1, part = mlp_forward(x0, part, evec, enc_mlp_w)
-        other = other_core(part)
-    inverse = 1.0 / band_weight
-    core = lax.axis_index("mp").astype(jnp.int32).reshape(1)
-    hidden_rows = (1.0 - kept_flags).reshape(-1, 1)
-    one_d, one_e = shape((1, D), F32), shape((1, E), F32)
-    dec_table = sine_table(gsd_scale, E, GRID)
-    if whole_tiles:
-        (gye, grad_dec_attn, grad_dec_up, grad_dec_down, grad_predict, grad_bridge, loss_parts, grad_pbias, dec_sums,
-         enc_sums) = decoder_all(
-            inverse, x1, part, other, evec, kept_index, kept_column, jnp.concatenate([hidden_rows, patch_weight], axis=1),
-            dec_table, dvec, pieces[14].reshape(1, -1), target, band_ids, dec_attn_w, dec_mlp_w, bridge_w, predict_w)
-        grad_mask, grad_dec_ga, grad_dec_ba, grad_dec_gb, grad_dec_bb, grad_dec_fg, grad_dec_fb = [
-            dec_sums[i : i + 1] for i in range(7)]
-        grad_enc_fg, grad_enc_fb = enc_sums[0:1], enc_sums[1:2]
-    else:
-        local_d = dec_attn_w.shape[1] // 4
-        x2, final_enc, xd, *dec_saved, part = run(
-            functools.partial(dec_in_kernel, keep_count, DDH),
-            [shape((rows, D), F32), shape((rows, D), BF16), shape((rows_d, E), F32), shape((3 * local_d, rows_d), BF16),
-             shape((local_d, rows_d), BF16), shape((local_d // DDH, rows_d), F32), shape((rows_d, E), BF16)],
-            [pltpu.VMEM((4 * local_d, E), BF16), pltpu.VMEM((rows, E), F32)],
-            (x1, part, other, evec, bridge_w, kept_index, hidden_rows, dec_table, dvec,
-             dec_attn_w),
-            rows_d * E * 8 * local_d + 2 * rows * D * E)
-        xd1, part = mlp_forward(xd, part, dvec, dec_mlp_w)
-        gyd, grad_predict, grad_pbias, loss_parts, grad_dec_fg, grad_dec_fb = head(
-            core, inverse, xd1, part, dvec, pieces[14].reshape(1, -1), predict_w, target, band_ids, patch_weight, patch_count)
-        grad_dec_up, grad_dec_down, part = mlp_backward(gyd, xd1, dvec, dec_mlp_w)
-        gxd, grad_dec_attn, grad_dec_gb, grad_dec_bb, part = attn_backward(
-            gyd, xd1, part, xd, dec_saved, dvec, dec_attn_w, patch_count, patch_count, DDH)
-        grad_dec_ga, grad_dec_ba, grad_mask, grad_bridge, grad_enc_fg, grad_enc_fb, gye = run(
-            functools.partial(between_kernel, keep_count),
-            [one_e, one_e, one_e, shape((D, E // 2), BF16), one_d, one_d, shape((rows, D), F32)],
-            [pltpu.VMEM((rows, E), BF16)],
-            (core, gxd, xd, part, other_core(part), dvec, kept_column, hidden_rows, final_enc, x2, evec, bridge_w),
-            3 * rows * D * E, 1)
-    wide_row = lambda row: jnp.pad(row, ((0, 0), (0, D - row.shape[1])))
-    no_row = jnp.zeros((1, D), F32)
-    late_rows = [grad_enc_fg, grad_enc_fb] + [wide_row(row) for row in (
-        grad_mask, grad_dec_ga, grad_dec_ba, grad_dec_gb, grad_dec_bb, grad_dec_fg, grad_dec_fb, grad_pbias)] + [no_row]
-    dec_grads = [grad_predict, grad_dec_up, grad_dec_down, grad_dec_attn, grad_bridge]
-    if whole_tiles:
-        sums, total_squares, loss, vec_sums = backward_all(
-            gye, x1, evec, jnp.concatenate([no_row] * 5 + late_rows), loss_parts, enc_saved, x0, enc_flat, kept_pixels,
-            enc_mlp_w, dec_grads, keep_count, DH)
-    else:
-        grad_enc_up, grad_enc_down, part = mlp_backward(gye, x1, evec, enc_mlp_w)
-        gxe, grad_enc_attn, grad_enc_gb, grad_enc_bb, part = attn_backward(
-            gye, x1, part, x0, enc_saved, evec, enc_attn_w, keep_count, group, DH)
-        grad_enc_ga, grad_enc_ba, grad_ebias, grad_embed = run(
-            enc_out_kernel,
-            [one_d, one_d, one_d, shape((D, pixel_count // 2), BF16)],
-            [], (core, gxe, x0, part, other_core(part), evec, kept_pixels), rows * D * pixel_count, 1)
-        vec_grads = jnp.concatenate([grad_ebias, grad_enc_ga, grad_enc_ba, grad_enc_gb, grad_enc_bb] + late_rows)
-        sums, total_squares, loss, vec_sums = reduce_plain(
-            dec_grads + [grad_enc_up, grad_enc_down, grad_enc_attn, grad_embed], loss_parts, vec_grads)
-    vec_grad = jnp.concatenate([vec_sums[:7].reshape(-1), vec_sums[7:14, :E].reshape(-1), vec_sums[14, :pixel_count]])
-    vec_grad = lax.dynamic_slice_in_dim(vec_grad, lax.axis_index("dp") * vec_shard, vec_shard)
-    reduced = (
-        jnp.stack(jnp.split(sums[7], 4, axis=1)),
-        jnp.stack(sums[5:7]),
-        jnp.stack(jnp.split(sums[3], 4, axis=1)),
-        jnp.stack(sums[1:3]),
-        join_cores(sums[8], core).T,
-        join_cores(sums[4], core),
-        join_cores(sums[0], core),
-        vec_grad,
-    )
+        sums, total_squares, loss, vec_sums, band_weight = plain_step(
+            pixels, target, band_ids, kept_index, intersection, gsd_scale, masters, enc_table, dec_table)
+        norms = jnp.broadcast_to(total_squares, (8, 128))
+        vec_grad = jnp.concatenate(
+            [vec_sums[:7].reshape(-1), vec_sums[7:14, :E].reshape(-1), vec_sums[14, : pixels.shape[1]]])
+    vec_grad = lax.dynamic_slice_in_dim(vec_grad.reshape(-1), vec_start, vec_shard)
     grad_norm = jnp.sqrt(total_squares)
     factor = CLIP / jnp.maximum(grad_norm, CLIP)
-    news, new_firsts, new_seconds = ([], [], [])
-    for position, master in enumerate(masters):
-        is_vec = position == 7
-        updated, first_new, second_new = adam_update(
-            master,
-            reduced[position] * factor,
-            firsts[position],
-            seconds[position],
-            RATE_VEC if is_vec else RATE_MAT,
-            0.0 if is_vec else DECAY_MAT,
-        )
-        news.append(updated)
-        new_firsts.append(first_new)
-        new_seconds.append(second_new)
-    ema_attn = EMA_KEEP * ema_enc_attn + (1.0 - EMA_KEEP) * news[0]
-    ema_mlp = EMA_KEEP * ema_enc_mlp + (1.0 - EMA_KEEP) * news[1]
-    ema_embed = EMA_KEEP * ema_patch_embed + (1.0 - EMA_KEEP) * news[4]
+    order = (7, 5, 6, 3, 1, 2, 8, 4, 0)
+    flip = lambda arrays, at: [a.T if number == at else a for number, a in enumerate(arrays)]
+    news, new_firsts, new_seconds, means = adam_all(
+        norms, [sums[at] for at in order], flip(masters[:7], 4), flip(firsts[:7], 4), flip(seconds[:7], 4),
+        flip(averages, 2))
+    news, new_firsts, new_seconds, means = flip(news, 4), flip(new_firsts, 4), flip(new_seconds, 4), flip(means, 2)
+    vec_new = adam_update(vectors, vec_grad * factor, firsts[7], seconds[7], RATE_VEC, 0.0)
+    news, new_firsts, new_seconds = [
+        list(many) + [one] for many, one in zip((news, new_firsts, new_seconds), vec_new)]
+    ema_attn, ema_mlp, ema_embed = means
     return (
         loss,
         band_weight,

time: 543 us -> 509 us (0.937); the launches traced: 540 us -> 500 us
  local copies, waits for them, and re-layouts: 24.1 us -> 2.72 us
  other arithmetic: 26.6 us -> 5.8 us
    add x3 -> x0, other arithmetic: 7.34 us -> none  [the longest x1 4.69 us: per_device(): ema_mlp = EMA_KEEP * ema_enc_mlp + (1.0 - EMA_KEEP) * news[1]]
    pallas_call x1, Pallas kernels: 173 us -> 178 us  [forward_all(): pl.pallas_call(functools.partial(forward_kernel, highs, shared, groups, c...]
  transfers between devices with their start and end apart: 3 -> 0, of which waited for: 0 -> 0; matrix products, arithmetic and copies ran while one was open for 4% -> 0% of each run, Pallas kernels for 0% -> 0%
where the time goes in v7:
time: 509 us; the launch traced here: 500 us
  Pallas kernels  487 us (96%)
  other arithmetic  5.8 us (1%)
    pallas_call x1, Pallas kernels, backward_all(): pl.pallas_call(functools.partial(backward_kernel, highs, (1.0,) * count,...  181 us
    pallas_call x1, Pallas kernels, forward_all(): pl.pallas_call(functools.partial(forward_kernel, highs, shared, groups, c...  178 us
    pallas_call x1, Pallas kernels, decoder_all(): pl.pallas_call(functools.partial(decoder_kernel, length, DDH), out_shape=...  118 us

profile of v7, /device:TPU:0, one launch (start us, length us, event | category | flops | bytes accessed | tf_op | source)
XLA Modules:
  0.0 499.9 jit_solution(2196233899168225182)
XLA Ops:
  0.7 0.7 convert_multiply_fusion
  1.4 0.1 broadcast_multiply_fusion
  1.4 0.8 reduce-precision_dynamic-update-slice_fusion
  2.2 0.6 reshape.146.refs_12_
  2.8 0.3 multiply_sine_fusion.1
  3.1 0.7 pad_maximum_fusion.1.table_ref
  3.8 0.5 multiply_sine_fusion
  4.4 0.7 pad_maximum_fusion.refs_11_
  5.1 178.5 %shard_map.544 = (bf16[2,4,4,64,384]{4,3,2,1,0:T(8,128)(2,1)}, bf16[4,4,64,2048]{3,2,1,0:T(8,128)(2,1)}, bf16[4,4,64,4096]{3,2,1,0:T(8,128)(2,1)}, bf16[4,4,32,1...) custom-call(f32[64,768]{1,0:T(8,128)} %bitcast.28, ...), custom_call_target="tpu_custom_call" | custom-call | bytes 33554432 | tf_op jit(solution)/shard_map/pallas_call | solution.py:878
  183.6 118.4 %shard_map.545 = (f32[512,1024]{1,0:T(8,128)}, bf16[512,1024]{1,0:T(8,128)(2,1)}, bf16[512,1024]{1,0:T(8,128)(2,1)}, bf16[512,1024]{1,0:T(8,128)(2,1)}, bf16[512...) custom-call(f32[512,1024]{1,0:T(8,128)} %get-tuple-element.91.x1e_ref.refs_1_, ...), custom_call_target="tpu_custom_call" | custom-call | bytes 33554432 | tf_op jit(solution)/shard_map/pallas_call | solution.py:1144
  302.0 1.3 slice_reduce_fusion
  303.4 0.0 copy-start
  303.4 0.0 copy-start.1
  303.4 0.0 copy-start.2
  303.4 180.6 %shard_map.546 = (f32[2,32,384]{2,1,0:T(8,128)}, f32[32,1024]{1,0:T(8,128)}, f32[32,1024]{1,0:T(8,128)}, f32[32,1024]{1,0:T(8,128)}, f32[2,64,256]{2,1,0:T(8,128...) custom-call(f32[512,1024]{1,0:T(8,128)} %get-tuple-element.102.refs_, ...), custom_call_target="tpu_custom_call" | custom-call | bytes 4063232 | tf_op jit(solution)/shard_map/pallas_call | solution.py:1518
  484.0 1.3 fusion.2
  486.6 0.8 copy.63
  487.4 0.0 copy-done
  487.4 0.0 copy-done.1
  487.5 0.0 copy-done.2
  487.5 0.7 multiply_subtract_fusion
  488.2 9.1 %shard_map.547 = (f32[4,64,512]{2,1,0:T(8,128)}, f32[2,64,2048]{2,1,0:T(8,128)}, f32[4,32,256]{2,1,0:T(8,128)}, f32[2,32,1024]{2,1,0:T(8,128)}, f32[64,768]{1,0:...) custom-call(f32[8,128]{1,0:T(8,128)} %get-tuple-element.117.sums_ref, ...), custom_call_target="tpu_custom_call" | custom-call | bytes 20287488 | tf_op jit(solution)/shard_map/pallas_call | solution.py:414
  (4 shorter events, 0.0 us)
Async XLA Ops:
  303.4 184.1 %copy-start = (f32[720]{0:T(1024)S(1)}, f32[720]{0:T(1024)}, u32[]{:S(2)}) copy-start(f32[720]{0:T(1024)} %param.46) | copy-start | bytes 8644
  303.4 184.1 %copy-start.1 = (f32[720]{0:T(1024)S(1)}, f32[720]{0:T(1024)}, u32[]{:S(2)}) copy-start(f32[720]{0:T(1024)} %param.54) | copy-start | bytes 8644
  303.4 184.1 %copy-start.2 = (f32[720]{0:T(1024)S(1)}, f32[720]{0:T(1024)}, u32[]{:S(2)}) copy-start(f32[720]{0:T(1024)} %param.62) | copy-start | bytes 8644

commit v8 on v7

--- a/solution.py
+++ b/solution.py
@@ -633,7 +633,7 @@
     (pix_ref, bands_v, embed_v, attn_v, mlp_v, part_ref, other_ref, low_ref, acc_ref, block_ref, near_ref,
      far_ref) = refs[:12]
     (own_sem, zs_sem, zr_sem, cs_sem, cr_sem, fs_sem, fr_sem, ms_sem, mr_sem, load_sem, xs_sem, xr_sem, ts_sem,
-     tr_sem) = refs[12:]
+     tr_sem, mload_sem) = refs[12:]
     core, low, high, low_x, low_y = place_of()
     at_x, at_y = (high * 4 + low_x, core), (high * 4 + low_y, core)
     at_high = [(lax.rem(high + k, highs) * 4 + low, core) for k in range(1, highs)]
@@ -747,11 +747,11 @@
     def mlp_block(piece, carry):
         size = 512
         hidden = mlp_v.shape[-1] // 2
-        start = pl.multiple_of(piece * size, size)
+        start = piece * size
         wide = x_ref.shape[1]
         up = dot_nn(low_ref[...], mlp_v[:, :, :, pl.ds(start, size)].reshape(wide, size))
         _, _, half = gelu_parts(up)
-        down = mlp_v[:, :, :, pl.ds(pl.multiple_of(hidden + start, size), size)].reshape(wide, size)
+        down = mlp_v[:, :, :, pl.ds(hidden + start, size)].reshape(wide, size)
         acc_ref[...] += dot_nt((up * half).astype(BF16), down)
         return carry
 
@@ -759,9 +759,13 @@
     load_pixels = pltpu.make_async_copy(pix_any, pix_ref, load_sem.at[4])
     load_attn = pltpu.make_async_copy(fulls[1], attn_v, load_sem.at[1])
     load_embed = pltpu.make_async_copy(fulls[0], embed_v, load_sem.at[2])
-    load_mlp = pltpu.make_async_copy(fulls[2], mlp_v, load_sem.at[3])
+
+    def load_mlp(at):
+        cols = pl.ds(groups[at][1], groups[at][2])
+        return pltpu.make_async_copy(fulls[2].at[:, :, :, cols], mlp_v.at[:, :, :, cols], mload_sem.at[groups[at][1] // 512])
+
     stages = functools.partial(total_blocks, block_ref, near_ref, far_ref, (ts_sem, tr_sem), low, high, core, highs)
-    embed_at, attn_at, mlp_at = pair_of(0) + 3, pair_of(1) + 3, pair_of(2) + 3
+    attn_at, blocks_done = pair_of(1) + 3, 0
     row_groups = x_ref.shape[0] // group
     swapped = set()
     for step in range(pairs + 3):
@@ -783,6 +787,8 @@
             for at in in_pair(step - 3):
                 column(at)[1 - at % 2].wait()
                 forward(at).wait()
+                if groups[at][0] == 2:
+                    load_mlp(at).start()
         for number in range(count):
             if shared[number] and number not in swapped and pair_of(number) + 3 <= step:
                 swap(number).start()
@@ -826,21 +832,26 @@
                 at = pl.ds(part * width, width)
                 flat_ref[at, :] = attn_v[:, :, :, at].reshape(-1, width).T
             load_embed.wait()
-        if attn_at <= step < mlp_at - 1:
-            share = -(-row_groups // (mlp_at - 1 - attn_at))
-            start, stop = (step - attn_at) * share, min((step - attn_at + 1) * share, row_groups)
-            if start < stop:
-                lax.fori_loop(start, stop, rows_step, 0)
-                if stop == row_groups:
-                    exchange(0, part_ref, other_ref).start()
-        if step == mlp_at:
-            load_mlp.start()
+        if attn_at <= step < attn_at + 2:
+            lax.fori_loop((step - attn_at) * row_groups // 2, (step - attn_at + 1) * row_groups // 2, rows_step, 0)
+            if step == attn_at + 1:
+                exchange(0, part_ref, other_ref).start()
+        if step == attn_at + 2:
             exchange(0, part_ref, other_ref).wait()
             mlp_first()
-            load_mlp.wait()
-            lax.fori_loop(0, mlp_v.shape[-1] // 1024, mlp_block, 0)
-            last_ref[...] = acc_ref[...].astype(BF16)
-            exchange(1, last_ref, far_out_ref).start()
+        if step >= attn_at + 2:
+            half = mlp_v.shape[-1] // 2
+            for tile in range(blocks_done, half // 512):
+                ends = [at for at in range(total) if groups[at][0] == 2 and groups[at][1] in (tile * 512, half + tile * 512)]
+                if max(ends) // 2 + 3 > step:
+                    break
+                for at in ends:
+                    load_mlp(at).wait()
+                mlp_block(tile, 0)
+                blocks_done = tile + 1
+                if blocks_done == half // 512:
+                    last_ref[...] = acc_ref[...].astype(BF16)
+                    exchange(1, last_ref, far_out_ref).start()
     exchange(1, last_ref, far_out_ref).wait()
     for number in range(1, count):
         if shared[number]:
@@ -858,6 +869,8 @@
         else:
             dims_of.append((master.shape[0], master.shape[1] // 2))
     groups = blocks_of([dims[1] for dims in dims_of], 512)
+    half = dims_of[2][1] // 2
+    groups.sort(key=lambda block: (block[0], block[1] % half if block[0] == 2 else 0, block[1]))
     total = len(groups)
     images, length = kept_index.shape
     rows, wide, local = images * length, D, dims_of[1][1] // 4
@@ -887,7 +900,7 @@
             pltpu.VMEM(block, F32), pltpu.VMEM((4,) + block, F32), pltpu.VMEM((highs,) + block, F32),
             dma((total,)), dma((total, highs - 1)), dma((total, highs - 1)), dma((total, 2)), dma((total, 2)),
             dma((total,)), dma((total,)), dma((count,)), dma((count,)), dma((5,)), dma((2,)), dma((2,)),
-            dma((highs + 2,)), dma((highs + 2,))],
+            dma((highs + 2,)), dma((highs + 2,)), dma((2 * half // 512,))],
         compiler_params=pltpu.CompilerParams(collective_id=0, has_side_effects=True, vmem_limit_bytes=62 * 2**20),
         cost_estimate=pl.CostEstimate(flops=0, bytes_accessed=2**25, transcendentals=0),
     )(*masters, pixels, band_ids, kept_index, intersection, table, placed)
@@ -908,27 +921,104 @@
     return fulls
 
 
-def decoder_kernel(length, head_dim, x1e_ref, mine_ref, other_ref, evec_ref, kept_ref, column_ref, rows_ref,
-                   table_ref, totals_ref, target_any, band_any, attn_any, mlp_any, bridge_any, predict_any,
-                   gy_out, gattn_ref, gup_ref, gdown_ref, gpred_ref, gbridge_ref, loss_ref, vgrad_ref,
-                   gbias_ref, sums_ref, esums_ref, final_ref, glat_ref, x_ref, x1_ref, gy_ref, qkv_ref, mixed_ref, lse_ref, part_ref, from_ref,
-                   lowt_ref, gradt_ref, z_ref, gu_ref, flat_ref, mlp_ref, bridge_ref, predict_ref, target_ref,
-                   band_ref, gp_ref, gpred_acc, gmix_ref, vec_ref, load_sem, stream_sem, send_sem, receive_sem):
+class Gatherer:
+    def __init__(self, highs, groups, shards, fulls, sems):
+        self.highs, self.groups, self.shards, self.fulls = highs, groups, shards, fulls
+        self.own_sem, self.zs_sem, self.zr_sem, self.cs_sem, self.cr_sem, self.fs_sem, self.fr_sem = sems
+        self.core, self.low, self.high, self.low_x, self.low_y = place_of()
+        self.at_x, self.at_y = (self.high * 4 + self.low_x, self.core), (self.high * 4 + self.low_y, self.core)
+        self.at_high = [(lax.rem(self.high + k, highs) * 4 + self.low, self.core) for k in range(1, highs)]
+        self.pairs = (len(groups) + 1) // 2
+
+    def in_pair(self, pair):
+        return [at for at in (2 * pair, 2 * pair + 1) if 0 <= at < len(self.groups)] if 0 <= pair < self.pairs else []
+
+    def full(self, at):
+        number, start, size = self.groups[at]
+        return self.fulls[number], pl.ds(start, size)
+
+    def first(self, at):
+        ref, cols = self.full(at)
+        shard = self.shards[self.groups[at][0]].at[:, cols]
+        mine = ref.at[self.high, self.low, :, cols]
+        return [pltpu.make_async_copy(shard, mine, self.own_sem.at[at])] + [
+            remote(shard, mine, self.zs_sem.at[at, k - 1], self.zr_sem.at[at, k - 1], self.at_high[k - 1])
+            for k in range(1, self.highs)]
+
+    def column(self, at, way):
+        ref, cols = self.full(at)
+        part = ref.at[:, self.low, :, cols]
+        return remote(part, part, self.cs_sem.at[at, way], self.cr_sem.at[at, way], (self.at_x, self.at_y)[way])
+
+    def forward(self, at):
+        ref, cols = self.full(at)
+        which, device = (self.low_x, self.at_y) if at % 2 == 0 else (self.low_y, self.at_x)
+        part = ref.at[:, which, :, cols]
+        return remote(part, part, self.fs_sem.at[at], self.fr_sem.at[at], device)
+
+    def step(self, step):
+        for at in self.in_pair(step):
+            for copy in self.first(at):
+                copy.start()
+        for at in self.in_pair(step - 1):
+            for copy in self.first(at):
+                copy.wait()
+            for way in range(2):
+                self.column(at, way).start()
+        for at in self.in_pair(step - 2):
+            self.column(at, at % 2).wait()
+            self.forward(at).start()
+        for at in self.in_pair(step - 3):
+            self.column(at, 1 - at % 2).wait()
+            self.forward(at).wait()
+
+
+def gatherer_sems(highs, groups):
+    dma, total = pltpu.SemaphoreType.DMA, len(groups)
+    return [dma((total,)), dma((total, highs - 1)), dma((total, highs - 1)), dma((total, 2)), dma((total, 2)),
+            dma((total,)), dma((total,))]
+
+
+def decoder_kernel(length, head_dim, highs, gathered, reduced, evec_ref, kept_ref, column_ref,
+                   rows_ref, table_ref, totals_ref, mlp_in, predict_in, x1e_any, mine_any, other_any, target_any, band_any, attn_any, bridge_any,
+                   gy_out, gattn_ref, gbridge_ref, rpred_ref, rup_ref, rdown_ref, norm_ref, loss_ref, vgrad_ref,
+                   gup_ref, gdown_ref, gpred_ref, mlp_shard, predict_shard,
+                   gbias_ref, sums_ref, esums_ref, final_ref, glat_ref, x_ref, x1_ref, gy_ref, qkv_ref, mixed_ref, lse_ref,
+                   part_ref, from_ref, lowt_ref, gradt_ref, z_ref, gu_ref, flat_ref, mlp_ref, bridge_ref, predict_ref,
+                   target_ref, band_ref, gp_ref, gpred_acc, gmix_ref, vec_ref, load_sem, stream_sem, send_sem, receive_sem,
+                   join_sem, *comm):
     core, index = lax.axis_index("mp"), lax.axis_index("dp")
     sibling = (index, 1 - core)
-    greet([sibling])
+    gather = Gatherer(highs, gathered, (mlp_shard, predict_shard), (mlp_ref, predict_ref.at[core]), comm[:7])
+    pred_view = rpred_ref.at[core]
+    red, _ = make_reducer(highs, reduced, (1.0,) * 3, (gpred_ref, gup_ref, gdown_ref), (pred_view, rup_ref, rdown_ref),
+                          norm_ref, comm[7:])
+    greet([sibling, gather.at_x, gather.at_y] + gather.at_high)
+    for part in range(2):
+        wide = mlp_in.shape[2]
+        mlp_shard[:, part * wide : (part + 1) * wide] = mlp_in[part].astype(BF16)
+    predict_shard[...] = predict_in[:, pl.ds(pl.multiple_of(core * predict_shard.shape[1], predict_shard.shape[1]),
+                                             predict_shard.shape[1])].astype(BF16)
+    gather.step(0)
     images, side, half = table_ref.shape
     patches = side * side
     width = mixed_ref.shape[0]
     hidden = z_ref.shape[1]
-    share = predict_ref.shape[2]
+    wide = x_ref.shape[1]
+    share = predict_ref.shape[-1]
+    w_up = lambda: mlp_ref[:, :, :, :hidden].reshape(wide, hidden)
+    w_down = lambda: mlp_ref[:, :, :, hidden:].reshape(wide, hidden)
+    predict_half = lambda half: predict_ref[half].reshape(wide, share)
     vec_ref[...] = totals_ref[14:22, :]
     bias = jnp.concatenate([totals_ref[21:22, :], totals_ref[22:23, : 2 * share - totals_ref.shape[1]]], axis=1)
     inverse = [1.0 / jnp.sum(totals_ref[24 + level : 25 + level, :], axis=1, keepdims=True) for level in range(NB)]
+    mine_ref = final_ref
+    other_ref = lowt_ref.at[pl.ds(0, other_any.shape[0]), pl.ds(0, other_any.shape[1])]
     attn_ref = z_ref.at[pl.ds(0, attn_any.shape[0]), pl.ds(0, 4 * width)]
 
     loads = [pltpu.make_async_copy(source, target, load_sem.at[at]) for at, (source, target) in enumerate(
-        ((attn_any, attn_ref), (bridge_any, bridge_ref), (mlp_any, mlp_ref), (predict_any, predict_ref)))]
+        ((attn_any, attn_ref), (bridge_any, bridge_ref), (x1e_any, gy_out),
+         (mine_any, mine_ref), (other_any, other_ref)))]
     for copy in loads:
         copy.start()
 
@@ -963,6 +1053,8 @@
         at = pl.ds(part * width, width)
         flat_ref[at, :] = attn_ref[:, at].T
     loads[1].wait()
+    for copy in loads[2:]:
+        copy.wait()
     ends = bridge_ref.shape[2]
     latent_ref = gy_ref
 
@@ -971,7 +1063,7 @@
 
     def enc_end(step, carry):
         rows = ends_rows(step)
-        out = x1e_ref[rows, :] + both(mine_ref, other_ref, rows)
+        out = gy_out[rows, :] + both(mine_ref, other_ref, rows)
         gy_out[rows, :] = out
         unit, _ = normalize(out)
         final = (unit * evec_ref[5:6, :] + evec_ref[6:7, :]).astype(BF16)
@@ -980,7 +1072,7 @@
         latent_ref[rows, ends:] = dot_nn(final, bridge_ref[1])
         return carry
 
-    lax.fori_loop(0, x1e_ref.shape[0] // 128, enc_end, 0)
+    lax.fori_loop(0, gy_out.shape[0] // 128, enc_end, 0)
 
     def phase_a(image, carry):
         rows = rows_of(image)
@@ -999,9 +1091,13 @@
         give(0, image, dot_nn(mixed_ref[:, rows].T, flat_ref[3 * width :, :]))
         return carry
 
-    lax.fori_loop(0, images, phase_a, 0)
-    loads[2].wait()
-    loads[3].wait()
+    swap = remote(predict_ref.at[core], predict_ref.at[core], join_sem.at[0], join_sem.at[1], sibling)
+    gather.step(1)
+    last = gather.pairs + 2
+    for step in range(2, last + 1):
+        lax.fori_loop((step - 2) * images // (last - 1), (step - 1) * images // (last - 1), phase_a, 0)
+        if step < last:
+            gather.step(step)
 
     def phase_b(image, carry):
         rows = rows_of(image)
@@ -1011,16 +1107,19 @@
         unit, _ = normalize(after)
         low = (unit * vec_ref[3:4, :] + vec_ref[4:5, :]).astype(BF16)
         lowt_ref[:, rows] = low.T
-        up = dot_nn(low, mlp_ref[:, :hidden])
+        up = dot_nn(low, w_up())
         square, bent, rise = gelu_parts(up)
         mid = (up * rise).astype(BF16)
         z_ref[rows, :] = mid
         slope = rise + (0.5 * GELU_C) * up * (1.0 - bent * bent) * (1.0 + (3.0 * 0.044715) * square)
         gu_ref[rows, :] = slope.astype(BF16)
-        give(1, image, dot_nt(mid, mlp_ref[:, hidden:]))
+        give(1, image, dot_nt(mid, w_down()))
         return carry
 
     lax.fori_loop(0, images, phase_b, 0)
+    gather.step(last)
+    swap.start()
+    swap.wait()
 
     def phase_c(image, carry):
         rows, slot = rows_of(image), lax.rem(image, 2)
@@ -1036,7 +1135,7 @@
         final = (unit * gain + vec_ref[6:7, :]).astype(BF16)
         for copy in stream(image):
             copy.wait()
-        predicted = jnp.concatenate([dot_nn(final, predict_ref[0]), dot_nn(final, predict_ref[1])], axis=1)
+        predicted = jnp.concatenate([dot_nn(final, predict_half(0)), dot_nn(final, predict_half(1))], axis=1)
         mismatch = predicted + bias - target_ref[slot].astype(F32)
         band = band_ref[slot]
         level = jnp.where(band == 0, inverse[0], jnp.where(band == 1, inverse[1], inverse[2]))
@@ -1049,25 +1148,28 @@
         gp_ref[...] = grad.astype(BF16)
         columns = pl.ds(pl.multiple_of(core * share, share), share)
         gpred_acc[...] += dot_tn(final, gp_ref[:, columns])
-        grad_final = dot_nt(gp_ref[:, :share], predict_ref[0]) + dot_nt(gp_ref[:, share:], predict_ref[1])
+        grad_final = dot_nt(gp_ref[:, :share], predict_half(0)) + dot_nt(gp_ref[:, share:], predict_half(1))
         grad_in, gain_sum, shift_sum = norm_back(grad_final, gain, unit, rstd)
         gy_ref[rows, :] = grad_in
         sums_ref[5:6, :] += gain_sum
         sums_ref[6:7, :] += shift_sum
         low = grad_in.astype(BF16)
         gradt_ref[:, rows] = low.T
-        grad_up = (dot_nn(low, mlp_ref[:, hidden:]) * gu_ref[rows, :].astype(F32)).astype(BF16)
+        grad_up = (dot_nn(low, w_down()) * gu_ref[rows, :].astype(F32)).astype(BF16)
         gu_ref[rows, :] = grad_up
-        give(2, image, dot_nt(grad_up, mlp_ref[:, :hidden]))
+        give(2, image, dot_nt(grad_up, w_up()))
         return carry
 
     lax.fori_loop(0, images, phase_c, 0)
-    gpred_ref[...] = gpred_acc[...].astype(BF16)
+    lead = gpred_ref.shape[:3]
+    norm_ref[...] = jnp.zeros_like(norm_ref)
+    gpred_ref[...] = gpred_acc[...].astype(BF16).reshape(gpred_ref.shape)
     tile = 256
     for start in range(0, hidden, tile):
         at = pl.ds(start, tile)
-        gup_ref[:, at] = dot_nn(lowt_ref[...], gu_ref[:, at]).astype(BF16)
-        gdown_ref[:, at] = dot_nn(gradt_ref[...], z_ref[:, at]).astype(BF16)
+        gup_ref[:, :, :, at] = dot_nn(lowt_ref[...], gu_ref[:, at]).astype(BF16).reshape(lead + (tile,))
+        gdown_ref[:, :, :, at] = dot_nn(gradt_ref[...], z_ref[:, at]).astype(BF16).reshape(lead + (tile,))
+    red.step(0)
 
     def phase_d(image, carry):
         rows = rows_of(image)
@@ -1087,7 +1189,11 @@
         give(3, image, dot_nn(qkv_ref[:, rows].T, flat_ref[: 3 * width, :]))
         return carry
 
-    lax.fori_loop(0, images, phase_d, 0)
+    final_step = red.pairs + 2
+    for step in range(1, final_step):
+        lax.fori_loop((step - 1) * images // (final_step - 1), step * images // (final_step - 1), phase_d, 0)
+        red.step(step)
+    join = remote(pred_view, pred_view, join_sem.at[2], join_sem.at[3], sibling)
     for part in range(3):
         at = pl.ds(part * width, width)
         gattn_ref[:, at] = dot_nt(lowt_ref[...], qkv_ref[at, :]).astype(BF16)
@@ -1108,6 +1214,8 @@
         return carry
 
     lax.fori_loop(0, images, phase_e, 0)
+    red.step(final_step)
+    join.start()
     columns = pl.ds(pl.multiple_of(core * ends, ends), ends)
     gbridge_ref[...] = dot_tn(final_ref[...], glat_ref[:, columns]).astype(BF16)
     esums_ref[...] = jnp.zeros_like(esums_ref)
@@ -1122,47 +1230,57 @@
         esums_ref[1:2, :] += shift_sum
         return carry
 
-    lax.fori_loop(0, x1e_ref.shape[0] // 128, enc_start, 0)
+    lax.fori_loop(0, gy_out.shape[0] // 128, enc_start, 0)
+    join.wait()
     vgrad_ref[...] = jnp.zeros_like(vgrad_ref)
     vgrad_ref[5:7, :] = esums_ref[0:2, :]
     vgrad_ref[7:14, : sums_ref.shape[1]] = sums_ref[0:7, :]
     vgrad_ref[14:15, : gbias_ref.shape[1]] = gbias_ref[...]
 
 
-def decoder_all(x1e, mine, other, evec, kept_index, kept_column, row_values, table, totals, target, band,
-                attn, mlp, bridge, predict):
+def decoder_all(x1e, mine, other, evec, kept_index, kept_column, row_values, table, totals, mlp, predict, target, band,
+                attn, bridge):
+    size = lax.axis_size("dp")
+    highs = size // 4
     rows_e, wide = x1e.shape
     images, length = kept_index.shape
     rows, pixel_count = target.shape
     patches = rows // images
-    low_wide = mlp.shape[0]
-    width, hidden, share, ends = attn.shape[1] // 4, mlp.shape[1] // 2, predict.shape[2], bridge.shape[2]
+    shard, hidden = mlp.shape[1], mlp.shape[2]
+    low_wide = shard * size
+    width, share, ends = attn.shape[1] // 4, predict.shape[1] // 2, bridge.shape[2]
+    lead = (highs, 4, shard)
+    gathered = blocks_of([2 * hidden, share], 512)
+    reduced = blocks_of([share, hidden, hidden], 512)
     in_vmem = pl.BlockSpec(memory_space=pltpu.VMEM)
     any_space = pl.BlockSpec(memory_space=pl.ANY)
     dma = pltpu.SemaphoreType.DMA
     vm = pltpu.VMEM
     return pl.pallas_call(
-        functools.partial(decoder_kernel, length, DDH),
+        functools.partial(decoder_kernel, length, DDH, highs, gathered, reduced),
         out_shape=(
-            shape((rows_e, wide), F32), shape((low_wide, 4 * width), BF16), shape((low_wide, hidden), BF16),
-            shape((low_wide, hidden), BF16), shape((low_wide, share), BF16), shape((wide, ends), BF16),
+            shape((rows_e, wide), F32), shape((low_wide, 4 * width), BF16), shape((wide, ends), BF16),
+            shape((2, shard, share), F32), shape((shard, hidden), F32), shape((shard, hidden), F32), shape((8, 128), F32),
             shape((1, pixel_count), F32), shape((16, wide), F32)),
-        in_specs=[in_vmem] * 9 + [any_space] * 6,
-        out_specs=tuple([in_vmem] * 8),
+        in_specs=[in_vmem] * 8 + [any_space] * 7,
+        out_specs=tuple([in_vmem] * 9),
         scratch_shapes=[
+            vm(lead + (hidden,), BF16), vm(lead + (hidden,), BF16), vm(lead + (share,), BF16),
+            vm((shard, 2 * hidden), BF16), vm((shard, share), BF16),
             vm((1, pixel_count), F32), vm((8, low_wide), F32), vm((8, wide), F32),
             vm((rows_e, wide), BF16), vm((rows_e, low_wide), BF16), vm((rows, low_wide), F32),
             vm((rows, low_wide), F32), vm((rows, low_wide), F32), vm((3 * width, rows), BF16), vm((width, rows), BF16),
             vm((width // DDH, rows), F32), vm((2, rows, low_wide), BF16), vm((2, rows, low_wide), BF16),
             vm((low_wide, rows), BF16), vm((low_wide, rows), BF16), vm((rows, hidden), BF16), vm((rows, hidden), BF16),
-            vm((4 * width, low_wide), BF16), vm(mlp.shape, BF16), vm(bridge.shape, BF16),
-            vm(predict.shape, BF16), vm((2, patches, pixel_count), BF16), vm((2, patches, pixel_count), jnp.int32),
+            vm((4 * width, low_wide), BF16), vm(lead + (2 * hidden,), BF16), vm(bridge.shape, BF16),
+            vm((2,) + lead + (share,), BF16), vm((2, patches, pixel_count), BF16), vm((2, patches, pixel_count), jnp.int32),
             vm((patches, pixel_count), BF16), vm((low_wide, share), F32), vm((width, patches), BF16),
             vm((8, low_wide), F32),
-            dma((4,)), dma((2, 2)), dma((4, images)), dma((4, images))],
+            dma((5,)), dma((2, 2)), dma((4, images)), dma((4, images)), dma((4,))]
+        + gatherer_sems(highs, gathered) + reducer_scratch(highs, reduced, [shard] * 3),
         compiler_params=pltpu.CompilerParams(collective_id=3, has_side_effects=True, vmem_limit_bytes=62 * 2**20),
         cost_estimate=pl.CostEstimate(flops=0, bytes_accessed=2**25, transcendentals=0),
-    )(x1e, mine, other, evec, kept_index, kept_column, row_values, table, totals, target, band, attn, mlp, bridge, predict)
+    )(evec, kept_index, kept_column, row_values, table, totals, mlp, predict, x1e, mine, other, target, band, attn, bridge)
 
 
 class Reducer:
@@ -1272,9 +1390,9 @@
 
 def backward_kernel(highs, weights, groups, ready, count, shared, length, group, head_dim, *refs):
     given = count - 4
-    gy_ref, x1_ref, vec_ref, vgrad_ref, loss_ref, lse_ref = refs[:6]
-    x_any, qkv_any, mixed_any, flat_any, pixk_any, mlp_any = refs[6:12]
-    refs = refs[12:]
+    gy_ref, x1_ref, vec_ref, vgrad_ref, loss_ref, lse_ref, norm_in = refs[:7]
+    x_any, qkv_any, mixed_any, flat_any, pixk_any, mlp_any = refs[7:13]
+    refs = refs[13:]
     grads, refs = refs[:given], refs[given:]
     outs, sums_ref, vflat_ref, refs = refs[:count], refs[count], refs[count + 1], refs[count + 2 :]
     made, refs = refs[:4], refs[4:]
@@ -1342,9 +1460,6 @@
         grad_up = (dot_nn(grad_ref[...], w_down) * slope).astype(BF16)
         acc_ref[...] += dot_nt(grad_up, w_up)
         slot = 2 * (tile % 2)
-        if tile >= 2:
-            store(slot, made[0], (tile - 2) * size).wait()
-            store(slot + 1, made[1], (tile - 2) * size).wait()
         staged(slot, dot_nn(lowt_ref[...], grad_up))
         store(slot, made[0], tile * size).start()
         staged(slot + 1, dot_nn(gradt_ref[...], mid))
@@ -1400,12 +1515,13 @@
     stages = functools.partial(total_blocks, vsum_ref, vnear_ref, vfar_ref, (ts_sem, tr_sem), low, high, core, highs)
     mlp_ready, attn_ready, embed_ready = ready
     row_groups = rows // group
-    norm_ref[...] = jnp.zeros_like(norm_ref)
+    norm_ref[...] = norm_in[...]
     vsum_ref[...] = vgrad_ref[...]
     for copy in weight_loads(0):
         copy.start()
+    work = {0: range(0, 1), 1: range(1, tiles - 1), 2: range(tiles - 1, tiles)}
     for step in range(red.pairs + 3):
-        if tiles - 2 <= step - mlp_ready < tiles:
+        if 0 <= step - mlp_ready < tiles:
             stores_done(step - mlp_ready)
         if step == attn_ready:
             for slot in range(4):
@@ -1417,22 +1533,18 @@
             for copy in late:
                 copy.start()
             mlp_first()
-        if step < tiles:
-            mlp_block(step)
-            if step == tiles - 1:
+        for tile in work.get(step, ()):
+            mlp_block(tile)
+            if tile == tiles - 1:
                 mlp_last()
-        if tiles <= step < attn_ready - 1:
-            if step == tiles:
-                for copy in late:
-                    copy.wait()
-                exchange(0, other_ref).wait()
-            share = -(-row_groups // (attn_ready - 1 - tiles))
-            start, stop = (step - tiles) * share, min((step - tiles + 1) * share, row_groups)
-            if start < stop:
-                lax.fori_loop(start, stop, rows_step, 0)
-                if stop == row_groups:
-                    exchange(1, last_ref).start()
-        if step == attn_ready - 1:
+        if step == 3:
+            for copy in late:
+                copy.wait()
+            exchange(0, other_ref).wait()
+            lax.fori_loop(0, row_groups // 2, rows_step, 0)
+        if step == 4:
+            lax.fori_loop(row_groups // 2, row_groups, rows_step, 0)
+            exchange(1, last_ref).start()
             attn_grads()
         if step == embed_ready - 1:
             exchange(1, last_ref).wait()
@@ -1489,7 +1601,7 @@
         copy.wait()
 
 
-def backward_all(gy, x1, evec, vec_grads, loss_parts, enc_saved, x0, flat, pixk, mlp, grads, shared, length, head_dim):
+def backward_all(gy, x1, evec, vec_grads, loss_parts, norm, enc_saved, x0, flat, pixk, mlp, grads, shared, length, head_dim):
     size = lax.axis_size("dp")
     highs = size // 4
     qkv, mixed, lse = enc_saved
@@ -1504,12 +1616,13 @@
     shards = [a.shape[0] // size for a in grads] + [shard] * 4
     count, given = len(widths), len(grads)
     blocks = blocks_of(widths, 512)
-    first = [b for b in blocks if b[0] < given]
-    if len(first) % 2:
-        raise ValueError("odd blocks")
+    first = [b for b in blocks if b[0] == 0]
+    last = [b for b in blocks if b[0] == given + 3] + [b for b in blocks if 0 < b[0] < given]
     middle = [b for at in range(0, hidden, 512) for b in ((given, at, 512), (given + 1, at, 512))]
     attn = [b for b in blocks if b[0] == given + 2]
-    groups = first + middle + attn + [b for b in blocks if b[0] == given + 3]
+    groups = first + middle + attn + last
+    if len(first) != 2 or hidden // 512 != 4 or len(attn) != 4:
+        raise ValueError("blocks")
     ready = (len(first) // 2, (len(first) + len(middle)) // 2, (len(first) + len(middle) + len(attn)) // 2)
     dma = pltpu.SemaphoreType.DMA
     small, vec_block = (8, 128), vec_grads.shape
@@ -1520,7 +1633,7 @@
         out_shape=tuple([shape((2, r, w) if split else (r, w), F32) for r, w, split in zip(shards, widths, shared)]
                         + [shape(small, F32), shape((24, 512), F32)]
                         + [shape(dims, BF16) for dims in fresh]),
-        in_specs=[in_vmem] * 6 + [any_space] * (6 + given),
+        in_specs=[in_vmem] * 7 + [any_space] * (6 + given),
         out_specs=tuple([in_vmem] * (count + 2) + [any_space] * 4),
         scratch_shapes=[
             pltpu.VMEM((rows, wide), F32), pltpu.VMEM(qkv.shape, BF16), pltpu.VMEM(mixed.shape, BF16),
@@ -1535,7 +1648,7 @@
             dma((highs - 1,)), dma((highs + 2,)), dma((highs + 2,)), dma((count,)), dma((count,))] + reducer_scratch(highs, groups, shards),
         compiler_params=pltpu.CompilerParams(collective_id=1, has_side_effects=True, vmem_limit_bytes=62 * 2**20),
         cost_estimate=pl.CostEstimate(flops=0, bytes_accessed=sum(a.size * 2 for a in grads), transcendentals=0),
-    )(gy, x1, evec, vec_grads, loss_parts, lse, x0, qkv, mixed, flat, pixk, mlp.reshape(lead + (2 * hidden,)),
+    )(gy, x1, evec, vec_grads, loss_parts, lse, norm, x0, qkv, mixed, flat, pixk, mlp.reshape(lead + (2 * hidden,)),
       *[a.reshape(highs, 4, r, a.shape[1]) for r, a in zip(shards, grads)])
     return list(result[:count]), result[count], result[count + 1]
 
@@ -1753,18 +1866,18 @@
         placed = lax.dynamic_update_slice(
             jnp.zeros((24 * 512,), F32), lax.reduce_precision(vectors, 8, 7), (vec_start,)).reshape(24, 512)
         weights, results = forward_all(
-            [patch_embed.T, enc_attn, enc_mlp, dec_attn, dec_mlp, bridge, predict],
-            (True, False, False, False, False, True, True), pixels, band_ids, kept_index, intersection, enc_table, placed)
-        embed_w, enc_attn_w, enc_mlp_w, dec_attn_w, dec_mlp_w, bridge_w, predict_w = weights
+            [patch_embed.T, enc_attn, enc_mlp, dec_attn, bridge], (True, False, False, False, True), pixels, band_ids,
+            kept_index, intersection, enc_table, placed)
+        embed_w, enc_attn_w, enc_mlp_w, dec_attn_w, bridge_w = weights
         x0, *enc_saved, kept_pixels, x1, part, other, totals, enc_flat, evec, row_values, kept_column = results
         band_weight = jnp.sum(totals[24 : 24 + NB], axis=1)
-        gye, grad_dec_attn, grad_dec_up, grad_dec_down, grad_predict, grad_bridge, loss_parts, vec_grads = decoder_all(
-            x1, part, other, evec, kept_index, kept_column, row_values, dec_table, totals, target, band_ids, dec_attn_w,
-            dec_mlp_w, bridge_w, predict_w)
+        gye, grad_dec_attn, grad_bridge, sum_predict, sum_up, sum_down, norm, loss_parts, vec_grads = decoder_all(
+            x1, part, other, evec, kept_index, kept_column, row_values, dec_table, totals, dec_mlp, predict, target,
+            band_ids, dec_attn_w, bridge_w)
         sums, norms, vec_grad = backward_all(
-            gye, x1, evec, vec_grads, loss_parts, enc_saved, x0, enc_flat, kept_pixels, enc_mlp_w,
-            [grad_predict, grad_dec_up, grad_dec_down, grad_dec_attn, grad_bridge],
-            (True, False, False, False, True, False, False, False, True), kept_index.shape[1], DH)
+            gye, x1, evec, vec_grads, loss_parts, norm, enc_saved, x0, enc_flat, kept_pixels, enc_mlp_w,
+            [grad_dec_attn, grad_bridge], (False, True, False, False, False, True), kept_index.shape[1], DH)
+        sums = [sum_predict, sum_up, sum_down] + sums
         total_squares, loss = norms[0, 0], 0.5 * norms[1, 0]
     else:
         sums, total_squares, loss, vec_sums, band_weight = plain_step(

time: 509 us -> 479 us (0.941)
  Pallas kernels: 487 us -> 459 us
    pallas_call x1, Pallas kernels: 178 us -> 153 us  [forward_all(): pl.pallas_call(functools.partial(forward_kernel, highs, shared, groups, c...]
    pallas_call x1, Pallas kernels: 181 us -> 158 us  [backward_all(): pl.pallas_call(functools.partial(backward_kernel, highs, (1.0,) * count,...]
    pallas_call x1, Pallas kernels: 118 us -> 138 us  [decoder_all(): pl.pallas_call(functools.partial(decoder_kernel, length, DDH, highs, gath...]
where the time goes in v8:
time: 479 us; the launch traced here: 473 us
  Pallas kernels  459 us (96%)
  other arithmetic  5.8 us (1%)
    pallas_call x1, Pallas kernels, backward_all(): pl.pallas_call(functools.partial(backward_kernel, highs, (1.0,) * count,...  158 us
    pallas_call x1, Pallas kernels, forward_all(): pl.pallas_call(functools.partial(forward_kernel, highs, shared, groups, c...  153 us
    pallas_call x1, Pallas kernels, decoder_all(): pl.pallas_call(functools.partial(decoder_kernel, length, DDH, highs, gath...  138 us

profile of v8, /device:TPU:0, one launch (start us, length us, event | category | flops | bytes accessed | tf_op | source)
XLA Modules:
  0.0 472.5 jit_solution(3385133252886425263)
XLA Ops:
  0.7 0.7 convert_multiply_fusion
  1.4 0.1 broadcast_multiply_fusion
  1.4 0.8 reduce-precision_dynamic-update-slice_fusion
  2.2 0.6 reshape.131.refs_10_
  2.8 0.3 multiply_sine_fusion.1
  3.1 0.7 pad_maximum_fusion.1.table_ref
  3.8 0.5 multiply_sine_fusion
  4.4 0.7 pad_maximum_fusion.refs_9_
  5.1 153.3 %shard_map.544 = (bf16[2,4,4,64,384]{4,3,2,1,0:T(8,128)(2,1)}, bf16[4,4,64,2048]{3,2,1,0:T(8,128)(2,1)}, bf16[4,4,64,4096]{3,2,1,0:T(8,128)(2,1)}, bf16[4,4,32,1...) custom-call(f32[64,768]{1,0:T(8,128)} %bitcast.19, ...), custom_call_target="tpu_custom_call" | custom-call | bytes 33554432 | tf_op jit(solution)/shard_map/pallas_call | solution.py:891
  158.4 138.4 %shard_map.545 = (f32[512,1024]{1,0:T(8,128)}, bf16[512,1024]{1,0:T(8,128)(2,1)}, bf16[1024,256]{1,0:T(8,128)(2,1)}, f32[2,32,384]{2,1,0:T(8,128)}, f32[32,1024]...) custom-call(f32[8,1024]{1,0:T(8,128)} %get-tuple-element.87.evec_ref.refs_2_, ...), custom_call_target="tpu_custom_call" | custom-call | bytes 33554432 | tf_op jit(solution)/shard_map/pallas_call | solution.py:1259
  296.9 1.3 slice_reduce_fusion
  298.2 0.0 copy-start
  298.2 0.0 copy-start.1
  298.2 0.0 copy-start.2
  298.2 158.4 %shard_map.546 = (f32[32,1024]{1,0:T(8,128)}, f32[2,64,256]{2,1,0:T(8,128)}, f32[64,2048]{1,0:T(8,128)}, f32[64,2048]{1,0:T(8,128)}, f32[64,2048]{1,0:T(8,128)},...) custom-call(f32[512,1024]{1,0:T(8,128)} %get-tuple-element.96.refs_0, ...), custom_call_target="tpu_custom_call" | custom-call | bytes 1572864 | tf_op jit(solution)/shard_map/pallas_call | solution.py:1631
  456.6 1.3 fusion.2
  459.2 0.8 copy.63
  460.0 0.0 copy-done
  460.0 0.0 copy-done.1
  460.1 0.0 copy-done.2
  460.1 0.7 multiply_subtract_fusion
  460.8 9.1 %shard_map.547 = (f32[4,64,512]{2,1,0:T(8,128)}, f32[2,64,2048]{2,1,0:T(8,128)}, f32[4,32,256]{2,1,0:T(8,128)}, f32[2,32,1024]{2,1,0:T(8,128)}, f32[64,768]{1,0:...) custom-call(f32[8,128]{1,0:T(8,128)} %get-tuple-element.109.sums_ref, ...), custom_call_target="tpu_custom_call" | custom-call | bytes 20287488 | tf_op jit(solution)/shard_map/pallas_call | solution.py:414
  (4 shorter events, 0.0 us)
Async XLA Ops:
  298.2 161.8 %copy-start = (f32[720]{0:T(1024)S(1)}, f32[720]{0:T(1024)}, u32[]{:S(2)}) copy-start(f32[720]{0:T(1024)} %param.46) | copy-start | bytes 8644
  298.2 161.8 %copy-start.1 = (f32[720]{0:T(1024)S(1)}, f32[720]{0:T(1024)}, u32[]{:S(2)}) copy-start(f32[720]{0:T(1024)} %param.54) | copy-start | bytes 8644
  298.2 161.9 %copy-start.2 = (f32[720]{0:T(1024)S(1)}, f32[720]{0:T(1024)}, u32[]{:S(2)}) copy-start(f32[720]{0:T(1024)} %param.62) | copy-start | bytes 8644

commit v9 on v8

--- a/solution.py
+++ b/solution.py
@@ -100,25 +100,27 @@
     return row_image == col_image
 
 
+LOG2E = math.log2(math.e)
+
+
 def attend(qkv_ref, mixed_ref, lse_ref, cols, width, head_dim, mask):
-    scale = head_dim ** (-0.5)
+    scale = head_dim ** (-0.5) * LOG2E
     for head in range(width // head_dim):
         at = pl.ds(head * head_dim, head_dim)
         queries = qkv_ref[at, cols]
         keys = qkv_ref[pl.ds(width + head * head_dim, head_dim), cols]
         values = qkv_ref[pl.ds(2 * width + head * head_dim, head_dim), cols]
-        scores = dot_tn(keys, queries) * scale
+        scores = dot_tn(keys, queries)
         if mask is not None:
             scores = jnp.where(mask, scores, -1e30)
         top = jnp.max(scores, axis=0, keepdims=True)
-        weights = jnp.exp(scores - top)
+        weights = jnp.exp2((scores - top) * scale)
         total = jnp.sum(weights, axis=0, keepdims=True)
-        lse_ref[pl.ds(head, 1), cols] = top + jnp.log(total)
-        soft = (weights * (1.0 / total)).astype(BF16)
-        mixed_ref[at, cols] = dot_nn(values, soft).astype(BF16)
-
-
-def attend_back(qkv_ref, grad_ref, lse_ref, out_ref, cols, width, head_dim, mask):
+        lse_ref[pl.ds(head, 1), cols] = top * scale + jnp.log2(total)
+        mixed_ref[at, cols] = (dot_nn(values, weights.astype(BF16)) * (1.0 / total)).astype(BF16)
+
+
+def attend_back(qkv_ref, grad_ref, lse_ref, out_ref, cols, out_cols, width, head_dim, mask):
     scale = head_dim ** (-0.5)
     for head in range(width // head_dim):
         at = pl.ds(head * head_dim, head_dim)
@@ -126,16 +128,16 @@
         at_v = pl.ds(2 * width + head * head_dim, head_dim)
         queries, keys, values = qkv_ref[at, cols], qkv_ref[at_k, cols], qkv_ref[at_v, cols]
         grad = grad_ref[at, :]
-        scores = dot_tn(keys, queries) * scale
+        scores = dot_tn(keys, queries)
         if mask is not None:
             scores = jnp.where(mask, scores, -1e30)
-        soft = jnp.exp(scores - lse_ref[pl.ds(head, 1), cols])
-        out_ref[at_v, cols] = dot_nt(grad, soft.astype(BF16)).astype(BF16)
+        soft = jnp.exp2(scores * (scale * LOG2E) - lse_ref[pl.ds(head, 1), cols])
+        out_ref[at_v, out_cols] = dot_nt(grad, soft.astype(BF16)).astype(BF16)
         grad_soft = dot_tn(values, grad)
         inner = jnp.sum(soft * grad_soft, axis=0, keepdims=True)
         grad_scores = (soft * (grad_soft - inner)).astype(BF16)
-        out_ref[at, cols] = (dot_nn(keys, grad_scores) * scale).astype(BF16)
-        out_ref[at_k, cols] = (dot_nt(queries, grad_scores) * scale).astype(BF16)
+        out_ref[at, out_cols] = (dot_nn(keys, grad_scores) * scale).astype(BF16)
+        out_ref[at_k, out_cols] = (dot_nt(queries, grad_scores) * scale).astype(BF16)
 
 
 def transposed_weights(attn_ref, flat_ref):
@@ -351,7 +353,7 @@
         low_grad = grad_in.astype(BF16)
         gradt_ref[:, rows] = low_grad.T
         gmix_ref[...] = dot_nt(flat_ref[3 * width :, :], low_grad).astype(BF16)
-        attend_back(qkv_ref, gmix_ref, lse_ref, gqkv_ref, rows, width, head_dim, mask)
+        attend_back(qkv_ref, gmix_ref, lse_ref, gqkv_ref, rows, rows, width, head_dim, mask)
         part_ref[rows, :] = dot_nn(gqkv_ref[:, rows].T, flat_ref[: 3 * width, :]).astype(BF16)
         unit_a, _ = normalize(x_ref[rows, :])
         lowt_ref[:, rows] = (unit_a * vec_ref[1:2, :] + vec_ref[2:3, :]).astype(BF16).T
@@ -596,12 +598,12 @@
     pl.semaphore_wait(barrier, len(partners))
 
 
-def blocks_of(widths, limit):
+def blocks_of(widths, limit, fine=()):
     found = []
     for number, width in enumerate(widths):
         start = 0
         while start < width:
-            size = min(limit, width - start)
+            size = min(limit // 2 if number in fine else limit, width - start)
             found.append((number, start, size))
             start += size
     return found
@@ -868,7 +870,7 @@
             dims_of.append((master.shape[1], master.shape[0] * master.shape[2]))
         else:
             dims_of.append((master.shape[0], master.shape[1] // 2))
-    groups = blocks_of([dims[1] for dims in dims_of], 512)
+    groups = blocks_of([dims[1] for dims in dims_of], 512, (0, 1))
     half = dims_of[2][1] // 2
     groups.sort(key=lambda block: (block[0], block[1] % half if block[0] == 2 else 0, block[1]))
     total = len(groups)
@@ -985,7 +987,7 @@
                    gup_ref, gdown_ref, gpred_ref, mlp_shard, predict_shard,
                    gbias_ref, sums_ref, esums_ref, final_ref, glat_ref, x_ref, x1_ref, gy_ref, qkv_ref, mixed_ref, lse_ref,
                    part_ref, from_ref, lowt_ref, gradt_ref, z_ref, gu_ref, flat_ref, mlp_ref, bridge_ref, predict_ref,
-                   target_ref, band_ref, gp_ref, gpred_acc, gmix_ref, vec_ref, load_sem, stream_sem, send_sem, receive_sem,
+                   target_ref, band_ref, gp_ref, gpred_acc, gmix_ref, gq_ref, vec_ref, load_sem, stream_sem, send_sem, receive_sem,
                    join_sem, *comm):
     core, index = lax.axis_index("mp"), lax.axis_index("dp")
     sibling = (index, 1 - core)
@@ -1056,33 +1058,42 @@
     for copy in loads[2:]:
         copy.wait()
     ends = bridge_ref.shape[2]
-    latent_ref = gy_ref
+    parts = 3
+    latent_start = attn_any.shape[0]
 
     def ends_rows(step):
         return pl.ds(pl.multiple_of(step * 128, 128), 128)
 
-    def enc_end(step, carry):
-        rows = ends_rows(step)
+    def enc_end(image, carry):
+        rows = pl.ds(pl.multiple_of(image * length, length), length)
         out = gy_out[rows, :] + both(mine_ref, other_ref, rows)
         gy_out[rows, :] = out
         unit, _ = normalize(out)
         final = (unit * evec_ref[5:6, :] + evec_ref[6:7, :]).astype(BF16)
         final_ref[rows, :] = final
-        latent_ref[rows, :ends] = dot_nn(final, bridge_ref[0])
-        latent_ref[rows, ends:] = dot_nn(final, bridge_ref[1])
+        for half in range(2):
+            rest = dot_nn(final, bridge_ref[half])
+            for part in range(parts):
+                value = rest.astype(BF16)
+                at = pl.multiple_of(latent_start + (image * parts + part) * length, length)
+                z_ref[pl.ds(at, length), half * ends : (half + 1) * ends] = value
+                rest = rest - value.astype(F32)
         return carry
 
-    lax.fori_loop(0, gy_out.shape[0] // 128, enc_end, 0)
+    lax.fori_loop(0, images, enc_end, 0)
 
     def phase_a(image, carry):
         rows = rows_of(image)
         hot = lax.broadcasted_iota(jnp.int32, (patches, length), 0) == kept_ref[pl.ds(image, 1), :]
-        latent = latent_ref[pl.ds(pl.multiple_of(image * length, length), length), :]
+        hot = jnp.where(hot, 1.0, 0.0).astype(BF16)
+        at = pl.multiple_of(latent_start + image * parts * length, length)
+        latent = z_ref[pl.ds(at, parts * length), : 2 * ends]
+        spread = dot_nn(jnp.concatenate([hot] * parts, axis=1), latent)
         table = table_ref[image]
         by_row = jnp.broadcast_to(table[:, None, :], (side, side, half)).reshape(patches, half)
         by_col = jnp.broadcast_to(table[None, :, :], (side, side, half)).reshape(patches, half)
         place = jnp.concatenate([by_row, by_col], axis=1)
-        rows_x = dot_exact(hot.astype(F32), latent) + rows_ref[rows, 0:1] * vec_ref[0:1, :] + place
+        rows_x = spread + rows_ref[rows, 0:1] * vec_ref[0:1, :] + place
         x_ref[rows, :] = rows_x
         unit, _ = normalize(rows_x)
         low = (unit * vec_ref[1:2, :] + vec_ref[2:3, :]).astype(BF16)
@@ -1183,10 +1194,11 @@
         low = grad_in.astype(BF16)
         gradt_ref[:, rows] = low.T
         gmix_ref[...] = dot_nt(flat_ref[3 * width :, :], low).astype(BF16)
-        attend_back(qkv_ref, gmix_ref, lse_ref, qkv_ref, rows, width, head_dim, None)
+        attend_back(qkv_ref, gmix_ref, lse_ref, gq_ref, rows, pl.ds(0, patches), width, head_dim, None)
+        qkv_ref[:, rows] = gq_ref[...]
         unit_a, _ = normalize(x_ref[rows, :])
         lowt_ref[:, rows] = (unit_a * vec_ref[1:2, :] + vec_ref[2:3, :]).astype(BF16).T
-        give(3, image, dot_nn(qkv_ref[:, rows].T, flat_ref[: 3 * width, :]))
+        give(3, image, dot_nn(gq_ref[...].T, flat_ref[: 3 * width, :]))
         return carry
 
     final_step = red.pairs + 2
@@ -1275,7 +1287,7 @@
             vm((4 * width, low_wide), BF16), vm(lead + (2 * hidden,), BF16), vm(bridge.shape, BF16),
             vm((2,) + lead + (share,), BF16), vm((2, patches, pixel_count), BF16), vm((2, patches, pixel_count), jnp.int32),
             vm((patches, pixel_count), BF16), vm((low_wide, share), F32), vm((width, patches), BF16),
-            vm((8, low_wide), F32),
+            vm((3 * width, patches), BF16), vm((8, low_wide), F32),
             dma((5,)), dma((2, 2)), dma((4, images)), dma((4, images)), dma((4,))]
         + gatherer_sems(highs, gathered) + reducer_scratch(highs, reduced, [shard] * 3),
         compiler_params=pltpu.CompilerParams(collective_id=3, has_side_effects=True, vmem_limit_bytes=62 * 2**20),
@@ -1485,7 +1497,7 @@
         low_grad = grad_in.astype(BF16)
         gradt_ref[:, at] = low_grad.T
         gmix_ref[...] = dot_nt(flat_ref[3 * width :, :], low_grad).astype(BF16)
-        attend_back(qkv_ref, gmix_ref, lse_ref, gqkv_ref, at, width, head_dim, mask)
+        attend_back(qkv_ref, gmix_ref, lse_ref, gqkv_ref, at, at, width, head_dim, mask)
         part_ref[at, :] = dot_nn(gqkv_ref[:, at].T, flat_ref[: 3 * width, :]).astype(BF16)
         unit_a, _ = normalize(x_ref[at, :])
         lowt_ref[:, at] = (unit_a * vec_ref[1:2, :] + vec_ref[2:3, :]).astype(BF16).T
@@ -1615,13 +1627,13 @@
     widths = [a.shape[1] for a in grads] + [dims[-1] for dims in fresh]
     shards = [a.shape[0] // size for a in grads] + [shard] * 4
     count, given = len(widths), len(grads)
-    blocks = blocks_of(widths, 512)
+    blocks = blocks_of(widths, 512, (given + 2,))
     first = [b for b in blocks if b[0] == 0]
     last = [b for b in blocks if b[0] == given + 3] + [b for b in blocks if 0 < b[0] < given]
     middle = [b for at in range(0, hidden, 512) for b in ((given, at, 512), (given + 1, at, 512))]
     attn = [b for b in blocks if b[0] == given + 2]
     groups = first + middle + attn + last
-    if len(first) != 2 or hidden // 512 != 4 or len(attn) != 4:
+    if len(first) != 2 or hidden // 512 != 4 or len(attn) != 8:
         raise ValueError("blocks")
     ready = (len(first) // 2, (len(first) + len(middle)) // 2, (len(first) + len(middle) + len(attn)) // 2)
     dma = pltpu.SemaphoreType.DMA

time: 479 us -> 465 us (0.971)
  Pallas kernels: 459 us -> 445 us
    pallas_call x1, Pallas kernels: 158 us -> 151 us  [backward_all(): pl.pallas_call(functools.partial(backward_kernel, highs, (1.0,) * count,...]
    pallas_call x1, Pallas kernels: 138 us -> 132 us  [decoder_all(): pl.pallas_call(functools.partial(decoder_kernel, length, DDH, highs, gath...]
where the time goes in v9:
time: 465 us; the launch traced here: 459 us
  Pallas kernels  445 us (96%)
  other arithmetic  5.8 us (1%)
    pallas_call x1, Pallas kernels, forward_all(): pl.pallas_call(functools.partial(forward_kernel, highs, shared, groups, c...  153 us
    pallas_call x1, Pallas kernels, backward_all(): pl.pallas_call(functools.partial(backward_kernel, highs, (1.0,) * count,...  151 us
    pallas_call x1, Pallas kernels, decoder_all(): pl.pallas_call(functools.partial(decoder_kernel, length, DDH, highs, gath...  132 us

profile of v9, /device:TPU:0, one launch (start us, length us, event | category | flops | bytes accessed | tf_op | source)
XLA Modules:
  0.0 458.5 jit_solution(10770594692747918087)
XLA Ops:
  0.7 0.7 convert_multiply_fusion
  1.4 0.1 broadcast_multiply_fusion
  1.4 0.8 reduce-precision_dynamic-update-slice_fusion
  2.2 0.6 reshape.131.refs_10_
  2.8 0.3 multiply_sine_fusion.1
  3.1 0.7 pad_maximum_fusion.1.table_ref
  3.8 0.5 multiply_sine_fusion
  4.4 0.7 pad_maximum_fusion.refs_9_
  5.1 153.2 %shard_map.544 = (bf16[2,4,4,64,384]{4,3,2,1,0:T(8,128)(2,1)}, bf16[4,4,64,2048]{3,2,1,0:T(8,128)(2,1)}, bf16[4,4,64,4096]{3,2,1,0:T(8,128)(2,1)}, bf16[4,4,32,1...) custom-call(f32[64,768]{1,0:T(8,128)} %bitcast.19, ...), custom_call_target="tpu_custom_call" | custom-call | bytes 33554432 | tf_op jit(solution)/shard_map/pallas_call | solution.py:893
  158.3 132.2 %shard_map.545 = (f32[512,1024]{1,0:T(8,128)}, bf16[512,1024]{1,0:T(8,128)(2,1)}, bf16[1024,256]{1,0:T(8,128)(2,1)}, f32[2,32,384]{2,1,0:T(8,128)}, f32[32,1024]...) custom-call(f32[8,1024]{1,0:T(8,128)} %get-tuple-element.87.evec_ref.refs_2_, ...), custom_call_target="tpu_custom_call" | custom-call | bytes 33554432 | tf_op jit(solution)/shard_map/pallas_call | solution.py:1271
  290.5 1.3 slice_reduce_fusion
  291.8 0.0 copy-start
  291.8 0.0 copy-start.1
  291.8 0.0 copy-start.2
  291.8 150.9 %shard_map.546 = (f32[32,1024]{1,0:T(8,128)}, f32[2,64,256]{2,1,0:T(8,128)}, f32[64,2048]{1,0:T(8,128)}, f32[64,2048]{1,0:T(8,128)}, f32[64,2048]{1,0:T(8,128)},...) custom-call(f32[512,1024]{1,0:T(8,128)} %get-tuple-element.96.refs_0, ...), custom_call_target="tpu_custom_call" | custom-call | bytes 1572864 | tf_op jit(solution)/shard_map/pallas_call | solution.py:1643
  442.8 1.3 fusion.2
  445.4 0.8 copy.63
  446.2 0.0 copy-done
  446.3 0.0 copy-done.1
  446.3 0.0 copy-done.2
  446.3 0.7 multiply_subtract_fusion
  447.0 9.1 %shard_map.547 = (f32[4,64,512]{2,1,0:T(8,128)}, f32[2,64,2048]{2,1,0:T(8,128)}, f32[4,32,256]{2,1,0:T(8,128)}, f32[2,32,1024]{2,1,0:T(8,128)}, f32[64,768]{1,0:...) custom-call(f32[8,128]{1,0:T(8,128)} %get-tuple-element.109.sums_ref, ...), custom_call_target="tpu_custom_call" | custom-call | bytes 20287488 | tf_op jit(solution)/shard_map/pallas_call | solution.py:416
  (4 shorter events, 0.0 us)
Async XLA Ops:
  291.8 154.4 %copy-start = (f32[720]{0:T(1024)S(1)}, f32[720]{0:T(1024)}, u32[]{:S(2)}) copy-start(f32[720]{0:T(1024)} %param.46) | copy-start | bytes 8644
  291.8 154.4 %copy-start.1 = (f32[720]{0:T(1024)S(1)}, f32[720]{0:T(1024)}, u32[]{:S(2)}) copy-start(f32[720]{0:T(1024)} %param.54) | copy-start | bytes 8644
  291.8 154.4 %copy-start.2 = (f32[720]{0:T(1024)S(1)}, f32[720]{0:T(1024)}, u32[]{:S(2)}) copy-start(f32[720]{0:T(1024)} %param.62) | copy-start | bytes 8644

commit v10 on v9

--- a/solution.py
+++ b/solution.py
@@ -120,7 +120,7 @@
         mixed_ref[at, cols] = (dot_nn(values, weights.astype(BF16)) * (1.0 / total)).astype(BF16)
 
 
-def attend_back(qkv_ref, grad_ref, lse_ref, out_ref, cols, out_cols, width, head_dim, mask):
+def attend_back(qkv_ref, mixed_ref, grad_ref, lse_ref, out_ref, cols, out_cols, width, head_dim, mask):
     scale = head_dim ** (-0.5)
     for head in range(width // head_dim):
         at = pl.ds(head * head_dim, head_dim)
@@ -134,7 +134,7 @@
         soft = jnp.exp2(scores * (scale * LOG2E) - lse_ref[pl.ds(head, 1), cols])
         out_ref[at_v, out_cols] = dot_nt(grad, soft.astype(BF16)).astype(BF16)
         grad_soft = dot_tn(values, grad)
-        inner = jnp.sum(soft * grad_soft, axis=0, keepdims=True)
+        inner = jnp.sum(grad.astype(F32) * mixed_ref[at, cols].astype(F32), axis=0, keepdims=True)
         grad_scores = (soft * (grad_soft - inner)).astype(BF16)
         out_ref[at, out_cols] = (dot_nn(keys, grad_scores) * scale).astype(BF16)
         out_ref[at_k, out_cols] = (dot_nt(queries, grad_scores) * scale).astype(BF16)
@@ -353,7 +353,7 @@
         low_grad = grad_in.astype(BF16)
         gradt_ref[:, rows] = low_grad.T
         gmix_ref[...] = dot_nt(flat_ref[3 * width :, :], low_grad).astype(BF16)
-        attend_back(qkv_ref, gmix_ref, lse_ref, gqkv_ref, rows, rows, width, head_dim, mask)
+        attend_back(qkv_ref, mixed_ref, gmix_ref, lse_ref, gqkv_ref, rows, rows, width, head_dim, mask)
         part_ref[rows, :] = dot_nn(gqkv_ref[:, rows].T, flat_ref[: 3 * width, :]).astype(BF16)
         unit_a, _ = normalize(x_ref[rows, :])
         lowt_ref[:, rows] = (unit_a * vec_ref[1:2, :] + vec_ref[2:3, :]).astype(BF16).T
@@ -1104,11 +1104,10 @@
 
     swap = remote(predict_ref.at[core], predict_ref.at[core], join_sem.at[0], join_sem.at[1], sibling)
     gather.step(1)
-    last = gather.pairs + 2
-    for step in range(2, last + 1):
-        lax.fori_loop((step - 2) * images // (last - 1), (step - 1) * images // (last - 1), phase_a, 0)
-        if step < last:
-            gather.step(step)
+    lax.fori_loop(0, images // 2, phase_a, 0)
+    gather.step(2)
+    lax.fori_loop(images // 2, images, phase_a, 0)
+    gather.step(3)
 
     def phase_b(image, carry):
         rows = rows_of(image)
@@ -1124,11 +1123,17 @@
         z_ref[rows, :] = mid
         slope = rise + (0.5 * GELU_C) * up * (1.0 - bent * bent) * (1.0 + (3.0 * 0.044715) * square)
         gu_ref[rows, :] = slope.astype(BF16)
-        give(1, image, dot_nt(mid, w_down()))
+        return carry
+
+    def phase_down(image, carry):
+        give(1, image, dot_nt(z_ref[rows_of(image), :], w_down()))
         return carry
 
     lax.fori_loop(0, images, phase_b, 0)
-    gather.step(last)
+    gather.step(4)
+    lax.fori_loop(0, images, phase_down, 0)
+    for step in range(5, gather.pairs + 3):
+        gather.step(step)
     swap.start()
     swap.wait()
 
@@ -1194,22 +1199,22 @@
         low = grad_in.astype(BF16)
         gradt_ref[:, rows] = low.T
         gmix_ref[...] = dot_nt(flat_ref[3 * width :, :], low).astype(BF16)
-        attend_back(qkv_ref, gmix_ref, lse_ref, gq_ref, rows, pl.ds(0, patches), width, head_dim, None)
+        attend_back(qkv_ref, mixed_ref, gmix_ref, lse_ref, gq_ref, rows, pl.ds(0, patches), width, head_dim, None)
         qkv_ref[:, rows] = gq_ref[...]
         unit_a, _ = normalize(x_ref[rows, :])
         lowt_ref[:, rows] = (unit_a * vec_ref[1:2, :] + vec_ref[2:3, :]).astype(BF16).T
         give(3, image, dot_nn(gq_ref[...].T, flat_ref[: 3 * width, :]))
         return carry
 
-    final_step = red.pairs + 2
-    for step in range(1, final_step):
-        lax.fori_loop((step - 1) * images // (final_step - 1), step * images // (final_step - 1), phase_d, 0)
+    for step in range(1, 4):
+        lax.fori_loop((step - 1) * images // 3, step * images // 3, phase_d, 0)
         red.step(step)
     join = remote(pred_view, pred_view, join_sem.at[2], join_sem.at[3], sibling)
     for part in range(3):
         at = pl.ds(part * width, width)
         gattn_ref[:, at] = dot_nt(lowt_ref[...], qkv_ref[at, :]).astype(BF16)
     gattn_ref[:, 3 * width :] = dot_nt(gradt_ref[...], mixed_ref[...]).astype(BF16)
+    red.step(4)
 
     def phase_e(image, carry):
         rows = rows_of(image)
@@ -1226,7 +1231,8 @@
         return carry
 
     lax.fori_loop(0, images, phase_e, 0)
-    red.step(final_step)
+    for step in range(5, red.pairs + 3):
+        red.step(step)
     join.start()
     columns = pl.ds(pl.multiple_of(core * ends, ends), ends)
     gbridge_ref[...] = dot_tn(final_ref[...], glat_ref[:, columns]).astype(BF16)
@@ -1497,7 +1503,7 @@
         low_grad = grad_in.astype(BF16)
         gradt_ref[:, at] = low_grad.T
         gmix_ref[...] = dot_nt(flat_ref[3 * width :, :], low_grad).astype(BF16)
-        attend_back(qkv_ref, gmix_ref, lse_ref, gqkv_ref, at, at, width, head_dim, mask)
+        attend_back(qkv_ref, mixed_ref, gmix_ref, lse_ref, gqkv_ref, at, at, width, head_dim, mask)
         part_ref[at, :] = dot_nn(gqkv_ref[:, at].T, flat_ref[: 3 * width, :]).astype(BF16)
         unit_a, _ = normalize(x_ref[at, :])
         lowt_ref[:, at] = (unit_a * vec_ref[1:2, :] + vec_ref[2:3, :]).astype(BF16).T
@@ -1722,8 +1728,23 @@
     like = lambda arrays: [shape(a.shape, F32) for a in arrays]
     outs = like(masters) * 3 + like(means)
     count = len(masters)
-    result = run(functools.partial(adam_kernel, count, len(means)), outs, [],
-                 (sums, *sources, *masters, *firsts, *seconds, *means), 0)
+    args = (*sources, *masters, *firsts, *seconds, *means)
+    rows = [a.shape[-2] for a in args]
+    cuts = 4 if all(r % 32 == 0 for r in rows) else 1
+
+    def tiled(a):
+        lead = a.shape[:-2]
+        return pl.BlockSpec(lead + (a.shape[-2] // cuts, a.shape[-1]), lambda i: (0,) * len(lead) + (i, 0))
+
+    result = pl.pallas_call(
+        functools.partial(adam_kernel, count, len(means)),
+        out_shape=tuple(outs),
+        grid=(cuts,),
+        in_specs=[pl.BlockSpec(sums.shape, lambda i: (0, 0))] + [tiled(a) for a in args],
+        out_specs=tuple(tiled(a) for a in outs),
+        compiler_params=pltpu.CompilerParams(vmem_limit_bytes=VMEM_LIMIT),
+        cost_estimate=pl.CostEstimate(flops=0, bytes_accessed=2 * sum(4 * a.size for a in args), transcendentals=0),
+    )(sums, *args)
     return (result[:count], result[count : 2 * count], result[2 * count : 3 * count], result[3 * count :])
 
 

time: 465 us -> 461 us (level)
  no operation moved by 1% of the time
where the time goes in v10:
time: 461 us; the launch traced here: 454 us
  Pallas kernels  441 us (96%)
  other arithmetic  5.8 us (1%)
    pallas_call x1, Pallas kernels, forward_all(): pl.pallas_call(functools.partial(forward_kernel, highs, shared, groups, c...  153 us
    pallas_call x1, Pallas kernels, backward_all(): pl.pallas_call(functools.partial(backward_kernel, highs, (1.0,) * count,...  151 us
    pallas_call x1, Pallas kernels, decoder_all(): pl.pallas_call(functools.partial(decoder_kernel, length, DDH, highs, gath...  128 us

profile of v10, /device:TPU:0, one launch (start us, length us, event | category | flops | bytes accessed | tf_op | source)
XLA Modules:
  0.0 454.4 jit_solution(2001305905847495653)
XLA Ops:
  0.7 0.7 convert_multiply_fusion
  1.4 0.1 broadcast_multiply_fusion
  1.4 0.8 reduce-precision_dynamic-update-slice_fusion
  2.2 0.6 reshape.131.refs_10_
  2.8 0.3 multiply_sine_fusion.1
  3.1 0.7 pad_maximum_fusion.1.table_ref
  3.8 0.5 multiply_sine_fusion
  4.4 0.7 pad_maximum_fusion.refs_9_
  5.1 153.2 %shard_map.544 = (bf16[2,4,4,64,384]{4,3,2,1,0:T(8,128)(2,1)}, bf16[4,4,64,2048]{3,2,1,0:T(8,128)(2,1)}, bf16[4,4,64,4096]{3,2,1,0:T(8,128)(2,1)}, bf16[4,4,32,1...) custom-call(f32[64,768]{1,0:T(8,128)} %bitcast.19, ...), custom_call_target="tpu_custom_call" | custom-call | bytes 33554432 | tf_op jit(solution)/shard_map/pallas_call | solution.py:893
  158.3 127.9 %shard_map.545 = (f32[512,1024]{1,0:T(8,128)}, bf16[512,1024]{1,0:T(8,128)(2,1)}, bf16[1024,256]{1,0:T(8,128)(2,1)}, f32[2,32,384]{2,1,0:T(8,128)}, f32[32,1024]...) custom-call(f32[8,1024]{1,0:T(8,128)} %get-tuple-element.87.evec_ref.refs_2_, ...), custom_call_target="tpu_custom_call" | custom-call | bytes 33554432 | tf_op jit(solution)/shard_map/pallas_call | solution.py:1277
  286.1 1.3 slice_reduce_fusion
  287.5 0.0 copy-start
  287.5 0.0 copy-start.1
  287.5 0.0 copy-start.2
  287.5 151.2 %shard_map.546 = (f32[32,1024]{1,0:T(8,128)}, f32[2,64,256]{2,1,0:T(8,128)}, f32[64,2048]{1,0:T(8,128)}, f32[64,2048]{1,0:T(8,128)}, f32[64,2048]{1,0:T(8,128)},...) custom-call(f32[512,1024]{1,0:T(8,128)} %get-tuple-element.96.refs_0, ...), custom_call_target="tpu_custom_call" | custom-call | bytes 1572864 | tf_op jit(solution)/shard_map/pallas_call | solution.py:1649
  438.7 1.3 fusion.2
  441.3 0.8 copy.63
  442.1 0.0 copy-done
  442.2 0.0 copy-done.1
  442.2 0.0 copy-done.2
  442.2 0.7 multiply_subtract_fusion
  442.9 9.0 %shard_map.547 = (f32[4,64,512]{2,1,0:T(8,128)}, f32[2,64,2048]{2,1,0:T(8,128)}, f32[4,32,256]{2,1,0:T(8,128)}, f32[2,32,1024]{2,1,0:T(8,128)}, f32[64,768]{1,0:...) custom-call(f32[8,128]{1,0:T(8,128)} %get-tuple-element.109.sums_ref, ...), custom_call_target="tpu_custom_call" | custom-call | bytes 22675456 | tf_op jit(solution)/shard_map/pallas_call | solution.py:1739
  (4 shorter events, 0.0 us)
Async XLA Ops:
  287.5 154.7 %copy-start = (f32[720]{0:T(1024)S(1)}, f32[720]{0:T(1024)}, u32[]{:S(2)}) copy-start(f32[720]{0:T(1024)} %param.46) | copy-start | bytes 8644
  287.5 154.7 %copy-start.1 = (f32[720]{0:T(1024)S(1)}, f32[720]{0:T(1024)}, u32[]{:S(2)}) copy-start(f32[720]{0:T(1024)} %param.54) | copy-start | bytes 8644
  287.5 154.7 %copy-start.2 = (f32[720]{0:T(1024)S(1)}, f32[720]{0:T(1024)}, u32[]{:S(2)}) copy-start(f32[720]{0:T(1024)} %param.62) | copy-start | bytes 8644
